TPU v7x, 32 devices: a whole 2x2x4 slice. The times are simulated.
32 devices in a mesh: dp: 16 (over z, y, core), tensor: 2 (over x).
Axes of the slice: x: 2, y: 2, z: 4, core: 2. Of those that a mesh axis runs over, the one named last changes fastest.
Arguments:
- layer_input: bfloat16 [16384, 2304], P(('dp', 'tensor')), may hold values from -6 to 6
- query_weight: bfloat16 [2304, 2048], P('dp', 'tensor'), may hold values from -0.125 to 0.125
- key_weight: bfloat16 [2304, 1024], P('dp', 'tensor'), may hold values from -0.125 to 0.125
- value_weight: bfloat16 [2304, 1024], P('dp', 'tensor'), may hold values from -0.125 to 0.125
- w_output: bfloat16 [2048, 2304], P('tensor', 'dp'), may hold values from -0.5 to 0.5
- w_gate: bfloat16 [2304, 9216], P('dp', 'tensor'), may hold values from -0.125 to 0.125
- w_up: bfloat16 [2304, 9216], P('dp', 'tensor'), may hold values from -0.125 to 0.125
- w_down: bfloat16 [9216, 2304], P('tensor', 'dp'), may hold values from -0.0625 to 0.0625
- gain_attn_in: float32 [2304], P(('dp', 'tensor')), may hold values from 0.25 to 1.75
- gain_attn_out: float32 [2304], P(('dp', 'tensor')), may hold values from 0.25 to 1.75
- gain_ffn_in: float32 [2304], P(('dp', 'tensor')), may hold values from 0.25 to 1.75
- gain_ffn_out: float32 [2304], P(('dp', 'tensor')), may hold values from 0.25 to 1.75
- cotangent: bfloat16 [16384, 2304], P(('dp', 'tensor')), may hold values from -6 to 6
Outputs:
- layer_output: bfloat16 [16384, 2304], P(('dp', 'tensor'))
- input_grad: float32 [16384, 2304], P(('dp', 'tensor'))
- grad_query: float32 [2304, 2048], P('dp', 'tensor')
- grad_key: float32 [2304, 1024], P('dp', 'tensor')
- grad_value: float32 [2304, 1024], P('dp', 'tensor')
- grad_output: float32 [2048, 2304], P('tensor', 'dp')
- grad_gate: float32 [2304, 9216], P('dp', 'tensor')
- grad_up: float32 [2304, 9216], P('dp', 'tensor')
- grad_down: float32 [9216, 2304], P('tensor', 'dp')
- grad_attn_in: float32 [2304], P(('dp', 'tensor'))
- grad_attn_out: float32 [2304], P(('dp', 'tensor'))
- grad_ffn_in: float32 [2304], P(('dp', 'tensor'))
- grad_ffn_out: float32 [2304], P(('dp', 'tensor'))
All inputs are finite; a program needn't handle non-finite values.
Results may differ from a plain program's by a relative error of at most 0.018.
Values may be sent and summed in bfloat16 or wider, within the bound.
A program may use at most 512 MiB of HBM per device.

v0:
```python
import jax
import jax.numpy as jnp
from jax import lax
from jax.sharding import PartitionSpec as P

QUERY_HEADS = 8
KEY_VALUE_HEADS = 4
HEAD_WIDTH = 256
SEQ_LEN = 1024


EPSILON = 1e-06
LOGIT_CAP = 50.0


def rms_norm(values, gain):
    return values * lax.rsqrt(jnp.mean(values * values, axis=-1, keepdims=True) + EPSILON) * gain


def matmul(left, right):
    return jnp.dot(left, right, preferred_element_type=jnp.float32)


def matmul_tn(left, right):
    return lax.dot_general(
        left, right, (((0,), (0,)), ((), ())), preferred_element_type=jnp.float32
    )


def matmul_nt(left, right):
    return lax.dot_general(
        left, right, (((1,), (1,)), ((), ())), preferred_element_type=jnp.float32
    )


def spread(rows):
    return lax.all_gather(rows, "tensor", axis=0, tiled=True)


def collect(partial_rows):
    return lax.psum_scatter(partial_rows, "tensor", scatter_dimension=0, tiled=True)


def spread_grad(rows):
    return lax.all_gather(rows, "tensor", axis=0, tiled=True)


def collect_grad(partial_rows):
    return lax.psum_scatter(
        partial_rows.astype(jnp.bfloat16), "tensor", scatter_dimension=0, tiled=True
    ).astype(jnp.float32)


def fetch_attn(query_weight, key_weight, value_weight, w_output):
    return (
        lax.all_gather(query_weight, "dp", axis=0, tiled=True),
        lax.all_gather(key_weight, "dp", axis=0, tiled=True),
        lax.all_gather(value_weight, "dp", axis=0, tiled=True),
        lax.all_gather(w_output, "dp", axis=1, tiled=True),
    )


def fetch_ffn(w_gate, w_up, w_down):
    return (
        lax.all_gather(w_gate, "dp", axis=0, tiled=True),
        lax.all_gather(w_up, "dp", axis=0, tiled=True),
        lax.all_gather(w_down, "dp", axis=1, tiled=True),
    )


def causal_allowed(block_rows, end_row, begin_row):
    key_place = lax.broadcasted_iota(jnp.int32, (block_rows, end_row), 1)
    query_place = lax.broadcasted_iota(jnp.int32, (block_rows, end_row), 0) + begin_row
    return key_place <= query_place


def attend(query_matrix_rows, key_matrix_rows, value_matrix_rows):
    sequence_length = query_matrix_rows.shape[1]
    head_size = query_matrix_rows.shape[4]
    block_rows = min(512, sequence_length)
    score_scale = head_size ** (-0.5)
    out_parts = []
    total_parts = []
    for block_index in range(sequence_length // block_rows):
        begin_row = block_index * block_rows
        end_row = begin_row + block_rows
        query_block = query_matrix_rows[:, begin_row:end_row]
        key_block = key_matrix_rows[:, :end_row]
        value_block = value_matrix_rows[:, :end_row]
        scores = (
            jnp.einsum(
                "sqhgd,skhd->shgqk", query_block, key_block, preferred_element_type=jnp.float32
            )
            * score_scale
        )
        capped = LOGIT_CAP * jnp.tanh(scores / LOGIT_CAP)
        capped = jnp.where(causal_allowed(block_rows, end_row, begin_row), capped, -jnp.inf)
        row_top = jnp.max(capped, axis=-1, keepdims=True)
        exp_terms = jnp.exp(capped - row_top)
        row_total = jnp.sum(exp_terms, axis=-1, keepdims=True)
        soft_low = (exp_terms / row_total).astype(jnp.bfloat16)
        attended = jnp.einsum(
            "shgqk,skhd->sqhgd", soft_low, value_block, preferred_element_type=jnp.float32
        )
        out_parts.append(attended.astype(jnp.bfloat16))
        total_parts.append(row_top + jnp.log(row_total))
    return (jnp.concatenate(out_parts, axis=1), jnp.concatenate(total_parts, axis=3))


def attend_back(query_matrix_rows, key_matrix_rows, value_matrix_rows, log_total, d_attended):
    sequence_length = query_matrix_rows.shape[1]
    head_size = query_matrix_rows.shape[4]
    block_rows = min(512, sequence_length)
    score_scale = head_size ** (-0.5)
    d_query_parts = []
    d_key = jnp.zeros(key_matrix_rows.shape, jnp.float32)
    d_value = jnp.zeros(value_matrix_rows.shape, jnp.float32)
    for block_index in range(sequence_length // block_rows):
        begin_row = block_index * block_rows
        end_row = begin_row + block_rows
        query_block = query_matrix_rows[:, begin_row:end_row]
        key_block = key_matrix_rows[:, :end_row]
        value_block = value_matrix_rows[:, :end_row]
        d_block = d_attended[:, begin_row:end_row]
        scores = (
            jnp.einsum(
                "sqhgd,skhd->shgqk", query_block, key_block, preferred_element_type=jnp.float32
            )
            * score_scale
        )
        tangent = jnp.tanh(scores / LOGIT_CAP)
        capped = jnp.where(
            causal_allowed(block_rows, end_row, begin_row), LOGIT_CAP * tangent, -jnp.inf
        )
        soft_weights = jnp.exp(capped - log_total[:, :, :, begin_row:end_row])
        soft_low = soft_weights.astype(jnp.bfloat16)
        d_soft = jnp.einsum(
            "sqhgd,skhd->shgqk", d_block, value_block, preferred_element_type=jnp.float32
        )
        d_capped = soft_weights * (d_soft - jnp.sum(soft_weights * d_soft, axis=-1, keepdims=True))
        d_scores = (d_capped * (1.0 - tangent * tangent)).astype(jnp.bfloat16)
        d_query_parts.append(
            jnp.einsum("shgqk,skhd->sqhgd", d_scores, key_block, preferred_element_type=jnp.float32)
            * score_scale
        )
        padding = ((0, 0), (0, sequence_length - end_row), (0, 0), (0, 0))
        key_term = (
            jnp.einsum(
                "shgqk,sqhgd->skhd", d_scores, query_block, preferred_element_type=jnp.float32
            )
            * score_scale
        )
        value_term = jnp.einsum(
            "shgqk,sqhgd->skhd", soft_low, d_block, preferred_element_type=jnp.float32
        )
        d_key = d_key + jnp.pad(key_term, padding)
        d_value = d_value + jnp.pad(value_term, padding)
    return (jnp.concatenate(d_query_parts, axis=1), d_key, d_value)


def gelu_product(gate, up_rows):
    return jax.nn.gelu(gate, approximate=True) * up_rows


def body(
    layer_input,
    query_weight,
    key_weight,
    value_weight,
    w_output,
    w_gate,
    w_up,
    w_down,
    gain_attn_in,
    gain_attn_out,
    gain_ffn_in,
    gain_ffn_out,
    cotangent,
):
    gain_a, gain_b, gain_c, gain_d = (
        lax.all_gather(gain_attn_in, ("dp", "tensor"), axis=0, tiled=True),
        lax.all_gather(gain_attn_out, ("dp", "tensor"), axis=0, tiled=True),
        lax.all_gather(gain_ffn_in, ("dp", "tensor"), axis=0, tiled=True),
        lax.all_gather(gain_ffn_out, ("dp", "tensor"), axis=0, tiled=True),
    )
    residual_in = layer_input.astype(jnp.float32)
    full_query, full_key, full_value, full_output = fetch_attn(
        query_weight, key_weight, value_weight, w_output
    )
    normalized_input = spread(rms_norm(residual_in, gain_a).astype(jnp.bfloat16))
    all_rows = normalized_input.shape[0]
    seq_count = all_rows // SEQ_LEN
    kv_local = full_key.shape[1] // HEAD_WIDTH
    head_group = QUERY_HEADS // KEY_VALUE_HEADS
    query_matrix_rows = (
        matmul(normalized_input, full_query)
        .astype(jnp.bfloat16)
        .reshape(seq_count, SEQ_LEN, kv_local, head_group, HEAD_WIDTH)
    )
    key_matrix_rows = (
        matmul(normalized_input, full_key)
        .astype(jnp.bfloat16)
        .reshape(seq_count, SEQ_LEN, kv_local, HEAD_WIDTH)
    )
    value_matrix_rows = (
        matmul(normalized_input, full_value)
        .astype(jnp.bfloat16)
        .reshape(seq_count, SEQ_LEN, kv_local, HEAD_WIDTH)
    )
    attended, log_total = attend(query_matrix_rows, key_matrix_rows, value_matrix_rows)
    attended = attended.reshape(all_rows, kv_local * head_group * HEAD_WIDTH)
    branch_attn = collect(matmul(attended, full_output))
    middle, pull_attn_out = jax.vjp(
        lambda values, gain: residual_in + rms_norm(values, gain), branch_attn, gain_b
    )
    full_gate, full_up, full_down = fetch_ffn(w_gate, w_up, w_down)
    normed_mid_local, pull_ffn_in = jax.vjp(rms_norm, middle, gain_c)
    normed_mid = spread(normed_mid_local.astype(jnp.bfloat16))
    gate = matmul(normed_mid, full_gate)
    up_rows = matmul(normed_mid, full_up)
    hidden_f, pull_glu = jax.vjp(gelu_product, gate, up_rows)
    hidden = hidden_f.astype(jnp.bfloat16)
    branch_ffn = collect(matmul(hidden, full_down))
    ffn_out, pull_ffn_out = jax.vjp(rms_norm, branch_ffn, gain_d)
    layer_output = (middle + ffn_out).astype(jnp.bfloat16)
    upstream = cotangent.astype(jnp.float32)
    d_ffn, grad_d = pull_ffn_out(upstream)
    back_gate, back_up, back_down = fetch_ffn(w_gate, w_up, w_down)
    d_ffn_rows = spread_grad(d_ffn.astype(jnp.bfloat16))
    d_hidden = matmul_nt(d_ffn_rows, back_down)
    d_gate_f, d_up_f = pull_glu(d_hidden)
    d_gate = d_gate_f.astype(jnp.bfloat16)
    d_up = d_up_f.astype(jnp.bfloat16)
    d_normed_mid = matmul_nt(d_gate, back_gate) + matmul_nt(d_up, back_up)
    ff_local = d_gate.shape[1]
    left = normed_mid
    ffn_all = lax.psum_scatter(
        jnp.concatenate(
            [
                jnp.concatenate([matmul_tn(left, d_gate), matmul_tn(left, d_up)], axis=1),
                matmul_tn(d_ffn_rows, hidden),
            ],
            axis=1,
        ),
        "dp",
        scatter_dimension=0,
        tiled=True,
    )
    grad_gate = ffn_all[:, :ff_local]
    grad_up = ffn_all[:, ff_local : 2 * ff_local]
    grad_down = ffn_all[:, 2 * ff_local :].T
    d_mid_norm, grad_c = pull_ffn_in(collect_grad(d_normed_mid))
    d_middle = upstream + d_mid_norm
    d_branch, grad_b = pull_attn_out(d_middle)
    back_query, back_key, back_value, back_output = fetch_attn(
        query_weight, key_weight, value_weight, w_output
    )
    d_branch_rows = spread_grad(d_branch.astype(jnp.bfloat16))
    d_attended = matmul_nt(d_branch_rows, back_output).astype(jnp.bfloat16)
    d_attended = d_attended.reshape(seq_count, SEQ_LEN, kv_local, head_group, HEAD_WIDTH)
    d_query_f, d_key_f, d_value_f = attend_back(
        query_matrix_rows, key_matrix_rows, value_matrix_rows, log_total, d_attended
    )
    query_cols = kv_local * head_group * HEAD_WIDTH
    key_cols = kv_local * HEAD_WIDTH
    d_query = d_query_f.reshape(all_rows, query_cols).astype(jnp.bfloat16)
    d_key = d_key_f.reshape(all_rows, key_cols).astype(jnp.bfloat16)
    d_value = d_value_f.reshape(all_rows, key_cols).astype(jnp.bfloat16)
    d_normed_in = (
        matmul_nt(d_query, back_query) + matmul_nt(d_key, back_key) + matmul_nt(d_value, back_value)
    )
    left = normalized_input
    attn_all = lax.psum_scatter(
        jnp.concatenate(
            [
                matmul_tn(left, d_query),
                matmul_tn(left, d_key),
                matmul_tn(left, d_value),
                matmul_tn(d_branch_rows, attended),
            ],
            axis=1,
        ),
        "dp",
        scatter_dimension=0,
        tiled=True,
    )
    grad_query = attn_all[:, :query_cols]
    grad_key = attn_all[:, query_cols : query_cols + key_cols]
    grad_value = attn_all[:, query_cols + key_cols : query_cols + 2 * key_cols]
    grad_output = attn_all[:, query_cols + 2 * key_cols :].T
    _, pull_attn_in = jax.vjp(rms_norm, residual_in, gain_a)
    d_input_norm, grad_a = pull_attn_in(collect_grad(d_normed_in))
    input_grad = d_middle + d_input_norm
    grad_attn_in, grad_attn_out, grad_ffn_in, grad_ffn_out = (
        lax.psum_scatter(grad_a, ("dp", "tensor"), scatter_dimension=0, tiled=True),
        lax.psum_scatter(grad_b, ("dp", "tensor"), scatter_dimension=0, tiled=True),
        lax.psum_scatter(grad_c, ("dp", "tensor"), scatter_dimension=0, tiled=True),
        lax.psum_scatter(grad_d, ("dp", "tensor"), scatter_dimension=0, tiled=True),
    )
    return (
        layer_output,
        input_grad,
        grad_query,
        grad_key,
        grad_value,
        grad_output,
        grad_gate,
        grad_up,
        grad_down,
        grad_attn_in,
        grad_attn_out,
        grad_ffn_in,
        grad_ffn_out,
    )


def solution(mesh):
    return jax.shard_map(
        body,
        mesh=mesh,
        in_specs=(
            P(("dp", "tensor"), None),
            P("dp", "tensor"),
            P("dp", "tensor"),
            P("dp", "tensor"),
            P("tensor", "dp"),
            P("dp", "tensor"),
            P("dp", "tensor"),
            P("tensor", "dp"),
            P(("dp", "tensor")),
            P(("dp", "tensor")),
            P(("dp", "tensor")),
            P(("dp", "tensor")),
            P(("dp", "tensor"), None),
        ),
        out_specs=(
            P(("dp", "tensor"), None),
            P(("dp", "tensor"), None),
            P("dp", "tensor"),
            P("dp", "tensor"),
            P("dp", "tensor"),
            P("tensor", "dp"),
            P("dp", "tensor"),
            P("dp", "tensor"),
            P("tensor", "dp"),
            P(("dp", "tensor")),
            P(("dp", "tensor")),
            P(("dp", "tensor")),
            P(("dp", "tensor")),
        ),
        check_vma=False,
    )
```

profile of v0, /device:TPU:0, one launch (start us, length us, event | category | flops | bytes accessed | tf_op | source)
XLA Modules:
  0.0 2853.2 jit_solution(10083692894113472531)
XLA Ops:
  11.4 43.6 %all-reduce.11 = (f32[2304]{0:T(1024)S(1)}, f32[2304]{0:T(1024)S(1)}, f32[2304]{0:T(1024)S(1)}, f32[2304]{0:T(1024)}) all-reduce(f32[2304]{0:T(1024)S(1)} %dynamic-update-slice, f32[2304]{0:T(1024)S(1)} %dynamic-update-slice.1, f32[2304]{0:T(1024)S(1)} %dynamic-update-slice.2, ...), channel_id=1, replica_groups=mesh['dp'=16,'tensor'=2] {'dp','tensor'}, use_global_device_ids=true, to_apply=%add.2 | all-reduce | flops 9216 | bytes 73728
  63.4 60.0 %all-gather.12.cloned.1.call-done = bf16[1024,2304]{1,0:T(8,128)(2,1)} async-done(((bf16[512,2304]{1,0:T(8,128)(2,1)}), bf16[1024,2304]{1,0:T(8,128)(2,1)}) %all-gather.12.cloned.1.call-update) | async-done | bytes 4718608 | tf_op jit(solution)/shard_map/all_gather | solution.py:37
  129.2 38.8 %all-gather.14.cloned.1.call-done = bf16[2304,512]{1,0:T(8,128)(2,1)} async-done(((bf16[144,512]{1,0:T(8,128)(2,1)}), bf16[2304,512]{1,0:T(8,128)(2,1)}) %all-gather.14.cloned.1.call-update) | async-done | bytes 2359312 | tf_op jit(solution)/shard_map/all_gather | solution.py:58
  173.8 48.6 %all-gather.18.cloned.1.call-done = bf16[2304,1024]{1,0:T(8,128)(2,1)} async-done(((bf16[144,1024]{1,0:T(8,128)(2,1)}), bf16[2304,1024]{1,0:T(8,128)(2,1)}) %all-gather.18.cloned.1.call-update) | async-done | bytes 4718608 | tf_op jit(solution)/shard_map/all_gather | solution.py:56
  222.4 8.8 convolution_convert_fusion.1
  244.9 31.6 %all-gather.20.cloned.1.call-done = bf16[1024,2304]{0,1:T(8,128)(2,1)} async-done(((bf16[1024,144]{0,1:T(8,128)(2,1)}), bf16[1024,2304]{0,1:T(8,128)(2,1)}) %all-gather.20.cloned.1.call-update) | async-done | bytes 4718608 | tf_op jit(solution)/shard_map/all_gather | solution.py:59
  276.5 9.9 fusion.117
  286.5 109.2 %reduce-scatter.9.cloned.1.call-done = f32[512,2304]{1,0:T(8,128)} async-done(((f32[1024,2304]{1,0:T(8,128)}), f32[512,2304]{1,0:T(8,128)}) %reduce-scatter.9.cloned.1.call-update) | async-done | bytes 4718608 | tf_op jit(solution)/shard_map/reduce_scatter | solution.py:41
  406.8 60.7 %all-gather.22.cloned.1.call-done = bf16[1024,2304]{1,0:T(8,128)(2,1)} async-done(((bf16[512,2304]{1,0:T(8,128)(2,1)}), bf16[1024,2304]{1,0:T(8,128)(2,1)}) %all-gather.22.cloned.1.call-update) | async-done | bytes 4718608 | tf_op jit(solution)/shard_map/all_gather | solution.py:37
  467.5 111.7 %all-gather.24.cloned.1.call-done = bf16[2304,4608]{1,0:T(8,128)(2,1)} async-done(((bf16[144,4608]{1,0:T(8,128)(2,1)}), bf16[2304,4608]{1,0:T(8,128)(2,1)}) %all-gather.24.cloned.1.call-update) | async-done | bytes 21233680 | tf_op jit(solution)/shard_map/all_gather | solution.py:65
  579.2 28.3 fusion.118
  607.5 83.4 %all-gather.26.cloned.1.call-done = bf16[2304,4608]{1,0:T(8,128)(2,1)} async-done(((bf16[144,4608]{1,0:T(8,128)(2,1)}), bf16[2304,4608]{1,0:T(8,128)(2,1)}) %all-gather.26.cloned.1.call-update) | async-done | bytes 21233680 | tf_op jit(solution)/shard_map/all_gather | solution.py:66
  690.9 34.8 %multiply_convert_fusion.1 = (bf16[1024,4608]{1,0:T(8,128)(2,1)}, f32[1024,4608]{1,0:T(8,128)}) fusion(f32[1024,4608]{1,0:T(8,128)} %fusion.118, bf16[1024,2304]{1,0:T(8,128)(2,1)} %all-gather.22.cloned.1.call-done, bf16[2304,4608]{1,0:T(8,128)(2,1)} %all-gather.26.cloned.1.call-done), kind=kOutput, calls=%fused_computation.12 | convolution fusion | flops 21790457856 | bytes 73138176 | tf_op jit(solution)/shard_map/dot_general | solution.py:21
  725.6 76.8 %all-gather.28.cloned.1.call-done = bf16[4608,2304]{0,1:T(8,128)(2,1)} async-done(((bf16[4608,144]{0,1:T(8,128)(2,1)}), bf16[4608,2304]{0,1:T(8,128)(2,1)}) %all-gather.28.cloned.1.call-update) | async-done | bytes 21233680 | tf_op jit(solution)/shard_map/all_gather | solution.py:67
  802.4 30.0 %fusion.119 = f32[1024,2304]{1,0:T(8,128)} fusion(bf16[1024,4608]{1,0:T(8,128)(2,1)} %get-tuple-element.73, bf16[4608,2304]{0,1:T(8,128)(2,1)} %all-gather.28.cloned.1.call-done), kind=kOutput, calls=%fused_computation.169 | convolution fusion | flops 21743271936 | bytes 40108032 | tf_op jit(solution)/shard_map/dot_general | solution.py:21
  832.9 110.2 %reduce-scatter.11.cloned.1.call-done = f32[512,2304]{1,0:T(8,128)} async-done(((f32[1024,2304]{1,0:T(8,128)}), f32[512,2304]{1,0:T(8,128)}) %reduce-scatter.11.cloned.1.call-update) | async-done | bytes 4718608 | tf_op jit(solution)/shard_map/reduce_scatter | solution.py:41
  954.3 62.8 %all-gather.30.cloned.1.call-done = bf16[1024,2304]{1,0:T(8,128)(2,1)} async-done(((bf16[512,2304]{1,0:T(8,128)(2,1)}), bf16[1024,2304]{1,0:T(8,128)(2,1)}) %all-gather.30.cloned.1.call-update) | async-done | bytes 4718608 | tf_op jit(solution)/shard_map/all_gather | solution.py:45
  1017.0 45.6 %multiply_convert_fusion = (bf16[1024,4608]{1,0:T(8,128)(2,1)}, bf16[1024,4608]{1,0:T(8,128)(2,1)}) fusion(f32[1024,4608]{1,0:T(8,128)} %fusion.118, f32[1024,4608]{1,0:T(8,128)} %get-tuple-element.74, bf16[1024,2304]{1,0:T(8,128)(2,1)} %all-gather.30.cloned.1.call-done, bf16[4608,2304]{0,1:T(8,128)(2,1)} %all-gather.28.cloned.1.call-done), kind=kOutput, calls=%fused_computation.11 | convolution fusion | flops 21856518144 | bytes 82575360 | tf_op jit(solution)/shard_map/dot_general | solution.py:31
  1062.7 29.8 %fusion.120 = f32[1024,2304]{1,0:T(8,128)} fusion(bf16[1024,4608]{1,0:T(8,128)(2,1)} %get-tuple-element.59, bf16[2304,4608]{1,0:T(8,128)(2,1)} %all-gather.24.cloned.1.call-done), kind=kOutput, calls=%fused_computation.170 | convolution fusion | flops 21743271936 | bytes 40108032 | tf_op jit(solution)/shard_map/dot_general | solution.py:31
  1092.5 30.5 %add_convert_fusion.1 = bf16[1024,2304]{1,0:T(8,128)(2,1)} fusion(f32[1024,2304]{1,0:T(8,128)} %fusion.120, bf16[1024,4608]{1,0:T(8,128)(2,1)} %get-tuple-element.58, bf16[2304,4608]{1,0:T(8,128)(2,1)} %all-gather.26.cloned.1.call-done), kind=kOutput, calls=%fused_computation.15 | convolution fusion | flops 21747990528 | bytes 44826624 | tf_op jit(solution)/shard_map/dot_general | solution.py:31
  1123.1 60.1 %reduce-scatter.13.cloned.1.call-done = bf16[512,2304]{1,0:T(8,128)(2,1)} async-done(((bf16[1024,2304]{1,0:T(8,128)(2,1)}), bf16[512,2304]{1,0:T(8,128)(2,1)}) %reduce-scatter.13.cloned.1.call-update) | async-done | bytes 2359312 | tf_op jit(solution)/shard_map/reduce_scatter | solution.py:49
  1199.8 62.7 %all-gather.32.cloned.1.call-done = bf16[1024,2304]{1,0:T(8,128)(2,1)} async-done(((bf16[512,2304]{1,0:T(8,128)(2,1)}), bf16[1024,2304]{1,0:T(8,128)(2,1)}) %all-gather.32.cloned.1.call-update) | async-done | bytes 4718608 | tf_op jit(solution)/shard_map/all_gather | solution.py:45
  1262.5 8.7 convolution_convert_fusion
  1336.7 17.2 pad_maximum_fusion.1
  1353.8 27.7 copy.108
  1381.7 36.1 %fusion.125 = f32[2304,4608]{1,0:T(8,128)} fusion(bf16[1024,2304]{1,0:T(8,128)(2,1)} %all-gather.30.cloned.1.call-done, bf16[1024,4608]{1,0:T(8,128)(2,1)} %get-tuple-element.73), kind=kOutput, calls=%fused_computation.175 | convolution fusion | flops 21743271936 | bytes 56623104 | tf_op jit(solution)/shard_map/dot_general | solution.py:25
  1417.8 31.6 %fusion.124 = f32[2304,4608]{1,0:T(8,128)} fusion(bf16[1024,2304]{1,0:T(8,128)(2,1)} %all-gather.22.cloned.1.call-done, bf16[1024,4608]{1,0:T(8,128)(2,1)} %get-tuple-element.58), kind=kOutput, calls=%fused_computation.174 | convolution fusion | flops 21743271936 | bytes 56623104 | tf_op jit(solution)/shard_map/dot_general | solution.py:25
  1449.4 27.5 fusion.123
  1476.9 85.3 %pad_maximum_fusion = f32[2304,13824]{1,0:T(8,128)} fusion(f32[2304,4608]{1,0:T(8,128)} %fusion.125, f32[2304,4608]{1,0:T(8,128)} %fusion.124, f32[2304,4608]{1,0:T(8,128)} %fusion.123), kind=kLoop, calls=%fused_computation | loop fusion | flops 63700992 | bytes 254803968 | tf_op jit(solution)/shard_map/concatenate | solution.py:238
  1567.6 41.8 %all-reduce.10 = (f32[2304]{0:T(1024)S(1)}, f32[2304]{0:T(1024)S(1)}, f32[2304]{0:T(1024)S(1)}, f32[2304]{0:T(1024)S(1)}) all-reduce(f32[2304]{0:T(1024)S(1)} %get-tuple-element.45, f32[2304]{0:T(1024)S(1)} %copy-done.28, f32[2304]{0:T(1024)S(1)} %copy-done.31, ...), channel_id=8, replica_groups=mesh['dp'=16,'tensor'=2] {'dp','tensor'}, use_global_device_ids=true, to_apply=%region_21.22.clone | all-reduce | flops 9216 | bytes 73728
  1618.3 33.8 %reduce-scatter.19.cloned.1.call-done = f32[144,3072]{1,0:T(8,128)} async-done(((f32[2304,3072]{1,0:T(8,128)}), f32[144,3072]{1,0:T(8,128)}) %reduce-scatter.19.cloned.1.call-update) | async-done | bytes 1769488
  1656.4 1183.0 %reduce-scatter.17.cloned.1.call-done = f32[144,13824]{1,0:T(8,128)} async-done(((f32[2304,13824]{1,0:T(8,128)}), f32[144,13824]{1,0:T(8,128)}) %reduce-scatter.17.cloned.1.call-update) | async-done | bytes 7962640 | tf_op jit(solution)/shard_map/reduce_scatter | solution.py:237
  (257 shorter events, 167.0 us)
Async XLA Ops:
  7.2 56.3 %all-gather.16.cloned.1.call-start = ((), (), s32[]{:S(2)}) async-start(), calls=%async_computation.8 | async-start | bytes 2506752 | tf_op jit(solution)/shard_map/all_gather | solution.py:57
  7.9 115.6 %all-gather.12.cloned.1.call-start = ((), (), s32[]{:S(2)}) async-start(), calls=%async_computation.6 | async-start | bytes 7077888 | tf_op jit(solution)/shard_map/all_gather | solution.py:37
  55.0 344.1 %copy-start.22 = (f32[2304]{0:T(1024)}, f32[2304]{0:T(1024)S(1)}, u32[]{:S(2)}) copy-start(f32[2304]{0:T(1024)S(1)} %get-tuple-element.52) | copy-start | bytes 27652
  55.0 346.1 %copy-start.26 = (f32[2304]{0:T(1024)}, f32[2304]{0:T(1024)S(1)}, u32[]{:S(2)}) copy-start(f32[2304]{0:T(1024)S(1)} %get-tuple-element.53) | copy-start | bytes 27652
  60.9 107.1 %all-gather.14.cloned.1.call-start = ((), (), s32[]{:S(2)}) async-start(), calls=%async_computation.7 | async-start | bytes 2506752 | tf_op jit(solution)/shard_map/all_gather | solution.py:58
  61.7 160.7 %all-gather.18.cloned.1.call-start = ((), (), s32[]{:S(2)}) async-start(), calls=%async_computation.9 | async-start | bytes 5013504 | tf_op jit(solution)/shard_map/all_gather | solution.py:56
  62.2 214.2 %all-gather.20.cloned.1.call-start = ((), (), s32[]{:S(2)}) async-start(), calls=%async_computation.10 | async-start | bytes 5013504 | tf_op jit(solution)/shard_map/all_gather | solution.py:59
  62.8 332.8 %reduce-scatter.9.cloned.1.call-start = ((), (), s32[]{:S(2)}) async-start(), calls=%async_computation.11 | async-start | bytes 14155776 | tf_op jit(solution)/shard_map/reduce_scatter | solution.py:41
  63.0 176.0 %copy-start.14 = (pred[512,512]{0,1:T(8,128)(4,1)}, pred[512,512]{0,1:T(8,128)(4,1)S(1)}, u32[]{:S(2)}) copy-start(pred[512,512]{0,1:T(8,128)(4,1)S(1)} %iota_compare_fusion.1) | copy-start | bytes 786436
  63.4 177.5 %copy-start.11 = (pred[512,1024]{0,1:T(8,128)(4,1)}, pred[512,1024]{0,1:T(8,128)(4,1)S(1)}, u32[]{:S(2)}) copy-start(pred[512,1024]{0,1:T(8,128)(4,1)S(1)} %iota_compare_fusion) | copy-start | bytes 1572868
  129.2 104.6 %copy-start.20 = (bf16[1024,512]{0,1:T(8,128)(2,1)}, bf16[1024,512]{0,1:T(8,128)(2,1)S(1)}, u32[]{:S(2)}) copy-start(bf16[1024,512]{0,1:T(8,128)(2,1)S(1)} %convolution_convert_fusion.2) | copy-start | bytes 3145732
  173.8 67.1 %copy-start.55 = (bf16[1024,512]{0,1:T(8,128)(2,1)}, bf16[1024,512]{0,1:T(8,128)(2,1)S(1)}, u32[]{:S(2)}) copy-start(bf16[1024,512]{0,1:T(8,128)(2,1)S(1)} %convolution_convert_fusion.3) | copy-start | bytes 3145732
  286.4 112.7 %copy-start.2 = (bf16[512,2304]{1,0:T(8,128)(2,1)S(1)}, bf16[512,2304]{1,0:T(8,128)(2,1)}, u32[]{:S(2)}) copy-start(bf16[512,2304]{1,0:T(8,128)(2,1)} %param.13) | copy-start | bytes 7077892
  286.4 181.1 %all-gather.22.cloned.1.call-start = ((), (), s32[]{:S(2)}) async-start(), calls=%async_computation.12 | async-start | bytes 7077888 | tf_op jit(solution)/shard_map/all_gather | solution.py:37
  404.6 174.5 %all-gather.24.cloned.1.call-start = ((), (), s32[]{:S(2)}) async-start(), calls=%async_computation.13 | async-start | bytes 22560768 | tf_op jit(solution)/shard_map/all_gather | solution.py:65
  405.4 285.5 %all-gather.26.cloned.1.call-start = ((), (), s32[]{:S(2)}) async-start(), calls=%async_computation.14 | async-start | bytes 22560768 | tf_op jit(solution)/shard_map/all_gather | solution.py:66
  406.1 396.3 %all-gather.28.cloned.1.call-start = ((), (), s32[]{:S(2)}) async-start(), calls=%async_computation.15 | async-start | bytes 22560768 | tf_op jit(solution)/shard_map/all_gather | solution.py:67
  406.7 536.5 %reduce-scatter.11.cloned.1.call-start = ((), (), s32[]{:S(2)}) async-start(), calls=%async_computation.16 | async-start | bytes 14155776 | tf_op jit(solution)/shard_map/reduce_scatter | solution.py:41
  832.5 113.6 %copy-start.7 = (bf16[512,2304]{1,0:T(8,128)(2,1)S(1)}, bf16[512,2304]{1,0:T(8,128)(2,1)}, u32[]{:S(2)}) copy-start(bf16[512,2304]{1,0:T(8,128)(2,1)} %param.25) | copy-start | bytes 7077892
  832.5 113.6 %copy-start.29 = (f32[2304]{0:T(1024)S(1)}, f32[2304]{0:T(1024)}, u32[]{:S(2)}) copy-start(f32[2304]{0:T(1024)} %get-tuple-element.54) | copy-start | bytes 27652
  832.5 184.5 %all-gather.30.cloned.1.call-start = ((), (), s32[]{:S(2)}) async-start(), calls=%async_computation.17 | async-start | bytes 7077888 | tf_op jit(solution)/shard_map/all_gather | solution.py:45
  954.2 229.0 %reduce-scatter.13.cloned.1.call-start = ((), (), s32[]{:S(2)}) async-start(), calls=%async_computation.18 | async-start | bytes 7077888 | tf_op jit(solution)/shard_map/reduce_scatter | solution.py:49
  1123.0 65.5 %copy-start.8 = (bf16[512,2304]{1,0:T(8,128)(2,1)S(1)}, bf16[512,2304]{1,0:T(8,128)(2,1)}, u32[]{:S(2)}) copy-start(bf16[512,2304]{1,0:T(8,128)(2,1)} %param.25) | copy-start | bytes 7077892
  1123.1 65.5 %copy-start.23 = (f32[2304]{0:T(1024)S(1)}, f32[2304]{0:T(1024)}, u32[]{:S(2)}) copy-start(f32[2304]{0:T(1024)} %copy-done.22) | copy-start | bytes 27652
  1123.1 139.4 %all-gather.32.cloned.1.call-start = ((), (), s32[]{:S(2)}) async-start(), calls=%async_computation.19 | async-start | bytes 7077888 | tf_op jit(solution)/shard_map/all_gather | solution.py:45
  1199.7 362.6 %reduce-scatter.15.cloned.1.call-start = ((), (), s32[]{:S(2)}) async-start(), calls=%async_computation.20 | async-start | bytes 7077888 | tf_op jit(solution)/shard_map/reduce_scatter | solution.py:49
  1199.8 71.4 %copy-start.15 = (pred[512,512]{0,1:T(8,128)(4,1)S(1)}, pred[512,512]{0,1:T(8,128)(4,1)}, u32[]{:S(2)}) copy-start(pred[512,512]{0,1:T(8,128)(4,1)} %copy-done.14) | copy-start | bytes 786436
  1310.5 341.6 %reduce-scatter.19.cloned.1.call-start = ((), (), s32[]{:S(2)}) async-start(), calls=%async_computation.22 | async-start | bytes 30081024
  1381.6 1457.9 %reduce-scatter.17.cloned.1.call-start = ((), (), s32[]{:S(2)}) async-start(), calls=%async_computation.21 | async-start | bytes 135364608 | tf_op jit(solution)/shard_map/reduce_scatter | solution.py:237
  1381.6 67.7 %slice-start.8 = ((s8[4718592]{0:T(1024)(128)(4,1)}), s8[4194304]{0:T(1024)(128)(4,1)S(1)}, s32[]{:S(2)}) async-start(s8[4718592]{0:T(1024)(128)(4,1)} %bitcast.338), calls=%async_computation.31 | async-start | bytes 8388608
  1381.6 67.7 %slice-start.12 = ((s8[9437184]{0:T(1024)(128)(4,1)}), s8[4194304]{0:T(1024)(128)(4,1)S(1)}, s32[]{:S(2)}) async-start(s8[9437184]{0:T(1024)(128)(4,1)} %bitcast.356), calls=%async_computation.35 | async-start | bytes 8388608
  1381.7 67.7 %slice-start.13 = ((s8[9437184]{0:T(1024)(128)(4,1)}), s8[4194304]{0:T(1024)(128)(4,1)S(1)}, s32[]{:S(2)}) async-start(s8[9437184]{0:T(1024)(128)(4,1)} %bitcast.356), calls=%async_computation.36 | async-start | bytes 8388608
  (58 other events, 630.7 us)
Sparse Core Ops, SparseCore 0:
  10.3 44.9 all-gather.15
  61.0 62.3 all-gather.11
  125.8 42.2 all-gather.13
  170.2 52.1 all-gather.17
  224.5 51.9 all-gather.19
  286.5 109.0 reduce-scatter.8
  404.8 62.6 all-gather.21
  469.1 110.0 all-gather.23
  580.8 110.0 all-gather.25
  692.3 110.0 all-gather.27
  832.6 110.5 reduce-scatter.10
  954.3 62.6 all-gather.29
  1123.2 59.9 reduce-scatter.12
  1199.8 62.6 all-gather.31
  1310.6 59.9 reduce-scatter.14
  1381.7 270.4 reduce-scatter.18
  1656.3 1183.1 reduce-scatter.16
where the time goes:
time: 2860 us; the launch traced here: 2850 us
  waiting for transfers between devices  2140 us (75%)
  matrix products  401 us (14%)
  other arithmetic  160 us (6%)
  blocking collectives  85.4 us (3%)
  local copies, waits for them, and re-layouts  52.4 us (2%)
    reduce_scatter x1, waiting for transfers between devices, body(): lax.psum_scatter(jnp.concatenate([jnp.concatenate([matmul_tn(left, d_gate...  1180 us
    reduce_scatter x2, waiting for transfers between devices, collect(): lax.psum_scatter(partial_rows, 'tensor', scatter_dimension=0, tiled=True)  219 us
    dot_general x7, matrix products, matmul_nt(): lax.dot_general(left, right, (((1,), (1,)), ((), ())), preferred_element_...  132 us
    all_gather x2, waiting for transfers between devices, spread_grad(): return lax.all_gather(rows, 'tensor', axis=0, tiled=True)  125 us
    dot_general x7, matrix products, matmul(): return jnp.dot(left, right, preferred_element_type=jnp.float32)  123 us
    dot_general x7, matrix products, matmul_tn(): lax.dot_general(left, right, (((0,), (0,)), ((), ())), preferred_element_...  121 us
    all_gather x2, waiting for transfers between devices, spread(): return lax.all_gather(rows, 'tensor', axis=0, tiled=True)  121 us
    all_gather x1, waiting for transfers between devices, fetch_ffn(): lax.all_gather(w_gate, 'dp', axis=0, tiled=True)  112 us
  transfers between devices with their start and end apart: 17, of which 15 were waited for; matrix products, arithmetic and copies ran while one was open for 13% of the time, Pallas kernels for 0%

commit v1 on v0

v1 whole, which is shorter than its diff:
```python
import jax
import jax.numpy as jnp
from jax import lax
from jax.sharding import PartitionSpec as P

QUERY_HEADS = 8
KEY_VALUE_HEADS = 4
HEAD_WIDTH = 256
SEQ_LEN = 1024


EPSILON = 1e-06
LOGIT_CAP = 50.0

BF16 = jnp.bfloat16
F32 = jnp.float32


def rms_norm(values, gain):
    return values * lax.rsqrt(jnp.mean(values * values, axis=-1, keepdims=True) + EPSILON) * gain


def matmul(left, right):
    return jnp.dot(left, right, preferred_element_type=F32)


def matmul_nt(left, right):
    return lax.dot_general(left, right, (((1,), (1,)), ((), ())), preferred_element_type=F32)


def swap(rows):
    return lax.ppermute(rows, "tensor", [(0, 1), (1, 0)])


def flip(array, bit, dp):
    return lax.ppermute(array, "dp", [(i, i ^ (1 << bit)) for i in range(dp)])


def gather_small(piece, dp):
    other = swap(piece)
    whole = jnp.where(
        lax.axis_index("tensor") == 0,
        jnp.concatenate([piece, other], axis=1),
        jnp.concatenate([other, piece], axis=1),
    )
    bit = 0
    while (1 << bit) < dp:
        other = flip(whole, bit, dp)
        high = (lax.axis_index("dp") >> bit) & 1
        whole = jnp.where(
            high == 0,
            jnp.concatenate([whole, other], axis=1),
            jnp.concatenate([other, whole], axis=1),
        )
        bit += 1
    return whole


def scatter_small(partial, dp):
    bit = dp.bit_length() - 2
    while bit >= 0:
        half = partial.shape[1] // 2
        low, high = partial[:, :half], partial[:, half:]
        mine = (lax.axis_index("dp") >> bit) & 1
        keep = jnp.where(mine == 0, low, high)
        give = jnp.where(mine == 0, high, low)
        partial = keep + flip(give, bit, dp)
        bit -= 1
    half = partial.shape[1] // 2
    low, high = partial[:, :half], partial[:, half:]
    mine = lax.axis_index("tensor")
    keep = jnp.where(mine == 0, low, high)
    give = jnp.where(mine == 0, high, low)
    return keep + swap(give)


def pick(array, index, axis):
    return lax.dynamic_index_in_dim(array, index, axis, keepdims=False)


def scatter_grad(left_t, right, dp):
    width, tokens = left_t.shape
    columns = right.shape[1]
    rest, rows = dp // 4, width // dp
    me = lax.axis_index("dp")
    core, side, place = me & 1, (me >> 1) & 1, me >> 2
    blocks = left_t.reshape(rest, 2, 2, rows, tokens)

    def product(part):
        flat = part.reshape(-1, tokens)
        return matmul(flat, right).reshape(part.shape[:-1] + (columns,))

    give = product(pick(blocks, 1 - core, 2)).astype(BF16)
    from_core = flip(give, 0, dp)
    mine = pick(blocks, core, 2)
    give = (
        product(pick(mine, 1 - side, 1)) + pick(from_core, 1 - side, 1).astype(F32)
    ).astype(BF16)
    from_side = flip(give, 1, dp)
    total = (
        product(pick(mine, side, 1))
        + pick(from_core, side, 1).astype(F32)
        + from_side.astype(F32)
    ).astype(BF16)
    result = pick(total, place, 0).astype(F32)
    for shift in range(1, rest):
        give = pick(total, (place + shift) % rest, 0)
        pairs = [(i, (i + 4 * shift) % dp) for i in range(dp)]
        result = result + lax.ppermute(give, "dp", pairs).astype(F32)
    return result


def causal_allowed(block_rows, end_row, begin_row):
    key_place = lax.broadcasted_iota(jnp.int32, (block_rows, end_row), 1)
    query_place = lax.broadcasted_iota(jnp.int32, (block_rows, end_row), 0) + begin_row
    return key_place <= query_place


def attend(query_matrix_rows, key_matrix_rows, value_matrix_rows):
    sequence_length = query_matrix_rows.shape[1]
    head_size = query_matrix_rows.shape[4]
    block_rows = min(512, sequence_length)
    score_scale = head_size ** (-0.5)
    out_parts = []
    total_parts = []
    for block_index in range(sequence_length // block_rows):
        begin_row = block_index * block_rows
        end_row = begin_row + block_rows
        query_block = query_matrix_rows[:, begin_row:end_row]
        key_block = key_matrix_rows[:, :end_row]
        value_block = value_matrix_rows[:, :end_row]
        scores = (
            jnp.einsum("sqhgd,skhd->shgqk", query_block, key_block, preferred_element_type=F32)
            * score_scale
        )
        capped = LOGIT_CAP * jnp.tanh(scores / LOGIT_CAP)
        capped = jnp.where(causal_allowed(block_rows, end_row, begin_row), capped, -jnp.inf)
        row_top = jnp.max(capped, axis=-1, keepdims=True)
        exp_terms = jnp.exp(capped - row_top)
        row_total = jnp.sum(exp_terms, axis=-1, keepdims=True)
        soft_low = (exp_terms / row_total).astype(BF16)
        attended = jnp.einsum(
            "shgqk,skhd->sqhgd", soft_low, value_block, preferred_element_type=F32
        )
        out_parts.append(attended.astype(BF16))
        total_parts.append(row_top + jnp.log(row_total))
    return (jnp.concatenate(out_parts, axis=1), jnp.concatenate(total_parts, axis=3))


def attend_back(query_matrix_rows, key_matrix_rows, value_matrix_rows, log_total, d_attended):
    sequence_length = query_matrix_rows.shape[1]
    head_size = query_matrix_rows.shape[4]
    block_rows = min(512, sequence_length)
    score_scale = head_size ** (-0.5)
    d_query_parts = []
    d_key = jnp.zeros(key_matrix_rows.shape, F32)
    d_value = jnp.zeros(value_matrix_rows.shape, F32)
    for block_index in range(sequence_length // block_rows):
        begin_row = block_index * block_rows
        end_row = begin_row + block_rows
        query_block = query_matrix_rows[:, begin_row:end_row]
        key_block = key_matrix_rows[:, :end_row]
        value_block = value_matrix_rows[:, :end_row]
        d_block = d_attended[:, begin_row:end_row]
        scores = (
            jnp.einsum("sqhgd,skhd->shgqk", query_block, key_block, preferred_element_type=F32)
            * score_scale
        )
        tangent = jnp.tanh(scores / LOGIT_CAP)
        capped = jnp.where(
            causal_allowed(block_rows, end_row, begin_row), LOGIT_CAP * tangent, -jnp.inf
        )
        soft_weights = jnp.exp(capped - log_total[:, :, :, begin_row:end_row])
        soft_low = soft_weights.astype(BF16)
        d_soft = jnp.einsum(
            "sqhgd,skhd->shgqk", d_block, value_block, preferred_element_type=F32
        )
        d_capped = soft_weights * (d_soft - jnp.sum(soft_weights * d_soft, axis=-1, keepdims=True))
        d_scores = (d_capped * (1.0 - tangent * tangent)).astype(BF16)
        d_query_parts.append(
            jnp.einsum("shgqk,skhd->sqhgd", d_scores, key_block, preferred_element_type=F32)
            * score_scale
        )
        padding = ((0, 0), (0, sequence_length - end_row), (0, 0), (0, 0))
        key_term = (
            jnp.einsum("shgqk,sqhgd->skhd", d_scores, query_block, preferred_element_type=F32)
            * score_scale
        )
        value_term = jnp.einsum(
            "shgqk,sqhgd->skhd", soft_low, d_block, preferred_element_type=F32
        )
        d_key = d_key + jnp.pad(key_term, padding)
        d_value = d_value + jnp.pad(value_term, padding)
    return (jnp.concatenate(d_query_parts, axis=1), d_key, d_value)


def gelu_product(gate, up_rows):
    return jax.nn.gelu(gate, approximate=True) * up_rows


def make_body(dp):
    def in_order(rows):
        other = swap(rows)
        return jnp.where(
            lax.axis_index("tensor") == 0,
            jnp.concatenate([rows, other], axis=0),
            jnp.concatenate([other, rows], axis=0),
        )

    def own_first(rows):
        return jnp.concatenate([rows, swap(rows)], axis=0)

    def collect_in_order(partial):
        half = partial.shape[0] // 2
        first = lax.axis_index("tensor") == 0
        low, high = partial[:half], partial[half:]
        give = jnp.where(first, high, low).astype(BF16)
        return jnp.where(first, low, high) + swap(give).astype(F32)

    def collect_own_first(partial):
        half = partial.shape[0] // 2
        return partial[:half] + swap(partial[half:].astype(BF16)).astype(F32)

    def body(
        layer_input,
        query_weight,
        key_weight,
        value_weight,
        w_output,
        w_gate,
        w_up,
        w_down,
        gain_attn_in,
        gain_attn_out,
        gain_ffn_in,
        gain_ffn_out,
        cotangent,
    ):
        gains = gather_small(
            jnp.stack([gain_attn_in, gain_attn_out, gain_ffn_in, gain_ffn_out]), dp
        )
        gain_a, gain_b, gain_c, gain_d = gains[0], gains[1], gains[2], gains[3]
        query_cols, key_cols = query_weight.shape[1], key_weight.shape[1]
        ff_local = w_gate.shape[1]
        qkv_cols = query_cols + 2 * key_cols
        full_attn = lax.all_gather(
            jnp.concatenate([query_weight, key_weight, value_weight, w_output.T], axis=1),
            "dp",
            axis=0,
            tiled=True,
        )
        full_qkv, full_output_t = full_attn[:, :qkv_cols], full_attn[:, qkv_cols:]
        full_gate = lax.all_gather(w_gate, "dp", axis=0, tiled=True)
        full_up = lax.all_gather(w_up, "dp", axis=0, tiled=True)
        full_down_t = lax.all_gather(w_down.T, "dp", axis=0, tiled=True)

        residual_in = layer_input.astype(F32)
        normalized_input = in_order(rms_norm(residual_in, gain_a).astype(BF16))
        all_rows = normalized_input.shape[0]
        seq_count = all_rows // SEQ_LEN
        kv_local = key_cols // HEAD_WIDTH
        head_group = QUERY_HEADS // KEY_VALUE_HEADS
        qkv = matmul(normalized_input, full_qkv).astype(BF16)
        query_matrix_rows = qkv[:, :query_cols].reshape(
            seq_count, SEQ_LEN, kv_local, head_group, HEAD_WIDTH
        )
        key_matrix_rows = qkv[:, query_cols : query_cols + key_cols].reshape(
            seq_count, SEQ_LEN, kv_local, HEAD_WIDTH
        )
        value_matrix_rows = qkv[:, query_cols + key_cols :].reshape(
            seq_count, SEQ_LEN, kv_local, HEAD_WIDTH
        )
        attended, log_total = attend(query_matrix_rows, key_matrix_rows, value_matrix_rows)
        attended = attended.reshape(all_rows, query_cols)
        branch_attn = collect_in_order(matmul_nt(attended, full_output_t))
        middle, pull_attn_out = jax.vjp(
            lambda values, gain: residual_in + rms_norm(values, gain), branch_attn, gain_b
        )
        normed_mid_local, pull_ffn_in = jax.vjp(rms_norm, middle, gain_c)
        normed_mid = own_first(normed_mid_local.astype(BF16))
        gate = matmul(normed_mid, full_gate)
        up_rows = matmul(normed_mid, full_up)
        hidden_f, pull_glu = jax.vjp(gelu_product, gate, up_rows)
        hidden = hidden_f.astype(BF16)
        branch_ffn = collect_own_first(matmul_nt(hidden, full_down_t))
        ffn_out, pull_ffn_out = jax.vjp(rms_norm, branch_ffn, gain_d)
        layer_output = (middle + ffn_out).astype(BF16)
        upstream = cotangent.astype(F32)
        d_ffn, grad_d = pull_ffn_out(upstream)
        d_ffn_rows = own_first(d_ffn.astype(BF16))
        grad_down = scatter_grad(d_ffn_rows.T, hidden, dp).T
        d_hidden = matmul(d_ffn_rows, full_down_t)
        d_gate_f, d_up_f = pull_glu(d_hidden)
        d_gate = d_gate_f.astype(BF16)
        d_up = d_up_f.astype(BF16)
        d_normed_mid = matmul_nt(d_gate, full_gate) + matmul_nt(d_up, full_up)
        normed_mid_t = normed_mid.T
        grad_gate = scatter_grad(normed_mid_t, d_gate, dp)
        grad_up = scatter_grad(normed_mid_t, d_up, dp)
        d_mid_norm, grad_c = pull_ffn_in(collect_own_first(d_normed_mid))
        d_middle = upstream + d_mid_norm
        d_branch, grad_b = pull_attn_out(d_middle)
        d_branch_rows = in_order(d_branch.astype(BF16))
        grad_output = scatter_grad(d_branch_rows.T, attended, dp).T
        d_attended = matmul(d_branch_rows, full_output_t).astype(BF16)
        d_attended = d_attended.reshape(seq_count, SEQ_LEN, kv_local, head_group, HEAD_WIDTH)
        d_query_f, d_key_f, d_value_f = attend_back(
            query_matrix_rows, key_matrix_rows, value_matrix_rows, log_total, d_attended
        )
        d_qkv = jnp.concatenate(
            [
                d_query_f.reshape(all_rows, query_cols).astype(BF16),
                d_key_f.reshape(all_rows, key_cols).astype(BF16),
                d_value_f.reshape(all_rows, key_cols).astype(BF16),
            ],
            axis=1,
        )
        grad_qkv = scatter_grad(normalized_input.T, d_qkv, dp)
        d_normed_in = matmul_nt(d_qkv, full_qkv)
        grad_query = grad_qkv[:, :query_cols]
        grad_key = grad_qkv[:, query_cols : query_cols + key_cols]
        grad_value = grad_qkv[:, query_cols + key_cols :]
        _, pull_attn_in = jax.vjp(rms_norm, residual_in, gain_a)
        d_input_norm, grad_a = pull_attn_in(collect_in_order(d_normed_in))
        input_grad = d_middle + d_input_norm
        small = scatter_small(jnp.stack([grad_a, grad_b, grad_c, grad_d]), dp)
        return (
            layer_output,
            input_grad,
            grad_query,
            grad_key,
            grad_value,
            grad_output,
            grad_gate,
            grad_up,
            grad_down,
            small[0],
            small[1],
            small[2],
            small[3],
        )

    return body


def solution(mesh):
    rows = P(("dp", "tensor"), None)
    gain = P(("dp", "tensor"))
    into, out_of = P("dp", "tensor"), P("tensor", "dp")
    return jax.shard_map(
        make_body(mesh.shape["dp"]),
        mesh=mesh,
        in_specs=(rows, into, into, into, out_of, into, into, out_of, gain, gain, gain, gain, rows),
        out_specs=(rows, rows, into, into, into, out_of, into, into, out_of, gain, gain, gain, gain),
        check_vma=False,
    )
```

time: 2860 us -> 1640 us (0.57)
  waiting for transfers between devices: 2140 us -> 970 us
  blocking collectives: 85.4 us -> 0 us
  other arithmetic: 160 us -> 92.6 us
  starting transfers between devices: 1.09 us -> 54.4 us
  matrix products: 401 us -> 431 us
    reduce_scatter x5 -> x0, waiting for transfers between devices: 1460 us -> none  [the longest x1 1180 us: body(): lax.psum_scatter(jnp.concatenate([jnp.concatenate([matmul_tn(left, d_gate...]
    ppermute x0 -> x43, waiting for transfers between devices: none -> 832 us  [the longest x10 331 us: swap(): return lax.ppermute(rows, 'tensor', [(0, 1), (1, 0)])]
    all_gather x11 -> x4, waiting for transfers between devices: 637 us -> 136 us  [the longest x1 77.3 us: body(): full_down_t = lax.all_gather(w_down.T, 'dp', axis=0, tiled=True)]
    concatenate x2 -> x1, other arithmetic: 103 us -> 2.32 us  [body(): jnp.concatenate([query_weight, key_weight, value_weight, w_output.T], axi...]
    unnamed x2 -> x0, blocking collectives: 85.4 us -> none
    ppermute x0 -> x43, starting transfers between devices: none -> 54.3 us  [the longest x15 19.6 us: scatter_grad(): result = result + lax.ppermute(give, 'dp', pairs).astype(F32)]
    dot_general x14 -> x20, matrix products: 244 us -> 288 us  [matmul(): return jnp.dot(left, right, preferred_element_type=F32)]
    unnamed x18 -> x4, waiting for transfers between devices: 38.3 us -> 1.92 us
  transfers between devices with their start and end apart: 17 -> 47, of which waited for: 15 -> 27; matrix products, arithmetic and copies ran while one was open for 13% -> 26% of each run, Pallas kernels for 0% -> 0%
where the time goes in v1:
time: 1640 us
  waiting for transfers between devices  970 us (59%)
  matrix products  431 us (26%)
  other arithmetic  92.6 us (6%)
  local copies, waits for them, and re-layouts  73.9 us (5%)
  starting transfers between devices  54.4 us (3%)
    ppermute x10, waiting for transfers between devices, swap(): return lax.ppermute(rows, 'tensor', [(0, 1), (1, 0)])  331 us
    ppermute x18, waiting for transfers between devices, flip(): return lax.ppermute(array, 'dp', [(i, i ^ 1 << bit) for i in range(dp)])  293 us
    dot_general x20, matrix products, matmul(): return jnp.dot(left, right, preferred_element_type=F32)  288 us
    ppermute x15, waiting for transfers between devices, scatter_grad(): result = result + lax.ppermute(give, 'dp', pairs).astype(F32)  209 us
    dot_general x5, matrix products, matmul_nt(): lax.dot_general(left, right, (((1,), (1,)), ((), ())), preferred_element_...  111 us
    all_gather x1, waiting for transfers between devices, body(): full_down_t = lax.all_gather(w_down.T, 'dp', axis=0, tiled=True)  77.3 us
    all_gather x1, waiting for transfers between devices, body(): lax.all_gather(jnp.concatenate([query_weight, key_weight, value_weight, w...  40.3 us
  transfers between devices with their start and end apart: 47, of which 27 were waited for; matrix products, arithmetic and copies ran while one was open for 26% of the time, Pallas kernels for 0%

profile of v1, /device:TPU:0, one launch (start us, length us, event | category | flops | bytes accessed | tf_op | source)
XLA Modules:
  0.0 1637.0 jit_solution(4444237598641196801)
XLA Ops:
  37.7 47.0 %collective-permute-done.5 = bf16[512,2304]{1,0:T(8,128)(2,1)} collective-permute-done((bf16[512,2304]{1,0:T(8,128)(2,1)S(1)}, bf16[512,2304]{1,0:T(8,128)(2,1)}, u32[]{:S(2)}, u32[]{:S(2)}) %collective-permute-start.5) | collective-permute-done | bytes 2359328 | tf_op jit(solution)/shard_map/ppermute | solution.py:32
  84.7 40.3 %all-gather.5.cloned.1.call-done = bf16[2304,3072]{1,0:T(8,128)(2,1)} async-done(((bf16[144,3072]{1,0:T(8,128)(2,1)}), bf16[2304,3072]{1,0:T(8,128)(2,1)}) %all-gather.5.cloned.1.call-update) | async-done | bytes 14155792 | tf_op jit(solution)/shard_map/all_gather | solution.py:246
  125.0 17.1 %fusion.83 = bf16[1024,2048]{1,0:T(8,128)(2,1)S(1)} fusion(bf16[2304,3072]{1,0:T(8,128)(2,1)} %all-gather.5.cloned.1.call-done, bf16[512,2304]{1,0:T(8,128)(2,1)} %collective-permute-done.5, bf16[512,2304]{1,0:T(8,128)(2,1)} %copy-done.10, pred[]{:T(512)S(6)} %eq.45), kind=kOutput, calls=%fused_computation.147 | convolution fusion | flops 9687007232 | bytes 18350080 | tf_op jit(solution)/shard_map/dot_general | solution.py:24
  190.4 51.8 %collective-permute-done.6 = bf16[512,2304]{1,0:T(8,128)(2,1)S(1)} collective-permute-done((bf16[512,2304]{1,0:T(8,128)(2,1)S(1)}, bf16[512,2304]{1,0:T(8,128)(2,1)S(1)}, u32[]{:S(2)}, u32[]{:S(2)}) %collective-permute-start.6) | collective-permute-done | bytes 2359328 | tf_op jit(solution)/shard_map/ppermute | solution.py:32
  249.7 51.1 %collective-permute-done.7 = bf16[512,2304]{1,0:T(8,128)(2,1)} collective-permute-done((bf16[512,2304]{1,0:T(8,128)(2,1)S(1)}, bf16[512,2304]{1,0:T(8,128)(2,1)}, u32[]{:S(2)}, u32[]{:S(2)}) %collective-permute-start.7) | collective-permute-done | bytes 2359328 | tf_op jit(solution)/shard_map/ppermute | solution.py:32
  300.9 27.6 %fusion.165 = f32[1024,4608]{1,0:T(8,128)} fusion(bf16[2304,4608]{1,0:T(8,128)(2,1)} %all-gather.7.cloned.1.call-done, bf16[512,2304]{1,0:T(8,128)(2,1)} %collective-permute-done.7, bf16[512,2304]{1,0:T(8,128)(2,1)S(1)} %multiply_convert_fusion.2), kind=kOutput, calls=%fused_computation.211 | convolution fusion | flops 21752709120 | bytes 44826624 | tf_op jit(solution)/shard_map/dot_general | solution.py:24
  328.5 18.1 %all-gather.9.cloned.1.call-done = bf16[2304,4608]{1,0:T(8,128)(2,1)} async-done(((bf16[144,4608]{1,0:T(8,128)(2,1)}), bf16[2304,4608]{1,0:T(8,128)(2,1)}) %all-gather.9.cloned.1.call-update) | async-done | bytes 21233680 | tf_op jit(solution)/shard_map/all_gather | solution.py:254
  346.5 34.2 %multiply_convert_fusion.1 = (bf16[1024,4608]{1,0:T(8,128)(2,1)}, f32[1024,4608]{1,0:T(8,128)}) fusion(f32[1024,4608]{1,0:T(8,128)} %fusion.165, bf16[2304,4608]{1,0:T(8,128)(2,1)} %all-gather.9.cloned.1.call-done, bf16[512,2304]{1,0:T(8,128)(2,1)} %collective-permute-done.7, bf16[512,2304]{1,0:T(8,128)(2,1)S(1)} %multiply_convert_fusion.2), kind=kOutput, calls=%fused_computation.10 | convolution fusion | flops 21799895040 | bytes 73138176 | tf_op jit(solution)/shard_map/dot_general | solution.py:24
  380.8 77.3 %all-gather.11.cloned.1.call-done = bf16[2304,4608]{1,0:T(8,128)(2,1)} async-done(((bf16[144,4608]{1,0:T(8,128)(2,1)}), bf16[2304,4608]{1,0:T(8,128)(2,1)}) %all-gather.11.cloned.1.call-update) | async-done | bytes 21233680 | tf_op jit(solution)/shard_map/all_gather | solution.py:255
  458.1 27.0 %fusion.271 = f32[1024,2304]{1,0:T(8,128)S(1)} fusion(bf16[1024,4608]{1,0:T(8,128)(2,1)} %get-tuple-element.64, bf16[2304,4608]{1,0:T(8,128)(2,1)} %all-gather.11.cloned.1.call-done), kind=kOutput, calls=%fused_computation.342 | convolution fusion | flops 21743271936 | bytes 40108032 | tf_op jit(solution)/shard_map/dot_general | solution.py:28
  486.8 51.9 %collective-permute-done.8 = bf16[512,2304]{1,0:T(8,128)(2,1)S(1)} collective-permute-done((bf16[512,2304]{1,0:T(8,128)(2,1)S(1)}, bf16[512,2304]{1,0:T(8,128)(2,1)S(1)}, u32[]{:S(2)}, u32[]{:S(2)}) %collective-permute-start.8) | collective-permute-done | bytes 2359328 | tf_op jit(solution)/shard_map/ppermute | solution.py:32
  548.8 51.1 %collective-permute-done.9 = bf16[512,2304]{1,0:T(8,128)(2,1)S(1)} collective-permute-done((bf16[512,2304]{1,0:T(8,128)(2,1)S(1)}, bf16[512,2304]{1,0:T(8,128)(2,1)S(1)}, u32[]{:S(2)}, u32[]{:S(2)}) %collective-permute-start.9) | collective-permute-done | bytes 2359328 | tf_op jit(solution)/shard_map/ppermute | solution.py:32
  600.0 45.6 %multiply_convert_fusion = (bf16[1024,4608]{1,0:T(8,128)(2,1)}, bf16[1024,4608]{1,0:T(8,128)(2,1)}) fusion(f32[1024,4608]{1,0:T(8,128)} %fusion.165, f32[1024,4608]{1,0:T(8,128)} %get-tuple-element.65, bf16[2304,4608]{1,0:T(8,128)(2,1)} %all-gather.11.cloned.1.call-done, bf16[512,2304]{1,0:T(8,128)(2,1)S(1)} %collective-permute-done.9, ...), kind=kOutput, calls=%fused_computation.9 | convolution fusion | flops 21865955328 | bytes 82575360 | tf_op jit(solution)/shard_map/dot_general | solution.py:24
  645.6 29.9 %fusion.272 = f32[1024,2304]{1,0:T(8,128)} fusion(bf16[1024,4608]{1,0:T(8,128)(2,1)} %get-tuple-element.32, bf16[2304,4608]{1,0:T(8,128)(2,1)} %all-gather.7.cloned.1.call-done), kind=kOutput, calls=%fused_computation.343 | convolution fusion | flops 21743271936 | bytes 40108032 | tf_op jit(solution)/shard_map/dot_general | solution.py:28
  675.5 31.2 %convolution_add_fusion = f32[1024,2304]{1,0:T(8,128)} fusion(f32[1024,2304]{1,0:T(8,128)} %fusion.272, bf16[1024,4608]{1,0:T(8,128)(2,1)} %get-tuple-element.31, bf16[2304,4608]{1,0:T(8,128)(2,1)} %all-gather.9.cloned.1.call-done), kind=kOutput, calls=%fused_computation.66 | convolution fusion | flops 21745631232 | bytes 49545216 | tf_op jit(solution)/shard_map/dot_general | solution.py:28
  749.5 13.1 collective-permute-done.10
  777.9 17.1 %convolution_convert_fusion.2 = bf16[4,2,144,4608]{3,2,0,1:T(8,128)(2,1)} fusion(bf16[1024,4608]{1,0:T(8,128)(2,1)} %get-tuple-element.32, bf16[4,2,2,144,1024]{4,3,2,1,0:T(8,128)(2,1)S(1)} %bitcast.512, s32[]{:T(128)S(6)} %select_n.276), kind=kOutput, calls=%fused_computation.29 | convolution fusion | flops 10876944384 | bytes 22413316 | tf_op jit(solution)/shard_map/dot_general | solution.py:24
  795.2 32.0 %collective-permute-done.11 = bf16[512,2304]{1,0:T(8,128)(2,1)S(1)} collective-permute-done((bf16[512,2304]{1,0:T(8,128)(2,1)S(1)}, bf16[512,2304]{1,0:T(8,128)(2,1)S(1)}, u32[]{:S(2)}, u32[]{:S(2)}) %collective-permute-start.11) | collective-permute-done | bytes 2359328 | tf_op jit(solution)/shard_map/ppermute | solution.py:32
  871.0 15.0 fusion.34
  893.3 17.6 %convolution_convert_fusion.1 = bf16[4,2,144,4608]{3,2,0,1:T(8,128)(2,1)} fusion(bf16[1024,4608]{1,0:T(8,128)(2,1)} %get-tuple-element.31, bf16[4,2,2,144,1024]{4,3,2,1,0:T(8,128)(2,1)} %bitcast.509, s32[]{:T(128)S(6)} %select_n.276), kind=kOutput, calls=%fused_computation.28 | convolution fusion | flops 10876944384 | bytes 22413316 | tf_op jit(solution)/shard_map/dot_general | solution.py:24
  911.0 31.0 %collective-permute-done.12 = bf16[512,2304]{1,0:T(8,128)(2,1)} collective-permute-done((bf16[512,2304]{1,0:T(8,128)(2,1)}, bf16[512,2304]{1,0:T(8,128)(2,1)}, u32[]{:S(2)}, u32[]{:S(2)}) %collective-permute-start.12) | collective-permute-done | bytes 2359328 | tf_op jit(solution)/shard_map/ppermute | solution.py:32
  949.6 17.1 %convolution_convert_fusion = bf16[4,2,144,4608]{3,2,0,1:T(8,128)(2,1)} fusion(bf16[1024,4608]{1,0:T(8,128)(2,1)} %get-tuple-element.64, bf16[4,2,2,144,1024]{4,3,2,1,0:T(8,128)(2,1)S(1)} %bitcast.504, s32[]{:T(128)S(6)} %select_n.276), kind=kOutput, calls=%fused_computation.27 | convolution fusion | flops 10876944384 | bytes 22413316 | tf_op jit(solution)/shard_map/dot_general | solution.py:24
  1015.8 12.0 fusion.13
  1042.7 12.1 fusion.10
  1054.9 31.7 %collective-permute-done.14 = bf16[4,144,2048]{2,1,0:T(8,128)(2,1)} collective-permute-done((bf16[4,144,2048]{2,1,0:T(8,128)(2,1)}, bf16[4,144,2048]{2,1,0:T(8,128)(2,1)}, u32[]{:S(2)}, u32[]{:S(2)}) %collective-permute-start.14) | collective-permute-done | bytes 2359328 | tf_op jit(solution)/shard_map/ppermute | solution.py:36
  1097.7 11.8 fusion.7
  1120.8 23.8 %collective-permute-done.16 = bf16[144,2048]{1,0:T(8,128)(2,1)S(1)} collective-permute-done((bf16[144,2048]{1,0:T(8,128)(2,1)S(1)}, bf16[144,2048]{1,0:T(8,128)(2,1)S(1)}, u32[]{:S(2)}, u32[]{:S(2)}) %collective-permute-start.16) | collective-permute-done | bytes 589856 | tf_op jit(solution)/shard_map/ppermute | solution.py:109
  1146.7 53.6 %collective-permute-done.24 = bf16[4,144,4608]{2,1,0:T(8,128)(2,1)} collective-permute-done((bf16[4,144,4608]{2,1,0:T(8,128)(2,1)}, bf16[4,144,4608]{2,1,0:T(8,128)(2,1)}, u32[]{:S(2)}, u32[]{:S(2)}) %collective-permute-start.24) | collective-permute-done | bytes 5308448 | tf_op jit(solution)/shard_map/ppermute | solution.py:36
  1217.9 96.2 %collective-permute-done.29 = bf16[4,144,4608]{2,1,0:T(8,128)(2,1)} collective-permute-done((bf16[4,144,4608]{2,1,0:T(8,128)(2,1)}, bf16[4,144,4608]{2,1,0:T(8,128)(2,1)}, u32[]{:S(2)}, u32[]{:S(2)}) %collective-permute-start.29) | collective-permute-done | bytes 5308448 | tf_op jit(solution)/shard_map/ppermute | solution.py:36
  1329.1 97.5 %collective-permute-done.34 = bf16[4,144,4608]{2,1,0:T(8,128)(2,1)} collective-permute-done((bf16[4,144,4608]{2,1,0:T(8,128)(2,1)}, bf16[4,144,4608]{2,1,0:T(8,128)(2,1)}, u32[]{:S(2)}, u32[]{:S(2)}) %collective-permute-start.34) | collective-permute-done | bytes 5308448 | tf_op jit(solution)/shard_map/ppermute | solution.py:36
  1460.1 113.3 %collective-permute-done.31 = bf16[144,4608]{1,0:T(8,128)(2,1)S(1)} collective-permute-done((bf16[144,4608]{1,0:T(8,128)(2,1)}, bf16[144,4608]{1,0:T(8,128)(2,1)S(1)}, u32[]{:S(2)}, u32[]{:S(2)}) %collective-permute-start.31) | collective-permute-done | bytes 1327136 | tf_op jit(solution)/shard_map/ppermute | solution.py:109
  1577.2 50.9 %collective-permute-done.36 = bf16[144,4608]{1,0:T(8,128)(2,1)S(1)} collective-permute-done((bf16[144,4608]{1,0:T(8,128)(2,1)S(1)}, bf16[144,4608]{1,0:T(8,128)(2,1)S(1)}, u32[]{:S(2)}, u32[]{:S(2)}) %collective-permute-start.36) | collective-permute-done | bytes 1327136 | tf_op jit(solution)/shard_map/ppermute | solution.py:109
  (405 shorter events, 374.2 us)
Async XLA Ops:
  7.2 117.7 %all-gather.5.cloned.1.call-start = ((), (), s32[]{:S(2)}) async-start(), calls=%async_computation | async-start | bytes 15040512 | tf_op jit(solution)/shard_map/all_gather | solution.py:246
  9.6 291.3 %all-gather.7.cloned.1.call-start = ((), (), s32[]{:S(2)}) async-start(), calls=%async_computation.1 | async-start | bytes 22560768 | tf_op jit(solution)/shard_map/all_gather | solution.py:253
  10.4 336.2 %all-gather.9.cloned.1.call-start = ((), (), s32[]{:S(2)}) async-start(), calls=%async_computation.2 | async-start | bytes 22560768 | tf_op jit(solution)/shard_map/all_gather | solution.py:254
  11.1 447.0 %all-gather.11.cloned.1.call-start = ((), (), s32[]{:S(2)}) async-start(), calls=%async_computation.3 | async-start | bytes 22560768 | tf_op jit(solution)/shard_map/all_gather | solution.py:255
  34.2 50.5 %collective-permute-start.5 = (bf16[512,2304]{1,0:T(8,128)(2,1)S(1)}, bf16[512,2304]{1,0:T(8,128)(2,1)}, u32[]{:S(2)}, u32[]{:S(2)}) collective-permute-start(bf16[512,2304]{1,0:T(8,128)(2,1)S(1)} %fusion.44), channel_id=1, source_target_pairs={{0,1},{1,0},{2,3},{3,2},{4,5},{5,4},{6,7},{7,6},{8,9},{9,8},{10,11... | collective-permute-start | bytes 7077896 | tf_op jit(solution)/shard_map/ppermute | solution.py:32
  188.9 53.4 %collective-permute-start.6 = (bf16[512,2304]{1,0:T(8,128)(2,1)S(1)}, bf16[512,2304]{1,0:T(8,128)(2,1)S(1)}, u32[]{:S(2)}, u32[]{:S(2)}) collective-permute-start(bf16[512,2304]{1,0:T(8,128)(2,1)S(1)} %select_convert_fusion.1), channel_id=1, source_target_pairs={{0,1},{1,0},{2,3},{3,2},{4,5},{5,4},{6,7},{7,6},{8,9},{9,8},{10,11... | collective-permute-start | bytes 7077896 | tf_op jit(solution)/shard_map/ppermute | solution.py:32
  248.2 52.7 %collective-permute-start.7 = (bf16[512,2304]{1,0:T(8,128)(2,1)S(1)}, bf16[512,2304]{1,0:T(8,128)(2,1)}, u32[]{:S(2)}, u32[]{:S(2)}) collective-permute-start(bf16[512,2304]{1,0:T(8,128)(2,1)S(1)} %multiply_convert_fusion.2), channel_id=1, source_target_pairs={{0,1},{1,0},{2,3},{3,2},{4,5},{5,4},{6,7},{7,6},{8,9},{9,8},{10,11... | collective-permute-start | bytes 7077896 | tf_op jit(solution)/shard_map/ppermute | solution.py:32
  485.3 53.5 %collective-permute-start.8 = (bf16[512,2304]{1,0:T(8,128)(2,1)S(1)}, bf16[512,2304]{1,0:T(8,128)(2,1)S(1)}, u32[]{:S(2)}, u32[]{:S(2)}) collective-permute-start(bf16[512,2304]{1,0:T(8,128)(2,1)S(1)} %slice.280), channel_id=1, source_target_pairs={{0,1},{1,0},{2,3},{3,2},{4,5},{5,4},{6,7},{7,6},{8,9},{9,8},{10,11... | collective-permute-start | bytes 7077896 | tf_op jit(solution)/shard_map/ppermute | solution.py:32
  547.4 52.6 %collective-permute-start.9 = (bf16[512,2304]{1,0:T(8,128)(2,1)S(1)}, bf16[512,2304]{1,0:T(8,128)(2,1)S(1)}, u32[]{:S(2)}, u32[]{:S(2)}) collective-permute-start(bf16[512,2304]{1,0:T(8,128)(2,1)S(1)} %get-tuple-element.33), channel_id=1, source_target_pairs={{0,1},{1,0},{2,3},{3,2},{4,5},{5,4},{6,7},{7,6},{8,9},{9,8},{10,11... | collective-permute-start | bytes 7077896 | tf_op jit(solution)/shard_map/ppermute | solution.py:32
  710.7 51.9 %collective-permute-start.10 = (bf16[512,2304]{1,0:T(8,128)(2,1)}, bf16[512,2304]{1,0:T(8,128)(2,1)S(1)}, u32[]{:S(2)}, u32[]{:S(2)}) collective-permute-start(bf16[512,2304]{1,0:T(8,128)(2,1)} %slice.279), channel_id=1, source_target_pairs={{0,1},{1,0},{2,3},{3,2},{4,5},{5,4},{6,7},{7,6},{8,9},{9,8},{10,11... | collective-permute-start | bytes 7077896 | tf_op jit(solution)/shard_map/ppermute | solution.py:32
  776.4 50.8 %collective-permute-start.11 = (bf16[512,2304]{1,0:T(8,128)(2,1)S(1)}, bf16[512,2304]{1,0:T(8,128)(2,1)S(1)}, u32[]{:S(2)}, u32[]{:S(2)}) collective-permute-start(bf16[512,2304]{1,0:T(8,128)(2,1)S(1)} %fusion.49), channel_id=1, source_target_pairs={{0,1},{1,0},{2,3},{3,2},{4,5},{5,4},{6,7},{7,6},{8,9},{9,8},{10,11... | collective-permute-start | bytes 7077896 | tf_op jit(solution)/shard_map/ppermute | solution.py:32
  795.1 220.7 %collective-permute-start.23 = (bf16[4,2,144,4608]{3,2,0,1:T(8,128)(2,1)}, bf16[4,2,144,4608]{3,2,0,1:T(8,128)(2,1)}, u32[]{:S(2)}, u32[]{:S(2)}) collective-permute-start(bf16[4,2,144,4608]{3,2,0,1:T(8,128)(2,1)} %convolution_convert_fusion.2), channel_id=1, source_target_pairs={{0,2},{2,0},{4,6},{6,4},{8,10},{10,8},{12,14},{14,12},{16,18},{18,... | collective-permute-start | bytes 31850504 | tf_op jit(solution)/shard_map/ppermute | solution.py:36
  891.8 50.2 %collective-permute-start.12 = (bf16[512,2304]{1,0:T(8,128)(2,1)}, bf16[512,2304]{1,0:T(8,128)(2,1)}, u32[]{:S(2)}, u32[]{:S(2)}) collective-permute-start(bf16[512,2304]{1,0:T(8,128)(2,1)} %select_convert_fusion), channel_id=1, source_target_pairs={{0,1},{1,0},{2,3},{3,2},{4,5},{5,4},{6,7},{7,6},{8,9},{9,8},{10,11... | collective-permute-start | bytes 7077896 | tf_op jit(solution)/shard_map/ppermute | solution.py:32
  910.9 129.2 %collective-permute-start.28 = (bf16[4,2,144,4608]{3,2,0,1:T(8,128)(2,1)}, bf16[4,2,144,4608]{3,2,0,1:T(8,128)(2,1)}, u32[]{:S(2)}, u32[]{:S(2)}) collective-permute-start(bf16[4,2,144,4608]{3,2,0,1:T(8,128)(2,1)} %convolution_convert_fusion.1), channel_id=1, source_target_pairs={{0,2},{2,0},{4,6},{6,4},{8,10},{10,8},{12,14},{14,12},{16,18},{18,... | collective-permute-start | bytes 31850504 | tf_op jit(solution)/shard_map/ppermute | solution.py:36
  966.7 131.0 %collective-permute-start.33 = (bf16[4,2,144,4608]{3,2,0,1:T(8,128)(2,1)}, bf16[4,2,144,4608]{3,2,0,1:T(8,128)(2,1)}, u32[]{:S(2)}, u32[]{:S(2)}) collective-permute-start(bf16[4,2,144,4608]{3,2,0,1:T(8,128)(2,1)} %convolution_convert_fusion), channel_id=1, source_target_pairs={{0,2},{2,0},{4,6},{6,4},{8,10},{10,8},{12,14},{14,12},{16,18},{18,... | collective-permute-start | bytes 31850504 | tf_op jit(solution)/shard_map/ppermute | solution.py:36
  977.2 32.1 %collective-permute-start.13 = (bf16[4,2,144,2048]{3,2,0,1:T(8,128)(2,1)}, bf16[4,2,144,2048]{3,2,0,1:T(8,128)(2,1)}, u32[]{:S(2)}, u32[]{:S(2)}) collective-permute-start(bf16[4,2,144,2048]{3,2,0,1:T(8,128)(2,1)} %fusion.79), channel_id=1, source_target_pairs={{0,2},{2,0},{4,6},{6,4},{8,10},{10,8},{12,14},{14,12},{16,18},{18,... | collective-permute-start | bytes 14155784 | tf_op jit(solution)/shard_map/ppermute | solution.py:36
  1015.4 71.2 %collective-permute-start.14 = (bf16[4,144,2048]{2,1,0:T(8,128)(2,1)}, bf16[4,144,2048]{2,1,0:T(8,128)(2,1)}, u32[]{:S(2)}, u32[]{:S(2)}) collective-permute-start(bf16[4,144,2048]{2,1,0:T(8,128)(2,1)} %fusion.53), channel_id=1, source_target_pairs={{0,4},{2,6},{4,0},{6,2},{8,12},{10,14},{12,8},{14,10},{16,20},{18,... | collective-permute-start | bytes 7077896 | tf_op jit(solution)/shard_map/ppermute | solution.py:36
  1027.9 172.5 %collective-permute-start.24 = (bf16[4,144,4608]{2,1,0:T(8,128)(2,1)}, bf16[4,144,4608]{2,1,0:T(8,128)(2,1)}, u32[]{:S(2)}, u32[]{:S(2)}) collective-permute-start(bf16[4,144,4608]{2,1,0:T(8,128)(2,1)} %fusion.13), channel_id=1, source_target_pairs={{0,4},{2,6},{4,0},{6,2},{8,12},{10,14},{12,8},{14,10},{16,20},{18,... | collective-permute-start | bytes 15925256 | tf_op jit(solution)/shard_map/ppermute | solution.py:36
  1040.1 53.7 %collective-permute-start.22 = (bf16[144,1024]{1,0:T(8,128)(2,1)S(1)}, bf16[144,1024]{1,0:T(8,128)(2,1)S(1)}, u32[]{:S(2)}, u32[]{:S(2)}) collective-permute-start(bf16[144,1024]{1,0:T(8,128)(2,1)S(1)} %get-tuple-element.52), channel_id=1, source_target_pairs={{0,24},{2,26},{4,28},{6,30},{8,0},{10,2},{12,4},{14,6},{16,8},{18,... | collective-permute-start | bytes 884744 | tf_op jit(solution)/shard_map/ppermute | solution.py:109
  1054.8 39.5 %collective-permute-start.21 = (bf16[144,1024]{1,0:T(8,128)(2,1)S(1)}, bf16[144,1024]{1,0:T(8,128)(2,1)S(1)}, u32[]{:S(2)}, u32[]{:S(2)}) collective-permute-start(bf16[144,1024]{1,0:T(8,128)(2,1)S(1)} %get-tuple-element.53), channel_id=1, source_target_pairs={{0,16},{2,18},{4,20},{6,22},{8,24},{10,26},{12,28},{14,30},{16,0},... | collective-permute-start | bytes 884744 | tf_op jit(solution)/shard_map/ppermute | solution.py:109
  1086.6 227.5 %collective-permute-start.29 = (bf16[4,144,4608]{2,1,0:T(8,128)(2,1)}, bf16[4,144,4608]{2,1,0:T(8,128)(2,1)}, u32[]{:S(2)}, u32[]{:S(2)}) collective-permute-start(bf16[4,144,4608]{2,1,0:T(8,128)(2,1)} %fusion.10), channel_id=1, source_target_pairs={{0,4},{2,6},{4,0},{6,2},{8,12},{10,14},{12,8},{14,10},{16,20},{18,... | collective-permute-start | bytes 15925256 | tf_op jit(solution)/shard_map/ppermute | solution.py:36
  1097.7 46.9 %collective-permute-start.16 = (bf16[144,2048]{1,0:T(8,128)(2,1)S(1)}, bf16[144,2048]{1,0:T(8,128)(2,1)S(1)}, u32[]{:S(2)}, u32[]{:S(2)}) collective-permute-start(bf16[144,2048]{1,0:T(8,128)(2,1)S(1)} %get-tuple-element.48), channel_id=1, source_target_pairs={{0,16},{2,18},{4,20},{6,22},{8,24},{10,26},{12,28},{14,30},{16,0},... | collective-permute-start | bytes 1769480 | tf_op jit(solution)/shard_map/ppermute | solution.py:109
  1111.9 314.7 %collective-permute-start.34 = (bf16[4,144,4608]{2,1,0:T(8,128)(2,1)}, bf16[4,144,4608]{2,1,0:T(8,128)(2,1)}, u32[]{:S(2)}, u32[]{:S(2)}) collective-permute-start(bf16[4,144,4608]{2,1,0:T(8,128)(2,1)} %fusion.7), channel_id=1, source_target_pairs={{0,4},{2,6},{4,0},{6,2},{8,12},{10,14},{12,8},{14,10},{16,20},{18,... | collective-permute-start | bytes 15925256 | tf_op jit(solution)/shard_map/ppermute | solution.py:36
  1214.0 225.3 %collective-permute-start.25 = (bf16[144,4608]{1,0:T(8,128)(2,1)}, bf16[144,4608]{1,0:T(8,128)(2,1)S(1)}, u32[]{:S(2)}, u32[]{:S(2)}) collective-permute-start(bf16[144,4608]{1,0:T(8,128)(2,1)} %get-tuple-element.41), channel_id=1, source_target_pairs={{0,8},{2,10},{4,12},{6,14},{8,16},{10,18},{12,20},{14,22},{16,24},... | collective-permute-start | bytes 3981320 | tf_op jit(solution)/shard_map/ppermute | solution.py:109
  1215.3 225.9 %collective-permute-start.27 = (bf16[144,4608]{1,0:T(8,128)(2,1)}, bf16[144,4608]{1,0:T(8,128)(2,1)}, u32[]{:S(2)}, u32[]{:S(2)}) collective-permute-start(bf16[144,4608]{1,0:T(8,128)(2,1)} %get-tuple-element.42), channel_id=1, source_target_pairs={{0,24},{2,26},{4,28},{6,30},{8,0},{10,2},{12,4},{14,6},{16,8},{18,... | collective-permute-start | bytes 3981320 | tf_op jit(solution)/shard_map/ppermute | solution.py:109
  1217.8 224.0 %collective-permute-start.26 = (bf16[144,4608]{1,0:T(8,128)(2,1)}, bf16[144,4608]{1,0:T(8,128)(2,1)}, u32[]{:S(2)}, u32[]{:S(2)}) collective-permute-start(bf16[144,4608]{1,0:T(8,128)(2,1)} %get-tuple-element.43), channel_id=1, source_target_pairs={{0,16},{2,18},{4,20},{6,22},{8,24},{10,26},{12,28},{14,30},{16,0},... | collective-permute-start | bytes 3981320 | tf_op jit(solution)/shard_map/ppermute | solution.py:109
  1327.9 117.2 %collective-permute-start.30 = (bf16[144,4608]{1,0:T(8,128)(2,1)}, bf16[144,4608]{1,0:T(8,128)(2,1)}, u32[]{:S(2)}, u32[]{:S(2)}) collective-permute-start(bf16[144,4608]{1,0:T(8,128)(2,1)} %get-tuple-element.38), channel_id=1, source_target_pairs={{0,8},{2,10},{4,12},{6,14},{8,16},{10,18},{12,20},{14,22},{16,24},... | collective-permute-start | bytes 3981320 | tf_op jit(solution)/shard_map/ppermute | solution.py:109
  1426.6 33.5 %collective-permute-start.32 = (bf16[144,4608]{1,0:T(8,128)(2,1)}, bf16[144,4608]{1,0:T(8,128)(2,1)}, u32[]{:S(2)}, u32[]{:S(2)}) collective-permute-start(bf16[144,4608]{1,0:T(8,128)(2,1)} %get-tuple-element.39), channel_id=1, source_target_pairs={{0,24},{2,26},{4,28},{6,30},{8,0},{10,2},{12,4},{14,6},{16,8},{18,... | collective-permute-start | bytes 3981320 | tf_op jit(solution)/shard_map/ppermute | solution.py:109
  1439.4 134.0 %collective-permute-start.31 = (bf16[144,4608]{1,0:T(8,128)(2,1)}, bf16[144,4608]{1,0:T(8,128)(2,1)S(1)}, u32[]{:S(2)}, u32[]{:S(2)}) collective-permute-start(bf16[144,4608]{1,0:T(8,128)(2,1)} %get-tuple-element.40), channel_id=1, source_target_pairs={{0,16},{2,18},{4,20},{6,22},{8,24},{10,26},{12,28},{14,30},{16,0},... | collective-permute-start | bytes 3981320 | tf_op jit(solution)/shard_map/ppermute | solution.py:109
  1441.2 136.0 %collective-permute-start.35 = (bf16[144,4608]{1,0:T(8,128)(2,1)S(1)}, bf16[144,4608]{1,0:T(8,128)(2,1)S(1)}, u32[]{:S(2)}, u32[]{:S(2)}) collective-permute-start(bf16[144,4608]{1,0:T(8,128)(2,1)S(1)} %get-tuple-element.35), channel_id=1, source_target_pairs={{0,8},{2,10},{4,12},{6,14},{8,16},{10,18},{12,20},{14,22},{16,24},... | collective-permute-start | bytes 3981320 | tf_op jit(solution)/shard_map/ppermute | solution.py:109
  1441.8 135.4 %collective-permute-start.37 = (bf16[144,4608]{1,0:T(8,128)(2,1)S(1)}, bf16[144,4608]{1,0:T(8,128)(2,1)S(1)}, u32[]{:S(2)}, u32[]{:S(2)}) collective-permute-start(bf16[144,4608]{1,0:T(8,128)(2,1)S(1)} %get-tuple-element.36), channel_id=1, source_target_pairs={{0,24},{2,26},{4,28},{6,30},{8,0},{10,2},{12,4},{14,6},{16,8},{18,... | collective-permute-start | bytes 3981320 | tf_op jit(solution)/shard_map/ppermute | solution.py:109
  1445.1 183.0 %collective-permute-start.36 = (bf16[144,4608]{1,0:T(8,128)(2,1)S(1)}, bf16[144,4608]{1,0:T(8,128)(2,1)S(1)}, u32[]{:S(2)}, u32[]{:S(2)}) collective-permute-start(bf16[144,4608]{1,0:T(8,128)(2,1)S(1)} %get-tuple-element.37), channel_id=1, source_target_pairs={{0,16},{2,18},{4,20},{6,22},{8,24},{10,26},{12,28},{14,30},{16,0},... | collective-permute-start | bytes 3981320 | tf_op jit(solution)/shard_map/ppermute | solution.py:109
  (115 other events, 2349.4 us)
Sparse Core Ops, SparseCore 0:
  10.9 113.9 all-gather.4
  126.6 108.2 all-gather.6
  236.4 110.0 all-gather.8
  348.0 110.0 all-gather.10

commit v2 on v1

v2 whole, which is shorter than its diff:
```python
import jax
import jax.numpy as jnp
from jax import lax
from jax.sharding import PartitionSpec as P

QUERY_HEADS = 8
KEY_VALUE_HEADS = 4
HEAD_WIDTH = 256
SEQ_LEN = 1024


EPSILON = 1e-06
LOGIT_CAP = 50.0

BF16 = jnp.bfloat16
F32 = jnp.float32


def rms_norm(values, gain):
    return values * lax.rsqrt(jnp.mean(values * values, axis=-1, keepdims=True) + EPSILON) * gain


def matmul(left, right):
    return jnp.dot(left, right, preferred_element_type=F32)


def matmul_nt(left, right):
    return lax.dot_general(left, right, (((1,), (1,)), ((), ())), preferred_element_type=F32)


def swap(rows):
    return lax.ppermute(rows, "tensor", [(0, 1), (1, 0)])


def flip(array, bit, dp):
    return lax.ppermute(array, "dp", [(i, i ^ (1 << bit)) for i in range(dp)])


def gather_small(piece, dp):
    other = swap(piece)
    whole = jnp.where(
        lax.axis_index("tensor") == 0,
        jnp.concatenate([piece, other], axis=1),
        jnp.concatenate([other, piece], axis=1),
    )
    bit = 0
    while (1 << bit) < dp:
        other = flip(whole, bit, dp)
        high = (lax.axis_index("dp") >> bit) & 1
        whole = jnp.where(
            high == 0,
            jnp.concatenate([whole, other], axis=1),
            jnp.concatenate([other, whole], axis=1),
        )
        bit += 1
    return whole


def scatter_small(partial, dp):
    bit = dp.bit_length() - 2
    while bit >= 0:
        half = partial.shape[1] // 2
        low, high = partial[:, :half], partial[:, half:]
        mine = (lax.axis_index("dp") >> bit) & 1
        keep = jnp.where(mine == 0, low, high)
        give = jnp.where(mine == 0, high, low)
        partial = keep + flip(give, bit, dp)
        bit -= 1
    half = partial.shape[1] // 2
    low, high = partial[:, :half], partial[:, half:]
    mine = lax.axis_index("tensor")
    keep = jnp.where(mine == 0, low, high)
    give = jnp.where(mine == 0, high, low)
    return keep + swap(give)


def tied(*arrays):
    return lax.optimization_barrier(arrays)


def pick(array, index, axis):
    return lax.dynamic_index_in_dim(array, index, axis, keepdims=False)


class Scatter:
    def __init__(self, dp, chunks):
        self.dp, self.chunks = dp, chunks
        me = lax.axis_index("dp")
        self.core, self.side = me & 1, (me >> 1) & 1
        self.taken = []

    def product(self, part, right):
        flat = part.reshape(-1, part.shape[-1])
        return matmul(flat, right).reshape(part.shape[:-1] + (right.shape[1],))

    def give(self, left_t, right):
        width, tokens = left_t.shape
        self.left, self.right = left_t.reshape(self.dp // 4, 2, 2, width // self.dp, tokens), right
        self.given = self.product(pick(self.left, 1 - self.core, 2), right).astype(BF16)
        return self.given

    def to_core(self):
        return self.given, lambda array: flip(array, 0, self.dp)

    def add(self, line, taken):
        product = self.product(pick(self.left, self.core, 2), line.next(self.right))
        self.sums = (product + taken.astype(F32)).astype(BF16)
        return self.sums

    def to_side(self, chunk):
        size = self.sums.shape[0] // self.chunks
        part = self.sums[chunk * size : (chunk + 1) * size]
        return pick(part, 1 - self.side, 1), lambda array: flip(array, 1, self.dp)

    def total(self, line):
        mine = pick(line.next(self.sums), self.side, 1).astype(F32)
        taken = jnp.concatenate(self.taken, axis=0) if self.chunks > 1 else self.taken[0]
        total = line.mark((mine + taken.astype(F32)).astype(BF16))
        rest = self.dp // 4
        groups = [[low + 4 * high for high in range(rest)] for low in range(4)]
        self.scattered = lax.psum_scatter(
            total.reshape(-1, total.shape[-1]),
            "dp",
            scatter_dimension=0,
            axis_index_groups=groups,
            tiled=True,
        )

    def result(self):
        return self.scattered.astype(F32)


def causal_allowed(block_rows, end_row, begin_row):
    key_place = lax.broadcasted_iota(jnp.int32, (block_rows, end_row), 1)
    query_place = lax.broadcasted_iota(jnp.int32, (block_rows, end_row), 0) + begin_row
    return key_place <= query_place


def attend(query_matrix_rows, key_matrix_rows, value_matrix_rows):
    sequence_length = query_matrix_rows.shape[1]
    head_size = query_matrix_rows.shape[4]
    block_rows = min(512, sequence_length)
    score_scale = head_size ** (-0.5)
    out_parts = []
    total_parts = []
    for block_index in range(sequence_length // block_rows):
        begin_row = block_index * block_rows
        end_row = begin_row + block_rows
        query_block = query_matrix_rows[:, begin_row:end_row]
        key_block = key_matrix_rows[:, :end_row]
        value_block = value_matrix_rows[:, :end_row]
        scores = (
            jnp.einsum("sqhgd,skhd->shgqk", query_block, key_block, preferred_element_type=F32)
            * score_scale
        )
        capped = LOGIT_CAP * jnp.tanh(scores / LOGIT_CAP)
        capped = jnp.where(causal_allowed(block_rows, end_row, begin_row), capped, -jnp.inf)
        row_top = jnp.max(capped, axis=-1, keepdims=True)
        exp_terms = jnp.exp(capped - row_top)
        row_total = jnp.sum(exp_terms, axis=-1, keepdims=True)
        soft_low = (exp_terms / row_total).astype(BF16)
        attended = jnp.einsum(
            "shgqk,skhd->sqhgd", soft_low, value_block, preferred_element_type=F32
        )
        out_parts.append(attended.astype(BF16))
        total_parts.append(row_top + jnp.log(row_total))
    return (jnp.concatenate(out_parts, axis=1), jnp.concatenate(total_parts, axis=3))


def attend_back(line, query_matrix_rows, key_matrix_rows, value_matrix_rows, log_total, d_attended, block_index):
    sequence_length = query_matrix_rows.shape[1]
    head_size = query_matrix_rows.shape[4]
    block_rows = min(512, sequence_length)
    score_scale = head_size ** (-0.5)
    begin_row = block_index * block_rows
    end_row = begin_row + block_rows
    query_block = query_matrix_rows[:, begin_row:end_row]
    key_block = key_matrix_rows[:, :end_row]
    value_block = value_matrix_rows[:, :end_row]
    d_block = line.next(d_attended)[:, begin_row:end_row]
    scores = (
        jnp.einsum("sqhgd,skhd->shgqk", query_block, key_block, preferred_element_type=F32)
        * score_scale
    )
    tangent = jnp.tanh(scores / LOGIT_CAP)
    capped = jnp.where(
        causal_allowed(block_rows, end_row, begin_row), LOGIT_CAP * tangent, -jnp.inf
    )
    soft_weights = jnp.exp(capped - log_total[:, :, :, begin_row:end_row])
    soft_low = soft_weights.astype(BF16)
    d_soft = jnp.einsum("sqhgd,skhd->shgqk", d_block, value_block, preferred_element_type=F32)
    d_capped = soft_weights * (d_soft - jnp.sum(soft_weights * d_soft, axis=-1, keepdims=True))
    d_scores = (d_capped * (1.0 - tangent * tangent)).astype(BF16)
    d_query = (
        jnp.einsum("shgqk,skhd->sqhgd", d_scores, key_block, preferred_element_type=F32)
        * score_scale
    )
    padding = ((0, 0), (0, sequence_length - end_row), (0, 0), (0, 0))
    key_term = (
        jnp.einsum("shgqk,sqhgd->skhd", d_scores, query_block, preferred_element_type=F32)
        * score_scale
    )
    value_term = jnp.einsum("shgqk,sqhgd->skhd", soft_low, d_block, preferred_element_type=F32)
    line.mark(d_scores)
    return d_query, jnp.pad(key_term, padding), jnp.pad(value_term, padding)


def gelu_and_slope(gate):
    return jax.jvp(lambda u: jax.nn.gelu(u, approximate=True), (gate,), (jnp.ones_like(gate),))


class Line:
    def __init__(self):
        self.last = None

    def next(self, array):
        if self.last is not None:
            array, _ = tied(array, self.last)
        return array

    def mark(self, array):
        self.last = array
        return array

    def open(self, *transfers):
        self.flying = [send(self.next(array)) for array, send in transfers]

    def close(self):
        *taken, self.last = tied(*self.flying, self.last)
        return taken


def make_body(dp):
    def in_order(own, other):
        return jnp.where(
            lax.axis_index("tensor") == 0,
            jnp.concatenate([own, other], axis=0),
            jnp.concatenate([other, own], axis=0),
        )

    def halves(rows):
        half = rows.shape[0] // 2
        low, high = rows[:half], rows[half:]
        first = lax.axis_index("tensor") == 0
        return jnp.where(first, low, high), jnp.where(first, high, low)

    def body(
        layer_input,
        query_weight,
        key_weight,
        value_weight,
        w_output,
        w_gate,
        w_up,
        w_down,
        gain_attn_in,
        gain_attn_out,
        gain_ffn_in,
        gain_ffn_out,
        cotangent,
    ):
        line = Line()
        query_cols, key_cols = query_weight.shape[1], key_weight.shape[1]
        qkv_cols = query_cols + 2 * key_cols
        attn_cols = qkv_cols + query_cols
        full_first = lax.all_gather(
            jnp.concatenate([query_weight, key_weight, value_weight, w_output.T, w_gate], axis=1),
            "dp",
            axis=0,
            tiled=True,
        )
        full_qkv = full_first[:, :qkv_cols]
        full_output_t = full_first[:, qkv_cols:attn_cols]
        full_gate = full_first[:, attn_cols:]
        full_up = lax.all_gather(w_up, "dp", axis=0, tiled=True)
        full_down_t = lax.all_gather(w_down.T, "dp", axis=0, tiled=True)
        gains = gather_small(
            jnp.stack([gain_attn_in, gain_attn_out, gain_ffn_in, gain_ffn_out]), dp
        )
        gain_a, gain_b, gain_c, gain_d = gains[0], gains[1], gains[2], gains[3]

        residual_in = layer_input.astype(F32)
        own = rms_norm(residual_in, gain_a).astype(BF16)
        normalized_input = in_order(own, swap(own))
        all_rows = normalized_input.shape[0]
        half = all_rows // 2
        seq_count = all_rows // SEQ_LEN
        kv_local = key_cols // HEAD_WIDTH
        head_group = QUERY_HEADS // KEY_VALUE_HEADS
        qkv = matmul(normalized_input, full_qkv).astype(BF16)
        query_matrix_rows = qkv[:, :query_cols].reshape(
            seq_count, SEQ_LEN, kv_local, head_group, HEAD_WIDTH
        )
        key_matrix_rows = qkv[:, query_cols : query_cols + key_cols].reshape(
            seq_count, SEQ_LEN, kv_local, HEAD_WIDTH
        )
        value_matrix_rows = qkv[:, query_cols + key_cols :].reshape(
            seq_count, SEQ_LEN, kv_local, HEAD_WIDTH
        )
        attended, log_total = attend(query_matrix_rows, key_matrix_rows, value_matrix_rows)
        attended = attended.reshape(all_rows, query_cols)
        attended_own, attended_other = halves(attended)
        give = line.mark(matmul_nt(attended_other, full_output_t).astype(BF16))
        taken = swap(give)
        kept = line.mark(matmul_nt(line.next(attended_own), full_output_t))
        branch_attn = kept + taken.astype(F32)
        middle, pull_attn_out = jax.vjp(
            lambda values, gain: residual_in + rms_norm(values, gain), branch_attn, gain_b
        )
        normed_mid_f, pull_ffn_in = jax.vjp(rms_norm, middle, gain_c)
        mid_own = normed_mid_f.astype(BF16)
        mid_other = swap(mid_own)

        def feed(mid):
            gate = line.mark(matmul(line.next(mid), full_gate))
            up_rows = matmul(line.next(mid), full_up)
            active, slope = gelu_and_slope(gate)
            hidden = line.mark((active * up_rows).astype(BF16))
            return hidden, active.astype(BF16), (slope * up_rows).astype(BF16)

        hidden_own, active_own, slope_own = feed(mid_own)
        hidden_other, active_other, slope_other = feed(mid_other)
        mid_t = line.mark(jnp.concatenate([mid_own, line.next(mid_other)], axis=0).T)
        input_t = line.mark(line.next(normalized_input).T)
        hidden = line.mark(jnp.concatenate([hidden_own, line.next(hidden_other)], axis=0))

        quarter = half // 2
        to_other = lambda array: (array, swap)

        def feed_out(rows):
            return matmul_nt(line.next(rows), full_down_t)

        upstream = cotangent.astype(F32)

        def ffn_back(kept, taken, middle, upstream):
            branch = kept + taken.astype(F32)
            ffn_out, pull = jax.vjp(rms_norm, branch, gain_d)
            d_ffn, grad_gain = pull(upstream)
            return (middle + ffn_out).astype(BF16), line.mark(d_ffn.astype(BF16)), grad_gain

        def hidden_back(d_rows, active, slope):
            d_hidden = matmul(line.next(d_rows), full_down_t)
            d_gate = line.mark((d_hidden * slope.astype(F32)).astype(BF16))
            return d_gate, (d_hidden * active.astype(F32)).astype(BF16)

        give_1 = line.mark(feed_out(hidden_other[:quarter]).astype(BF16))
        line.open(to_other(give_1))
        give_2 = line.mark(feed_out(hidden_other[quarter:]).astype(BF16))
        kept_1 = line.mark(feed_out(hidden_own[:quarter]))
        kept_2 = line.mark(feed_out(hidden_own[quarter:]))
        (taken_1,) = line.close()
        line.open(to_other(give_2))
        output_1, d_ffn_1, grad_d_1 = ffn_back(
            line.next(kept_1), taken_1, middle[:quarter], upstream[:quarter]
        )
        (taken_2,) = line.close()
        line.open(to_other(d_ffn_1))
        output_2, d_ffn_2, grad_d_2 = ffn_back(
            line.next(kept_2), taken_2, middle[quarter:], upstream[quarter:]
        )
        d_gate_1, d_up_1 = hidden_back(d_ffn_1, active_own[:quarter], slope_own[:quarter])
        (d_ffn_3,) = line.close()
        line.open(to_other(d_ffn_2))
        d_gate_2, d_up_2 = hidden_back(d_ffn_2, active_own[quarter:], slope_own[quarter:])
        d_gate_3, d_up_3 = hidden_back(d_ffn_3, active_other[:quarter], slope_other[:quarter])
        (d_ffn_4,) = line.close()
        layer_output = jnp.concatenate([output_1, output_2], axis=0)
        grad_d = grad_d_1 + grad_d_2

        chunks = 4
        down = Scatter(dp, chunks)
        gate_grad = Scatter(dp, chunks)
        up_grad = Scatter(dp, chunks)
        output_grad = Scatter(dp, 1)
        query_grad = Scatter(dp, 1)
        pair_grad = Scatter(dp, 1)
        d_ffn_t = line.mark(
            jnp.concatenate([d_ffn_1, d_ffn_2, d_ffn_3, line.next(d_ffn_4)], axis=0).T
        )
        line.mark(down.give(line.next(d_ffn_t), hidden))
        line.open(down.to_core())
        d_gate_4, d_up_4 = hidden_back(d_ffn_4, active_other[quarter:], slope_other[quarter:])
        d_gate_other = jnp.concatenate([d_gate_3, line.next(d_gate_4)], axis=0)
        d_up_other = jnp.concatenate([d_up_3, d_up_4], axis=0)
        (taken,) = line.close()
        line.mark(down.add(line, taken))

        def mid_back(d_gate, d_up):
            return matmul_nt(line.next(d_gate), full_gate) + matmul_nt(d_up, full_up)

        line.open(down.to_side(0))
        give = line.mark(mid_back(d_gate_other, d_up_other).astype(BF16))
        down.taken += line.close()

        line.open(down.to_side(1), to_other(give[:quarter]))
        d_gate = jnp.concatenate([line.next(d_gate_1), d_gate_2, d_gate_3, d_gate_4], axis=0)
        line.mark(gate_grad.give(mid_t, d_gate))
        side, taken_1 = line.close()
        down.taken.append(side)

        line.open(down.to_side(2), to_other(give[quarter:]), gate_grad.to_core())
        d_gate_own = jnp.concatenate([d_gate_1, d_gate_2], axis=0)
        d_up_own = jnp.concatenate([d_up_1, d_up_2], axis=0)
        kept = line.mark(mid_back(d_gate_own, d_up_own))
        side, taken_2, core = line.close()
        down.taken.append(side)

        line.open(down.to_side(3))
        taken = jnp.concatenate([taken_1, taken_2], axis=0)
        d_mid_norm, grad_c = pull_ffn_in(line.next(kept) + taken.astype(F32))
        d_middle = upstream + d_mid_norm
        d_branch, grad_b = pull_attn_out(d_middle)
        d_branch_own = line.mark(d_branch.astype(BF16))
        line.mark(gate_grad.add(line, core))
        down.taken += line.close()

        line.open(gate_grad.to_side(0), to_other(d_branch_own[:quarter]))
        down.total(line)
        d_up = jnp.concatenate([line.next(d_up_1), d_up_2, d_up_3, d_up_4], axis=0)
        line.mark(up_grad.give(mid_t, d_up))
        side, taken_1 = line.close()
        gate_grad.taken.append(side)

        line.open(gate_grad.to_side(1), to_other(d_branch_own[quarter:]), up_grad.to_core())
        side, taken_2, core = line.close()
        gate_grad.taken.append(side)

        line.open(gate_grad.to_side(2))
        d_branch_other = jnp.concatenate([taken_1, line.next(taken_2)], axis=0)
        d_branch_rows = in_order(d_branch_own, d_branch_other)
        d_attended = line.mark(matmul(d_branch_rows, full_output_t).astype(BF16))
        line.mark(up_grad.add(line, core))
        gate_grad.taken += line.close()

        line.open(gate_grad.to_side(3))
        d_branch_t = line.mark(line.next(d_branch_rows).T)
        line.mark(output_grad.give(line.next(d_branch_t), attended))
        d_attended = d_attended.reshape(seq_count, SEQ_LEN, kv_local, head_group, HEAD_WIDTH)
        back_args = query_matrix_rows, key_matrix_rows, value_matrix_rows, log_total, d_attended
        d_query_1, d_key_1, d_value_1 = attend_back(line, *back_args, 0)
        gate_grad.taken += line.close()

        line.open(up_grad.to_side(0), output_grad.to_core())
        gate_grad.total(line)
        d_query_2, d_key_2, d_value_2 = attend_back(line, *back_args, 1)
        d_qkv = line.mark(
            jnp.concatenate(
                [
                    jnp.concatenate([d_query_1, d_query_2], axis=1)
                    .reshape(all_rows, query_cols)
                    .astype(BF16),
                    (d_key_1 + d_key_2).reshape(all_rows, key_cols).astype(BF16),
                    (d_value_1 + d_value_2).reshape(all_rows, key_cols).astype(BF16),
                ],
                axis=1,
            )
        )
        side, core = line.close()
        up_grad.taken.append(side)

        line.open(up_grad.to_side(1))
        d_qkv_own, d_qkv_other = halves(line.next(d_qkv))
        give = line.mark(matmul_nt(d_qkv_other, full_qkv).astype(BF16))
        line.mark(query_grad.give(input_t, line.next(d_qkv)[:, :query_cols]))
        line.mark(pair_grad.give(input_t, line.next(d_qkv)[:, query_cols:]))
        line.mark(output_grad.add(line, core))
        up_grad.taken += line.close()

        line.open(
            up_grad.to_side(2), query_grad.to_core(), pair_grad.to_core(), to_other(give[:quarter])
        )
        kept = line.mark(matmul_nt(line.next(d_qkv_own), full_qkv))
        side, query_core, pair_core, taken_1 = line.close()
        up_grad.taken.append(side)

        line.open(up_grad.to_side(3), to_other(give[quarter:]))
        line.mark(query_grad.add(line, query_core))
        line.mark(pair_grad.add(line, pair_core))
        side, taken_2 = line.close()
        up_grad.taken.append(side)

        line.open(output_grad.to_side(0))
        up_grad.total(line)
        _, pull_attn_in = jax.vjp(rms_norm, residual_in, gain_a)
        taken = jnp.concatenate([taken_1, taken_2], axis=0)
        d_input_norm, grad_a = pull_attn_in(line.next(kept) + taken.astype(F32))
        input_grad = line.mark(d_middle + d_input_norm)
        output_grad.taken += line.close()
        small = scatter_small(jnp.stack([grad_a, grad_b, grad_c, grad_d]), dp)

        line.open(query_grad.to_side(0))
        output_grad.total(line)
        query_grad.taken += line.close()

        line.open(pair_grad.to_side(0))
        query_grad.total(line)
        pair_grad.taken += line.close()
        pair_grad.total(line)
        grad_pair = pair_grad.result()
        return (
            layer_output,
            input_grad,
            query_grad.result(),
            grad_pair[:, :key_cols],
            grad_pair[:, key_cols:],
            output_grad.result().T,
            gate_grad.result(),
            up_grad.result(),
            down.result().T,
            small[0],
            small[1],
            small[2],
            small[3],
        )

    return body


def solution(mesh):
    rows = P(("dp", "tensor"), None)
    gain = P(("dp", "tensor"))
    into, out_of = P("dp", "tensor"), P("tensor", "dp")
    return jax.shard_map(
        make_body(mesh.shape["dp"]),
        mesh=mesh,
        in_specs=(rows, into, into, into, out_of, into, into, out_of, gain, gain, gain, gain, rows),
        out_specs=(rows, rows, into, into, into, out_of, into, into, out_of, gain, gain, gain, gain),
        check_vma=False,
    )
```

time: 1640 us -> 1400 us (0.85)
  waiting for transfers between devices: 970 us -> 541 us
  other arithmetic: 92.6 us -> 175 us
  local copies, waits for them, and re-layouts: 73.9 us -> 135 us
  matrix products: 431 us -> 480 us
    ppermute x15 -> x0, waiting for transfers between devices: 209 us -> none  [scatter_grad(): result = result + lax.ppermute(give, 'dp', pairs).astype(F32)]
    ppermute x18 -> x29, waiting for transfers between devices: 293 us -> 135 us  [flip(): return lax.ppermute(array, 'dp', [(i, i ^ 1 << bit) for i in range(dp)])]
    ppermute x10 -> x15, waiting for transfers between devices: 331 us -> 209 us  [swap(): return lax.ppermute(rows, 'tensor', [(0, 1), (1, 0)])]
    reduce_scatter x0 -> x6, waiting for transfers between devices: none -> 91 us  [total(): lax.psum_scatter(total.reshape(-1, total.shape[-1]), 'dp', scatter_dimens...]
    all_gather x1, waiting for transfers between devices: 77.3 us -> 0.01 us  [body(): full_down_t = lax.all_gather(w_down.T, 'dp', axis=0, tiled=True)]
    all_gather x1, waiting for transfers between devices: 40.3 us -> 104 us  [body(): lax.all_gather(jnp.concatenate([query_weight, key_weight, value_weight, w...]
    convert_element_type x6 -> x20, other arithmetic: 12.1 us -> 72.8 us  [the longest x5 31.5 us: add(): self.sums = (product + taken.astype(F32)).astype(BF16)]
    concatenate x2 -> x10, other arithmetic: 2.59 us -> 35.4 us  [the longest x1 11.5 us: body(): jnp.concatenate([line.next(d_gate_1), d_gate_2, d_gate_3, d_gate_4], axis=0)]
  transfers between devices with their start and end apart: 47 -> 53, of which waited for: 27 -> 32; matrix products, arithmetic and copies ran while one was open for 26% -> 49% of each run, Pallas kernels for 0% -> 0%
where the time goes in v2:
time: 1400 us
  waiting for transfers between devices  541 us (39%)
  matrix products  480 us (34%)
  other arithmetic  175 us (12%)
  local copies, waits for them, and re-layouts  135 us (10%)
  starting transfers between devices  48.3 us (3%)
  between operations  16.1 us (1%)
    dot_general x22, matrix products, matmul(): return jnp.dot(left, right, preferred_element_type=F32)  299 us
    ppermute x15, waiting for transfers between devices, swap(): return lax.ppermute(rows, 'tensor', [(0, 1), (1, 0)])  209 us
    dot_general x12, matrix products, matmul_nt(): lax.dot_general(left, right, (((1,), (1,)), ((), ())), preferred_element_...  140 us
    ppermute x29, waiting for transfers between devices, flip(): return lax.ppermute(array, 'dp', [(i, i ^ 1 << bit) for i in range(dp)])  135 us
    all_gather x1, waiting for transfers between devices, body(): lax.all_gather(jnp.concatenate([query_weight, key_weight, value_weight, w...  104 us
    reduce_scatter x6, waiting for transfers between devices, total(): lax.psum_scatter(total.reshape(-1, total.shape[-1]), 'dp', scatter_dimens...  91 us
    convert_element_type x5, other arithmetic, add(): self.sums = (product + taken.astype(F32)).astype(BF16)  31.5 us
  transfers between devices with their start and end apart: 53, of which 32 were waited for; matrix products, arithmetic and copies ran while one was open for 49% of the time, Pallas kernels for 0%

profile of v2, /device:TPU:0, one launch (start us, length us, event | category | flops | bytes accessed | tf_op | source)
XLA Modules:
  0.0 1396.1 jit_solution(17580343226040451107)
XLA Ops:
  42.0 47.2 %collective-permute-done.5 = bf16[512,2304]{1,0:T(8,128)(2,1)S(1)} collective-permute-done((bf16[512,2304]{1,0:T(8,128)(2,1)S(1)}, bf16[512,2304]{1,0:T(8,128)(2,1)S(1)}, u32[]{:S(2)}, u32[]{:S(2)}) %collective-permute-start.5) | collective-permute-done | bytes 2359328 | tf_op jit(solution)/shard_map/ppermute | solution.py:32
  92.5 104.1 %all-gather.4.cloned.1.call-done = bf16[2304,7680]{1,0:T(8,128)(2,1)} async-done(((bf16[144,7680]{1,0:T(8,128)(2,1)}), bf16[2304,7680]{1,0:T(8,128)(2,1)}) %all-gather.4.cloned.1.call-update) | async-done | bytes 35389456 | tf_op jit(solution)/shard_map/all_gather | solution.py:266
  196.6 13.9 fusion.92
  258.9 47.8 %collective-permute-done.6 = bf16[512,2304]{1,0:T(8,128)(2,1)} collective-permute-done((bf16[512,2304]{1,0:T(8,128)(2,1)}, bf16[512,2304]{1,0:T(8,128)(2,1)}, u32[]{:S(2)}, u32[]{:S(2)}) %collective-permute-start.6) | collective-permute-done | bytes 2359328 | tf_op jit(solution)/shard_map/ppermute | solution.py:32
  322.0 18.0 %fusion.6 = f32[512,4608]{1,0:T(8,128)} fusion(bf16[512,2304]{1,0:T(8,128)(2,1)S(1)} %multiply_convert_fusion.10, bf16[2304,7680]{1,0:T(8,128)(2,1)} %all-gather.4.cloned.1.call-done), kind=kOutput, calls=%fused_computation.9 | convolution fusion | flops 10871635968 | bytes 33030144 | tf_op jit(solution)/shard_map/dot_general | solution.py:24
  340.1 25.9 %fusion.22 = (bf16[512,4608]{1,0:T(8,128)(2,1)}, bf16[512,4608]{1,0:T(8,128)(2,1)}, bf16[512,4608]{1,0:T(8,128)(2,1)}) fusion(f32[512,4608]{1,0:T(8,128)} %fusion.6, bf16[512,2304]{1,0:T(8,128)(2,1)S(1)} %multiply_convert_fusion.10, bf16[2304,4608]{1,0:T(8,128)(2,1)} %all-gather.6.cloned.1.call-done), kind=kOutput, calls=%fused_computation.35 | convolution fusion | flops 10923540480 | bytes 47185920 | tf_op jit(solution)/shard_map/dot_general | solution.py:24
  373.0 18.3 %fusion.4 = f32[512,4608]{1,0:T(8,128)} fusion(bf16[512,2304]{1,0:T(8,128)(2,1)} %collective-permute-done.7, bf16[2304,7680]{1,0:T(8,128)(2,1)} %all-gather.4.cloned.1.call-done), kind=kOutput, calls=%fused_computation.7 | convolution fusion | flops 10871635968 | bytes 33030144 | tf_op jit(solution)/shard_map/dot_general | solution.py:24
  391.4 25.0 %fusion.34 = (bf16[512,4608]{1,0:T(8,128)(2,1)}, bf16[512,4608]{1,0:T(8,128)(2,1)}, bf16[512,4608]{1,0:T(8,128)(2,1)}) fusion(f32[512,4608]{1,0:T(8,128)} %fusion.4, bf16[512,2304]{1,0:T(8,128)(2,1)} %collective-permute-done.7, bf16[2304,4608]{1,0:T(8,128)(2,1)} %all-gather.6.cloned.1.call-done), kind=kOutput, calls=%fused_computation.47 | convolution fusion | flops 10923540480 | bytes 47185920 | tf_op jit(solution)/shard_map/dot_general | solution.py:24
  464.9 12.2 fusion.267
  477.0 12.9 collective-permute-done.8
  495.1 21.0 %collective-permute-done.9 = bf16[256,2304]{1,0:T(8,128)(2,1)S(1)} collective-permute-done((bf16[256,2304]{1,0:T(8,128)(2,1)}, bf16[256,2304]{1,0:T(8,128)(2,1)S(1)}, u32[]{:S(2)}, u32[]{:S(2)}) %collective-permute-start.9) | collective-permute-done | bytes 1179680 | tf_op jit(solution)/shard_map/ppermute | solution.py:32
  534.7 17.1 %multiply_convert_fusion.3 = (bf16[256,4608]{1,0:T(8,128)(2,1)}, bf16[256,4608]{1,0:T(8,128)(2,1)}, bf16[256,4608]{1,0:T(8,128)(2,1)}, bf16[256,4608]{1,0:T(8,128)(2,1)}) fusion(bf16[512,4608]{1,0:T(8,128)(2,1)} %get-tuple-element.279, f32[256,4608]{1,0:T(8,128)} %fusion.268, bf16[512,4608]{1,0:T(8,128)(2,1)} %get-tuple-element.265, ...), kind=kOutput, calls=%fused_computation.127 | convolution fusion | flops 5449973760 | bytes 46006272 | tf_op jit(solution)/shard_map/dot_general | solution.py:24
  551.9 14.8 %multiply_convert_fusion.7 = (bf16[256,4608]{1,0:T(8,128)(2,1)S(1)}, f32[256,4608]{1,0:T(8,128)}) fusion(bf16[512,4608]{1,0:T(8,128)(2,1)} %get-tuple-element.263, bf16[256,2304]{1,0:T(8,128)(2,1)S(1)} %collective-permute-done.10, bf16[2304,4608]{1,0:T(8,128)(2,1)} %all-gather.8.cloned.1.call-done), kind=kOutput, calls=%fused_computation.131 | convolution fusion | flops 5439356928 | bytes 31850496 | tf_op jit(solution)/shard_map/dot_general | solution.py:24
  581.9 16.9 %convolution_convert_fusion.2 = bf16[4,2,144,4608]{3,2,1,0:T(8,128)(2,1)} fusion(bf16[4,2,2,144,1024]{4,3,2,1,0:T(8,128)(2,1)} %bitcast.507, s32[]{:T(128)S(6)} %select_n.209, bf16[512,4608]{1,0:T(8,128)(2,1)} %get-tuple-element.137, bf16[512,4608]{1,0:T(8,128)(2,1)} %get-tuple-element.266), kind=kOutput, calls=%fused_computation.23 | convolution fusion | flops 10895818752 | bytes 22413316 | tf_op jit(solution)/shard_map/dot_general | solution.py:24
  605.4 17.2 %multiply_convert_fusion.5 = (bf16[256,4608]{1,0:T(8,128)(2,1)S(1)}, bf16[256,4608]{1,0:T(8,128)(2,1)}, bf16[256,4608]{1,0:T(8,128)(2,1)S(1)}) fusion(f32[256,4608]{1,0:T(8,128)} %get-tuple-element.321, bf16[512,4608]{1,0:T(8,128)(2,1)} %get-tuple-element.280, bf16[512,4608]{1,0:T(8,128)(2,1)} %get-tuple-element.263, ...), kind=kOutput, calls=%fused_computation.129 | convolution fusion | flops 5446434816 | bytes 41287680 | tf_op jit(solution)/shard_map/dot_general | solution.py:24
  624.0 18.6 %fusion.42 = f32[4,2,144,4608]{3,2,1,0:T(8,128)} fusion(bf16[1024,4608]{1,0:T(8,128)(2,1)} %pad_maximum_fusion, bf16[4,2,2,144,1024]{4,3,2,1,0:T(8,128)(2,1)} %bitcast.508, s32[]{:T(128)S(6)} %select_n.208), kind=kOutput, calls=%fused_computation.58 | convolution fusion | flops 10871635968 | bytes 33030148 | tf_op jit(solution)/shard_map/dot_general | solution.py:24
  661.7 15.7 %fusion.2 = f32[512,2304]{1,0:T(8,128)} fusion(bf16[512,4608]{1,0:T(8,128)(2,1)S(1)} %pad_maximum_fusion.7, bf16[2304,7680]{1,0:T(8,128)(2,1)} %all-gather.4.cloned.1.call-done), kind=kOutput, calls=%fused_computation.5 | convolution fusion | flops 10871635968 | bytes 30670848 | tf_op jit(solution)/shard_map/dot_general | solution.py:28
  677.5 16.3 %fusion.70 = bf16[512,2304]{1,0:T(8,128)(2,1)} fusion(f32[512,2304]{1,0:T(8,128)} %fusion.2, bf16[2304,4608]{1,0:T(8,128)(2,1)} %all-gather.6.cloned.1.call-done, bf16[256,4608]{1,0:T(8,128)(2,1)S(1)} %copy-done.37, bf16[256,4608]{1,0:T(8,128)(2,1)S(1)} %get-tuple-element.287), kind=kOutput, calls=%fused_computation.138 | convolution fusion | flops 10883432448 | bytes 33030144 | tf_op jit(solution)/shard_map/dot_general | solution.py:28
  700.4 16.6 %convolution_convert_fusion.1 = bf16[4,2,144,4608]{3,2,1,0:T(8,128)(2,1)} fusion(bf16[4,2,2,144,1024]{4,3,2,1,0:T(8,128)(2,1)} %bitcast.497, s32[]{:T(128)S(6)} %select_n.209, bf16[256,4608]{1,0:T(8,128)(2,1)} %copy-done.19, bf16[256,4608]{1,0:T(8,128)(2,1)} %copy-done.17, bf16[256,4608]{1,0:T(8,128)(2,1)S(1)} %copy-done.15, ...), kind=kOutput, calls=%fused_computation.22 | convolution fusion | flops 10914693120 | bytes 22413316 | tf_op jit(solution)/shard_map/dot_general | solution.py:24
  750.2 15.8 %fusion = f32[512,2304]{1,0:T(8,128)} fusion(bf16[512,4608]{1,0:T(8,128)(2,1)S(1)} %pad_maximum_fusion.6, bf16[2304,7680]{1,0:T(8,128)(2,1)} %all-gather.4.cloned.1.call-done), kind=kOutput, calls=%fused_computation.3 | convolution fusion | flops 10871635968 | bytes 30670848 | tf_op jit(solution)/shard_map/dot_general | solution.py:28
  766.0 16.4 %convolution_add_fusion = f32[512,2304]{1,0:T(8,128)S(1)} fusion(f32[512,2304]{1,0:T(8,128)} %fusion, bf16[2304,4608]{1,0:T(8,128)(2,1)} %all-gather.6.cloned.1.call-done, bf16[256,4608]{1,0:T(8,128)(2,1)} %get-tuple-element.284, bf16[256,4608]{1,0:T(8,128)(2,1)} %get-tuple-element.283), kind=kOutput, calls=%fused_computation.96 | convolution fusion | flops 10882252800 | bytes 35389440 | tf_op jit(solution)/shard_map/dot_general | solution.py:28
  799.6 18.5 %add_convert_fusion.1 = bf16[4,2,144,4608]{3,2,1,0:T(8,128)(2,1)} fusion(bf16[4,2,144,4608]{3,2,1,0:T(8,128)(2,1)} %collective-permute-done.18, bf16[1024,4608]{1,0:T(8,128)(2,1)} %get-tuple-element.174, bf16[4,2,2,144,1024]{4,3,2,1,0:T(8,128)(2,1)} %bitcast.498, s32[]{:T(128)S(6)} %select_n.208), kind=kOutput, calls=%fused_computation.1 | convolution fusion | flops 10887561216 | bytes 33030148 | tf_op jit(solution)/shard_map/dot_general | solution.py:24
  830.3 17.1 %convolution_convert_fusion = bf16[4,2,144,4608]{3,2,1,0:T(8,128)(2,1)} fusion(bf16[4,2,2,144,1024]{4,3,2,1,0:T(8,128)(2,1)} %bitcast.499, s32[]{:T(128)S(6)} %select_n.209, bf16[256,4608]{1,0:T(8,128)(2,1)} %get-tuple-element.288, bf16[256,4608]{1,0:T(8,128)(2,1)} %copy-done.36, bf16[256,4608]{1,0:T(8,128)(2,1)} %get-tuple-element.284, ...), kind=kOutput, calls=%fused_computation.21 | convolution fusion | flops 10914693120 | bytes 22413316 | tf_op jit(solution)/shard_map/dot_general | solution.py:24
  889.8 23.2 %collective-permute-done.23 = bf16[256,2304]{1,0:T(8,128)(2,1)S(1)} collective-permute-done((bf16[256,2304]{1,0:T(8,128)(2,1)}, bf16[256,2304]{1,0:T(8,128)(2,1)S(1)}, u32[]{:S(2)}, u32[]{:S(2)}) %collective-permute-start.23) | collective-permute-done | bytes 1179680 | tf_op jit(solution)/shard_map/ppermute | solution.py:32
  930.9 17.8 %fusion.35 = f32[4,2,144,4608]{3,2,1,0:T(8,128)} fusion(bf16[1024,4608]{1,0:T(8,128)(2,1)} %get-tuple-element.189, bf16[4,2,2,144,1024]{4,3,2,1,0:T(8,128)(2,1)S(1)} %bitcast.502, s32[]{:T(128)S(6)} %select_n.208), kind=kOutput, calls=%fused_computation.51 | convolution fusion | flops 10871635968 | bytes 33030148 | tf_op jit(solution)/shard_map/dot_general | solution.py:24
  1045.5 17.1 %collective-permute-done.27 = bf16[1,144,4608]{2,1,0:T(8,128)(2,1)} collective-permute-done((bf16[1,144,4608]{2,1,0:T(8,128)(2,1)}, bf16[1,144,4608]{2,1,0:T(8,128)(2,1)}, u32[]{:S(2)}, u32[]{:S(2)}) %collective-permute-start.27) | collective-permute-done | bytes 1327136 | tf_op jit(solution)/shard_map/ppermute | solution.py:36
  1085.4 20.5 %collective-permute-done.29 = bf16[1,144,4608]{2,1,0:T(8,128)(2,1)S(1)} collective-permute-done((bf16[1,144,4608]{2,1,0:T(8,128)(2,1)S(1)}, bf16[1,144,4608]{2,1,0:T(8,128)(2,1)S(1)}, u32[]{:S(2)}, u32[]{:S(2)}) %collective-permute-start.29) | collective-permute-done | bytes 1327136 | tf_op jit(solution)/shard_map/ppermute | solution.py:36
  1120.3 18.2 %collective-permute-done.33 = bf16[256,2304]{1,0:T(8,128)(2,1)S(1)} collective-permute-done((bf16[256,2304]{1,0:T(8,128)(2,1)}, bf16[256,2304]{1,0:T(8,128)(2,1)S(1)}, u32[]{:S(2)}, u32[]{:S(2)}) %collective-permute-start.33) | collective-permute-done | bytes 1179680 | tf_op jit(solution)/shard_map/ppermute | solution.py:32
  1181.7 16.5 %collective-permute-done.36 = bf16[4,144,1024]{2,1,0:T(8,128)(2,1)S(1)} collective-permute-done((bf16[4,144,1024]{2,1,0:T(8,128)(2,1)S(1)}, bf16[4,144,1024]{2,1,0:T(8,128)(2,1)S(1)}, u32[]{:S(2)}, u32[]{:S(2)}) %collective-permute-start.36) | collective-permute-done | bytes 1179680 | tf_op jit(solution)/shard_map/ppermute | solution.py:36
  1202.3 23.8 %collective-permute-done.37 = bf16[4,144,1024]{2,1,0:T(8,128)(2,1)S(1)} collective-permute-done((bf16[4,144,1024]{2,1,0:T(8,128)(2,1)S(1)}, bf16[4,144,1024]{2,1,0:T(8,128)(2,1)S(1)}, u32[]{:S(2)}, u32[]{:S(2)}) %collective-permute-start.37) | collective-permute-done | bytes 1179680 | tf_op jit(solution)/shard_map/ppermute | solution.py:36
  1230.2 23.0 %collective-permute-done.38 = bf16[4,144,1024]{2,1,0:T(8,128)(2,1)S(1)} collective-permute-done((bf16[4,144,1024]{2,1,0:T(8,128)(2,1)S(1)}, bf16[4,144,1024]{2,1,0:T(8,128)(2,1)S(1)}, u32[]{:S(2)}, u32[]{:S(2)}) %collective-permute-start.38) | collective-permute-done | bytes 1179680 | tf_op jit(solution)/shard_map/ppermute | solution.py:36
  1295.0 91.0 %reduce-scatter.15.cloned.1.call-done = bf16[144,4608]{1,0:T(8,128)(2,1)} async-done(((bf16[576,4608]{1,0:T(8,128)(2,1)}), bf16[144,4608]{1,0:T(8,128)(2,1)}) %reduce-scatter.15.cloned.1.call-update) | async-done | bytes 1327120 | tf_op jit(solution)/shard_map/reduce_scatter | solution.py:121
  (516 shorter events, 581.5 us)
Async XLA Ops:
  7.2 189.4 %all-gather.4.cloned.1.call-start = ((), (), s32[]{:S(2)}) async-start(), calls=%async_computation.6 | async-start | bytes 37601280 | tf_op jit(solution)/shard_map/all_gather | solution.py:266
  16.5 323.6 %all-gather.6.cloned.1.call-start = ((), (), s32[]{:S(2)}) async-start(), calls=%async_computation.7 | async-start | bytes 22560768 | tf_op jit(solution)/shard_map/all_gather | solution.py:275
  17.2 411.8 %all-gather.8.cloned.1.call-start = ((), (), s32[]{:S(2)}) async-start(), calls=%async_computation.8 | async-start | bytes 22560768 | tf_op jit(solution)/shard_map/all_gather | solution.py:276
  18.0 1264.2 %reduce-scatter.17.cloned.1.call-start = ((), (), s32[]{:S(2)}) async-start(), calls=%async_computation.14 | async-start | bytes 6635520 | tf_op jit(solution)/shard_map/reduce_scatter | solution.py:121
  38.2 51.1 %collective-permute-start.5 = (bf16[512,2304]{1,0:T(8,128)(2,1)S(1)}, bf16[512,2304]{1,0:T(8,128)(2,1)S(1)}, u32[]{:S(2)}, u32[]{:S(2)}) collective-permute-start(bf16[512,2304]{1,0:T(8,128)(2,1)S(1)} %fusion.57), channel_id=1, source_target_pairs={{0,1},{1,0},{2,3},{3,2},{4,5},{5,4},{6,7},{7,6},{8,9},{9,8},{10,11... | collective-permute-start | bytes 7077896 | tf_op jit(solution)/shard_map/ppermute | solution.py:32
  253.2 53.5 %collective-permute-start.6 = (bf16[512,2304]{1,0:T(8,128)(2,1)}, bf16[512,2304]{1,0:T(8,128)(2,1)}, u32[]{:S(2)}, u32[]{:S(2)}) collective-permute-start(bf16[512,2304]{1,0:T(8,128)(2,1)} %convolution_convert_fusion.3), channel_id=1, source_target_pairs={{0,1},{1,0},{2,3},{3,2},{4,5},{5,4},{6,7},{7,6},{8,9},{9,8},{10,11... | collective-permute-start | bytes 7077896 | tf_op jit(solution)/shard_map/ppermute | solution.py:32
  320.5 52.6 %collective-permute-start.7 = (bf16[512,2304]{1,0:T(8,128)(2,1)S(1)}, bf16[512,2304]{1,0:T(8,128)(2,1)}, u32[]{:S(2)}, u32[]{:S(2)}) collective-permute-start(bf16[512,2304]{1,0:T(8,128)(2,1)S(1)} %multiply_convert_fusion.10), channel_id=1, source_target_pairs={{0,1},{1,0},{2,3},{3,2},{4,5},{5,4},{6,7},{7,6},{8,9},{9,8},{10,11... | collective-permute-start | bytes 7077896 | tf_op jit(solution)/shard_map/ppermute | solution.py:32
  521.0 30.9 %collective-permute-start.10 = (bf16[256,2304]{1,0:T(8,128)(2,1)}, bf16[256,2304]{1,0:T(8,128)(2,1)S(1)}, u32[]{:S(2)}, u32[]{:S(2)}) collective-permute-start(bf16[256,2304]{1,0:T(8,128)(2,1)} %fusion.102), channel_id=1, source_target_pairs={{0,1},{1,0},{2,3},{3,2},{4,5},{5,4},{6,7},{7,6},{8,9},{9,8},{10,11... | collective-permute-start | bytes 3538952 | tf_op jit(solution)/shard_map/ppermute | solution.py:32
  522.4 48.5 %collective-permute-start.11 = (bf16[256,2304]{1,0:T(8,128)(2,1)}, bf16[256,2304]{1,0:T(8,128)(2,1)S(1)}, u32[]{:S(2)}, u32[]{:S(2)}) collective-permute-start(bf16[256,2304]{1,0:T(8,128)(2,1)} %get-tuple-element.296), channel_id=1, source_target_pairs={{0,1},{1,0},{2,3},{3,2},{4,5},{5,4},{6,7},{7,6},{8,9},{9,8},{10,11... | collective-permute-start | bytes 3538952 | tf_op jit(solution)/shard_map/ppermute | solution.py:32
  598.8 43.9 %collective-permute-start.12 = (bf16[4,2,144,4608]{3,2,1,0:T(8,128)(2,1)}, bf16[4,2,144,4608]{3,2,1,0:T(8,128)(2,1)}, u32[]{:S(2)}, u32[]{:S(2)}) collective-permute-start(bf16[4,2,144,4608]{3,2,1,0:T(8,128)(2,1)} %convolution_convert_fusion.2), channel_id=1, source_target_pairs={{0,2},{2,0},{4,6},{6,4},{8,10},{10,8},{12,14},{14,12},{16,18},{18,... | collective-permute-start | bytes 31850504 | tf_op jit(solution)/shard_map/ppermute | solution.py:36
  660.2 38.0 %collective-permute-start.13 = (bf16[1,144,4608]{2,1,0:T(8,128)(2,1)}, bf16[1,144,4608]{2,1,0:T(8,128)(2,1)}, u32[]{:S(2)}, u32[]{:S(2)}) collective-permute-start(bf16[1,144,4608]{2,1,0:T(8,128)(2,1)} %dynamic-slice_bitcast_fusion.10), channel_id=1, source_target_pairs={{0,4},{2,6},{4,0},{6,2},{8,12},{10,14},{12,8},{14,10},{16,20},{18,... | collective-permute-start | bytes 3981320 | tf_op jit(solution)/shard_map/ppermute | solution.py:36
  699.8 31.3 %collective-permute-start.14 = (bf16[1,144,4608]{2,1,0:T(8,128)(2,1)}, bf16[1,144,4608]{2,1,0:T(8,128)(2,1)}, u32[]{:S(2)}, u32[]{:S(2)}) collective-permute-start(bf16[1,144,4608]{2,1,0:T(8,128)(2,1)} %dynamic-slice_bitcast_fusion.11), channel_id=1, source_target_pairs={{0,4},{2,6},{4,0},{6,2},{8,12},{10,14},{12,8},{14,10},{16,20},{18,... | collective-permute-start | bytes 3981320 | tf_op jit(solution)/shard_map/ppermute | solution.py:36
  731.1 51.4 %collective-permute-start.18 = (bf16[4,2,144,4608]{3,2,1,0:T(8,128)(2,1)}, bf16[4,2,144,4608]{3,2,1,0:T(8,128)(2,1)}, u32[]{:S(2)}, u32[]{:S(2)}) collective-permute-start(bf16[4,2,144,4608]{3,2,1,0:T(8,128)(2,1)} %convolution_convert_fusion.1), channel_id=1, source_target_pairs={{0,2},{2,0},{4,6},{6,4},{8,10},{10,8},{12,14},{14,12},{16,18},{18,... | collective-permute-start | bytes 31850504 | tf_op jit(solution)/shard_map/ppermute | solution.py:36
  749.1 33.3 %collective-permute-start.17 = (bf16[256,2304]{1,0:T(8,128)(2,1)}, bf16[256,2304]{1,0:T(8,128)(2,1)}, u32[]{:S(2)}, u32[]{:S(2)}) collective-permute-start(bf16[256,2304]{1,0:T(8,128)(2,1)} %get-tuple-element.168), channel_id=1, source_target_pairs={{0,1},{1,0},{2,3},{3,2},{4,5},{5,4},{6,7},{7,6},{8,9},{9,8},{10,11... | collective-permute-start | bytes 3538952 | tf_op jit(solution)/shard_map/ppermute | solution.py:32
  749.6 32.8 %collective-permute-start.16 = (bf16[1,144,4608]{2,1,0:T(8,128)(2,1)}, bf16[1,144,4608]{2,1,0:T(8,128)(2,1)}, u32[]{:S(2)}, u32[]{:S(2)}) collective-permute-start(bf16[1,144,4608]{2,1,0:T(8,128)(2,1)} %get-tuple-element.167), channel_id=1, source_target_pairs={{0,4},{2,6},{4,0},{6,2},{8,12},{10,14},{12,8},{14,10},{16,20},{18,... | collective-permute-start | bytes 3981320 | tf_op jit(solution)/shard_map/ppermute | solution.py:36
  782.6 45.5 %collective-permute-start.19 = (bf16[1,144,4608]{2,1,0:T(8,128)(2,1)}, bf16[1,144,4608]{2,1,0:T(8,128)(2,1)}, u32[]{:S(2)}, u32[]{:S(2)}) collective-permute-start(bf16[1,144,4608]{2,1,0:T(8,128)(2,1)} %get-tuple-element.176), channel_id=1, source_target_pairs={{0,4},{2,6},{4,0},{6,2},{8,12},{10,14},{12,8},{14,10},{16,20},{18,... | collective-permute-start | bytes 3981320 | tf_op jit(solution)/shard_map/ppermute | solution.py:36
  829.6 31.2 %collective-permute-start.20 = (bf16[1,144,4608]{2,1,0:T(8,128)(2,1)}, bf16[1,144,4608]{2,1,0:T(8,128)(2,1)}, u32[]{:S(2)}, u32[]{:S(2)}) collective-permute-start(bf16[1,144,4608]{2,1,0:T(8,128)(2,1)} %dynamic-slice_bitcast_fusion.8), channel_id=1, source_target_pairs={{0,4},{2,6},{4,0},{6,2},{8,12},{10,14},{12,8},{14,10},{16,20},{18,... | collective-permute-start | bytes 3981320 | tf_op jit(solution)/shard_map/ppermute | solution.py:36
  860.8 55.7 %collective-permute-start.24 = (bf16[4,2,144,4608]{3,2,1,0:T(8,128)(2,1)}, bf16[4,2,144,4608]{3,2,1,0:T(8,128)(2,1)}, u32[]{:S(2)}, u32[]{:S(2)}) collective-permute-start(bf16[4,2,144,4608]{3,2,1,0:T(8,128)(2,1)} %convolution_convert_fusion), channel_id=1, source_target_pairs={{0,2},{2,0},{4,6},{6,4},{8,10},{10,8},{12,14},{14,12},{16,18},{18,... | collective-permute-start | bytes 31850504 | tf_op jit(solution)/shard_map/ppermute | solution.py:36
  885.0 31.6 %collective-permute-start.22 = (bf16[1,144,4608]{2,1,0:T(8,128)(2,1)}, bf16[1,144,4608]{2,1,0:T(8,128)(2,1)}, u32[]{:S(2)}, u32[]{:S(2)}) collective-permute-start(bf16[1,144,4608]{2,1,0:T(8,128)(2,1)} %dynamic-slice_bitcast_fusion.6), channel_id=1, source_target_pairs={{0,4},{2,6},{4,0},{6,2},{8,12},{10,14},{12,8},{14,10},{16,20},{18,... | collective-permute-start | bytes 3981320 | tf_op jit(solution)/shard_map/ppermute | solution.py:36
  889.7 396.6 %reduce-scatter.13.cloned.1.call-start = ((), (), s32[]{:S(2)}) async-start(), calls=%async_computation.12 | async-start | bytes 6635520 | tf_op jit(solution)/shard_map/reduce_scatter | solution.py:121
  948.7 31.8 %collective-permute-start.25 = (bf16[1,144,4608]{2,1,0:T(8,128)(2,1)}, bf16[1,144,4608]{2,1,0:T(8,128)(2,1)S(1)}, u32[]{:S(2)}, u32[]{:S(2)}) collective-permute-start(bf16[1,144,4608]{2,1,0:T(8,128)(2,1)} %dynamic-slice_bitcast_fusion.5), channel_id=1, source_target_pairs={{0,4},{2,6},{4,0},{6,2},{8,12},{10,14},{12,8},{14,10},{16,20},{18,... | collective-permute-start | bytes 3981320 | tf_op jit(solution)/shard_map/ppermute | solution.py:36
  980.5 50.2 %collective-permute-start.26 = (bf16[1,144,4608]{2,1,0:T(8,128)(2,1)}, bf16[1,144,4608]{2,1,0:T(8,128)(2,1)}, u32[]{:S(2)}, u32[]{:S(2)}) collective-permute-start(bf16[1,144,4608]{2,1,0:T(8,128)(2,1)} %dynamic-slice_bitcast_fusion.3), channel_id=1, source_target_pairs={{0,4},{2,6},{4,0},{6,2},{8,12},{10,14},{12,8},{14,10},{16,20},{18,... | collective-permute-start | bytes 3981320 | tf_op jit(solution)/shard_map/ppermute | solution.py:36
  1030.7 31.9 %collective-permute-start.28 = (bf16[4,2,144,1024]{3,2,1,0:T(8,128)(2,1)}, bf16[4,2,144,1024]{3,2,1,0:T(8,128)(2,1)}, u32[]{:S(2)}, u32[]{:S(2)}) collective-permute-start(bf16[4,2,144,1024]{3,2,1,0:T(8,128)(2,1)} %fusion.158), channel_id=1, source_target_pairs={{0,2},{2,0},{4,6},{6,4},{8,10},{10,8},{12,14},{14,12},{16,18},{18,... | collective-permute-start | bytes 7077896 | tf_op jit(solution)/shard_map/ppermute | solution.py:36
  1030.7 31.9 %collective-permute-start.27 = (bf16[1,144,4608]{2,1,0:T(8,128)(2,1)}, bf16[1,144,4608]{2,1,0:T(8,128)(2,1)}, u32[]{:S(2)}, u32[]{:S(2)}) collective-permute-start(bf16[1,144,4608]{2,1,0:T(8,128)(2,1)} %dynamic-slice_bitcast_fusion.4), channel_id=1, source_target_pairs={{0,4},{2,6},{4,0},{6,2},{8,12},{10,14},{12,8},{14,10},{16,20},{18,... | collective-permute-start | bytes 3981320 | tf_op jit(solution)/shard_map/ppermute | solution.py:36
  1042.0 247.4 %reduce-scatter.11.cloned.1.call-start = ((), (), s32[]{:S(2)}) async-start(), calls=%async_computation.11 | async-start | bytes 1474560 | tf_op jit(solution)/shard_map/reduce_scatter | solution.py:121
  1075.2 30.7 %collective-permute-start.29 = (bf16[1,144,4608]{2,1,0:T(8,128)(2,1)S(1)}, bf16[1,144,4608]{2,1,0:T(8,128)(2,1)S(1)}, u32[]{:S(2)}, u32[]{:S(2)}) collective-permute-start(bf16[1,144,4608]{2,1,0:T(8,128)(2,1)S(1)} %copy-done.49), channel_id=1, source_target_pairs={{0,4},{2,6},{4,0},{6,2},{8,12},{10,14},{12,8},{14,10},{16,20},{18,... | collective-permute-start | bytes 3981320 | tf_op jit(solution)/shard_map/ppermute | solution.py:36
  1105.9 35.0 %collective-permute-start.32 = (bf16[4,2,144,1024]{3,2,1,0:T(8,128)(2,1)}, bf16[4,2,144,1024]{3,2,1,0:T(8,128)(2,1)}, u32[]{:S(2)}, u32[]{:S(2)}) collective-permute-start(bf16[4,2,144,1024]{3,2,1,0:T(8,128)(2,1)} %fusion.166), channel_id=1, source_target_pairs={{0,2},{2,0},{4,6},{6,4},{8,10},{10,8},{12,14},{14,12},{16,18},{18,... | collective-permute-start | bytes 7077896 | tf_op jit(solution)/shard_map/ppermute | solution.py:36
  1105.9 35.0 %collective-permute-start.31 = (bf16[4,2,144,1024]{3,2,1,0:T(8,128)(2,1)}, bf16[4,2,144,1024]{3,2,1,0:T(8,128)(2,1)}, u32[]{:S(2)}, u32[]{:S(2)}) collective-permute-start(bf16[4,2,144,1024]{3,2,1,0:T(8,128)(2,1)} %fusion.161), channel_id=1, source_target_pairs={{0,2},{2,0},{4,6},{6,4},{8,10},{10,8},{12,14},{14,12},{16,18},{18,... | collective-permute-start | bytes 7077896 | tf_op jit(solution)/shard_map/ppermute | solution.py:36
  1109.5 31.4 %collective-permute-start.30 = (bf16[1,144,4608]{2,1,0:T(8,128)(2,1)}, bf16[1,144,4608]{2,1,0:T(8,128)(2,1)}, u32[]{:S(2)}, u32[]{:S(2)}) collective-permute-start(bf16[1,144,4608]{2,1,0:T(8,128)(2,1)} %dynamic-slice_bitcast_fusion.1), channel_id=1, source_target_pairs={{0,4},{2,6},{4,0},{6,2},{8,12},{10,14},{12,8},{14,10},{16,20},{18,... | collective-permute-start | bytes 3981320 | tf_op jit(solution)/shard_map/ppermute | solution.py:36
  1199.7 91.5 %reduce-scatter.7.cloned.1.call-start = ((), (), s32[]{:S(2)}) async-start(), calls=%async_computation.9 | async-start | bytes 1474560 | tf_op jit(solution)/shard_map/reduce_scatter | solution.py:121
  1228.9 64.2 %reduce-scatter.9.cloned.1.call-start = ((), (), s32[]{:S(2)}) async-start(), calls=%async_computation.10 | async-start | bytes 1474560 | tf_op jit(solution)/shard_map/reduce_scatter | solution.py:121
  1254.7 131.2 %reduce-scatter.15.cloned.1.call-start = ((), (), s32[]{:S(2)}) async-start(), calls=%async_computation.13 | async-start | bytes 6635520 | tf_op jit(solution)/shard_map/reduce_scatter | solution.py:121
  (140 other events, 2413.2 us)
Sparse Core Ops, SparseCore 0:
  16.6 180.0 all-gather.3
  198.2 110.0 all-gather.5
  309.9 110.0 all-gather.7
  889.8 95.8 reduce-scatter.16
  1042.1 95.1 reduce-scatter.12
  1199.9 28.8 reduce-scatter.10
  1231.6 27.8 reduce-scatter.6
  1261.8 28.1 reduce-scatter.8
  1292.4 93.5 reduce-scatter.14

commit v3 on v1

v3 whole, which is shorter than its diff:
```python
import jax
import jax.numpy as jnp
from jax import lax
from jax.experimental import pallas as pl
from jax.experimental.pallas import tpu as pltpu
from jax.sharding import PartitionSpec as P

QUERY_HEADS = 8
KEY_VALUE_HEADS = 4
HEAD_WIDTH = 256
SEQ_LEN = 1024

EPSILON = 1e-06
LOGIT_CAP = 50.0

BF16 = jnp.bfloat16
F32 = jnp.float32
VMEM_BYTES = 56 * 1024 * 1024


def rms_norm(values, gain):
    return values * lax.rsqrt(jnp.mean(values * values, axis=-1, keepdims=True) + EPSILON) * gain


def swap(rows):
    return lax.ppermute(rows, "tensor", [(0, 1), (1, 0)])


def flip(array, bit, dp):
    return lax.ppermute(array, "dp", [(i, i ^ (1 << bit)) for i in range(dp)])


def gather_small(piece, dp):
    other = swap(piece)
    whole = jnp.where(
        lax.axis_index("tensor") == 0,
        jnp.concatenate([piece, other], axis=1),
        jnp.concatenate([other, piece], axis=1),
    )
    bit = 0
    while (1 << bit) < dp:
        other = flip(whole, bit, dp)
        high = (lax.axis_index("dp") >> bit) & 1
        whole = jnp.where(
            high == 0,
            jnp.concatenate([whole, other], axis=1),
            jnp.concatenate([other, whole], axis=1),
        )
        bit += 1
    return whole


def scatter_small(partial, dp):
    bit = dp.bit_length() - 2
    while bit >= 0:
        half = partial.shape[1] // 2
        low, high = partial[:, :half], partial[:, half:]
        mine = (lax.axis_index("dp") >> bit) & 1
        keep = jnp.where(mine == 0, low, high)
        give = jnp.where(mine == 0, high, low)
        partial = keep + flip(give, bit, dp)
        bit -= 1
    half = partial.shape[1] // 2
    low, high = partial[:, :half], partial[:, half:]
    mine = lax.axis_index("tensor")
    keep = jnp.where(mine == 0, low, high)
    give = jnp.where(mine == 0, high, low)
    return keep + swap(give)


def dot(left, right):
    return lax.dot_general(left, right, (((1,), (0,)), ((), ())), preferred_element_type=F32)


def dot_nt(left, right):
    return lax.dot_general(left, right, (((1,), (1,)), ((), ())), preferred_element_type=F32)


def call(kernel, steps, scalars, inputs, outputs, scratch=()):
    in_specs = [
        pl.BlockSpec(block, index, pipeline_mode=pl.Buffered(1) if whole else None)
        for _, block, index, whole in inputs
    ]
    out_specs = [pl.BlockSpec(block, index) for _, _, block, index in outputs]
    shapes = [jax.ShapeDtypeStruct(shape, dtype) for shape, dtype, _, _ in outputs]
    return pl.pallas_call(
        kernel,
        grid_spec=pltpu.PrefetchScalarGridSpec(
            num_scalar_prefetch=1,
            grid=(steps,),
            in_specs=in_specs,
            out_specs=out_specs,
            scratch_shapes=list(scratch),
        ),
        out_shape=shapes,
        compiler_params=pltpu.CompilerParams(vmem_limit_bytes=VMEM_BYTES),
        cost_estimate=pl.CostEstimate(flops=1, bytes_accessed=1, transcendentals=0),
    )(jnp.stack(scalars).astype(jnp.int32), *(array for array, *_ in inputs))


def tile_of(extent, most=512):
    tile = most
    while extent % tile:
        tile //= 2
    return tile


def turned(pieces, scalars):
    rows = [piece.shape[0] for piece in pieces]
    width = pieces[0].shape[1]
    tile = tile_of(width, 768)

    def kernel(_, *refs):
        *ins, out = refs
        row = lax.broadcasted_iota(jnp.int32, (tile, tile), 0)
        column = lax.broadcasted_iota(jnp.int32, (tile, tile), 1)
        same = (row == column).astype(F32).astype(BF16)
        at = 0
        for ref, count in zip(ins, rows):
            out[:, at : at + count] = dot_nt(same, ref[...]).astype(BF16)
            at += count

    (out,) = call(
        kernel,
        width // tile,
        scalars,
        [(piece, (count, tile), lambda j, s: (0, j), False) for piece, count in zip(pieces, rows)],
        [((width, sum(rows)), BF16, (tile, sum(rows)), lambda j, s: (j, 0))],
    )
    return out


def feed(mid, full_first, gate_at, full_up, scalars):
    rows, width = mid.shape
    columns = full_up.shape[1]
    tile = tile_of(columns)

    def kernel(_, mid_ref, gate_ref, up_ref, hidden_ref, active_ref, slope_ref):
        gate = dot(mid_ref[...], gate_ref[...])
        up = dot(mid_ref[...], up_ref[...])
        inner = 0.7978845608028654 * (gate + 0.044715 * gate * gate * gate)
        bent = jnp.tanh(inner)
        half = 0.5 * (1.0 + bent)
        active = gate * half
        slope = half + gate * (0.5 * (1.0 - bent * bent)) * (
            0.7978845608028654 * (1.0 + 3 * 0.044715 * gate * gate)
        )
        hidden_ref[...] = (active * up).astype(BF16)
        active_ref[...] = active.astype(BF16)
        slope_ref[...] = (slope * up).astype(BF16)

    out = ((rows, columns), BF16, (rows, tile), lambda j, s: (0, j))
    first = gate_at // tile
    return call(
        kernel,
        columns // tile,
        scalars,
        [
            (mid, (rows, width), lambda j, s: (0, 0), True),
            (full_first, (width, tile), lambda j, s: (0, first + j), False),
            (full_up, (width, tile), lambda j, s: (0, j), False),
        ],
        [out] * 3,
    )


def feed_out(hidden, block, size, full_down_t, dtype, scalars):
    inner = hidden.shape[1]
    width = full_down_t.shape[0]
    tile = tile_of(width, 256)

    def kernel(_, hidden_ref, down_ref, out):
        out[...] = dot_nt(hidden_ref[...], down_ref[...]).astype(dtype)

    (out,) = call(
        kernel,
        width // tile,
        scalars,
        [
            (hidden, (size, inner), lambda j, s: (block, 0), True),
            (full_down_t, (tile, inner), lambda j, s: (j, 0), False),
        ],
        [((size, width), dtype, (size, tile), lambda j, s: (0, j))],
    )
    return out


def hidden_back(line, pieces, full_down_t, scalars):
    width, columns = full_down_t.shape
    tile = tile_of(columns)
    count = len(pieces)
    sizes = [piece[0].shape[0] for piece in pieces]

    def kernel(_, *refs):
        down = refs[3 * count][...]
        for index in range(count):
            rows_ref, active_ref, slope_ref = refs[index::count][:3]
            gate_ref, up_ref = refs[3 * count + 1 + index :: count][:2]
            d_hidden = dot(rows_ref[...], down)
            gate_ref[...] = (d_hidden * slope_ref[...].astype(F32)).astype(BF16)
            up_ref[...] = (d_hidden * active_ref[...].astype(F32)).astype(BF16)

    rows = [line.next(piece[0]) if index == 0 else piece[0] for index, piece in enumerate(pieces)]
    place = lambda j, s: (0, j)
    factors = [
        (piece[factor], (size, tile), lambda j, s, block=piece[3]: (block, j), False)
        for factor in (1, 2)
        for piece, size in zip(pieces, sizes)
    ]
    outs = line.mark(
        call(
            kernel,
            columns // tile,
            scalars,
            [(array, array.shape, lambda j, s: (0, 0), True) for array in rows]
            + factors
            + [(full_down_t, (width, tile), lambda j, s: (0, j), False)],
            [((size, columns), BF16, (size, tile), place) for size in sizes] * 2,
        )
    )
    return outs[:count], outs[count:]


def mid_back(d_gate, d_up, full_first, gate_at, full_up, dtype, scalars):
    inner = d_gate[0].shape[1]
    width = full_up.shape[0]
    tile = tile_of(width, 256)
    part = 1536
    parts = inner // part
    count = len(d_gate)

    def kernel(_, *refs):
        gates, ups, refs = refs[:count], refs[count : 2 * count], refs[2 * count :]
        for gate_ref, up_ref, out in zip(gates, ups, refs[parts + 1 :]):
            total = dot_nt(up_ref[...], refs[parts][...])
            for index in range(parts):
                here = slice(index * part, (index + 1) * part)
                total += dot_nt(gate_ref[:, here], refs[index][...])
            out[...] = total.astype(dtype)

    return call(
        kernel,
        width // tile,
        scalars,
        [(piece, piece.shape, lambda j, s: (0, 0), True) for piece in [*d_gate, *d_up]]
        + [
            (full_first, (tile, part), lambda j, s, index=index: (j, gate_at // part + index), False)
            for index in range(parts)
        ]
        + [(full_up, (tile, inner), lambda j, s: (j, 0), False)],
        [
            ((piece.shape[0], width), dtype, (piece.shape[0], tile), lambda j, s: (0, j))
            for piece in d_gate
        ],
    )


def dot_tn(left, right):
    return lax.dot_general(left, right, (((0,), (0,)), ((), ())), preferred_element_type=F32)


def soft(query, keys, start):
    scores = dot_nt(query, keys)
    tangent = jnp.tanh(scores * (HEAD_WIDTH**-0.5 / LOGIT_CAP))
    row = lax.broadcasted_iota(jnp.int32, scores.shape, 0) + start
    column = lax.broadcasted_iota(jnp.int32, scores.shape, 1)
    capped = jnp.where(column <= row, LOGIT_CAP * tangent, -jnp.inf)
    terms = jnp.exp(capped - jnp.max(capped, axis=1, keepdims=True))
    return terms / jnp.sum(terms, axis=1, keepdims=True), tangent


def attend(qkv, heads, group, length, scalars, block=256):
    total = qkv.shape[0]
    block = min(block, length)
    seqs = total // length

    def kernel(_, query_ref, key_ref, value_ref, out_ref):
        for start in range(0, length, block):
            end = start + block
            weights, _ = soft(query_ref[start:end, :], key_ref[:end, :], start)
            out_ref[start:end, :] = dot(weights.astype(BF16), value_ref[:end, :]).astype(BF16)

    shape = (length, HEAD_WIDTH)
    (out,) = call(
        kernel,
        seqs * heads,
        scalars,
        [
            (qkv, shape, lambda j, s: (j // heads, j % heads), False),
            (qkv, shape, lambda j, s: (j // heads, heads + 2 * (j % heads // group)), False),
            (qkv, shape, lambda j, s: (j // heads, heads + 2 * (j % heads // group) + 1), False),
        ],
        [((total, heads * HEAD_WIDTH), BF16, shape, lambda j, s: (j // heads, j % heads))],
    )
    return out


def attend_back(qkv, d_attended, heads, group, length, scalars, block=256):
    total = qkv.shape[0]
    block = min(block, length)
    seqs = total // length
    key_heads = heads // group
    scale = HEAD_WIDTH**-0.5

    def kernel(_, query_ref, pair_ref, d_ref, d_query_ref, d_pair_ref, d_key, d_value):
        d_key[...] = jnp.zeros_like(d_key)
        d_value[...] = jnp.zeros_like(d_value)
        for member in range(group):
            columns = slice(member * HEAD_WIDTH, (member + 1) * HEAD_WIDTH)
            for start in range(0, length, block):
                end = start + block
                query = query_ref[start:end, columns]
                d_rows = d_ref[start:end, columns]
                keys, values = pair_ref[:end, :HEAD_WIDTH], pair_ref[:end, HEAD_WIDTH:]
                weights, tangent = soft(query, keys, start)
                d_soft = dot_nt(d_rows, values)
                d_capped = weights * (
                    d_soft - jnp.sum(weights * d_soft, axis=1, keepdims=True)
                )
                d_scores = (d_capped * (1.0 - tangent * tangent)).astype(BF16)
                d_query_ref[start:end, columns] = (dot(d_scores, keys) * scale).astype(BF16)
                d_key[:end, :] += dot_tn(d_scores, query)
                d_value[:end, :] += dot_tn(weights.astype(BF16), d_rows)
        d_pair_ref[:, :HEAD_WIDTH] = (d_key[...] * scale).astype(BF16)
        d_pair_ref[:, HEAD_WIDTH:] = d_value[...].astype(BF16)

    wide, pair = (length, group * HEAD_WIDTH), (length, 2 * HEAD_WIDTH)
    first_pair = heads // 2
    place = lambda j, s: (j // key_heads, j % key_heads)
    return call(
        kernel,
        seqs * key_heads,
        scalars,
        [
            (qkv, wide, place, False),
            (qkv, pair, lambda j, s: (j // key_heads, first_pair + j % key_heads), False),
            (d_attended, wide, place, False),
        ],
        [
            ((total, heads * HEAD_WIDTH), BF16, wide, place),
            ((total, key_heads * 2 * HEAD_WIDTH), BF16, pair, place),
        ],
        scratch=[pltpu.VMEM((length, HEAD_WIDTH), F32)] * 2,
    )


class Grad:
    def __init__(self, dp, chunks, lefts, rights, first_column, columns, scalars):
        self.dp, self.chunks, self.scalars = dp, chunks, scalars
        width = lefts[0].shape[0]
        self.rest, self.rows = dp // 4, width // dp
        self.lefts = [left.reshape(self.rest, 2, 2, self.rows, left.shape[1]) for left in lefts]
        self.rights = rights
        self.columns, self.tile = columns, tile_of(columns)
        self.first = first_column // self.tile
        self.count = len(lefts) + len(rights)

    def inputs(self, block, place):
        return [
            (
                left,
                (self.rest, block, None, *left.shape[3:]),
                lambda j, s: (0, *place(s), 0, 0),
                True,
            )
            for left in self.lefts
        ] + [
            (array, (size, self.tile), lambda j, s, row=row: (row(s), self.first + j), False)
            for array, size, row in self.rights
        ]

    def product(self, refs):
        return sum_of_products(refs[: len(self.lefts)], refs[len(self.lefts) : self.count])

    def run(self, kernel, inputs, outputs):
        return call(kernel, self.columns // self.tile, self.scalars, inputs, outputs)

    def give(self):
        def kernel(_, *refs):
            refs[-1][...] = self.product(refs).astype(BF16)

        shape = (self.rest, 2, self.rows)
        (self.given,) = self.run(
            kernel,
            self.inputs(2, lambda s: (0, 1 - s[0])),
            [((*shape, self.columns), BF16, (*shape, self.tile), lambda j, s: (0, 0, 0, j))],
        )
        return self.given

    def to_core(self):
        return self.given, lambda array: flip(array, 0, self.dp)

    def side(self, from_core):
        self.from_core = from_core
        size = self.rest // self.chunks

        def kernel(_, *refs):
            core = refs[self.count]
            result = (self.product(refs) + core[...].astype(F32)).astype(BF16)
            for index, out in enumerate(refs[self.count + 1 :]):
                out[...] = result[index * size : (index + 1) * size]

        self.give_side = self.run(
            kernel,
            self.inputs(None, lambda s: (1 - s[1], s[0]))
            + [
                (
                    from_core,
                    (self.rest, None, self.rows, self.tile),
                    lambda j, s: (0, 1 - s[1], 0, j),
                    False,
                )
            ],
            [
                (
                    (size, self.rows, self.columns),
                    BF16,
                    (size, self.rows, self.tile),
                    lambda j, s: (0, 0, j),
                )
            ]
            * self.chunks,
        )
        return self.give_side[0]

    def to_side(self, chunk):
        return self.give_side[chunk], lambda array: flip(array, 1, self.dp)

    def own(self, *from_side):
        size = self.rest // self.chunks

        def kernel(_, *refs):
            core, sides, out = refs[self.count], refs[self.count + 1 : -1], refs[-1]
            result = self.product(refs) + core[...].astype(F32)
            for index, ref in enumerate(sides):
                here = slice(index * size, (index + 1) * size)
                out[here] = (result[here] + ref[...].astype(F32)).astype(BF16)

        place = lambda j, s: (0, 0, j)
        (self.total,) = self.run(
            kernel,
            self.inputs(None, lambda s: (s[1], s[0]))
            + [
                (
                    self.from_core,
                    (self.rest, None, self.rows, self.tile),
                    lambda j, s: (0, s[1], 0, j),
                    False,
                )
            ]
            + [(part, (size, self.rows, self.tile), place, False) for part in from_side],
            [
                (
                    (self.rest, self.rows, self.columns),
                    BF16,
                    (self.rest, self.rows, self.tile),
                    place,
                )
            ],
        )
        return self.total

    def along_rest(self, line):
        groups = [[low + 4 * high for high in range(self.rest)] for low in range(4)]
        self.sums = lax.psum_scatter(
            line.next(self.total).reshape(-1, self.columns),
            "dp",
            scatter_dimension=0,
            axis_index_groups=groups,
            tiled=True,
        )

    def arrive(self, line):
        (self.sums,) = line.land(self.sums)

    def result(self):
        return self.sums.astype(F32)


def sum_of_products(lefts, rights):
    *lead, rows, _ = lefts[0].shape
    columns = rights[0].shape[1]
    count = 1
    for extent in lead:
        count *= extent
    rights = [right[...] for right in rights]
    pairs, index = [], 0
    for left in lefts:
        left, at = left[...], 0
        while at < left.shape[-1]:
            size = rights[index].shape[0]
            pairs.append((left[..., at : at + size], rights[index]))
            at += size
            index += 1

    def total(pick_block):
        result = None
        for left, right in pairs:
            term = dot(pick_block(left), right)
            result = term if result is None else result + term
        return result

    if rows % 16 == 0:
        blocks = total(lambda left: left.reshape(count * rows, left.shape[-1]))
    else:
        blocks = jnp.stack(
            [
                total(lambda left, block=block: left.reshape(count, rows, -1)[block])
                for block in range(count)
            ]
        )
    return blocks.reshape(*lead, rows, columns)


def tied(*arrays):
    return lax.optimization_barrier(arrays)


class Line:
    def __init__(self):
        self.last = None

    def next(self, array):
        if self.last is not None:
            array, _ = tied(array, self.last)
        return array

    def mark(self, array):
        self.last = array[0] if isinstance(array, (list, tuple)) else array
        return array

    def send(self, *transfers):
        return [send(self.next(array)) for array, send in transfers]

    def land(self, *flying):
        *taken, self.last = tied(*flying, self.last)
        return taken


def projected(pieces, weights, first_column, columns, scalars):
    count = len(pieces)
    half = sum(piece.shape[0] for piece in pieces) // 2
    width = pieces[0].shape[1]
    tile = tile_of(columns)

    def kernel(scalar_ref, *refs):
        *ins, weight_ref, out = refs
        weight = weight_ref[...]
        at = 0
        for ref in ins:
            owner = scalar_ref[2] if at < half else 1 - scalar_ref[2]
            size = ref.shape[0]
            start = pl.multiple_of(owner * half + at % half, size)
            out[pl.ds(start, size), :] = dot(ref[...], weight).astype(BF16)
            at += size

    (out,) = call(
        kernel,
        columns // tile,
        scalars,
        [(piece, piece.shape, lambda j, s: (0, 0), True) for piece in pieces]
        + [(weights, (width, tile), lambda j, s: (0, first_column // tile + j), False)],
        [((2 * half, columns), BF16, (2 * half, tile), lambda j, s: (0, j))],
    )
    return out


def projected_back(sources, weights, owner, pieces, dtype, scalars):
    half = sources[0][0].shape[0] // 2
    width = weights.shape[0]
    tile = tile_of(width, 256)
    size = half // pieces
    count = len(sources)

    def kernel(_, *refs):
        total = None
        for rows, weight in zip(refs[:count], refs[count : 2 * count]):
            term = dot_nt(rows[...], weight[...])
            total = term if total is None else total + term
        result = total.astype(dtype)
        for index, out in enumerate(refs[2 * count :]):
            out[...] = result[index * size : (index + 1) * size]

    return call(
        kernel,
        width // tile,
        scalars,
        [
            (array, (half, array.shape[1]), lambda j, s: (owner(s), 0), True)
            for array, _ in sources
        ]
        + [
            (weights, (tile, array.shape[1]), lambda j, s, block=block: (j, block), False)
            for array, block in sources
        ],
        [((size, width), dtype, (size, tile), lambda j, s: (0, j))] * pieces,
    )


def make_body(dp):
    def body(
        layer_input,
        query_weight,
        key_weight,
        value_weight,
        w_output,
        w_gate,
        w_up,
        w_down,
        gain_attn_in,
        gain_attn_out,
        gain_ffn_in,
        gain_ffn_out,
        cotangent,
    ):
        line = Line()
        place, turn = lax.axis_index("dp"), lax.axis_index("tensor")
        scalars = [place & 1, (place >> 1) & 1, turn]
        to_other = lambda array: (array, swap)
        mine, theirs = (lambda s: s[2]), (lambda s: 1 - s[2])
        query_cols, key_cols = query_weight.shape[1], key_weight.shape[1]
        qkv_cols = query_cols + 2 * key_cols
        gate_at = qkv_cols + query_cols
        columns = w_gate.shape[1]
        half = layer_input.shape[0]
        quarter = half // 2
        heads = query_cols // HEAD_WIDTH
        group = QUERY_HEADS // KEY_VALUE_HEADS
        pairs = []
        for head in range(key_cols // HEAD_WIDTH):
            here = slice(head * HEAD_WIDTH, (head + 1) * HEAD_WIDTH)
            pairs += [key_weight[:, here], value_weight[:, here]]
        full_first = lax.all_gather(
            jnp.concatenate([query_weight, *pairs, w_output.T, w_gate], axis=1),
            "dp",
            axis=0,
            tiled=True,
        )
        full_up = lax.all_gather(w_up, "dp", axis=0, tiled=True)
        full_down_t = lax.all_gather(w_down.T, "dp", axis=0, tiled=True)
        gains = gather_small(
            jnp.stack([gain_attn_in, gain_attn_out, gain_ffn_in, gain_ffn_out]), dp
        )
        gain_a, gain_b, gain_c, gain_d = gains[0], gains[1], gains[2], gains[3]

        residual_in = layer_input.astype(F32)
        upstream = cotangent.astype(F32)
        input_own = line.mark(rms_norm(residual_in, gain_a).astype(BF16))
        input_other = swap(input_own)
        input_own_t = line.mark(turned([input_own], scalars))
        (input_other,) = line.land(input_other)
        input_other_t = line.mark(turned([input_other], scalars))
        qkv = line.mark(
            projected([input_own, line.next(input_other)], full_first, 0, qkv_cols, scalars)
        )
        attended = line.mark(attend(qkv, heads, group, SEQ_LEN, scalars))
        output_block = qkv_cols // query_cols
        (give,) = line.mark(
            projected_back([(attended, output_block)], full_first, theirs, 1, BF16, scalars)
        )
        (taken,) = line.send(to_other(give))
        (kept,) = line.mark(
            projected_back(
                [(line.next(attended), output_block)], full_first, mine, 1, F32, scalars
            )
        )
        branch_attn = kept + taken.astype(F32)
        middle, pull_attn_out = jax.vjp(
            lambda values, gain: residual_in + rms_norm(values, gain), branch_attn, gain_b
        )
        normed_mid_f, pull_ffn_in = jax.vjp(rms_norm, middle, gain_c)
        mid_own = line.mark(normed_mid_f.astype(BF16))
        (mid_other,) = line.send(to_other(mid_own))
        hidden_own, active_own, slope_own = line.mark(
            feed(mid_own, full_first, gate_at, full_up, scalars)
        )
        mid_own_t = line.mark(turned([line.next(mid_own)], scalars))
        (mid_other,) = line.land(mid_other)
        hidden_other, active_other, slope_other = line.mark(
            feed(line.next(mid_other), full_first, gate_at, full_up, scalars)
        )
        mid_other_t = line.mark(turned([line.next(mid_other)], scalars))

        def ffn_back(kept, taken, middle, upstream):
            branch = kept + taken.astype(F32)
            ffn_out, pull = jax.vjp(rms_norm, branch, gain_d)
            d_ffn, grad_gain = pull(upstream)
            return (middle + ffn_out).astype(BF16), line.mark(d_ffn.astype(BF16)), grad_gain

        low, high = slice(0, quarter), slice(quarter, half)
        give_1 = line.mark(
            feed_out(line.next(hidden_other), 0, quarter, full_down_t, BF16, scalars)
        )
        (taken_1,) = line.send(to_other(give_1))
        give_2 = line.mark(
            feed_out(line.next(hidden_other), 1, quarter, full_down_t, BF16, scalars)
        )
        (taken_1,) = line.land(taken_1)
        (taken_2,) = line.send(to_other(give_2))
        kept = line.mark(feed_out(line.next(hidden_own), 0, half, full_down_t, F32, scalars))
        output_1, d_ffn_1, grad_d_1 = ffn_back(
            line.next(kept)[low], taken_1, middle[low], upstream[low]
        )
        (taken_2,) = line.land(taken_2)
        (d_ffn_3,) = line.send(to_other(d_ffn_1))
        output_2, d_ffn_2, grad_d_2 = ffn_back(
            line.next(kept)[high], taken_2, middle[high], upstream[high]
        )
        d_ffn_own_t = line.mark(turned([line.next(d_ffn_1), d_ffn_2], scalars))
        (d_gate_1,), (d_up_1,) = hidden_back(
            line, [(d_ffn_1, active_own, slope_own, 0)], full_down_t, scalars
        )
        (d_ffn_3,) = line.land(d_ffn_3)
        (d_ffn_4,) = line.send(to_other(d_ffn_2))
        layer_output = jnp.concatenate([output_1, output_2], axis=0)
        grad_d = grad_d_1 + grad_d_2
        (d_gate_2, d_gate_3), (d_up_2, d_up_3) = hidden_back(
            line,
            [(d_ffn_2, active_own, slope_own, 1), (d_ffn_3, active_other, slope_other, 0)],
            full_down_t,
            scalars,
        )
        (d_ffn_4,) = line.land(d_ffn_4)
        d_ffn_other_t = line.mark(turned([line.next(d_ffn_3), d_ffn_4], scalars))

        first = lambda s: 0
        tile = tile_of(columns)
        tiles = columns // tile
        cuts = [0, 2 * tile, 5 * tile, columns]
        split = tile * -(-tiles // 2)
        halves = [(0, split), (split, columns - split)]
        hidden_rights = [(hidden_own, half, first), (hidden_other, half, first)]
        mid_lefts = [mid_own_t, mid_other_t]

        def down_part(part, chunks):
            lefts = [line.next(d_ffn_own_t), d_ffn_other_t]
            start, end = cuts[part], cuts[part + 1]
            return Grad(dp, chunks, lefts, hidden_rights, start, end - start, scalars)

        def mid_part(pieces, part):
            rights = [(line.next(piece), quarter, first) for piece in pieces]
            return Grad(dp, 2, mid_lefts, rights, *halves[part], scalars)

        def mid_back_of(gates, ups, dtype):
            gates = [line.next(gates[0]), *gates[1:]]
            return line.mark(mid_back(gates, ups, full_first, gate_at, full_up, dtype, scalars))

        down_0 = down_part(0, 1)
        line.mark(down_0.give())
        (core_0,) = line.send(down_0.to_core())
        down_1 = down_part(1, 1)
        line.mark(down_1.give())
        (core_0,) = line.land(core_0)
        line.mark(down_0.side(line.next(core_0)))

        down_0_side, core_1 = line.send(down_0.to_side(0), down_1.to_core())
        down_2 = down_part(2, 2)
        line.mark(down_2.give())
        (core_1,) = line.land(core_1)
        line.mark(down_1.side(line.next(core_1)))
        (d_gate_4,), (d_up_4,) = hidden_back(
            line, [(d_ffn_4, active_other, slope_other, 1)], full_down_t, scalars
        )
        (down_0_side,) = line.land(down_0_side)
        d_gates = [d_gate_1, d_gate_2, d_gate_3, d_gate_4]
        d_ups = [d_up_1, d_up_2, d_up_3, d_up_4]

        down_1_side, core_2 = line.send(down_1.to_side(0), down_2.to_core())
        line.mark(down_0.own(line.next(down_0_side)))
        gate_0 = mid_part(d_gates, 0)
        line.mark(gate_0.give())
        (core_2,) = line.land(core_2)
        line.mark(down_2.side(line.next(core_2)))
        gate_1 = mid_part(d_gates, 1)
        line.mark(gate_1.give())
        (down_1_side,) = line.land(down_1_side)

        side_0, core_0, core_1 = line.send(
            down_2.to_side(0), gate_0.to_core(), gate_1.to_core()
        )
        down_0.along_rest(line)
        line.mark(down_1.own(line.next(down_1_side)))
        core_0, core_1 = line.land(core_0, core_1)
        line.mark(gate_0.side(line.next(core_0)))
        (side_0,) = line.land(side_0)
        down_0.arrive(line)

        (side_1,) = line.send(down_2.to_side(1))
        down_1.along_rest(line)
        give_1, give_2 = mid_back_of(d_gates[2:], d_ups[2:], BF16)
        (side_1,) = line.land(side_1)

        gate_0_side_0, taken_1 = line.send(gate_0.to_side(0), to_other(give_1))
        line.mark(down_2.own(line.next(side_0), side_1))
        line.mark(gate_1.side(line.next(core_1)))
        up_0 = mid_part(d_ups, 0)
        line.mark(up_0.give())
        gate_0_side_0, taken_1 = line.land(gate_0_side_0, taken_1)
        down_1.arrive(line)

        gate_0_side_1, taken_2, core_0 = line.send(
            gate_0.to_side(1), to_other(give_2), up_0.to_core()
        )
        down_2.along_rest(line)
        kept_1, kept_2 = mid_back_of(d_gates[:2], d_ups[:2], F32)
        gate_0_side_1, taken_2, core_0 = line.land(gate_0_side_1, taken_2, core_0)

        (gate_1_side_0,) = line.send(gate_1.to_side(0))
        line.mark(gate_0.own(line.next(gate_0_side_0), gate_0_side_1))
        taken = jnp.concatenate([taken_1, taken_2], axis=0).astype(F32)
        d_mid_norm, grad_c = pull_ffn_in(
            jnp.concatenate([line.next(kept_1), kept_2], axis=0) + taken
        )
        d_middle = upstream + d_mid_norm
        d_branch, grad_b = pull_attn_out(d_middle)
        d_branch_own = line.mark(d_branch.astype(BF16))
        (gate_1_side_0,) = line.land(gate_1_side_0)
        down_2.arrive(line)

        gate_1_side_1, d_branch_3 = line.send(gate_1.to_side(1), to_other(d_branch_own[low]))
        gate_0.along_rest(line)
        line.mark(up_0.side(line.next(core_0)))
        up_1 = mid_part(d_ups, 1)
        line.mark(up_1.give())
        gate_1_side_1, d_branch_3 = line.land(gate_1_side_1, d_branch_3)

        up_0_side_0, core_1, d_branch_4 = line.send(
            up_0.to_side(0), up_1.to_core(), to_other(d_branch_own[high])
        )
        line.mark(gate_1.own(line.next(gate_1_side_0), gate_1_side_1))
        d_branch_own_t = line.mark(turned([line.next(d_branch_own)], scalars))
        (core_1,) = line.land(core_1)
        line.mark(up_1.side(line.next(core_1)))
        up_0_side_0, d_branch_4 = line.land(up_0_side_0, d_branch_4)
        gate_0.arrive(line)

        (up_0_side_1,) = line.send(up_0.to_side(1))
        gate_1.along_rest(line)
        d_attended = line.mark(
            projected(
                [line.next(d_branch_own), d_branch_3, d_branch_4],
                full_first,
                qkv_cols,
                query_cols,
                scalars,
            )
        )
        d_branch_other_t = line.mark(turned([line.next(d_branch_3), d_branch_4], scalars))
        output = Grad(
            dp,
            1,
            [d_branch_own_t, line.next(d_branch_other_t)],
            [(attended, half, mine), (attended, half, theirs)],
            0,
            query_cols,
            scalars,
        )
        line.mark(output.give())
        (up_0_side_1,) = line.land(up_0_side_1)

        up_1_side_0, core = line.send(up_1.to_side(0), output.to_core())
        line.mark(up_0.own(line.next(up_0_side_0), up_0_side_1))
        d_query, d_pair = line.mark(
            attend_back(qkv, line.next(d_attended), heads, group, SEQ_LEN, scalars)
        )
        up_1_side_0, core = line.land(up_1_side_0, core)
        gate_1.arrive(line)

        (up_1_side_1,) = line.send(up_1.to_side(1))
        up_0.along_rest(line)
        line.mark(output.side(line.next(core)))

        def input_part(array, width):
            rights = [(line.next(array), half, mine), (array, half, theirs)]
            return Grad(dp, 1, [input_own_t, input_other_t], rights, 0, width, scalars)

        query = input_part(d_query, query_cols)
        line.mark(query.give())
        pair = input_part(d_pair, 2 * key_cols)
        line.mark(pair.give())
        (up_1_side_1,) = line.land(up_1_side_1)

        output_side, query_core, pair_core = line.send(
            output.to_side(0), query.to_core(), pair.to_core()
        )
        line.mark(up_1.own(line.next(up_1_side_0), up_1_side_1))
        query_core, pair_core = line.land(query_core, pair_core)
        line.mark(query.side(line.next(query_core)))
        line.mark(pair.side(line.next(pair_core)))
        (output_side,) = line.land(output_side)
        up_0.arrive(line)

        (query_side,) = line.send(query.to_side(0))
        up_1.along_rest(line)
        line.mark(output.own(line.next(output_side)))
        give_1, give_2 = line.mark(
            projected_back(
                [(line.next(d_query), 0), (d_pair, 1)], full_first, theirs, 2, BF16, scalars
            )
        )
        (query_side,) = line.land(query_side)

        pair_side, taken_1, taken_2 = line.send(
            pair.to_side(0), to_other(give_1), to_other(give_2)
        )
        line.mark(query.own(line.next(query_side)))
        (kept,) = line.mark(
            projected_back(
                [(line.next(d_query), 0), (d_pair, 1)], full_first, mine, 1, F32, scalars
            )
        )
        (pair_side,) = line.land(pair_side)
        line.mark(pair.own(line.next(pair_side)))
        up_1.arrive(line)
        output.along_rest(line)
        output.arrive(line)
        query.along_rest(line)
        taken_1, taken_2 = line.land(taken_1, taken_2)
        _, pull_attn_in = jax.vjp(rms_norm, residual_in, gain_a)
        taken = jnp.concatenate([taken_1, taken_2], axis=0).astype(F32)
        d_input_norm, grad_a = pull_attn_in(line.next(kept) + taken)
        input_grad = line.mark(d_middle + d_input_norm)
        query.arrive(line)
        pair.along_rest(line)
        small = scatter_small(jnp.stack([grad_a, grad_b, grad_c, grad_d]), dp)

        down, gate, up = [down_0, down_1, down_2], [gate_0, gate_1], [up_0, up_1]
        grad_pair = pair.result().reshape(-1, key_cols // HEAD_WIDTH, 2, HEAD_WIDTH)
        grad_down = jnp.concatenate([part.result() for part in down], axis=1).T
        return (
            layer_output,
            input_grad,
            query.result(),
            grad_pair[:, :, 0].reshape(-1, key_cols),
            grad_pair[:, :, 1].reshape(-1, key_cols),
            output.result().T,
            jnp.concatenate([part.result() for part in gate], axis=1),
            jnp.concatenate([part.result() for part in up], axis=1),
            grad_down,
            small[0],
            small[1],
            small[2],
            small[3],
        )

    return body


def solution(mesh):
    rows = P(("dp", "tensor"), None)
    gain = P(("dp", "tensor"))
    into, out_of = P("dp", "tensor"), P("tensor", "dp")
    return jax.shard_map(
        make_body(mesh.shape["dp"]),
        mesh=mesh,
        in_specs=(rows, into, into, into, out_of, into, into, out_of, gain, gain, gain, gain, rows),
        out_specs=(rows, rows, into, into, into, out_of, into, into, out_of, gain, gain, gain, gain),
        check_vma=False,
    )
```

time: 1640 us -> 1180 us (0.72)
  Pallas kernels: 0 us -> 600 us
  waiting for transfers between devices: 970 us -> 406 us
  matrix products: 431 us -> 0 us
  local copies, waits for them, and re-layouts: 73.9 us -> 41 us
  other arithmetic: 92.6 us -> 62.9 us
    pallas_call x0 -> x56, Pallas kernels: none -> 600 us  [call(): pl.pallas_call(kernel, grid_spec=pltpu.PrefetchScalarGridSpec(num_scalar_...]
    dot_general x37 -> x0, matrix products: 431 us -> none  [the longest x20 288 us: matmul(): return jnp.dot(left, right, preferred_element_type=F32)]
    ppermute x15 -> x0, waiting for transfers between devices: 209 us -> none  [scatter_grad(): result = result + lax.ppermute(give, 'dp', pairs).astype(F32)]
    ppermute x10 -> x15, waiting for transfers between devices: 331 us -> 130 us  [swap(): return lax.ppermute(rows, 'tensor', [(0, 1), (1, 0)])]
    ppermute x18 -> x33, waiting for transfers between devices: 293 us -> 94 us  [flip(): return lax.ppermute(array, 'dp', [(i, i ^ 1 << bit) for i in range(dp)])]
    all_gather x2 -> x1, waiting for transfers between devices: 40.3 us -> 101 us  [body(): lax.all_gather(jnp.concatenate([query_weight, *pairs, w_output.T, w_gate]...]
    all_gather x1, waiting for transfers between devices: 77.3 us -> 36.9 us  [body(): full_down_t = lax.all_gather(w_down.T, 'dp', axis=0, tiled=True)]
    reduce_scatter x0 -> x10, waiting for transfers between devices: none -> 31.8 us  [along_rest(): lax.psum_scatter(line.next(self.total).reshape(-1, self.columns), 'dp', s...]
  transfers between devices with their start and end apart: 47 -> 61, of which waited for: 27 -> 35; matrix products, arithmetic and copies ran while one was open for 26% -> 6% of each run, Pallas kernels for 0% -> 48%
where the time goes in v3:
time: 1180 us
  Pallas kernels  600 us (51%)
  waiting for transfers between devices  406 us (34%)
  other arithmetic  62.9 us (5%)
  starting transfers between devices  51.3 us (4%)
  local copies, waits for them, and re-layouts  41 us (3%)
  between operations  15.1 us (1%)
    pallas_call x56, Pallas kernels, call(): pl.pallas_call(kernel, grid_spec=pltpu.PrefetchScalarGridSpec(num_scalar_...  600 us
    ppermute x15, waiting for transfers between devices, swap(): return lax.ppermute(rows, 'tensor', [(0, 1), (1, 0)])  130 us
    all_gather x1, waiting for transfers between devices, body(): lax.all_gather(jnp.concatenate([query_weight, *pairs, w_output.T, w_gate]...  101 us
    ppermute x33, waiting for transfers between devices, flip(): return lax.ppermute(array, 'dp', [(i, i ^ 1 << bit) for i in range(dp)])  94 us
    all_gather x1, waiting for transfers between devices, body(): full_down_t = lax.all_gather(w_down.T, 'dp', axis=0, tiled=True)  36.9 us
    reduce_scatter x10, waiting for transfers between devices, along_rest(): lax.psum_scatter(line.next(self.total).reshape(-1, self.columns), 'dp', s...  31.8 us
    unnamed x174, local copies, waits for them, and re-layouts  30.2 us
    ppermute x33, starting transfers between devices, flip(): return lax.ppermute(array, 'dp', [(i, i ^ 1 << bit) for i in range(dp)])  29 us
  transfers between devices with their start and end apart: 61, of which 35 were waited for; matrix products, arithmetic and copies ran while one was open for 6% of the time, Pallas kernels for 48%

profile of v3, /device:TPU:0, one launch (start us, length us, event | category | flops | bytes accessed | tf_op | source)
XLA Modules:
  0.0 1176.8 jit_solution(7291986341171491164)
XLA Ops:
  49.0 42.9 %collective-permute-done.5.refs_0_.refs_1_ = bf16[512,2304]{1,0:T(8,128)(2,1)} collective-permute-done((bf16[512,2304]{1,0:T(8,128)(2,1)}, bf16[512,2304]{1,0:T(8,128)(2,1)}, u32[]{:S(2)}, u32[]{:S(2)}) %collective-permute-start.5) | collective-permute-done | bytes 2359328 | tf_op jit(solution)/shard_map/ppermute | solution.py:26
  97.6 100.5 %all-gather.4.cloned.1.call-done.refs_2_.refs_1_.gate_ref.refs_4_.refs_5_.refs_6_.refs_3_ = bf16[2304,7680]{1,0:T(8,128)(2,1)} async-done(((bf16[144,7680]{1,0:T(8,128)(2,1)}), bf16[2304,7680]{1,0:T(8,128)(2,1)}) %all-gather.4.cloned.1.call-update) | async-done | bytes 35389456 | tf_op jit(solution)/shard_map/all_gather | solution.py:633
  198.2 15.3 %shard_map.230.query_ref.key_ref.value_ref.pair_ref = bf16[1024,2048]{1,0:T(8,128)(2,1)} custom-call(s32[3]{0:T(128)} %pad_add_fusion._.scalar_ref, bf16[512,2304]{1,0:T(8,128)(2,1)} %fusion.2.refs_0_, bf16[512,2304]{1,0:T(8,128)(2,1)} %collective-permute-done.5.refs_0_.refs_1_, ...), custom_call_target="tpu_custom_call" | custom-call | flops 1 | bytes 1 | tf_op jit(solution)/shard_map/pallas_call | solution.py:86
  213.5 11.4 shard_map.231.refs_0_.refs_2_.refs_3_
  224.8 9.9 shard_map.232
  236.2 10.4 shard_map.233
  246.5 41.8 %collective-permute-done.6 = bf16[512,2304]{1,0:T(8,128)(2,1)S(1)} collective-permute-done((bf16[512,2304]{1,0:T(8,128)(2,1)}, bf16[512,2304]{1,0:T(8,128)(2,1)S(1)}, u32[]{:S(2)}, u32[]{:S(2)}) %collective-permute-start.6) | collective-permute-done | bytes 2359328 | tf_op jit(solution)/shard_map/ppermute | solution.py:26
  297.8 12.1 %all-gather.6.cloned.1.call-done.up_ref.refs_7_ = bf16[2304,4608]{1,0:T(8,128)(2,1)} async-done(((bf16[144,4608]{1,0:T(8,128)(2,1)}), bf16[2304,4608]{1,0:T(8,128)(2,1)}) %all-gather.6.cloned.1.call-update) | async-done | bytes 21233680 | tf_op jit(solution)/shard_map/all_gather | solution.py:639
  309.9 30.8 %shard_map.234 = (bf16[512,4608]{1,0:T(8,128)(2,1)}, bf16[512,4608]{1,0:T(8,128)(2,1)}, bf16[512,4608]{1,0:T(8,128)(2,1)}) custom-call(s32[3]{0:T(128)} %pad_add_fusion._.scalar_ref, bf16[512,2304]{1,0:T(8,128)(2,1)} %copy-done.10, bf16[2304,7680]{1,0:T(8,128)(2,1)} %all-gather.4.cloned.1.call-done.refs_2_.refs_1_.gate_ref.refs_4_.refs_5_.refs_6_.refs_3_, ...), custom_call_target="tpu_custom_call" | custom-call | flops 1 | bytes 1 | tf_op jit(solution)/shard_map/pallas_call | solution.py:86
  349.1 29.8 %shard_map.236 = (bf16[512,4608]{1,0:T(8,128)(2,1)}, bf16[512,4608]{1,0:T(8,128)(2,1)}, bf16[512,4608]{1,0:T(8,128)(2,1)}) custom-call(s32[3]{0:T(128)} %pad_add_fusion._.scalar_ref, bf16[512,2304]{1,0:T(8,128)(2,1)} %collective-permute-done.7.mid_ref.refs_0_, ...), custom_call_target="tpu_custom_call" | custom-call | flops 1 | bytes 1 | tf_op jit(solution)/shard_map/pallas_call | solution.py:86
  384.7 36.9 %all-gather.8.cloned.1.call-done.down_ref.refs_3_.refs_6_ = bf16[2304,4608]{1,0:T(8,128)(2,1)} async-done(((bf16[144,4608]{1,0:T(8,128)(2,1)}), bf16[2304,4608]{1,0:T(8,128)(2,1)}) %all-gather.8.cloned.1.call-update) | async-done | bytes 21233680 | tf_op jit(solution)/shard_map/all_gather | solution.py:640
  421.6 15.2 %shard_map.238 = bf16[256,2304]{1,0:T(8,128)(2,1)} custom-call(s32[3]{0:T(128)} %pad_add_fusion._.scalar_ref, bf16[512,4608]{1,0:T(8,128)(2,1)} %get-tuple-element.233.hidden_ref.refs_3_, bf16[2304,4608]{1,0:T(8,128)(2,1)} %all-gather.8.cloned.1.call-done.down_ref.refs_3_.refs_6_), custom_call_target="tpu_custom_call" | custom-call | flops 1 | bytes 1 | tf_op jit(solution)/shard_map/pallas_call | solution.py:86
  440.9 15.4 %shard_map.239 = bf16[256,2304]{1,0:T(8,128)(2,1)} custom-call(s32[3]{0:T(128)} %pad_add_fusion._.scalar_ref, bf16[512,4608]{1,0:T(8,128)(2,1)} %get-tuple-element.233.hidden_ref.refs_3_, bf16[2304,4608]{1,0:T(8,128)(2,1)} %all-gather.8.cloned.1.call-done.down_ref.refs_3_.refs_6_), custom_call_target="tpu_custom_call" | custom-call | flops 1 | bytes 1 | tf_op jit(solution)/shard_map/pallas_call | solution.py:86
  466.7 19.2 %shard_map.240 = f32[512,2304]{1,0:T(8,128)} custom-call(s32[3]{0:T(128)} %pad_add_fusion._.scalar_ref, bf16[512,4608]{1,0:T(8,128)(2,1)} %get-tuple-element.235.hidden_ref.refs_2_, bf16[2304,4608]{1,0:T(8,128)(2,1)} %all-gather.8.cloned.1.call-done.down_ref.refs_3_.refs_6_), custom_call_target="tpu_custom_call" | custom-call | flops 1 | bytes 1 | tf_op jit(solution)/shard_map/pallas_call | solution.py:86
  506.3 16.8 %shard_map.242 = (bf16[256,4608]{1,0:T(8,128)(2,1)}, bf16[256,4608]{1,0:T(8,128)(2,1)}) custom-call(s32[3]{0:T(128)} %pad_add_fusion._.scalar_ref, bf16[256,2304]{1,0:T(8,128)(2,1)} %copy-done.14, bf16[512,4608]{1,0:T(8,128)(2,1)} %get-tuple-element.244.refs_1_.refs_2_, bf16[512,4608]{1,0:T(8,128)(2,1)} %get-tuple-element.245.refs_2_.refs_4_, ...), custom_call_target="tpu_custom_call" | custom-call | flops 1 | bytes 1 | tf_op jit(solution)/shard_map/pallas_call | solution.py:86
  525.4 21.2 %shard_map.243 = (bf16[256,4608]{1,0:T(8,128)(2,1)}, bf16[256,4608]{1,0:T(8,128)(2,1)}, bf16[256,4608]{1,0:T(8,128)(2,1)}, bf16[256,4608]{1,0:T(8,128)(2,1)}) custom-call(s32[3]{0:T(128)} %pad_add_fusion._.scalar_ref, bf16[256,2304]{1,0:T(8,128)(2,1)} %copy-done.15, bf16[256,2304]{1,0:T(8,128)(2,1)} %collective-permute-done.10.refs_1_.refs_0_, ...), custom_call_target="tpu_custom_call" | custom-call | flops 1 | bytes 1 | tf_op jit(solution)/shard_map/pallas_call | solution.py:86
  596.5 16.9 %shard_map.250 = (bf16[256,4608]{1,0:T(8,128)(2,1)}, bf16[256,4608]{1,0:T(8,128)(2,1)}) custom-call(s32[3]{0:T(128)} %pad_add_fusion._.scalar_ref, bf16[256,2304]{1,0:T(8,128)(2,1)} %copy-done.26, bf16[512,4608]{1,0:T(8,128)(2,1)} %get-tuple-element.249.refs_3_.refs_1_, bf16[512,4608]{1,0:T(8,128)(2,1)} %get-tuple-element.250.refs_5_.refs_2_, ...), custom_call_target="tpu_custom_call" | custom-call | flops 1 | bytes 1 | tf_op jit(solution)/shard_map/pallas_call | solution.py:86
  620.5 11.2 shard_map.252
  686.3 31.2 %shard_map.257 = (bf16[256,2304]{1,0:T(8,128)(2,1)}, bf16[256,2304]{1,0:T(8,128)(2,1)}) custom-call(s32[3]{0:T(128)} %pad_add_fusion._.scalar_ref, bf16[256,4608]{1,0:T(8,128)(2,1)} %get-tuple-element.291.refs_4_.refs_0_, bf16[256,4608]{1,0:T(8,128)(2,1)} %get-tuple-element.277.refs_5_.refs_1_, bf16[256,4608]{1,0:T(8,128)(2,1)} %get-tuple-element.340.refs_2_.refs_4_, ...), custom_call_target="tpu_custom_call" | custom-call | flops 1 | bytes 1 | tf_op jit(solution)/shard_map/pallas_call | solution.py:86
  734.7 11.2 shard_map.260
  753.2 31.4 %shard_map.261 = (f32[256,2304]{1,0:T(8,128)}, f32[256,2304]{1,0:T(8,128)}) custom-call(s32[3]{0:T(128)} %pad_add_fusion._.scalar_ref, bf16[256,4608]{1,0:T(8,128)(2,1)} %get-tuple-element.312.refs_2_.refs_0_, bf16[256,4608]{1,0:T(8,128)(2,1)} %get-tuple-element.275.refs_3_.refs_1_, bf16[256,4608]{1,0:T(8,128)(2,1)} %get-tuple-element.338.refs_2_, ...), custom_call_target="tpu_custom_call" | custom-call | flops 1 | bytes 1 | tf_op jit(solution)/shard_map/pallas_call | solution.py:86
  786.2 10.2 shard_map.262
  812.4 11.8 %collective-permute-done.26.refs_7_ = bf16[2,144,2048]{2,1,0:T(8,128)(2,1)} collective-permute-done((bf16[2,144,2048]{2,1,0:T(8,128)(2,1)}, bf16[2,144,2048]{2,1,0:T(8,128)(2,1)}, u32[]{:S(2)}, u32[]{:S(2)}) %collective-permute-start.26) | collective-permute-done | bytes 1179680 | tf_op jit(solution)/shard_map/ppermute | solution.py:30
  888.1 10.5 shard_map.268.d_ref
  911.0 10.5 collective-permute-done.32.refs_8_
  922.7 9.8 shard_map.271
  932.4 18.1 %shard_map.272 = (bf16[1024,1024]{1,0:T(8,128)(2,1)}, bf16[1024,1024]{1,0:T(8,128)(2,1)}) custom-call(s32[3]{0:T(128)} %pad_add_fusion._.scalar_ref, bf16[1024,2048]{1,0:T(8,128)(2,1)} %shard_map.230.query_ref.key_ref.value_ref.pair_ref, bf16[1024,2048]{1,0:T(8,128)(2,1)} %shard_map.230.query_ref.key_ref.value_ref.pair_ref, bf16[1024,1024]{1,0:T(8,128)(2,1)} %shard_map.268.d_ref), custom_call_target="tpu_custom_call" | custom-call | flops 1 | bytes 1 | tf_op jit(solution)/shard_map/pallas_call | solution.py:86
  1014.0 12.3 %shard_map.280 = (bf16[256,2304]{1,0:T(8,128)(2,1)}, bf16[256,2304]{1,0:T(8,128)(2,1)}) custom-call(s32[3]{0:T(128)} %pad_add_fusion._.scalar_ref, bf16[1024,1024]{1,0:T(8,128)(2,1)} %get-tuple-element.397.refs_2_.refs_3_.refs_0_, bf16[1024,1024]{1,0:T(8,128)(2,1)} %get-tuple-element.377.refs_2_.refs_3_.refs_1_, ...), custom_call_target="tpu_custom_call" | custom-call | flops 1 | bytes 1 | tf_op jit(solution)/shard_map/pallas_call | solution.py:86
  1041.0 12.9 %shard_map.282 = f32[512,2304]{1,0:T(8,128)} custom-call(s32[3]{0:T(128)} %pad_add_fusion._.scalar_ref, bf16[1024,1024]{1,0:T(8,128)(2,1)} %get-tuple-element.397.refs_2_.refs_3_.refs_0_, bf16[1024,1024]{1,0:T(8,128)(2,1)} %get-tuple-element.377.refs_2_.refs_3_.refs_1_, ...), custom_call_target="tpu_custom_call" | custom-call | flops 1 | bytes 1 | tf_op jit(solution)/shard_map/pallas_call | solution.py:86
  1078.1 18.3 %reduce-scatter.25.cloned.1.call-done = bf16[144,1024]{1,0:T(8,128)(2,1)} async-done(((bf16[576,1024]{1,0:T(8,128)(2,1)}), bf16[144,1024]{1,0:T(8,128)(2,1)}) %reduce-scatter.25.cloned.1.call-update) | async-done | bytes 294928 | tf_op jit(solution)/shard_map/reduce_scatter | solution.py:465
  1096.4 21.4 %collective-permute-done.41 = bf16[256,2304]{1,0:T(8,128)(2,1)} collective-permute-done((bf16[256,2304]{1,0:T(8,128)(2,1)}, bf16[256,2304]{1,0:T(8,128)(2,1)}, u32[]{:S(2)}, u32[]{:S(2)}) %collective-permute-start.41) | collective-permute-done | bytes 1179680 | tf_op jit(solution)/shard_map/ppermute | solution.py:26
  1154.8 13.1 %reduce-scatter.27.cloned.1.call-done = bf16[144,1024]{1,0:T(8,128)(2,1)} async-done(((bf16[576,1024]{1,0:T(8,128)(2,1)}), bf16[144,1024]{1,0:T(8,128)(2,1)}) %reduce-scatter.27.cloned.1.call-update) | async-done | bytes 294928 | tf_op jit(solution)/shard_map/reduce_scatter | solution.py:465
  (397 shorter events, 481.3 us)
Async XLA Ops:
  7.2 191.0 %all-gather.4.cloned.1.call-start = ((), (), s32[]{:S(2)}) async-start(), calls=%async_computation.10 | async-start | bytes 37601280 | tf_op jit(solution)/shard_map/all_gather | solution.py:633
  18.0 291.9 %all-gather.6.cloned.1.call-start = ((), (), s32[]{:S(2)}) async-start(), calls=%async_computation.11 | async-start | bytes 22560768 | tf_op jit(solution)/shard_map/all_gather | solution.py:639
  18.8 402.8 %all-gather.8.cloned.1.call-start = ((), (), s32[]{:S(2)}) async-start(), calls=%async_computation.12 | async-start | bytes 22560768 | tf_op jit(solution)/shard_map/all_gather | solution.py:640
  19.5 665.2 %reduce-scatter.11.cloned.1.call-start = ((), (), s32[]{:S(2)}) async-start(), calls=%async_computation.13 | async-start | bytes 1474560 | tf_op jit(solution)/shard_map/reduce_scatter | solution.py:465
  40.6 51.3 %collective-permute-start.5 = (bf16[512,2304]{1,0:T(8,128)(2,1)}, bf16[512,2304]{1,0:T(8,128)(2,1)}, u32[]{:S(2)}, u32[]{:S(2)}) collective-permute-start(bf16[512,2304]{1,0:T(8,128)(2,1)} %fusion.2.refs_0_), channel_id=1, source_target_pairs={{0,1},{1,0},{2,3},{3,2},{4,5},{5,4},{6,7},{7,6},{8,9},{9,8},{10,11... | collective-permute-start | bytes 7077896 | tf_op jit(solution)/shard_map/ppermute | solution.py:26
  234.7 53.6 %collective-permute-start.6 = (bf16[512,2304]{1,0:T(8,128)(2,1)}, bf16[512,2304]{1,0:T(8,128)(2,1)S(1)}, u32[]{:S(2)}, u32[]{:S(2)}) collective-permute-start(bf16[512,2304]{1,0:T(8,128)(2,1)} %shard_map.232), channel_id=1, source_target_pairs={{0,1},{1,0},{2,3},{3,2},{4,5},{5,4},{6,7},{7,6},{8,9},{9,8},{10,11... | collective-permute-start | bytes 7077896 | tf_op jit(solution)/shard_map/ppermute | solution.py:26
  296.3 52.8 %collective-permute-start.7 = (bf16[512,2304]{1,0:T(8,128)(2,1)S(1)}, bf16[512,2304]{1,0:T(8,128)(2,1)}, u32[]{:S(2)}, u32[]{:S(2)}) collective-permute-start(bf16[512,2304]{1,0:T(8,128)(2,1)S(1)} %multiply_convert_fusion.mid_ref.refs_0_), channel_id=1, source_target_pairs={{0,1},{1,0},{2,3},{3,2},{4,5},{5,4},{6,7},{7,6},{8,9},{9,8},{10,11... | collective-permute-start | bytes 7077896 | tf_op jit(solution)/shard_map/ppermute | solution.py:26
  465.2 29.1 %collective-permute-start.9 = (bf16[256,2304]{1,0:T(8,128)(2,1)}, bf16[256,2304]{1,0:T(8,128)(2,1)S(1)}, u32[]{:S(2)}, u32[]{:S(2)}) collective-permute-start(bf16[256,2304]{1,0:T(8,128)(2,1)} %shard_map.239), channel_id=1, source_target_pairs={{0,1},{1,0},{2,3},{3,2},{4,5},{5,4},{6,7},{7,6},{8,9},{9,8},{10,11... | collective-permute-start | bytes 3538952 | tf_op jit(solution)/shard_map/ppermute | solution.py:26
  496.3 29.1 %collective-permute-start.10 = (bf16[256,2304]{1,0:T(8,128)(2,1)S(1)}, bf16[256,2304]{1,0:T(8,128)(2,1)}, u32[]{:S(2)}, u32[]{:S(2)}) collective-permute-start(bf16[256,2304]{1,0:T(8,128)(2,1)S(1)} %get-tuple-element.247.refs_0_), channel_id=1, source_target_pairs={{0,1},{1,0},{2,3},{3,2},{4,5},{5,4},{6,7},{7,6},{8,9},{9,8},{10,11... | collective-permute-start | bytes 3538952 | tf_op jit(solution)/shard_map/ppermute | solution.py:26
  499.1 49.6 %collective-permute-start.11 = (bf16[256,2304]{1,0:T(8,128)(2,1)S(1)}, bf16[256,2304]{1,0:T(8,128)(2,1)S(1)}, u32[]{:S(2)}, u32[]{:S(2)}) collective-permute-start(bf16[256,2304]{1,0:T(8,128)(2,1)S(1)} %get-tuple-element.439.refs_1_.refs_0_), channel_id=1, source_target_pairs={{0,1},{1,0},{2,3},{3,2},{4,5},{5,4},{6,7},{7,6},{8,9},{9,8},{10,11... | collective-permute-start | bytes 3538952 | tf_op jit(solution)/shard_map/ppermute | solution.py:26
  577.0 36.4 %collective-permute-start.14 = (bf16[4,144,1024]{2,1,0:T(8,128)(2,1)}, bf16[4,144,1024]{2,1,0:T(8,128)(2,1)S(1)}, u32[]{:S(2)}, u32[]{:S(2)}) collective-permute-start(bf16[4,144,1024]{2,1,0:T(8,128)(2,1)} %shard_map.247), channel_id=1, source_target_pairs={{0,4},{2,6},{4,0},{6,2},{8,12},{10,14},{12,8},{14,10},{16,20},{18,... | collective-permute-start | bytes 3538952 | tf_op jit(solution)/shard_map/ppermute | solution.py:30
  614.5 41.0 %collective-permute-start.15 = (bf16[4,144,1536]{2,1,0:T(8,128)(2,1)S(1)}, bf16[4,144,1536]{2,1,0:T(8,128)(2,1)S(1)}, u32[]{:S(2)}, u32[]{:S(2)}) collective-permute-start(bf16[4,144,1536]{2,1,0:T(8,128)(2,1)S(1)} %copy-done.32), channel_id=1, source_target_pairs={{0,4},{2,6},{4,0},{6,2},{8,12},{10,14},{12,8},{14,10},{16,20},{18,... | collective-permute-start | bytes 5308424 | tf_op jit(solution)/shard_map/ppermute | solution.py:30
  656.0 95.1 %reduce-scatter.13.cloned.1.call-start = ((), (), s32[]{:S(2)}) async-start(), calls=%async_computation.14 | async-start | bytes 2211840 | tf_op jit(solution)/shard_map/reduce_scatter | solution.py:465
  684.7 139.6 %reduce-scatter.15.cloned.1.call-start = ((), (), s32[]{:S(2)}) async-start(), calls=%async_computation.15 | async-start | bytes 2949120 | tf_op jit(solution)/shard_map/reduce_scatter | solution.py:465
  684.8 32.7 %collective-permute-start.20 = (bf16[2,144,2048]{2,1,0:T(8,128)(2,1)S(1)}, bf16[2,144,2048]{2,1,0:T(8,128)(2,1)S(1)}, u32[]{:S(2)}, u32[]{:S(2)}) collective-permute-start(bf16[2,144,2048]{2,1,0:T(8,128)(2,1)S(1)} %copy-done.75), channel_id=1, source_target_pairs={{0,4},{2,6},{4,0},{6,2},{8,12},{10,14},{12,8},{14,10},{16,20},{18,... | collective-permute-start | bytes 3538952 | tf_op jit(solution)/shard_map/ppermute | solution.py:30
  717.5 33.6 %collective-permute-start.21 = (bf16[2,144,2560]{2,1,0:T(8,128)(2,1)S(1)}, bf16[2,144,2560]{2,1,0:T(8,128)(2,1)}, u32[]{:S(2)}, u32[]{:S(2)}) collective-permute-start(bf16[2,144,2560]{2,1,0:T(8,128)(2,1)S(1)} %copy-done.74), channel_id=1, source_target_pairs={{0,4},{2,6},{4,0},{6,2},{8,12},{10,14},{12,8},{14,10},{16,20},{18,... | collective-permute-start | bytes 4423688 | tf_op jit(solution)/shard_map/ppermute | solution.py:30
  751.1 35.0 %collective-permute-start.25 = (bf16[4,2,144,2560]{3,2,1,0:T(8,128)(2,1)}, bf16[4,2,144,2560]{3,2,1,0:T(8,128)(2,1)}, u32[]{:S(2)}, u32[]{:S(2)}) collective-permute-start(bf16[4,2,144,2560]{3,2,1,0:T(8,128)(2,1)} %shard_map.260), channel_id=1, source_target_pairs={{0,2},{2,0},{4,6},{6,4},{8,10},{10,8},{12,14},{14,12},{16,18},{18,... | collective-permute-start | bytes 17694728 | tf_op jit(solution)/shard_map/ppermute | solution.py:30
  751.1 35.0 %collective-permute-start.23 = (bf16[2,144,2560]{2,1,0:T(8,128)(2,1)}, bf16[2,144,2560]{2,1,0:T(8,128)(2,1)}, u32[]{:S(2)}, u32[]{:S(2)}) collective-permute-start(bf16[2,144,2560]{2,1,0:T(8,128)(2,1)} %get-tuple-element.316), channel_id=1, source_target_pairs={{0,4},{2,6},{4,0},{6,2},{8,12},{10,14},{12,8},{14,10},{16,20},{18,... | collective-permute-start | bytes 4423688 | tf_op jit(solution)/shard_map/ppermute | solution.py:30
  751.7 32.9 %collective-permute-start.24 = (bf16[256,2304]{1,0:T(8,128)(2,1)}, bf16[256,2304]{1,0:T(8,128)(2,1)S(1)}, u32[]{:S(2)}, u32[]{:S(2)}) collective-permute-start(bf16[256,2304]{1,0:T(8,128)(2,1)} %get-tuple-element.318), channel_id=1, source_target_pairs={{0,1},{1,0},{2,3},{3,2},{4,5},{5,4},{6,7},{7,6},{8,9},{9,8},{10,11... | collective-permute-start | bytes 3538952 | tf_op jit(solution)/shard_map/ppermute | solution.py:26
  753.1 134.1 %reduce-scatter.17.cloned.1.call-start = ((), (), s32[]{:S(2)}) async-start(), calls=%async_computation.16 | async-start | bytes 3686400 | tf_op jit(solution)/shard_map/reduce_scatter | solution.py:465
  826.4 124.2 %reduce-scatter.19.cloned.1.call-start = ((), (), s32[]{:S(2)}) async-start(), calls=%async_computation.17 | async-start | bytes 2949120 | tf_op jit(solution)/shard_map/reduce_scatter | solution.py:465
  852.3 35.0 %collective-permute-start.29 = (bf16[2,144,2560]{2,1,0:T(8,128)(2,1)}, bf16[2,144,2560]{2,1,0:T(8,128)(2,1)}, u32[]{:S(2)}, u32[]{:S(2)}) collective-permute-start(bf16[2,144,2560]{2,1,0:T(8,128)(2,1)} %get-tuple-element.343), channel_id=1, source_target_pairs={{0,4},{2,6},{4,0},{6,2},{8,12},{10,14},{12,8},{14,10},{16,20},{18,... | collective-permute-start | bytes 4423688 | tf_op jit(solution)/shard_map/ppermute | solution.py:30
  887.3 119.9 %reduce-scatter.21.cloned.1.call-start = ((), (), s32[]{:S(2)}) async-start(), calls=%async_computation.18 | async-start | bytes 3686400 | tf_op jit(solution)/shard_map/reduce_scatter | solution.py:465
  887.4 34.2 %collective-permute-start.32 = (bf16[2,144,2560]{2,1,0:T(8,128)(2,1)}, bf16[2,144,2560]{2,1,0:T(8,128)(2,1)S(1)}, u32[]{:S(2)}, u32[]{:S(2)}) collective-permute-start(bf16[2,144,2560]{2,1,0:T(8,128)(2,1)} %get-tuple-element.359), channel_id=1, source_target_pairs={{0,4},{2,6},{4,0},{6,2},{8,12},{10,14},{12,8},{14,10},{16,20},{18,... | collective-permute-start | bytes 4423688 | tf_op jit(solution)/shard_map/ppermute | solution.py:30
  921.6 29.0 %collective-permute-start.34 = (bf16[4,2,144,1024]{3,2,1,0:T(8,128)(2,1)}, bf16[4,2,144,1024]{3,2,1,0:T(8,128)(2,1)S(1)}, u32[]{:S(2)}, u32[]{:S(2)}) collective-permute-start(bf16[4,2,144,1024]{3,2,1,0:T(8,128)(2,1)} %shard_map.270), channel_id=1, source_target_pairs={{0,2},{2,0},{4,6},{6,4},{8,10},{10,8},{12,14},{14,12},{16,18},{18,... | collective-permute-start | bytes 7077896 | tf_op jit(solution)/shard_map/ppermute | solution.py:30
  921.6 29.0 %collective-permute-start.33 = (bf16[2,144,2048]{2,1,0:T(8,128)(2,1)S(1)}, bf16[2,144,2048]{2,1,0:T(8,128)(2,1)S(1)}, u32[]{:S(2)}, u32[]{:S(2)}) collective-permute-start(bf16[2,144,2048]{2,1,0:T(8,128)(2,1)S(1)} %copy-done.76), channel_id=1, source_target_pairs={{0,4},{2,6},{4,0},{6,2},{8,12},{10,14},{12,8},{14,10},{16,20},{18,... | collective-permute-start | bytes 3538952 | tf_op jit(solution)/shard_map/ppermute | solution.py:30
  950.6 116.2 %reduce-scatter.23.cloned.1.call-start = ((), (), s32[]{:S(2)}) async-start(), calls=%async_computation.19 | async-start | bytes 2949120 | tf_op jit(solution)/shard_map/reduce_scatter | solution.py:465
  1007.3 89.1 %reduce-scatter.25.cloned.1.call-start = ((), (), s32[]{:S(2)}) async-start(), calls=%async_computation.20 | async-start | bytes 1474560 | tf_op jit(solution)/shard_map/reduce_scatter | solution.py:465
  1066.9 62.9 %reduce-scatter.29.cloned.1.call-start = ((), (), s32[]{:S(2)}) async-start(), calls=%async_computation.22 | async-start | bytes 1474560 | tf_op jit(solution)/shard_map/reduce_scatter | solution.py:465
  1066.9 29.5 %collective-permute-start.40 = (bf16[256,2304]{1,0:T(8,128)(2,1)}, bf16[256,2304]{1,0:T(8,128)(2,1)S(1)}, u32[]{:S(2)}, u32[]{:S(2)}) collective-permute-start(bf16[256,2304]{1,0:T(8,128)(2,1)} %get-tuple-element.399), channel_id=1, source_target_pairs={{0,1},{1,0},{2,3},{3,2},{4,5},{5,4},{6,7},{7,6},{8,9},{9,8},{10,11... | collective-permute-start | bytes 3538952 | tf_op jit(solution)/shard_map/ppermute | solution.py:26
  1068.4 49.4 %collective-permute-start.41 = (bf16[256,2304]{1,0:T(8,128)(2,1)}, bf16[256,2304]{1,0:T(8,128)(2,1)}, u32[]{:S(2)}, u32[]{:S(2)}) collective-permute-start(bf16[256,2304]{1,0:T(8,128)(2,1)} %get-tuple-element.401), channel_id=1, source_target_pairs={{0,1},{1,0},{2,3},{3,2},{4,5},{5,4},{6,7},{7,6},{8,9},{9,8},{10,11... | collective-permute-start | bytes 3538952 | tf_op jit(solution)/shard_map/ppermute | solution.py:26
  1073.2 94.7 %reduce-scatter.27.cloned.1.call-start = ((), (), s32[]{:S(2)}) async-start(), calls=%async_computation.21 | async-start | bytes 1474560 | tf_op jit(solution)/shard_map/reduce_scatter | solution.py:465
  (112 other events, 1831.8 us)
Sparse Core Ops, SparseCore 0:
  18.1 180.0 all-gather.3
  199.8 110.0 all-gather.5
  311.5 110.0 all-gather.7
  656.1 28.4 reduce-scatter.10
  686.8 37.0 reduce-scatter.12
  753.3 46.4 reduce-scatter.14
  826.5 55.5 reduce-scatter.16
  887.4 46.2 reduce-scatter.18
  950.8 55.1 reduce-scatter.20
  1008.2 47.9 reduce-scatter.22
  1067.0 29.3 reduce-scatter.24
  1098.7 27.8 reduce-scatter.28
  1138.5 29.3 reduce-scatter.26

commit v4 on v3

--- a/solution.py
+++ b/solution.py
@@ -48,24 +48,6 @@
         )
         bit += 1
     return whole
-
-
-def scatter_small(partial, dp):
-    bit = dp.bit_length() - 2
-    while bit >= 0:
-        half = partial.shape[1] // 2
-        low, high = partial[:, :half], partial[:, half:]
-        mine = (lax.axis_index("dp") >> bit) & 1
-        keep = jnp.where(mine == 0, low, high)
-        give = jnp.where(mine == 0, high, low)
-        partial = keep + flip(give, bit, dp)
-        bit -= 1
-    half = partial.shape[1] // 2
-    low, high = partial[:, :half], partial[:, half:]
-    mine = lax.axis_index("tensor")
-    keep = jnp.where(mine == 0, low, high)
-    give = jnp.where(mine == 0, high, low)
-    return keep + swap(give)
 
 
 def dot(left, right):
@@ -470,6 +452,22 @@
             tiled=True,
         )
 
+    def to_owner(self):
+        place = lax.axis_index("dp") >> 2
+        transfers = []
+        for shift in range(1, self.rest):
+            pairs = [(i, (i + 4 * shift) % self.dp) for i in range(self.dp)]
+            part = lax.dynamic_index_in_dim(
+                self.total, (place + shift) % self.rest, 0, keepdims=False
+            )
+            transfers.append((part, lambda array, pairs=pairs: lax.ppermute(array, "dp", pairs)))
+        return transfers
+
+    def gather(self, parts):
+        place = lax.axis_index("dp") >> 2
+        total = lax.dynamic_index_in_dim(self.total, place, 0, keepdims=False).astype(F32)
+        self.sums = sum((part.astype(F32) for part in parts), total)
+
     def arrive(self, line):
         (self.sums,) = line.land(self.sums)
 
@@ -595,6 +593,84 @@
         ],
         [((size, width), dtype, (size, tile), lambda j, s: (0, j))] * pieces,
     )
+
+
+def norms_back(line, sums, middle, gain_mid, upstream, branch, gain_branch, scalars):
+    rows, width = middle.shape
+    count = len(sums)
+    size = sums[0][0].shape[0]
+    block = 64
+    steps, each = rows // block, size // block
+    given = [(middle, gain_mid)] + ([] if branch is None else [(branch, gain_branch)])
+    norms = len(given)
+    outs = 1 if branch is None else 1 + count
+
+    def back(values, gain, d_normed):
+        values = values.astype(F32)
+        scale = lax.rsqrt(jnp.mean(values * values, axis=1, keepdims=True) + EPSILON)
+        normed = values * scale
+        weighted = d_normed * gain
+        inner = jnp.mean(weighted * normed, axis=1, keepdims=True)
+        grad = scale * (weighted - normed * inner)
+        return grad, jnp.sum(d_normed * normed, axis=0, keepdims=True)
+
+    def kernel(_, *refs):
+        parts, upstream_ref, refs = refs[: 2 * count], refs[2 * count], refs[2 * count + 1 :]
+        values_refs, gain_refs, refs = refs[:norms], refs[norms : 2 * norms], refs[2 * norms :]
+        grad_refs, gain_grad_refs = refs[:outs], refs[outs:]
+        step = pl.program_id(0)
+
+        @pl.when(step == 0)
+        def _():
+            for ref in gain_grad_refs:
+                ref[...] = jnp.zeros_like(ref)
+
+        for index in range(count):
+
+            @pl.when(step // each == index)
+            def _(index=index):
+                d_normed = parts[2 * index][...] + parts[2 * index + 1][...].astype(F32)
+                grad, grad_gain = back(values_refs[0][...], gain_refs[0][...], d_normed)
+                gain_grad_refs[0][...] += grad_gain
+                total = upstream_ref[...].astype(F32) + grad
+                grad_refs[0][...] = total
+                if norms > 1:
+                    grad, grad_gain = back(values_refs[1][...], gain_refs[1][...], total)
+                    gain_grad_refs[1][...] += grad_gain
+                    grad_refs[1 + index][...] = grad.astype(BF16)
+
+    def piece(index):
+        return lambda j, s: (jnp.clip(j - index * each, 0, each - 1), 0)
+
+    shape = (block, width)
+    every = lambda j, s: (j, 0)
+    once = lambda j, s: (0, 0)
+    (first, *others), *later = sums
+    sums = [(line.next(first), *others), *later]
+    return line.mark(
+        call(
+            kernel,
+            steps,
+            scalars,
+            [
+                (array, shape, piece(index), False)
+                for index, pair in enumerate(sums)
+                for array in pair
+            ]
+            + [(array, shape, every, False) for array in (upstream, *(v for v, _ in given))]
+            + [(gain[None], (1, width), once, True) for _, gain in given],
+            [((rows, width), F32, shape, every)]
+            + [((size, width), BF16, shape, piece(index)) for index in range(outs - 1)]
+            + [((1, width), F32, (1, width), once)] * norms,
+        )
+    )
+
+
+def to_owners(partial):
+    count, width = partial.shape
+    devices = lax.axis_size("dp") * lax.axis_size("tensor")
+    parts = partial.reshape(count, devices, width // devices).transpose(1, 0, 2)
+    return lax.all_to_all(parts, ("dp", "tensor"), 0, 0, tiled=True)
 
 
 def make_body(dp):
@@ -665,11 +741,8 @@
             )
         )
         branch_attn = kept + taken.astype(F32)
-        middle, pull_attn_out = jax.vjp(
-            lambda values, gain: residual_in + rms_norm(values, gain), branch_attn, gain_b
-        )
-        normed_mid_f, pull_ffn_in = jax.vjp(rms_norm, middle, gain_c)
-        mid_own = line.mark(normed_mid_f.astype(BF16))
+        middle = residual_in + rms_norm(branch_attn, gain_b)
+        mid_own = line.mark(rms_norm(middle, gain_c).astype(BF16))
         (mid_other,) = line.send(to_other(mid_own))
         hidden_own, active_own, slope_own = line.mark(
             feed(mid_own, full_first, gate_at, full_up, scalars)
@@ -758,37 +831,35 @@
         line.mark(down_2.give())
         (core_1,) = line.land(core_1)
         line.mark(down_1.side(line.next(core_1)))
+        (down_0_side,) = line.land(down_0_side)
+
+        down_1_side, core_2 = line.send(down_1.to_side(0), down_2.to_core())
         (d_gate_4,), (d_up_4,) = hidden_back(
             line, [(d_ffn_4, active_other, slope_other, 1)], full_down_t, scalars
         )
-        (down_0_side,) = line.land(down_0_side)
         d_gates = [d_gate_1, d_gate_2, d_gate_3, d_gate_4]
         d_ups = [d_up_1, d_up_2, d_up_3, d_up_4]
-
-        down_1_side, core_2 = line.send(down_1.to_side(0), down_2.to_core())
         line.mark(down_0.own(line.next(down_0_side)))
         gate_0 = mid_part(d_gates, 0)
         line.mark(gate_0.give())
         (core_2,) = line.land(core_2)
         line.mark(down_2.side(line.next(core_2)))
+        (down_1_side,) = line.land(down_1_side)
+
+        side_0, core_0 = line.send(down_2.to_side(0), gate_0.to_core())
+        down_0.along_rest(line)
+        line.mark(down_1.own(line.next(down_1_side)))
         gate_1 = mid_part(d_gates, 1)
         line.mark(gate_1.give())
-        (down_1_side,) = line.land(down_1_side)
-
-        side_0, core_0, core_1 = line.send(
-            down_2.to_side(0), gate_0.to_core(), gate_1.to_core()
-        )
-        down_0.along_rest(line)
-        line.mark(down_1.own(line.next(down_1_side)))
-        core_0, core_1 = line.land(core_0, core_1)
+        (core_0,) = line.land(core_0)
         line.mark(gate_0.side(line.next(core_0)))
         (side_0,) = line.land(side_0)
         down_0.arrive(line)
 
-        (side_1,) = line.send(down_2.to_side(1))
+        side_1, core_1 = line.send(down_2.to_side(1), gate_1.to_core())
         down_1.along_rest(line)
         give_1, give_2 = mid_back_of(d_gates[2:], d_ups[2:], BF16)
-        (side_1,) = line.land(side_1)
+        side_1, core_1 = line.land(side_1, core_1)
 
         gate_0_side_0, taken_1 = line.send(gate_0.to_side(0), to_other(give_1))
         line.mark(down_2.own(line.next(side_0), side_1))
@@ -807,17 +878,20 @@
 
         (gate_1_side_0,) = line.send(gate_1.to_side(0))
         line.mark(gate_0.own(line.next(gate_0_side_0), gate_0_side_1))
-        taken = jnp.concatenate([taken_1, taken_2], axis=0).astype(F32)
-        d_mid_norm, grad_c = pull_ffn_in(
-            jnp.concatenate([line.next(kept_1), kept_2], axis=0) + taken
-        )
-        d_middle = upstream + d_mid_norm
-        d_branch, grad_b = pull_attn_out(d_middle)
-        d_branch_own = line.mark(d_branch.astype(BF16))
+        d_middle, d_branch_1, d_branch_2, grad_c, grad_b = norms_back(
+            line,
+            [(kept_1, taken_1), (kept_2, taken_2)],
+            middle,
+            gain_c,
+            cotangent,
+            branch_attn,
+            gain_b,
+            scalars,
+        )
         (gate_1_side_0,) = line.land(gate_1_side_0)
         down_2.arrive(line)
 
-        gate_1_side_1, d_branch_3 = line.send(gate_1.to_side(1), to_other(d_branch_own[low]))
+        gate_1_side_1, d_branch_3 = line.send(gate_1.to_side(1), to_other(d_branch_1))
         gate_0.along_rest(line)
         line.mark(up_0.side(line.next(core_0)))
         up_1 = mid_part(d_ups, 1)
@@ -825,10 +899,10 @@
         gate_1_side_1, d_branch_3 = line.land(gate_1_side_1, d_branch_3)
 
         up_0_side_0, core_1, d_branch_4 = line.send(
-            up_0.to_side(0), up_1.to_core(), to_other(d_branch_own[high])
+            up_0.to_side(0), up_1.to_core(), to_other(d_branch_2)
         )
         line.mark(gate_1.own(line.next(gate_1_side_0), gate_1_side_1))
-        d_branch_own_t = line.mark(turned([line.next(d_branch_own)], scalars))
+        d_branch_own_t = line.mark(turned([line.next(d_branch_1), d_branch_2], scalars))
         (core_1,) = line.land(core_1)
         line.mark(up_1.side(line.next(core_1)))
         up_0_side_0, d_branch_4 = line.land(up_0_side_0, d_branch_4)
@@ -838,7 +912,7 @@
         gate_1.along_rest(line)
         d_attended = line.mark(
             projected(
-                [line.next(d_branch_own), d_branch_3, d_branch_4],
+                [line.next(d_branch_1), d_branch_2, d_branch_3, d_branch_4],
                 full_first,
                 qkv_cols,
                 query_cols,
@@ -878,51 +952,56 @@
         line.mark(query.give())
         pair = input_part(d_pair, 2 * key_cols)
         line.mark(pair.give())
+        give_1, give_2 = line.mark(
+            projected_back(
+                [(line.next(d_query), 0), (d_pair, 1)], full_first, theirs, 2, BF16, scalars
+            )
+        )
         (up_1_side_1,) = line.land(up_1_side_1)
 
-        output_side, query_core, pair_core = line.send(
-            output.to_side(0), query.to_core(), pair.to_core()
+        output_side, query_core, pair_core, taken_1 = line.send(
+            output.to_side(0), query.to_core(), pair.to_core(), to_other(give_1)
         )
         line.mark(up_1.own(line.next(up_1_side_0), up_1_side_1))
         query_core, pair_core = line.land(query_core, pair_core)
         line.mark(query.side(line.next(query_core)))
         line.mark(pair.side(line.next(pair_core)))
-        (output_side,) = line.land(output_side)
+        output_side, taken_1 = line.land(output_side, taken_1)
         up_0.arrive(line)
 
-        (query_side,) = line.send(query.to_side(0))
+        query_side, taken_2 = line.send(query.to_side(0), to_other(give_2))
         up_1.along_rest(line)
         line.mark(output.own(line.next(output_side)))
-        give_1, give_2 = line.mark(
+        kept_1, kept_2 = line.mark(
             projected_back(
-                [(line.next(d_query), 0), (d_pair, 1)], full_first, theirs, 2, BF16, scalars
+                [(line.next(d_query), 0), (d_pair, 1)], full_first, mine, 2, F32, scalars
             )
         )
-        (query_side,) = line.land(query_side)
-
-        pair_side, taken_1, taken_2 = line.send(
-            pair.to_side(0), to_other(give_1), to_other(give_2)
-        )
+        query_side, taken_2 = line.land(query_side, taken_2)
         line.mark(query.own(line.next(query_side)))
-        (kept,) = line.mark(
-            projected_back(
-                [(line.next(d_query), 0), (d_pair, 1)], full_first, mine, 1, F32, scalars
-            )
+
+        pair_side, *query_parts = line.send(pair.to_side(0), *query.to_owner())
+        input_grad, grad_a = norms_back(
+            line,
+            [(kept_1, taken_1), (kept_2, taken_2)],
+            layer_input,
+            gain_a,
+            d_middle,
+            None,
+            None,
+            scalars,
         )
         (pair_side,) = line.land(pair_side)
+        up_1.arrive(line)
         line.mark(pair.own(line.next(pair_side)))
-        up_1.arrive(line)
+        query_parts = line.land(*query_parts)
+
+        gain_grads = jnp.stack([grad_a[0], grad_b[0], grad_c[0], grad_d])
+        gain_parts, *pair_parts = line.send((gain_grads, to_owners), *pair.to_owner())
         output.along_rest(line)
-        output.arrive(line)
-        query.along_rest(line)
-        taken_1, taken_2 = line.land(taken_1, taken_2)
-        _, pull_attn_in = jax.vjp(rms_norm, residual_in, gain_a)
-        taken = jnp.concatenate([taken_1, taken_2], axis=0).astype(F32)
-        d_input_norm, grad_a = pull_attn_in(line.next(kept) + taken)
-        input_grad = line.mark(d_middle + d_input_norm)
-        query.arrive(line)
-        pair.along_rest(line)
-        small = scatter_small(jnp.stack([grad_a, grad_b, grad_c, grad_d]), dp)
+        small = jnp.sum(gain_parts, axis=0)
+        query.gather(query_parts)
+        pair.gather(pair_parts)
 
         down, gate, up = [down_0, down_1, down_2], [gate_0, gate_1], [up_0, up_1]
         grad_pair = pair.result().reshape(-1, key_cols // HEAD_WIDTH, 2, HEAD_WIDTH)

time: 1180 us -> 1150 us (0.975); the launches traced: 1180 us -> 1130 us
  waiting for transfers between devices: 406 us -> 358 us
  other arithmetic: 62.9 us -> 37.5 us
  Pallas kernels: 600 us -> 624 us
  starting transfers between devices: 51.3 us -> 64.9 us
    reduce_scatter x10 -> x8, waiting for transfers between devices: 31.8 us -> 0.11 us  [along_rest(): lax.psum_scatter(line.next(self.total).reshape(-1, self.columns), 'dp', s...]
    ppermute x0 -> x6, waiting for transfers between devices: none -> 29.8 us  [to_owner(): lax.ppermute(array, 'dp', pairs)]
    ppermute x33 -> x29, waiting for transfers between devices: 94 us -> 67.1 us  [flip(): return lax.ppermute(array, 'dp', [(i, i ^ 1 << bit) for i in range(dp)])]
    pallas_call x56 -> x58, Pallas kernels: 600 us -> 624 us  [call(): pl.pallas_call(kernel, grid_spec=pltpu.PrefetchScalarGridSpec(num_scalar_...]
    ppermute x15 -> x14, waiting for transfers between devices: 130 us -> 107 us  [swap(): return lax.ppermute(rows, 'tensor', [(0, 1), (1, 0)])]
    reduce_sum x5 -> x2, other arithmetic: 20 us -> 5.36 us  [rms_norm(): values * lax.rsqrt(jnp.mean(values * values, axis=-1, keepdims=True) + EP...]
    ppermute x33 -> x29, starting transfers between devices: 29 us -> 24.3 us  [flip(): return lax.ppermute(array, 'dp', [(i, i ^ 1 << bit) for i in range(dp)])]
    unnamed x174 -> x146, local copies, waits for them, and re-layouts: 30.2 us -> 27.7 us
  transfers between devices with their start and end apart: 61 -> 61, of which waited for: 35 -> 33; matrix products, arithmetic and copies ran while one was open for 6% -> 4% of each run, Pallas kernels for 48% -> 52%
where the time goes in v4:
time: 1150 us; the launch traced here: 1130 us
  Pallas kernels  624 us (54%)
  waiting for transfers between devices  358 us (31%)
  starting transfers between devices  64.9 us (6%)
  other arithmetic  37.5 us (3%)
  local copies, waits for them, and re-layouts  34.4 us (3%)
  between operations  14.9 us (1%)
    pallas_call x58, Pallas kernels, call(): pl.pallas_call(kernel, grid_spec=pltpu.PrefetchScalarGridSpec(num_scalar_...  624 us
    ppermute x14, waiting for transfers between devices, swap(): return lax.ppermute(rows, 'tensor', [(0, 1), (1, 0)])  107 us
    all_gather x1, waiting for transfers between devices, body(): lax.all_gather(jnp.concatenate([query_weight, *pairs, w_output.T, w_gate]...  100 us
    ppermute x29, waiting for transfers between devices, flip(): return lax.ppermute(array, 'dp', [(i, i ^ 1 << bit) for i in range(dp)])  67.1 us
    all_gather x1, waiting for transfers between devices, body(): full_down_t = lax.all_gather(w_down.T, 'dp', axis=0, tiled=True)  37.4 us
    ppermute x6, waiting for transfers between devices, to_owner(): lax.ppermute(array, 'dp', pairs)  29.8 us
    unnamed x146, local copies, waits for them, and re-layouts  27.7 us
    ppermute x29, starting transfers between devices, flip(): return lax.ppermute(array, 'dp', [(i, i ^ 1 << bit) for i in range(dp)])  24.3 us
  transfers between devices with their start and end apart: 61, of which 33 were waited for; matrix products, arithmetic and copies ran while one was open for 4% of the time, Pallas kernels for 52%

profile of v4, /device:TPU:0, one launch (start us, length us, event | category | flops | bytes accessed | tf_op | source)
XLA Modules:
  0.0 1133.9 jit_solution(5653684765194003358)
XLA Ops:
  49.4 43.0 %collective-permute-done.5.refs_0_.refs_1_ = bf16[512,2304]{1,0:T(8,128)(2,1)} collective-permute-done((bf16[512,2304]{1,0:T(8,128)(2,1)}, bf16[512,2304]{1,0:T(8,128)(2,1)}, u32[]{:S(2)}, u32[]{:S(2)}) %collective-permute-start.5) | collective-permute-done | bytes 2359328 | tf_op jit(solution)/shard_map/ppermute | solution.py:26
  98.1 100.1 %all-gather.4.cloned.1.call-done.refs_2_.refs_1_.gate_ref.refs_4_.refs_5_.refs_6_.refs_3_ = bf16[2304,7680]{1,0:T(8,128)(2,1)} async-done(((bf16[144,7680]{1,0:T(8,128)(2,1)}), bf16[2304,7680]{1,0:T(8,128)(2,1)}) %all-gather.4.cloned.1.call-update) | async-done | bytes 35389456 | tf_op jit(solution)/shard_map/all_gather | solution.py:709
  198.2 15.3 %shard_map.230.query_ref.key_ref.value_ref.pair_ref = bf16[1024,2048]{1,0:T(8,128)(2,1)} custom-call(s32[3]{0:T(128)} %pad_add_fusion._.scalar_ref, bf16[512,2304]{1,0:T(8,128)(2,1)} %fusion.2.refs_0_, bf16[512,2304]{1,0:T(8,128)(2,1)} %collective-permute-done.5.refs_0_.refs_1_, ...), custom_call_target="tpu_custom_call" | custom-call | flops 1 | bytes 1 | tf_op jit(solution)/shard_map/pallas_call | solution.py:68
  213.5 11.4 %shard_map.231.refs_0_.refs_2_.refs_3_ = bf16[1024,1024]{1,0:T(8,128)(2,1)} custom-call(s32[3]{0:T(128)} %pad_add_fusion._.scalar_ref, bf16[1024,2048]{1,0:T(8,128)(2,1)} %shard_map.230.query_ref.key_ref.value_ref.pair_ref, bf16[1024,2048]{1,0:T(8,128)(2,1)} %shard_map.230.query_ref.key_ref.value_ref.pair_ref, ...), custom_call_target="tpu_custom_call" | custom-call | flops 1 | bytes 1 | tf_op jit(solution)/shard_map/pallas_call | solution.py:68
  224.9 9.9 shard_map.232
  236.2 10.3 shard_map.233
  246.5 41.8 %collective-permute-done.6 = bf16[512,2304]{1,0:T(8,128)(2,1)S(1)} collective-permute-done((bf16[512,2304]{1,0:T(8,128)(2,1)}, bf16[512,2304]{1,0:T(8,128)(2,1)S(1)}, u32[]{:S(2)}, u32[]{:S(2)}) %collective-permute-start.6) | collective-permute-done | bytes 2359328 | tf_op jit(solution)/shard_map/ppermute | solution.py:26
  297.2 12.6 %all-gather.6.cloned.1.call-done.up_ref.refs_7_ = bf16[2304,4608]{1,0:T(8,128)(2,1)} async-done(((bf16[144,4608]{1,0:T(8,128)(2,1)}), bf16[2304,4608]{1,0:T(8,128)(2,1)}) %all-gather.6.cloned.1.call-update) | async-done | bytes 21233680 | tf_op jit(solution)/shard_map/all_gather | solution.py:715
  309.9 30.8 %shard_map.234 = (bf16[512,4608]{1,0:T(8,128)(2,1)}, bf16[512,4608]{1,0:T(8,128)(2,1)}, bf16[512,4608]{1,0:T(8,128)(2,1)}) custom-call(s32[3]{0:T(128)} %pad_add_fusion._.scalar_ref, bf16[512,2304]{1,0:T(8,128)(2,1)} %copy-done.5, bf16[2304,7680]{1,0:T(8,128)(2,1)} %all-gather.4.cloned.1.call-done.refs_2_.refs_1_.gate_ref.refs_4_.refs_5_.refs_6_.refs_3_, ...), custom_call_target="tpu_custom_call" | custom-call | flops 1 | bytes 1 | tf_op jit(solution)/shard_map/pallas_call | solution.py:68
  348.6 29.8 %shard_map.236 = (bf16[512,4608]{1,0:T(8,128)(2,1)}, bf16[512,4608]{1,0:T(8,128)(2,1)}, bf16[512,4608]{1,0:T(8,128)(2,1)}) custom-call(s32[3]{0:T(128)} %pad_add_fusion._.scalar_ref, bf16[512,2304]{1,0:T(8,128)(2,1)} %collective-permute-done.7.mid_ref.refs_0_, ...), custom_call_target="tpu_custom_call" | custom-call | flops 1 | bytes 1 | tf_op jit(solution)/shard_map/pallas_call | solution.py:68
  384.2 37.4 %all-gather.8.cloned.1.call-done.down_ref.refs_3_.refs_6_ = bf16[2304,4608]{1,0:T(8,128)(2,1)} async-done(((bf16[144,4608]{1,0:T(8,128)(2,1)}), bf16[2304,4608]{1,0:T(8,128)(2,1)}) %all-gather.8.cloned.1.call-update) | async-done | bytes 21233680 | tf_op jit(solution)/shard_map/all_gather | solution.py:716
  421.6 15.2 %shard_map.238 = bf16[256,2304]{1,0:T(8,128)(2,1)} custom-call(s32[3]{0:T(128)} %pad_add_fusion._.scalar_ref, bf16[512,4608]{1,0:T(8,128)(2,1)} %get-tuple-element.246.hidden_ref.refs_3_, bf16[2304,4608]{1,0:T(8,128)(2,1)} %all-gather.8.cloned.1.call-done.down_ref.refs_3_.refs_6_), custom_call_target="tpu_custom_call" | custom-call | flops 1 | bytes 1 | tf_op jit(solution)/shard_map/pallas_call | solution.py:68
  440.8 15.4 %shard_map.239 = bf16[256,2304]{1,0:T(8,128)(2,1)} custom-call(s32[3]{0:T(128)} %pad_add_fusion._.scalar_ref, bf16[512,4608]{1,0:T(8,128)(2,1)} %get-tuple-element.246.hidden_ref.refs_3_, bf16[2304,4608]{1,0:T(8,128)(2,1)} %all-gather.8.cloned.1.call-done.down_ref.refs_3_.refs_6_), custom_call_target="tpu_custom_call" | custom-call | flops 1 | bytes 1 | tf_op jit(solution)/shard_map/pallas_call | solution.py:68
  466.6 19.2 %shard_map.240 = f32[512,2304]{1,0:T(8,128)} custom-call(s32[3]{0:T(128)} %pad_add_fusion._.scalar_ref, bf16[512,4608]{1,0:T(8,128)(2,1)} %get-tuple-element.248.hidden_ref.refs_2_, bf16[2304,4608]{1,0:T(8,128)(2,1)} %all-gather.8.cloned.1.call-done.down_ref.refs_3_.refs_6_), custom_call_target="tpu_custom_call" | custom-call | flops 1 | bytes 1 | tf_op jit(solution)/shard_map/pallas_call | solution.py:68
  506.2 16.7 %shard_map.242 = (bf16[256,4608]{1,0:T(8,128)(2,1)}, bf16[256,4608]{1,0:T(8,128)(2,1)}) custom-call(s32[3]{0:T(128)} %pad_add_fusion._.scalar_ref, bf16[256,2304]{1,0:T(8,128)(2,1)} %copy-done.9, bf16[512,4608]{1,0:T(8,128)(2,1)} %get-tuple-element.257.refs_1_.refs_2_, bf16[512,4608]{1,0:T(8,128)(2,1)} %get-tuple-element.258.refs_2_.refs_4_, ...), custom_call_target="tpu_custom_call" | custom-call | flops 1 | bytes 1 | tf_op jit(solution)/shard_map/pallas_call | solution.py:68
  525.3 21.2 %shard_map.243 = (bf16[256,4608]{1,0:T(8,128)(2,1)}, bf16[256,4608]{1,0:T(8,128)(2,1)}, bf16[256,4608]{1,0:T(8,128)(2,1)}, bf16[256,4608]{1,0:T(8,128)(2,1)}) custom-call(s32[3]{0:T(128)} %pad_add_fusion._.scalar_ref, bf16[256,2304]{1,0:T(8,128)(2,1)} %copy-done.10, bf16[256,2304]{1,0:T(8,128)(2,1)} %collective-permute-done.10.refs_1_.refs_0_, ...), custom_call_target="tpu_custom_call" | custom-call | flops 1 | bytes 1 | tf_op jit(solution)/shard_map/pallas_call | solution.py:68
  606.5 16.8 %shard_map.250 = (bf16[256,4608]{1,0:T(8,128)(2,1)}, bf16[256,4608]{1,0:T(8,128)(2,1)}) custom-call(s32[3]{0:T(128)} %pad_add_fusion._.scalar_ref, bf16[256,2304]{1,0:T(8,128)(2,1)} %copy-done.18, bf16[512,4608]{1,0:T(8,128)(2,1)} %get-tuple-element.262.refs_3_.refs_1_, bf16[512,4608]{1,0:T(8,128)(2,1)} %get-tuple-element.263.refs_5_.refs_2_, ...), custom_call_target="tpu_custom_call" | custom-call | flops 1 | bytes 1 | tf_op jit(solution)/shard_map/pallas_call | solution.py:68
  628.4 11.3 shard_map.252
  657.7 9.6 shard_map.255
  679.8 31.2 %shard_map.257 = (bf16[256,2304]{1,0:T(8,128)(2,1)}, bf16[256,2304]{1,0:T(8,128)(2,1)}) custom-call(s32[3]{0:T(128)} %pad_add_fusion._.scalar_ref, bf16[256,4608]{1,0:T(8,128)(2,1)} %get-tuple-element.305.refs_4_.refs_0_, bf16[256,4608]{1,0:T(8,128)(2,1)} %get-tuple-element.296.refs_5_.refs_1_, bf16[256,4608]{1,0:T(8,128)(2,1)} %get-tuple-element.356.refs_2_.refs_4_, ...), custom_call_target="tpu_custom_call" | custom-call | flops 1 | bytes 1 | tf_op jit(solution)/shard_map/pallas_call | solution.py:68
  728.2 11.3 shard_map.260
  747.4 31.4 %shard_map.261 = (f32[256,2304]{1,0:T(8,128)}, f32[256,2304]{1,0:T(8,128)}) custom-call(s32[3]{0:T(128)} %pad_add_fusion._.scalar_ref, bf16[256,4608]{1,0:T(8,128)(2,1)} %get-tuple-element.326.refs_2_.refs_0_, bf16[256,4608]{1,0:T(8,128)(2,1)} %get-tuple-element.294.refs_3_.refs_1_, bf16[256,4608]{1,0:T(8,128)(2,1)} %get-tuple-element.354.refs_2_, ...), custom_call_target="tpu_custom_call" | custom-call | flops 1 | bytes 1 | tf_op jit(solution)/shard_map/pallas_call | solution.py:68
  781.8 9.6 shard_map.262
  791.4 13.9 %shard_map.263 = (f32[512,2304]{1,0:T(8,128)}, bf16[256,2304]{1,0:T(8,128)(2,1)}, bf16[256,2304]{1,0:T(8,128)(2,1)}, f32[1,2304]{1,0:T(1,128)}, f32[1,2304]{1,0:T(1,128)}) custom-call(s32[3]{0:T(128)} %pad_add_fusion._.scalar_ref, f32[256,2304]{1,0:T(8,128)} %get-tuple-element.337.refs_0_, bf16[256,2304]{1,0:T(8,128)(2,1)} %copy-done.31, ...), custom_call_target="tpu_custom_call" | custom-call | flops 1 | bytes 1 | tf_op jit(solution)/shard_map/pallas_call | solution.py:68
  819.1 9.7 shard_map.265
  872.5 10.6 shard_map.269.d_ref
  906.4 9.7 shard_map.272
  916.1 18.1 %shard_map.273 = (bf16[1024,1024]{1,0:T(8,128)(2,1)}, bf16[1024,1024]{1,0:T(8,128)(2,1)}) custom-call(s32[3]{0:T(128)} %pad_add_fusion._.scalar_ref, bf16[1024,2048]{1,0:T(8,128)(2,1)} %shard_map.230.query_ref.key_ref.value_ref.pair_ref, bf16[1024,2048]{1,0:T(8,128)(2,1)} %shard_map.230.query_ref.key_ref.value_ref.pair_ref, bf16[1024,1024]{1,0:T(8,128)(2,1)} %shard_map.269.d_ref), custom_call_target="tpu_custom_call" | custom-call | flops 1 | bytes 1 | tf_op jit(solution)/shard_map/pallas_call | solution.py:68
  953.9 12.5 %shard_map.277 = (bf16[256,2304]{1,0:T(8,128)(2,1)}, bf16[256,2304]{1,0:T(8,128)(2,1)}) custom-call(s32[3]{0:T(128)} %pad_add_fusion._.scalar_ref, bf16[1024,1024]{1,0:T(8,128)(2,1)} %get-tuple-element.413.refs_2_.refs_3_.refs_0_, bf16[1024,1024]{1,0:T(8,128)(2,1)} %get-tuple-element.394.refs_2_.refs_3_.refs_1_, ...), custom_call_target="tpu_custom_call" | custom-call | flops 1 | bytes 1 | tf_op jit(solution)/shard_map/pallas_call | solution.py:68
  1005.3 12.5 %shard_map.282 = (f32[256,2304]{1,0:T(8,128)}, f32[256,2304]{1,0:T(8,128)}) custom-call(s32[3]{0:T(128)} %pad_add_fusion._.scalar_ref, bf16[1024,1024]{1,0:T(8,128)(2,1)} %get-tuple-element.413.refs_2_.refs_3_.refs_0_, bf16[1024,1024]{1,0:T(8,128)(2,1)} %get-tuple-element.394.refs_2_.refs_3_.refs_1_, ...), custom_call_target="tpu_custom_call" | custom-call | flops 1 | bytes 1 | tf_op jit(solution)/shard_map/pallas_call | solution.py:68
  1039.6 11.2 shard_map.284
  1087.6 21.0 %collective-permute-done.47 = bf16[144,1024]{1,0:T(8,128)(2,1)S(1)} collective-permute-done((bf16[144,1024]{1,0:T(8,128)(2,1)S(1)}, bf16[144,1024]{1,0:T(8,128)(2,1)S(1)}, u32[]{:S(2)}, u32[]{:S(2)}) %collective-permute-start.47) | collective-permute-done | bytes 294944 | tf_op jit(solution)/shard_map/ppermute | solution.py:463
  (351 shorter events, 448.8 us)
Async XLA Ops:
  7.2 191.0 %all-gather.4.cloned.1.call-start = ((), (), s32[]{:S(2)}) async-start(), calls=%async_computation.9 | async-start | bytes 37601280 | tf_op jit(solution)/shard_map/all_gather | solution.py:709
  18.0 291.9 %all-gather.6.cloned.1.call-start = ((), (), s32[]{:S(2)}) async-start(), calls=%async_computation.10 | async-start | bytes 22560768 | tf_op jit(solution)/shard_map/all_gather | solution.py:715
  18.8 402.8 %all-gather.8.cloned.1.call-start = ((), (), s32[]{:S(2)}) async-start(), calls=%async_computation.11 | async-start | bytes 22560768 | tf_op jit(solution)/shard_map/all_gather | solution.py:716
  19.5 658.7 %reduce-scatter.9.cloned.1.call-start = ((), (), s32[]{:S(2)}) async-start(), calls=%async_computation.12 | async-start | bytes 1474560 | tf_op jit(solution)/shard_map/reduce_scatter | solution.py:447
  41.1 51.3 %collective-permute-start.5 = (bf16[512,2304]{1,0:T(8,128)(2,1)}, bf16[512,2304]{1,0:T(8,128)(2,1)}, u32[]{:S(2)}, u32[]{:S(2)}) collective-permute-start(bf16[512,2304]{1,0:T(8,128)(2,1)} %fusion.2.refs_0_), channel_id=1, source_target_pairs={{0,1},{1,0},{2,3},{3,2},{4,5},{5,4},{6,7},{7,6},{8,9},{9,8},{10,11... | collective-permute-start | bytes 7077896 | tf_op jit(solution)/shard_map/ppermute | solution.py:26
  234.7 53.6 %collective-permute-start.6 = (bf16[512,2304]{1,0:T(8,128)(2,1)}, bf16[512,2304]{1,0:T(8,128)(2,1)S(1)}, u32[]{:S(2)}, u32[]{:S(2)}) collective-permute-start(bf16[512,2304]{1,0:T(8,128)(2,1)} %shard_map.232), channel_id=1, source_target_pairs={{0,1},{1,0},{2,3},{3,2},{4,5},{5,4},{6,7},{7,6},{8,9},{9,8},{10,11... | collective-permute-start | bytes 7077896 | tf_op jit(solution)/shard_map/ppermute | solution.py:26
  295.8 52.8 %collective-permute-start.7 = (bf16[512,2304]{1,0:T(8,128)(2,1)S(1)}, bf16[512,2304]{1,0:T(8,128)(2,1)}, u32[]{:S(2)}, u32[]{:S(2)}) collective-permute-start(bf16[512,2304]{1,0:T(8,128)(2,1)S(1)} %multiply_convert_fusion.mid_ref.refs_0_), channel_id=1, source_target_pairs={{0,1},{1,0},{2,3},{3,2},{4,5},{5,4},{6,7},{7,6},{8,9},{9,8},{10,11... | collective-permute-start | bytes 7077896 | tf_op jit(solution)/shard_map/ppermute | solution.py:26
  465.2 29.1 %collective-permute-start.9 = (bf16[256,2304]{1,0:T(8,128)(2,1)}, bf16[256,2304]{1,0:T(8,128)(2,1)S(1)}, u32[]{:S(2)}, u32[]{:S(2)}) collective-permute-start(bf16[256,2304]{1,0:T(8,128)(2,1)} %shard_map.239), channel_id=1, source_target_pairs={{0,1},{1,0},{2,3},{3,2},{4,5},{5,4},{6,7},{7,6},{8,9},{9,8},{10,11... | collective-permute-start | bytes 3538952 | tf_op jit(solution)/shard_map/ppermute | solution.py:26
  496.3 29.1 %collective-permute-start.10 = (bf16[256,2304]{1,0:T(8,128)(2,1)S(1)}, bf16[256,2304]{1,0:T(8,128)(2,1)}, u32[]{:S(2)}, u32[]{:S(2)}) collective-permute-start(bf16[256,2304]{1,0:T(8,128)(2,1)S(1)} %get-tuple-element.260.refs_0_), channel_id=1, source_target_pairs={{0,1},{1,0},{2,3},{3,2},{4,5},{5,4},{6,7},{7,6},{8,9},{9,8},{10,11... | collective-permute-start | bytes 3538952 | tf_op jit(solution)/shard_map/ppermute | solution.py:26
  499.1 49.5 %collective-permute-start.11 = (bf16[256,2304]{1,0:T(8,128)(2,1)S(1)}, bf16[256,2304]{1,0:T(8,128)(2,1)S(1)}, u32[]{:S(2)}, u32[]{:S(2)}) collective-permute-start(bf16[256,2304]{1,0:T(8,128)(2,1)S(1)} %get-tuple-element.462.refs_1_.refs_0_), channel_id=1, source_target_pairs={{0,1},{1,0},{2,3},{3,2},{4,5},{5,4},{6,7},{7,6},{8,9},{9,8},{10,11... | collective-permute-start | bytes 3538952 | tf_op jit(solution)/shard_map/ppermute | solution.py:26
  605.2 34.5 %collective-permute-start.16 = (bf16[4,2,144,2048]{3,2,1,0:T(8,128)(2,1)}, bf16[4,2,144,2048]{3,2,1,0:T(8,128)(2,1)S(1)}, u32[]{:S(2)}, u32[]{:S(2)}) collective-permute-start(bf16[4,2,144,2048]{3,2,1,0:T(8,128)(2,1)} %shard_map.248), channel_id=1, source_target_pairs={{0,2},{2,0},{4,6},{6,4},{8,10},{10,8},{12,14},{14,12},{16,18},{18,... | collective-permute-start | bytes 14155784 | tf_op jit(solution)/shard_map/ppermute | solution.py:30
  605.2 44.0 %collective-permute-start.15 = (bf16[4,144,1536]{2,1,0:T(8,128)(2,1)}, bf16[4,144,1536]{2,1,0:T(8,128)(2,1)S(1)}, u32[]{:S(2)}, u32[]{:S(2)}) collective-permute-start(bf16[4,144,1536]{2,1,0:T(8,128)(2,1)} %shard_map.249), channel_id=1, source_target_pairs={{0,4},{2,6},{4,0},{6,2},{8,12},{10,14},{12,8},{14,10},{16,20},{18,... | collective-permute-start | bytes 5308424 | tf_op jit(solution)/shard_map/ppermute | solution.py:30
  649.5 96.0 %reduce-scatter.11.cloned.1.call-start = ((), (), s32[]{:S(2)}) async-start(), calls=%async_computation.13 | async-start | bytes 2211840 | tf_op jit(solution)/shard_map/reduce_scatter | solution.py:447
  678.2 32.9 %collective-permute-start.20 = (bf16[4,2,144,2048]{3,2,1,0:T(8,128)(2,1)}, bf16[4,2,144,2048]{3,2,1,0:T(8,128)(2,1)}, u32[]{:S(2)}, u32[]{:S(2)}) collective-permute-start(bf16[4,2,144,2048]{3,2,1,0:T(8,128)(2,1)} %shard_map.255), channel_id=1, source_target_pairs={{0,2},{2,0},{4,6},{6,4},{8,10},{10,8},{12,14},{14,12},{16,18},{18,... | collective-permute-start | bytes 14155784 | tf_op jit(solution)/shard_map/ppermute | solution.py:30
  678.2 130.3 %reduce-scatter.13.cloned.1.call-start = ((), (), s32[]{:S(2)}) async-start(), calls=%async_computation.14 | async-start | bytes 2949120 | tf_op jit(solution)/shard_map/reduce_scatter | solution.py:447
  678.3 32.8 %collective-permute-start.19 = (bf16[2,144,2048]{2,1,0:T(8,128)(2,1)S(1)}, bf16[2,144,2048]{2,1,0:T(8,128)(2,1)S(1)}, u32[]{:S(2)}, u32[]{:S(2)}) collective-permute-start(bf16[2,144,2048]{2,1,0:T(8,128)(2,1)S(1)} %copy-done.65), channel_id=1, source_target_pairs={{0,4},{2,6},{4,0},{6,2},{8,12},{10,14},{12,8},{14,10},{16,20},{18,... | collective-permute-start | bytes 3538952 | tf_op jit(solution)/shard_map/ppermute | solution.py:30
  711.1 34.5 %collective-permute-start.21 = (bf16[2,144,2560]{2,1,0:T(8,128)(2,1)S(1)}, bf16[2,144,2560]{2,1,0:T(8,128)(2,1)S(1)}, u32[]{:S(2)}, u32[]{:S(2)}) collective-permute-start(bf16[2,144,2560]{2,1,0:T(8,128)(2,1)S(1)} %copy-done.62), channel_id=1, source_target_pairs={{0,4},{2,6},{4,0},{6,2},{8,12},{10,14},{12,8},{14,10},{16,20},{18,... | collective-permute-start | bytes 4423688 | tf_op jit(solution)/shard_map/ppermute | solution.py:30
  745.5 35.1 %collective-permute-start.25 = (bf16[4,2,144,2560]{3,2,1,0:T(8,128)(2,1)}, bf16[4,2,144,2560]{3,2,1,0:T(8,128)(2,1)}, u32[]{:S(2)}, u32[]{:S(2)}) collective-permute-start(bf16[4,2,144,2560]{3,2,1,0:T(8,128)(2,1)} %shard_map.260), channel_id=1, source_target_pairs={{0,2},{2,0},{4,6},{6,4},{8,10},{10,8},{12,14},{14,12},{16,18},{18,... | collective-permute-start | bytes 17694728 | tf_op jit(solution)/shard_map/ppermute | solution.py:30
  745.6 125.1 %reduce-scatter.15.cloned.1.call-start = ((), (), s32[]{:S(2)}) async-start(), calls=%async_computation.15 | async-start | bytes 3686400 | tf_op jit(solution)/shard_map/reduce_scatter | solution.py:447
  745.6 35.0 %collective-permute-start.23 = (bf16[2,144,2560]{2,1,0:T(8,128)(2,1)}, bf16[2,144,2560]{2,1,0:T(8,128)(2,1)S(1)}, u32[]{:S(2)}, u32[]{:S(2)}) collective-permute-start(bf16[2,144,2560]{2,1,0:T(8,128)(2,1)} %get-tuple-element.330), channel_id=1, source_target_pairs={{0,4},{2,6},{4,0},{6,2},{8,12},{10,14},{12,8},{14,10},{16,20},{18,... | collective-permute-start | bytes 4423688 | tf_op jit(solution)/shard_map/ppermute | solution.py:30
  746.0 32.9 %collective-permute-start.24 = (bf16[256,2304]{1,0:T(8,128)(2,1)}, bf16[256,2304]{1,0:T(8,128)(2,1)S(1)}, u32[]{:S(2)}, u32[]{:S(2)}) collective-permute-start(bf16[256,2304]{1,0:T(8,128)(2,1)} %get-tuple-element.332), channel_id=1, source_target_pairs={{0,1},{1,0},{2,3},{3,2},{4,5},{5,4},{6,7},{7,6},{8,9},{9,8},{10,11... | collective-permute-start | bytes 3538952 | tf_op jit(solution)/shard_map/ppermute | solution.py:26
  810.2 124.1 %reduce-scatter.17.cloned.1.call-start = ((), (), s32[]{:S(2)}) async-start(), calls=%async_computation.16 | async-start | bytes 2949120 | tf_op jit(solution)/shard_map/reduce_scatter | solution.py:447
  835.6 35.0 %collective-permute-start.29 = (bf16[2,144,2560]{2,1,0:T(8,128)(2,1)}, bf16[2,144,2560]{2,1,0:T(8,128)(2,1)}, u32[]{:S(2)}, u32[]{:S(2)}) collective-permute-start(bf16[2,144,2560]{2,1,0:T(8,128)(2,1)} %get-tuple-element.359), channel_id=1, source_target_pairs={{0,4},{2,6},{4,0},{6,2},{8,12},{10,14},{12,8},{14,10},{16,20},{18,... | collective-permute-start | bytes 4423688 | tf_op jit(solution)/shard_map/ppermute | solution.py:30
  870.7 126.3 %reduce-scatter.19.cloned.1.call-start = ((), (), s32[]{:S(2)}) async-start(), calls=%async_computation.17 | async-start | bytes 3686400 | tf_op jit(solution)/shard_map/reduce_scatter | solution.py:447
  870.7 33.9 %collective-permute-start.32 = (bf16[2,144,2560]{2,1,0:T(8,128)(2,1)S(1)}, bf16[2,144,2560]{2,1,0:T(8,128)(2,1)S(1)}, u32[]{:S(2)}, u32[]{:S(2)}) collective-permute-start(bf16[2,144,2560]{2,1,0:T(8,128)(2,1)S(1)} %copy-done.61), channel_id=1, source_target_pairs={{0,4},{2,6},{4,0},{6,2},{8,12},{10,14},{12,8},{14,10},{16,20},{18,... | collective-permute-start | bytes 4423688 | tf_op jit(solution)/shard_map/ppermute | solution.py:30
  904.6 29.6 %collective-permute-start.34 = (bf16[4,2,144,1024]{3,2,1,0:T(8,128)(2,1)}, bf16[4,2,144,1024]{3,2,1,0:T(8,128)(2,1)S(1)}, u32[]{:S(2)}, u32[]{:S(2)}) collective-permute-start(bf16[4,2,144,1024]{3,2,1,0:T(8,128)(2,1)} %shard_map.271), channel_id=1, source_target_pairs={{0,2},{2,0},{4,6},{6,4},{8,10},{10,8},{12,14},{14,12},{16,18},{18,... | collective-permute-start | bytes 7077896 | tf_op jit(solution)/shard_map/ppermute | solution.py:30
  904.6 29.6 %collective-permute-start.33 = (bf16[2,144,2048]{2,1,0:T(8,128)(2,1)S(1)}, bf16[2,144,2048]{2,1,0:T(8,128)(2,1)S(1)}, u32[]{:S(2)}, u32[]{:S(2)}) collective-permute-start(bf16[2,144,2048]{2,1,0:T(8,128)(2,1)S(1)} %copy-done.66), channel_id=1, source_target_pairs={{0,4},{2,6},{4,0},{6,2},{8,12},{10,14},{12,8},{14,10},{16,20},{18,... | collective-permute-start | bytes 3538952 | tf_op jit(solution)/shard_map/ppermute | solution.py:30
  934.4 188.1 %reduce-scatter.23.cloned.1.call-start = ((), (), s32[]{:S(2)}) async-start(), calls=%async_computation.19 | async-start | bytes 2949120 | tf_op jit(solution)/shard_map/reduce_scatter | solution.py:447
  934.4 32.0 %collective-permute-start.35 = (bf16[2,144,2048]{2,1,0:T(8,128)(2,1)}, bf16[2,144,2048]{2,1,0:T(8,128)(2,1)S(1)}, u32[]{:S(2)}, u32[]{:S(2)}) collective-permute-start(bf16[2,144,2048]{2,1,0:T(8,128)(2,1)} %get-tuple-element.391), channel_id=1, source_target_pairs={{0,4},{2,6},{4,0},{6,2},{8,12},{10,14},{12,8},{14,10},{16,20},{18,... | collective-permute-start | bytes 3538952 | tf_op jit(solution)/shard_map/ppermute | solution.py:30
  997.0 128.3 %reduce-scatter.21.cloned.1.call-start = ((), (), s32[]{:S(2)}) async-start(), calls=%async_computation.18 | async-start | bytes 1474560 | tf_op jit(solution)/shard_map/reduce_scatter | solution.py:447
  1078.0 30.5 %collective-permute-start.47 = (bf16[144,1024]{1,0:T(8,128)(2,1)S(1)}, bf16[144,1024]{1,0:T(8,128)(2,1)S(1)}, u32[]{:S(2)}, u32[]{:S(2)}) collective-permute-start(bf16[144,1024]{1,0:T(8,128)(2,1)S(1)} %get-tuple-element.434), channel_id=1, source_target_pairs={{0,16},{2,18},{4,20},{6,22},{8,24},{10,26},{12,28},{14,30},{16,0},... | collective-permute-start | bytes 884744 | tf_op jit(solution)/shard_map/ppermute | solution.py:463
  1082.2 35.2 %collective-permute-start.46 = (bf16[144,1024]{1,0:T(8,128)(2,1)S(1)}, bf16[144,1024]{1,0:T(8,128)(2,1)}, u32[]{:S(2)}, u32[]{:S(2)}) collective-permute-start(bf16[144,1024]{1,0:T(8,128)(2,1)S(1)} %get-tuple-element.433), channel_id=1, source_target_pairs={{0,8},{2,10},{4,12},{6,14},{8,16},{10,18},{12,20},{14,22},{16,24},... | collective-permute-start | bytes 884744 | tf_op jit(solution)/shard_map/ppermute | solution.py:463
  (98 other events, 1236.7 us)
Sparse Core Ops, SparseCore 0:
  18.1 180.0 all-gather.3
  199.8 110.0 all-gather.5
  311.5 110.0 all-gather.7
  649.6 28.4 reduce-scatter.8
  680.3 37.1 reduce-scatter.10
  745.7 46.1 reduce-scatter.12
  810.4 56.3 reduce-scatter.14
  870.8 47.1 reduce-scatter.16
  934.5 55.5 reduce-scatter.18
  997.1 55.8 reduce-scatter.22
  1063.8 49.2 reduce-scatter.20

commit v5 on v4

--- a/solution.py
+++ b/solution.py
@@ -405,6 +405,30 @@
         )
         return self.give_side[0]
 
+    def both(self, from_core):
+        def kernel(_, *refs):
+            result = self.product(refs) + refs[self.count][...].astype(F32)
+            refs[-1][...] = result.astype(BF16)
+
+        shape = (self.rest, 2, self.rows)
+        place = lambda j, s: (0, 0, 0, j)
+        (self.total,) = self.run(
+            kernel,
+            self.inputs(2, lambda s: (0, s[0]))
+            + [(from_core, (*shape, self.tile), place, False)],
+            [((*shape, self.columns), BF16, (*shape, self.tile), place)],
+        )
+        return self.total
+
+    def to_side_last(self):
+        side = (lax.axis_index("dp") >> 1) & 1
+        parts = self.sums.reshape(2, self.rows, self.columns)
+        self.sums = pick(parts, side)
+        return pick(parts, 1 - side), lambda array: flip(array, 1, self.dp)
+
+    def add_side(self, part):
+        self.sums = self.sums.astype(F32) + part.astype(F32)
+
     def to_side(self, chunk):
         return self.give_side[chunk], lambda array: flip(array, 1, self.dp)
 
@@ -457,22 +481,21 @@
         transfers = []
         for shift in range(1, self.rest):
             pairs = [(i, (i + 4 * shift) % self.dp) for i in range(self.dp)]
-            part = lax.dynamic_index_in_dim(
-                self.total, (place + shift) % self.rest, 0, keepdims=False
-            )
+            part = pick(self.total, (place + shift) % self.rest)
             transfers.append((part, lambda array, pairs=pairs: lax.ppermute(array, "dp", pairs)))
         return transfers
 
     def gather(self, parts):
         place = lax.axis_index("dp") >> 2
-        total = lax.dynamic_index_in_dim(self.total, place, 0, keepdims=False).astype(F32)
+        total = pick(self.total, place).astype(F32)
         self.sums = sum((part.astype(F32) for part in parts), total)
-
-    def arrive(self, line):
-        (self.sums,) = line.land(self.sums)
 
     def result(self):
         return self.sums.astype(F32)
+
+
+def pick(array, index):
+    return lax.dynamic_index_in_dim(array, index, 0, keepdims=False)
 
 
 def sum_of_products(lefts, rights):
@@ -530,9 +553,12 @@
     def send(self, *transfers):
         return [send(self.next(array)) for array, send in transfers]
 
-    def land(self, *flying):
-        *taken, self.last = tied(*flying, self.last)
-        return taken
+    def land(self, *flying, sums=()):
+        count = len(flying)
+        *taken, self.last = tied(*flying, *(grad.sums for grad in sums), self.last)
+        for grad, value in zip(sums, taken[count:]):
+            grad.sums = value
+        return taken[:count]
 
 
 def projected(pieces, weights, first_column, columns, scalars):
@@ -799,7 +825,7 @@
         first = lambda s: 0
         tile = tile_of(columns)
         tiles = columns // tile
-        cuts = [0, 2 * tile, 5 * tile, columns]
+        cuts = [0, 2 * tile, 4 * tile, columns]
         split = tile * -(-tiles // 2)
         halves = [(0, split), (split, columns - split)]
         hidden_rights = [(hidden_own, half, first), (hidden_other, half, first)]
@@ -821,63 +847,59 @@
         down_0 = down_part(0, 1)
         line.mark(down_0.give())
         (core_0,) = line.send(down_0.to_core())
+        down_2 = down_part(2, 2)
+        line.mark(down_2.give())
+        (core_0,) = line.land(core_0)
+        line.mark(down_0.side(line.next(core_0)))
+
+        down_0_side, core_2 = line.send(down_0.to_side(0), down_2.to_core())
         down_1 = down_part(1, 1)
         line.mark(down_1.give())
-        (core_0,) = line.land(core_0)
-        line.mark(down_0.side(line.next(core_0)))
-
-        down_0_side, core_1 = line.send(down_0.to_side(0), down_1.to_core())
-        down_2 = down_part(2, 2)
-        line.mark(down_2.give())
-        (core_1,) = line.land(core_1)
-        line.mark(down_1.side(line.next(core_1)))
-        (down_0_side,) = line.land(down_0_side)
-
-        down_1_side, core_2 = line.send(down_1.to_side(0), down_2.to_core())
         (d_gate_4,), (d_up_4,) = hidden_back(
             line, [(d_ffn_4, active_other, slope_other, 1)], full_down_t, scalars
         )
         d_gates = [d_gate_1, d_gate_2, d_gate_3, d_gate_4]
         d_ups = [d_up_1, d_up_2, d_up_3, d_up_4]
+        (core_2,) = line.land(core_2)
+        line.mark(down_2.side(line.next(core_2)))
+        (down_0_side,) = line.land(down_0_side)
+
+        side_0, core_1 = line.send(down_2.to_side(0), down_1.to_core())
         line.mark(down_0.own(line.next(down_0_side)))
         gate_0 = mid_part(d_gates, 0)
         line.mark(gate_0.give())
-        (core_2,) = line.land(core_2)
-        line.mark(down_2.side(line.next(core_2)))
-        (down_1_side,) = line.land(down_1_side)
-
-        side_0, core_0 = line.send(down_2.to_side(0), gate_0.to_core())
-        down_0.along_rest(line)
-        line.mark(down_1.own(line.next(down_1_side)))
+        (core_1,) = line.land(core_1)
+        line.mark(down_1.both(line.next(core_1)))
         gate_1 = mid_part(d_gates, 1)
         line.mark(gate_1.give())
-        (core_0,) = line.land(core_0)
+        (side_0,) = line.land(side_0)
+
+        side_1, core_0, core_1 = line.send(
+            down_2.to_side(1), gate_0.to_core(), gate_1.to_core()
+        )
+        down_0.along_rest(line)
+        give_1, give_2 = mid_back_of(d_gates[2:], d_ups[2:], BF16)
+        core_0, core_1 = line.land(core_0, core_1)
         line.mark(gate_0.side(line.next(core_0)))
-        (side_0,) = line.land(side_0)
-        down_0.arrive(line)
-
-        side_1, core_1 = line.send(down_2.to_side(1), gate_1.to_core())
+        (side_1,) = line.land(
+            side_1, sums=[down_0]
+        )
+
+        gate_0_side_0, gate_0_side_1, taken_1, taken_2 = line.send(
+            gate_0.to_side(0), gate_0.to_side(1), to_other(give_1), to_other(give_2)
+        )
         down_1.along_rest(line)
-        give_1, give_2 = mid_back_of(d_gates[2:], d_ups[2:], BF16)
-        side_1, core_1 = line.land(side_1, core_1)
-
-        gate_0_side_0, taken_1 = line.send(gate_0.to_side(0), to_other(give_1))
         line.mark(down_2.own(line.next(side_0), side_1))
         line.mark(gate_1.side(line.next(core_1)))
         up_0 = mid_part(d_ups, 0)
         line.mark(up_0.give())
-        gate_0_side_0, taken_1 = line.land(gate_0_side_0, taken_1)
-        down_1.arrive(line)
-
-        gate_0_side_1, taken_2, core_0 = line.send(
-            gate_0.to_side(1), to_other(give_2), up_0.to_core()
-        )
+        kept_1, kept_2 = mid_back_of(d_gates[:2], d_ups[:2], F32)
+        gate_0_side_0, gate_0_side_1, taken_1, taken_2 = line.land(
+            gate_0_side_0, gate_0_side_1, taken_1, taken_2, sums=[down_1]
+        )
+
+        gate_1_side_0, core_0 = line.send(gate_1.to_side(0), up_0.to_core())
         down_2.along_rest(line)
-        kept_1, kept_2 = mid_back_of(d_gates[:2], d_ups[:2], F32)
-        gate_0_side_1, taken_2, core_0 = line.land(gate_0_side_1, taken_2, core_0)
-
-        (gate_1_side_0,) = line.send(gate_1.to_side(0))
-        line.mark(gate_0.own(line.next(gate_0_side_0), gate_0_side_1))
         d_middle, d_branch_1, d_branch_2, grad_c, grad_b = norms_back(
             line,
             [(kept_1, taken_1), (kept_2, taken_2)],
@@ -888,25 +910,30 @@
             gain_b,
             scalars,
         )
+        (core_0,) = line.land(core_0)
+        line.mark(up_0.side(line.next(core_0)))
         (gate_1_side_0,) = line.land(gate_1_side_0)
-        down_2.arrive(line)
-
-        gate_1_side_1, d_branch_3 = line.send(gate_1.to_side(1), to_other(d_branch_1))
-        gate_0.along_rest(line)
-        line.mark(up_0.side(line.next(core_0)))
+
+        gate_1_side_1, d_branch_3, down_1_side = line.send(
+            gate_1.to_side(1), to_other(d_branch_1), down_1.to_side_last()
+        )
+        line.mark(gate_0.own(line.next(gate_0_side_0), gate_0_side_1))
         up_1 = mid_part(d_ups, 1)
         line.mark(up_1.give())
-        gate_1_side_1, d_branch_3 = line.land(gate_1_side_1, d_branch_3)
+        d_branch_own_t = line.mark(turned([line.next(d_branch_1), d_branch_2], scalars))
+        gate_1_side_1, d_branch_3, down_1_side = line.land(
+            gate_1_side_1, d_branch_3, down_1_side, sums=[down_2]
+        )
+        down_1.add_side(down_1_side)
 
         up_0_side_0, core_1, d_branch_4 = line.send(
             up_0.to_side(0), up_1.to_core(), to_other(d_branch_2)
         )
+        gate_0.along_rest(line)
         line.mark(gate_1.own(line.next(gate_1_side_0), gate_1_side_1))
-        d_branch_own_t = line.mark(turned([line.next(d_branch_1), d_branch_2], scalars))
         (core_1,) = line.land(core_1)
         line.mark(up_1.side(line.next(core_1)))
         up_0_side_0, d_branch_4 = line.land(up_0_side_0, d_branch_4)
-        gate_0.arrive(line)
 
         (up_0_side_1,) = line.send(up_0.to_side(1))
         gate_1.along_rest(line)
@@ -920,6 +947,15 @@
             )
         )
         d_branch_other_t = line.mark(turned([line.next(d_branch_3), d_branch_4], scalars))
+        d_query, d_pair = line.mark(
+            attend_back(qkv, line.next(d_attended), heads, group, SEQ_LEN, scalars)
+        )
+        (up_0_side_1,) = line.land(
+            up_0_side_1, sums=[gate_0]
+        )
+
+        (up_1_side_0,) = line.send(up_1.to_side(0))
+        line.mark(up_0.own(line.next(up_0_side_0), up_0_side_1))
         output = Grad(
             dp,
             1,
@@ -930,19 +966,6 @@
             scalars,
         )
         line.mark(output.give())
-        (up_0_side_1,) = line.land(up_0_side_1)
-
-        up_1_side_0, core = line.send(up_1.to_side(0), output.to_core())
-        line.mark(up_0.own(line.next(up_0_side_0), up_0_side_1))
-        d_query, d_pair = line.mark(
-            attend_back(qkv, line.next(d_attended), heads, group, SEQ_LEN, scalars)
-        )
-        up_1_side_0, core = line.land(up_1_side_0, core)
-        gate_1.arrive(line)
-
-        (up_1_side_1,) = line.send(up_1.to_side(1))
-        up_0.along_rest(line)
-        line.mark(output.side(line.next(core)))
 
         def input_part(array, width):
             rights = [(line.next(array), half, mine), (array, half, theirs)]
@@ -952,32 +975,36 @@
         line.mark(query.give())
         pair = input_part(d_pair, 2 * key_cols)
         line.mark(pair.give())
+        (up_1_side_0,) = line.land(up_1_side_0)
+
+        up_1_side_1, core, query_core, pair_core = line.send(
+            up_1.to_side(1), output.to_core(), query.to_core(), pair.to_core()
+        )
+        up_0.along_rest(line)
         give_1, give_2 = line.mark(
             projected_back(
                 [(line.next(d_query), 0), (d_pair, 1)], full_first, theirs, 2, BF16, scalars
             )
         )
-        (up_1_side_1,) = line.land(up_1_side_1)
-
-        output_side, query_core, pair_core, taken_1 = line.send(
-            output.to_side(0), query.to_core(), pair.to_core(), to_other(give_1)
-        )
-        line.mark(up_1.own(line.next(up_1_side_0), up_1_side_1))
-        query_core, pair_core = line.land(query_core, pair_core)
+        core, query_core, pair_core = line.land(core, query_core, pair_core)
+        line.mark(output.side(line.next(core)))
         line.mark(query.side(line.next(query_core)))
         line.mark(pair.side(line.next(pair_core)))
-        output_side, taken_1 = line.land(output_side, taken_1)
-        up_0.arrive(line)
-
-        query_side, taken_2 = line.send(query.to_side(0), to_other(give_2))
-        up_1.along_rest(line)
-        line.mark(output.own(line.next(output_side)))
+        (up_1_side_1,) = line.land(up_1_side_1, sums=[gate_1])
+
+        output_side, taken_1 = line.send(output.to_side(0), to_other(give_1))
+        line.mark(up_1.own(line.next(up_1_side_0), up_1_side_1))
         kept_1, kept_2 = line.mark(
             projected_back(
                 [(line.next(d_query), 0), (d_pair, 1)], full_first, mine, 2, F32, scalars
             )
         )
-        query_side, taken_2 = line.land(query_side, taken_2)
+        output_side, taken_1 = line.land(output_side, taken_1)
+
+        query_side, taken_2 = line.send(query.to_side(0), to_other(give_2))
+        up_1.along_rest(line)
+        line.mark(output.own(line.next(output_side)))
+        query_side, taken_2 = line.land(query_side, taken_2, sums=[up_0])
         line.mark(query.own(line.next(query_side)))
 
         pair_side, *query_parts = line.send(pair.to_side(0), *query.to_owner())
@@ -992,13 +1019,13 @@
             scalars,
         )
         (pair_side,) = line.land(pair_side)
-        up_1.arrive(line)
         line.mark(pair.own(line.next(pair_side)))
-        query_parts = line.land(*query_parts)
-
+        query_parts = line.land(*query_parts, sums=[up_1])
         gain_grads = jnp.stack([grad_a[0], grad_b[0], grad_c[0], grad_d])
-        gain_parts, *pair_parts = line.send((gain_grads, to_owners), *pair.to_owner())
+        *pair_parts, gain_parts = line.send(*pair.to_owner(), (gain_grads, to_owners))
         output.along_rest(line)
+        pair_parts = line.land(*pair_parts)
+        (gain_parts,) = line.land(gain_parts)
         small = jnp.sum(gain_parts, axis=0)
         query.gather(query_parts)
         pair.gather(pair_parts)

time: 1150 us -> 1140 us (level)
    ppermute x29, waiting for transfers between devices: 67.1 us -> 54.8 us  [flip(): return lax.ppermute(array, 'dp', [(i, i ^ 1 << bit) for i in range(dp)])]
    pallas_call x58 -> x57, Pallas kernels: 624 us -> 619 us  [call(): pl.pallas_call(kernel, grid_spec=pltpu.PrefetchScalarGridSpec(num_scalar_...]
    unnamed x146 -> x124, local copies, waits for them, and re-layouts: 27.7 us -> 26.3 us
  transfers between devices with their start and end apart: 61 -> 61, of which waited for: 33 -> 27; matrix products, arithmetic and copies ran while one was open for 4% -> 4% of each run, Pallas kernels for 52% -> 52%
where the time goes in v5:
time: 1140 us; the launch traced here: 1130 us
  Pallas kernels  619 us (54%)
  waiting for transfers between devices  350 us (31%)
  starting transfers between devices  64.6 us (6%)
  other arithmetic  40.5 us (4%)
  local copies, waits for them, and re-layouts  36.8 us (3%)
  between operations  14.8 us (1%)
    pallas_call x57, Pallas kernels, call(): pl.pallas_call(kernel, grid_spec=pltpu.PrefetchScalarGridSpec(num_scalar_...  619 us
    ppermute x14, waiting for transfers between devices, swap(): return lax.ppermute(rows, 'tensor', [(0, 1), (1, 0)])  113 us
    all_gather x1, waiting for transfers between devices, body(): lax.all_gather(jnp.concatenate([query_weight, *pairs, w_output.T, w_gate]...  100 us
    ppermute x29, waiting for transfers between devices, flip(): return lax.ppermute(array, 'dp', [(i, i ^ 1 << bit) for i in range(dp)])  54.8 us
    all_gather x1, waiting for transfers between devices, body(): full_down_t = lax.all_gather(w_down.T, 'dp', axis=0, tiled=True)  37.5 us
    ppermute x6, waiting for transfers between devices, to_owner(): lax.ppermute(array, 'dp', pairs)  30.6 us
    unnamed x124, local copies, waits for them, and re-layouts  26.3 us
    ppermute x29, starting transfers between devices, flip(): return lax.ppermute(array, 'dp', [(i, i ^ 1 << bit) for i in range(dp)])  24.7 us
  transfers between devices with their start and end apart: 61, of which 27 were waited for; matrix products, arithmetic and copies ran while one was open for 4% of the time, Pallas kernels for 52%

profile of v5, /device:TPU:0, one launch (start us, length us, event | category | flops | bytes accessed | tf_op | source)
XLA Modules:
  0.0 1126.1 jit_solution(11811152224340279986)
XLA Ops:
  49.4 42.9 %collective-permute-done.5.refs_0_.refs_1_ = bf16[512,2304]{1,0:T(8,128)(2,1)} collective-permute-done((bf16[512,2304]{1,0:T(8,128)(2,1)}, bf16[512,2304]{1,0:T(8,128)(2,1)}, u32[]{:S(2)}, u32[]{:S(2)}) %collective-permute-start.5) | collective-permute-done | bytes 2359328 | tf_op jit(solution)/shard_map/ppermute | solution.py:26
  98.2 100.0 %all-gather.4.cloned.1.call-done.refs_2_.refs_1_.gate_ref.refs_4_.refs_5_.refs_6_.refs_3_ = bf16[2304,7680]{1,0:T(8,128)(2,1)} async-done(((bf16[144,7680]{1,0:T(8,128)(2,1)}), bf16[2304,7680]{1,0:T(8,128)(2,1)}) %all-gather.4.cloned.1.call-update) | async-done | bytes 35389456 | tf_op jit(solution)/shard_map/all_gather | solution.py:735
  198.2 15.3 %shard_map.230.query_ref.key_ref.value_ref.pair_ref = bf16[1024,2048]{1,0:T(8,128)(2,1)} custom-call(s32[3]{0:T(128)} %pad_add_fusion._.scalar_ref, bf16[512,2304]{1,0:T(8,128)(2,1)} %fusion.2.refs_0_, bf16[512,2304]{1,0:T(8,128)(2,1)} %collective-permute-done.5.refs_0_.refs_1_, ...), custom_call_target="tpu_custom_call" | custom-call | flops 1 | bytes 1 | tf_op jit(solution)/shard_map/pallas_call | solution.py:68
  213.5 11.4 %shard_map.231.refs_0_.refs_2_.refs_3_ = bf16[1024,1024]{1,0:T(8,128)(2,1)} custom-call(s32[3]{0:T(128)} %pad_add_fusion._.scalar_ref, bf16[1024,2048]{1,0:T(8,128)(2,1)} %shard_map.230.query_ref.key_ref.value_ref.pair_ref, bf16[1024,2048]{1,0:T(8,128)(2,1)} %shard_map.230.query_ref.key_ref.value_ref.pair_ref, ...), custom_call_target="tpu_custom_call" | custom-call | flops 1 | bytes 1 | tf_op jit(solution)/shard_map/pallas_call | solution.py:68
  224.9 9.9 shard_map.232
  236.2 10.3 shard_map.233
  246.5 41.8 %collective-permute-done.6 = bf16[512,2304]{1,0:T(8,128)(2,1)S(1)} collective-permute-done((bf16[512,2304]{1,0:T(8,128)(2,1)}, bf16[512,2304]{1,0:T(8,128)(2,1)S(1)}, u32[]{:S(2)}, u32[]{:S(2)}) %collective-permute-start.6) | collective-permute-done | bytes 2359328 | tf_op jit(solution)/shard_map/ppermute | solution.py:26
  297.3 12.6 %all-gather.6.cloned.1.call-done.up_ref.refs_7_ = bf16[2304,4608]{1,0:T(8,128)(2,1)} async-done(((bf16[144,4608]{1,0:T(8,128)(2,1)}), bf16[2304,4608]{1,0:T(8,128)(2,1)}) %all-gather.6.cloned.1.call-update) | async-done | bytes 21233680 | tf_op jit(solution)/shard_map/all_gather | solution.py:741
  309.9 30.8 %shard_map.234 = (bf16[512,4608]{1,0:T(8,128)(2,1)}, bf16[512,4608]{1,0:T(8,128)(2,1)}, bf16[512,4608]{1,0:T(8,128)(2,1)}) custom-call(s32[3]{0:T(128)} %pad_add_fusion._.scalar_ref, bf16[512,2304]{1,0:T(8,128)(2,1)} %copy-done.6, bf16[2304,7680]{1,0:T(8,128)(2,1)} %all-gather.4.cloned.1.call-done.refs_2_.refs_1_.gate_ref.refs_4_.refs_5_.refs_6_.refs_3_, ...), custom_call_target="tpu_custom_call" | custom-call | flops 1 | bytes 1 | tf_op jit(solution)/shard_map/pallas_call | solution.py:68
  348.5 29.8 %shard_map.236 = (bf16[512,4608]{1,0:T(8,128)(2,1)}, bf16[512,4608]{1,0:T(8,128)(2,1)}, bf16[512,4608]{1,0:T(8,128)(2,1)}) custom-call(s32[3]{0:T(128)} %pad_add_fusion._.scalar_ref, bf16[512,2304]{1,0:T(8,128)(2,1)} %collective-permute-done.7.mid_ref.refs_0_, ...), custom_call_target="tpu_custom_call" | custom-call | flops 1 | bytes 1 | tf_op jit(solution)/shard_map/pallas_call | solution.py:68
  384.1 37.5 %all-gather.8.cloned.1.call-done.down_ref.refs_3_.refs_6_ = bf16[2304,4608]{1,0:T(8,128)(2,1)} async-done(((bf16[144,4608]{1,0:T(8,128)(2,1)}), bf16[2304,4608]{1,0:T(8,128)(2,1)}) %all-gather.8.cloned.1.call-update) | async-done | bytes 21233680 | tf_op jit(solution)/shard_map/all_gather | solution.py:742
  421.6 15.4 %shard_map.238 = bf16[256,2304]{1,0:T(8,128)(2,1)} custom-call(s32[3]{0:T(128)} %pad_add_fusion._.scalar_ref, bf16[512,4608]{1,0:T(8,128)(2,1)} %get-tuple-element.242.hidden_ref.refs_3_, bf16[2304,4608]{1,0:T(8,128)(2,1)} %all-gather.8.cloned.1.call-done.down_ref.refs_3_.refs_6_), custom_call_target="tpu_custom_call" | custom-call | flops 1 | bytes 1 | tf_op jit(solution)/shard_map/pallas_call | solution.py:68
  441.0 15.4 %shard_map.239 = bf16[256,2304]{1,0:T(8,128)(2,1)} custom-call(s32[3]{0:T(128)} %pad_add_fusion._.scalar_ref, bf16[512,4608]{1,0:T(8,128)(2,1)} %get-tuple-element.242.hidden_ref.refs_3_, bf16[2304,4608]{1,0:T(8,128)(2,1)} %all-gather.8.cloned.1.call-done.down_ref.refs_3_.refs_6_), custom_call_target="tpu_custom_call" | custom-call | flops 1 | bytes 1 | tf_op jit(solution)/shard_map/pallas_call | solution.py:68
  466.8 19.2 %shard_map.240 = f32[512,2304]{1,0:T(8,128)} custom-call(s32[3]{0:T(128)} %pad_add_fusion._.scalar_ref, bf16[512,4608]{1,0:T(8,128)(2,1)} %get-tuple-element.244.hidden_ref.refs_2_, bf16[2304,4608]{1,0:T(8,128)(2,1)} %all-gather.8.cloned.1.call-done.down_ref.refs_3_.refs_6_), custom_call_target="tpu_custom_call" | custom-call | flops 1 | bytes 1 | tf_op jit(solution)/shard_map/pallas_call | solution.py:68
  506.5 16.7 %shard_map.242 = (bf16[256,4608]{1,0:T(8,128)(2,1)}, bf16[256,4608]{1,0:T(8,128)(2,1)}) custom-call(s32[3]{0:T(128)} %pad_add_fusion._.scalar_ref, bf16[256,2304]{1,0:T(8,128)(2,1)} %copy-done.8, bf16[512,4608]{1,0:T(8,128)(2,1)} %get-tuple-element.253.refs_1_.refs_2_, bf16[512,4608]{1,0:T(8,128)(2,1)} %get-tuple-element.254.refs_2_.refs_4_, ...), custom_call_target="tpu_custom_call" | custom-call | flops 1 | bytes 1 | tf_op jit(solution)/shard_map/pallas_call | solution.py:68
  525.6 21.2 %shard_map.243 = (bf16[256,4608]{1,0:T(8,128)(2,1)}, bf16[256,4608]{1,0:T(8,128)(2,1)}, bf16[256,4608]{1,0:T(8,128)(2,1)}, bf16[256,4608]{1,0:T(8,128)(2,1)}) custom-call(s32[3]{0:T(128)} %pad_add_fusion._.scalar_ref, bf16[256,2304]{1,0:T(8,128)(2,1)} %copy-done.9, bf16[256,2304]{1,0:T(8,128)(2,1)} %collective-permute-done.10.refs_1_.refs_0_, ...), custom_call_target="tpu_custom_call" | custom-call | flops 1 | bytes 1 | tf_op jit(solution)/shard_map/pallas_call | solution.py:68
  562.1 11.3 %shard_map.246 = bf16[4,2,144,2560]{3,2,1,0:T(8,128)(2,1)} custom-call(s32[3]{0:T(128)} %pad_add_fusion._.scalar_ref, bf16[4,2,2,144,512]{4,3,2,1,0:T(8,128)(2,1)} %bitcast.96, bf16[4,2,2,144,512]{4,3,2,1,0:T(8,128)(2,1)} %bitcast.104, bf16[512,4608]{1,0:T(8,128)(2,1)} %get-tuple-element.244.hidden_ref.refs_2_, ...), custom_call_target="tpu_custom_call" | custom-call | flops 1 | bytes 1 | tf_op jit(solution)/shard_map/pallas_call | solution.py:68
  588.0 17.0 %shard_map.249 = (bf16[256,4608]{1,0:T(8,128)(2,1)}, bf16[256,4608]{1,0:T(8,128)(2,1)}) custom-call(s32[3]{0:T(128)} %pad_add_fusion._.scalar_ref, bf16[256,2304]{1,0:T(8,128)(2,1)} %copy-done.18, bf16[512,4608]{1,0:T(8,128)(2,1)} %get-tuple-element.259.refs_3_.refs_1_, bf16[512,4608]{1,0:T(8,128)(2,1)} %get-tuple-element.260.refs_5_.refs_2_, ...), custom_call_target="tpu_custom_call" | custom-call | flops 1 | bytes 1 | tf_op jit(solution)/shard_map/pallas_call | solution.py:68
  622.5 11.2 shard_map.252
  653.8 31.0 %shard_map.255 = (bf16[256,2304]{1,0:T(8,128)(2,1)}, bf16[256,2304]{1,0:T(8,128)(2,1)}) custom-call(s32[3]{0:T(128)} %pad_add_fusion._.scalar_ref, bf16[256,4608]{1,0:T(8,128)(2,1)} %get-tuple-element.291.refs_4_.refs_0_, bf16[256,4608]{1,0:T(8,128)(2,1)} %get-tuple-element.286.refs_5_.refs_1_, bf16[256,4608]{1,0:T(8,128)(2,1)} %get-tuple-element.344.refs_2_.refs_4_, ...), custom_call_target="tpu_custom_call" | custom-call | flops 1 | bytes 1 | tf_op jit(solution)/shard_map/pallas_call | solution.py:68
  697.7 9.9 shard_map.257
  715.1 11.2 shard_map.259
  726.3 30.9 %shard_map.260 = (f32[256,2304]{1,0:T(8,128)}, f32[256,2304]{1,0:T(8,128)}) custom-call(s32[3]{0:T(128)} %pad_add_fusion._.scalar_ref, bf16[256,4608]{1,0:T(8,128)(2,1)} %get-tuple-element.312.refs_2_.refs_0_, bf16[256,4608]{1,0:T(8,128)(2,1)} %get-tuple-element.284.refs_3_.refs_1_, bf16[256,4608]{1,0:T(8,128)(2,1)} %get-tuple-element.342.refs_2_, ...), custom_call_target="tpu_custom_call" | custom-call | flops 1 | bytes 1 | tf_op jit(solution)/shard_map/pallas_call | solution.py:68
  760.6 14.1 %shard_map.261 = (f32[512,2304]{1,0:T(8,128)}, bf16[256,2304]{1,0:T(8,128)(2,1)}, bf16[256,2304]{1,0:T(8,128)(2,1)}, f32[1,2304]{1,0:T(1,128)}, f32[1,2304]{1,0:T(1,128)}) custom-call(s32[3]{0:T(128)} %pad_add_fusion._.scalar_ref, f32[256,2304]{1,0:T(8,128)} %get-tuple-element.322.refs_0_, bf16[256,2304]{1,0:T(8,128)(2,1)} %copy-done.29, ...), custom_call_target="tpu_custom_call" | custom-call | flops 1 | bytes 1 | tf_op jit(solution)/shard_map/pallas_call | solution.py:68
  860.0 10.4 shard_map.268.d_ref
  876.1 18.2 %shard_map.270 = (bf16[1024,1024]{1,0:T(8,128)(2,1)}, bf16[1024,1024]{1,0:T(8,128)(2,1)}) custom-call(s32[3]{0:T(128)} %pad_add_fusion._.scalar_ref, bf16[1024,2048]{1,0:T(8,128)(2,1)} %shard_map.230.query_ref.key_ref.value_ref.pair_ref, bf16[1024,2048]{1,0:T(8,128)(2,1)} %shard_map.230.query_ref.key_ref.value_ref.pair_ref, bf16[1024,1024]{1,0:T(8,128)(2,1)} %shard_map.268.d_ref), custom_call_target="tpu_custom_call" | custom-call | flops 1 | bytes 1 | tf_op jit(solution)/shard_map/pallas_call | solution.py:68
  926.7 12.1 %shard_map.275 = (bf16[256,2304]{1,0:T(8,128)(2,1)}, bf16[256,2304]{1,0:T(8,128)(2,1)}) custom-call(s32[3]{0:T(128)} %pad_add_fusion._.scalar_ref, bf16[1024,1024]{1,0:T(8,128)(2,1)} %get-tuple-element.394.refs_2_.refs_3_.refs_0_, bf16[1024,1024]{1,0:T(8,128)(2,1)} %get-tuple-element.375.refs_2_.refs_3_.refs_1_, ...), custom_call_target="tpu_custom_call" | custom-call | flops 1 | bytes 1 | tf_op jit(solution)/shard_map/pallas_call | solution.py:68
  966.0 12.5 %shard_map.280 = (f32[256,2304]{1,0:T(8,128)}, f32[256,2304]{1,0:T(8,128)}) custom-call(s32[3]{0:T(128)} %pad_add_fusion._.scalar_ref, bf16[1024,1024]{1,0:T(8,128)(2,1)} %get-tuple-element.394.refs_2_.refs_3_.refs_0_, bf16[1024,1024]{1,0:T(8,128)(2,1)} %get-tuple-element.375.refs_2_.refs_3_.refs_1_, ...), custom_call_target="tpu_custom_call" | custom-call | flops 1 | bytes 1 | tf_op jit(solution)/shard_map/pallas_call | solution.py:68
  992.3 19.6 %collective-permute-done.40.refs_5_ = bf16[4,144,1024]{2,1,0:T(8,128)(2,1)S(1)} collective-permute-done((bf16[4,144,1024]{2,1,0:T(8,128)(2,1)S(1)}, bf16[4,144,1024]{2,1,0:T(8,128)(2,1)S(1)}, u32[]{:S(2)}, u32[]{:S(2)}) %collective-permute-start.40) | collective-permute-done | bytes 1179680 | tf_op jit(solution)/shard_map/ppermute | solution.py:30
  1029.3 11.2 shard_map.283
  1065.8 10.2 all-to-all-start
  1096.0 16.4 %collective-permute-done.47 = bf16[144,1024]{1,0:T(8,128)(2,1)} collective-permute-done((bf16[144,1024]{1,0:T(8,128)(2,1)}, bf16[144,1024]{1,0:T(8,128)(2,1)}, u32[]{:S(2)}, u32[]{:S(2)}) %collective-permute-start.47) | collective-permute-done | bytes 294944 | tf_op jit(solution)/shard_map/ppermute | solution.py:485
  (332 shorter events, 434.1 us)
Async XLA Ops:
  7.2 191.0 %all-gather.4.cloned.1.call-start = ((), (), s32[]{:S(2)}) async-start(), calls=%async_computation.9 | async-start | bytes 37601280 | tf_op jit(solution)/shard_map/all_gather | solution.py:735
  18.0 291.9 %all-gather.6.cloned.1.call-start = ((), (), s32[]{:S(2)}) async-start(), calls=%async_computation.10 | async-start | bytes 22560768 | tf_op jit(solution)/shard_map/all_gather | solution.py:741
  18.8 402.8 %all-gather.8.cloned.1.call-start = ((), (), s32[]{:S(2)}) async-start(), calls=%async_computation.11 | async-start | bytes 22560768 | tf_op jit(solution)/shard_map/all_gather | solution.py:742
  19.5 674.0 %reduce-scatter.9.cloned.1.call-start = ((), (), s32[]{:S(2)}) async-start(), calls=%async_computation.12 | async-start | bytes 1474560 | tf_op jit(solution)/shard_map/reduce_scatter | solution.py:471
  41.1 51.3 %collective-permute-start.5 = (bf16[512,2304]{1,0:T(8,128)(2,1)}, bf16[512,2304]{1,0:T(8,128)(2,1)}, u32[]{:S(2)}, u32[]{:S(2)}) collective-permute-start(bf16[512,2304]{1,0:T(8,128)(2,1)} %fusion.2.refs_0_), channel_id=1, source_target_pairs={{0,1},{1,0},{2,3},{3,2},{4,5},{5,4},{6,7},{7,6},{8,9},{9,8},{10,11... | collective-permute-start | bytes 7077896 | tf_op jit(solution)/shard_map/ppermute | solution.py:26
  234.7 53.6 %collective-permute-start.6 = (bf16[512,2304]{1,0:T(8,128)(2,1)}, bf16[512,2304]{1,0:T(8,128)(2,1)S(1)}, u32[]{:S(2)}, u32[]{:S(2)}) collective-permute-start(bf16[512,2304]{1,0:T(8,128)(2,1)} %shard_map.232), channel_id=1, source_target_pairs={{0,1},{1,0},{2,3},{3,2},{4,5},{5,4},{6,7},{7,6},{8,9},{9,8},{10,11... | collective-permute-start | bytes 7077896 | tf_op jit(solution)/shard_map/ppermute | solution.py:26
  295.8 52.8 %collective-permute-start.7 = (bf16[512,2304]{1,0:T(8,128)(2,1)S(1)}, bf16[512,2304]{1,0:T(8,128)(2,1)}, u32[]{:S(2)}, u32[]{:S(2)}) collective-permute-start(bf16[512,2304]{1,0:T(8,128)(2,1)S(1)} %multiply_convert_fusion.mid_ref.refs_0_), channel_id=1, source_target_pairs={{0,1},{1,0},{2,3},{3,2},{4,5},{5,4},{6,7},{7,6},{8,9},{9,8},{10,11... | collective-permute-start | bytes 7077896 | tf_op jit(solution)/shard_map/ppermute | solution.py:26
  499.3 49.6 %collective-permute-start.11 = (bf16[256,2304]{1,0:T(8,128)(2,1)S(1)}, bf16[256,2304]{1,0:T(8,128)(2,1)S(1)}, u32[]{:S(2)}, u32[]{:S(2)}) collective-permute-start(bf16[256,2304]{1,0:T(8,128)(2,1)S(1)} %get-tuple-element.453.refs_1_.refs_0_), channel_id=1, source_target_pairs={{0,1},{1,0},{2,3},{3,2},{4,5},{5,4},{6,7},{7,6},{8,9},{9,8},{10,11... | collective-permute-start | bytes 3538952 | tf_op jit(solution)/shard_map/ppermute | solution.py:26
  580.3 36.0 %collective-permute-start.13 = (bf16[4,144,1024]{2,1,0:T(8,128)(2,1)}, bf16[4,144,1024]{2,1,0:T(8,128)(2,1)}, u32[]{:S(2)}, u32[]{:S(2)}) collective-permute-start(bf16[4,144,1024]{2,1,0:T(8,128)(2,1)} %shard_map.247), channel_id=1, source_target_pairs={{0,4},{2,6},{4,0},{6,2},{8,12},{10,14},{12,8},{14,10},{16,20},{18,... | collective-permute-start | bytes 3538952 | tf_op jit(solution)/shard_map/ppermute | solution.py:30
  616.4 35.4 %collective-permute-start.16 = (bf16[2,144,2560]{2,1,0:T(8,128)(2,1)}, bf16[2,144,2560]{2,1,0:T(8,128)(2,1)}, u32[]{:S(2)}, u32[]{:S(2)}) collective-permute-start(bf16[2,144,2560]{2,1,0:T(8,128)(2,1)} %get-tuple-element.287), channel_id=1, source_target_pairs={{0,4},{2,6},{4,0},{6,2},{8,12},{10,14},{12,8},{14,10},{16,20},{18,... | collective-permute-start | bytes 4423688 | tf_op jit(solution)/shard_map/ppermute | solution.py:30
  651.8 32.9 %collective-permute-start.17 = (bf16[4,2,144,2560]{3,2,1,0:T(8,128)(2,1)}, bf16[4,2,144,2560]{3,2,1,0:T(8,128)(2,1)}, u32[]{:S(2)}, u32[]{:S(2)}) collective-permute-start(bf16[4,2,144,2560]{3,2,1,0:T(8,128)(2,1)} %shard_map.252), channel_id=1, source_target_pairs={{0,2},{2,0},{4,6},{6,4},{8,10},{10,8},{12,14},{14,12},{16,18},{18,... | collective-permute-start | bytes 17694728 | tf_op jit(solution)/shard_map/ppermute | solution.py:30
  652.1 32.7 %collective-permute-start.18 = (bf16[4,2,144,2048]{3,2,1,0:T(8,128)(2,1)}, bf16[4,2,144,2048]{3,2,1,0:T(8,128)(2,1)}, u32[]{:S(2)}, u32[]{:S(2)}) collective-permute-start(bf16[4,2,144,2048]{3,2,1,0:T(8,128)(2,1)} %shard_map.254), channel_id=1, source_target_pairs={{0,2},{2,0},{4,6},{6,4},{8,10},{10,8},{12,14},{14,12},{16,18},{18,... | collective-permute-start | bytes 14155784 | tf_op jit(solution)/shard_map/ppermute | solution.py:30
  652.4 107.2 %reduce-scatter.11.cloned.1.call-start = ((), (), s32[]{:S(2)}) async-start(), calls=%async_computation.13 | async-start | bytes 2949120 | tf_op jit(solution)/shard_map/reduce_scatter | solution.py:471
  652.5 41.0 %collective-permute-start.19 = (bf16[2,144,2560]{2,1,0:T(8,128)(2,1)S(1)}, bf16[2,144,2560]{2,1,0:T(8,128)(2,1)S(1)}, u32[]{:S(2)}, u32[]{:S(2)}) collective-permute-start(bf16[2,144,2560]{2,1,0:T(8,128)(2,1)S(1)} %copy-done.53), channel_id=1, source_target_pairs={{0,4},{2,6},{4,0},{6,2},{8,12},{10,14},{12,8},{14,10},{16,20},{18,... | collective-permute-start | bytes 4423688 | tf_op jit(solution)/shard_map/ppermute | solution.py:30
  693.6 124.3 %reduce-scatter.13.cloned.1.call-start = ((), (), s32[]{:S(2)}) async-start(), calls=%async_computation.14 | async-start | bytes 3686400 | tf_op jit(solution)/shard_map/reduce_scatter | solution.py:471
  693.6 63.5 %collective-permute-start.20 = (bf16[2,144,2560]{2,1,0:T(8,128)(2,1)}, bf16[2,144,2560]{2,1,0:T(8,128)(2,1)}, u32[]{:S(2)}, u32[]{:S(2)}) collective-permute-start(bf16[2,144,2560]{2,1,0:T(8,128)(2,1)} %get-tuple-element.314), channel_id=1, source_target_pairs={{0,4},{2,6},{4,0},{6,2},{8,12},{10,14},{12,8},{14,10},{16,20},{18,... | collective-permute-start | bytes 4423688 | tf_op jit(solution)/shard_map/ppermute | solution.py:30
  694.5 65.2 %collective-permute-start.21 = (bf16[2,144,2560]{2,1,0:T(8,128)(2,1)}, bf16[2,144,2560]{2,1,0:T(8,128)(2,1)}, u32[]{:S(2)}, u32[]{:S(2)}) collective-permute-start(bf16[2,144,2560]{2,1,0:T(8,128)(2,1)} %get-tuple-element.316), channel_id=1, source_target_pairs={{0,4},{2,6},{4,0},{6,2},{8,12},{10,14},{12,8},{14,10},{16,20},{18,... | collective-permute-start | bytes 4423688 | tf_op jit(solution)/shard_map/ppermute | solution.py:30
  695.7 61.4 %collective-permute-start.22 = (bf16[256,2304]{1,0:T(8,128)(2,1)}, bf16[256,2304]{1,0:T(8,128)(2,1)S(1)}, u32[]{:S(2)}, u32[]{:S(2)}) collective-permute-start(bf16[256,2304]{1,0:T(8,128)(2,1)} %get-tuple-element.317), channel_id=1, source_target_pairs={{0,1},{1,0},{2,3},{3,2},{4,5},{5,4},{6,7},{7,6},{8,9},{9,8},{10,11... | collective-permute-start | bytes 3538952 | tf_op jit(solution)/shard_map/ppermute | solution.py:26
  696.2 60.9 %collective-permute-start.23 = (bf16[256,2304]{1,0:T(8,128)(2,1)}, bf16[256,2304]{1,0:T(8,128)(2,1)}, u32[]{:S(2)}, u32[]{:S(2)}) collective-permute-start(bf16[256,2304]{1,0:T(8,128)(2,1)} %get-tuple-element.319), channel_id=1, source_target_pairs={{0,1},{1,0},{2,3},{3,2},{4,5},{5,4},{6,7},{7,6},{8,9},{9,8},{10,11... | collective-permute-start | bytes 3538952 | tf_op jit(solution)/shard_map/ppermute | solution.py:26
  759.7 134.6 %reduce-scatter.15.cloned.1.call-start = ((), (), s32[]{:S(2)}) async-start(), calls=%async_computation.15 | async-start | bytes 3686400 | tf_op jit(solution)/shard_map/reduce_scatter | solution.py:471
  789.5 34.3 %collective-permute-start.26 = (bf16[2,144,2048]{2,1,0:T(8,128)(2,1)}, bf16[2,144,2048]{2,1,0:T(8,128)(2,1)}, u32[]{:S(2)}, u32[]{:S(2)}) collective-permute-start(bf16[2,144,2048]{2,1,0:T(8,128)(2,1)} %get-tuple-element.334), channel_id=1, source_target_pairs={{0,4},{2,6},{4,0},{6,2},{8,12},{10,14},{12,8},{14,10},{16,20},{18,... | collective-permute-start | bytes 3538952 | tf_op jit(solution)/shard_map/ppermute | solution.py:30
  790.3 33.5 %collective-permute-start.27 = (bf16[256,2304]{1,0:T(8,128)(2,1)S(1)}, bf16[256,2304]{1,0:T(8,128)(2,1)S(1)}, u32[]{:S(2)}, u32[]{:S(2)}) collective-permute-start(bf16[256,2304]{1,0:T(8,128)(2,1)S(1)} %copy-done.15), channel_id=1, source_target_pairs={{0,1},{1,0},{2,3},{3,2},{4,5},{5,4},{6,7},{7,6},{8,9},{9,8},{10,11... | collective-permute-start | bytes 3538952 | tf_op jit(solution)/shard_map/ppermute | solution.py:26
  791.4 32.4 %collective-permute-start.28 = (bf16[144,1024]{1,0:T(8,128)(2,1)}, bf16[144,1024]{1,0:T(8,128)(2,1)}, u32[]{:S(2)}, u32[]{:S(2)}) collective-permute-start(bf16[144,1024]{1,0:T(8,128)(2,1)} %dynamic-slice_bitcast_fusion.6), channel_id=1, source_target_pairs={{0,4},{2,6},{4,0},{6,2},{8,12},{10,14},{12,8},{14,10},{16,20},{18,... | collective-permute-start | bytes 884744 | tf_op jit(solution)/shard_map/ppermute | solution.py:30
  823.9 131.5 %reduce-scatter.17.cloned.1.call-start = ((), (), s32[]{:S(2)}) async-start(), calls=%async_computation.16 | async-start | bytes 2949120 | tf_op jit(solution)/shard_map/reduce_scatter | solution.py:471
  824.0 35.0 %collective-permute-start.29 = (bf16[2,144,2560]{2,1,0:T(8,128)(2,1)}, bf16[2,144,2560]{2,1,0:T(8,128)(2,1)}, u32[]{:S(2)}, u32[]{:S(2)}) collective-permute-start(bf16[2,144,2560]{2,1,0:T(8,128)(2,1)} %get-tuple-element.349), channel_id=1, source_target_pairs={{0,4},{2,6},{4,0},{6,2},{8,12},{10,14},{12,8},{14,10},{16,20},{18,... | collective-permute-start | bytes 4423688 | tf_op jit(solution)/shard_map/ppermute | solution.py:30
  859.0 153.4 %reduce-scatter.19.cloned.1.call-start = ((), (), s32[]{:S(2)}) async-start(), calls=%async_computation.17 | async-start | bytes 3686400 | tf_op jit(solution)/shard_map/reduce_scatter | solution.py:471
  859.1 35.2 %collective-permute-start.32 = (bf16[2,144,2560]{2,1,0:T(8,128)(2,1)}, bf16[2,144,2560]{2,1,0:T(8,128)(2,1)S(1)}, u32[]{:S(2)}, u32[]{:S(2)}) collective-permute-start(bf16[2,144,2560]{2,1,0:T(8,128)(2,1)} %get-tuple-element.365), channel_id=1, source_target_pairs={{0,4},{2,6},{4,0},{6,2},{8,12},{10,14},{12,8},{14,10},{16,20},{18,... | collective-permute-start | bytes 4423688 | tf_op jit(solution)/shard_map/ppermute | solution.py:30
  924.8 133.5 %reduce-scatter.21.cloned.1.call-start = ((), (), s32[]{:S(2)}) async-start(), calls=%async_computation.18 | async-start | bytes 2949120 | tf_op jit(solution)/shard_map/reduce_scatter | solution.py:471
  984.9 132.7 %reduce-scatter.23.cloned.1.call-start = ((), (), s32[]{:S(2)}) async-start(), calls=%async_computation.19 | async-start | bytes 1474560 | tf_op jit(solution)/shard_map/reduce_scatter | solution.py:471
  1022.0 35.6 %collective-permute-start.43 = (bf16[144,1024]{1,0:T(8,128)(2,1)S(1)}, bf16[144,1024]{1,0:T(8,128)(2,1)S(1)}, u32[]{:S(2)}, u32[]{:S(2)}) collective-permute-start(bf16[144,1024]{1,0:T(8,128)(2,1)S(1)} %get-tuple-element.412), channel_id=1, source_target_pairs={{0,16},{2,18},{4,20},{6,22},{8,24},{10,26},{12,28},{14,30},{16,0},... | collective-permute-start | bytes 884744 | tf_op jit(solution)/shard_map/ppermute | solution.py:485
  1024.2 34.1 %collective-permute-start.44 = (bf16[144,1024]{1,0:T(8,128)(2,1)S(1)}, bf16[144,1024]{1,0:T(8,128)(2,1)}, u32[]{:S(2)}, u32[]{:S(2)}) collective-permute-start(bf16[144,1024]{1,0:T(8,128)(2,1)S(1)} %get-tuple-element.413), channel_id=1, source_target_pairs={{0,24},{2,26},{4,28},{6,30},{8,0},{10,2},{12,4},{14,6},{16,8},{18,... | collective-permute-start | bytes 884744 | tf_op jit(solution)/shard_map/ppermute | solution.py:485
  1077.8 34.6 %collective-permute-start.47 = (bf16[144,1024]{1,0:T(8,128)(2,1)}, bf16[144,1024]{1,0:T(8,128)(2,1)}, u32[]{:S(2)}, u32[]{:S(2)}) collective-permute-start(bf16[144,1024]{1,0:T(8,128)(2,1)} %get-tuple-element.422), channel_id=1, source_target_pairs={{0,16},{2,18},{4,20},{6,22},{8,24},{10,26},{12,28},{14,30},{16,0},... | collective-permute-start | bytes 884744 | tf_op jit(solution)/shard_map/ppermute | solution.py:485
  (87 other events, 1034.5 us)
Sparse Core Ops, SparseCore 0:
  18.1 180.0 all-gather.3
  199.8 110.0 all-gather.5
  311.5 110.0 all-gather.7
  652.5 28.2 reduce-scatter.8
  693.7 47.2 reduce-scatter.10
  759.8 56.5 reduce-scatter.12
  824.0 56.4 reduce-scatter.14
  882.8 47.9 reduce-scatter.16
  933.1 56.6 reduce-scatter.18
  992.0 65.6 reduce-scatter.20
  1060.1 45.7 reduce-scatter.22

commit v6 on v5

--- a/solution.py
+++ b/solution.py
@@ -692,10 +692,36 @@
     )
 
 
-def to_owners(partial):
+def joined(weights):
+    rows = weights[0].shape[0]
+    width = sum(weight.shape[1] for weight in weights)
+
+    def kernel(query_ref, key_ref, value_ref, output_ref, gate_ref, out_ref):
+        parts = [query_ref[...]]
+        for head in range(key_ref.shape[1] // HEAD_WIDTH):
+            here = slice(head * HEAD_WIDTH, (head + 1) * HEAD_WIDTH)
+            parts += [key_ref[:, here], value_ref[:, here]]
+        at = 0
+        for part in [*parts, output_ref[...], gate_ref[...]]:
+            out_ref[:, at : at + part.shape[1]] = part
+            at += part.shape[1]
+
+    return pl.pallas_call(
+        kernel,
+        out_shape=jax.ShapeDtypeStruct((rows, width), BF16),
+        in_specs=[pl.BlockSpec(memory_space=pltpu.VMEM)] * 5,
+        out_specs=pl.BlockSpec(memory_space=pltpu.VMEM),
+        compiler_params=pltpu.CompilerParams(vmem_limit_bytes=VMEM_BYTES),
+    )(*weights)
+
+
+def owner_parts(partial):
     count, width = partial.shape
     devices = lax.axis_size("dp") * lax.axis_size("tensor")
-    parts = partial.reshape(count, devices, width // devices).transpose(1, 0, 2)
+    return partial.reshape(count, devices, width // devices).transpose(1, 0, 2)
+
+
+def to_owners(parts):
     return lax.all_to_all(parts, ("dp", "tensor"), 0, 0, tiled=True)
 
 
@@ -728,12 +754,8 @@
         quarter = half // 2
         heads = query_cols // HEAD_WIDTH
         group = QUERY_HEADS // KEY_VALUE_HEADS
-        pairs = []
-        for head in range(key_cols // HEAD_WIDTH):
-            here = slice(head * HEAD_WIDTH, (head + 1) * HEAD_WIDTH)
-            pairs += [key_weight[:, here], value_weight[:, here]]
         full_first = lax.all_gather(
-            jnp.concatenate([query_weight, *pairs, w_output.T, w_gate], axis=1),
+            joined([query_weight, key_weight, value_weight, w_output.T, w_gate]),
             "dp",
             axis=0,
             tiled=True,
@@ -1018,10 +1040,11 @@
             None,
             scalars,
         )
+        gain_grads = jnp.stack([grad_a[0], grad_b[0], grad_c[0], grad_d])
+        gain_grads = line.mark(owner_parts(gain_grads))
         (pair_side,) = line.land(pair_side)
         line.mark(pair.own(line.next(pair_side)))
         query_parts = line.land(*query_parts, sums=[up_1])
-        gain_grads = jnp.stack([grad_a[0], grad_b[0], grad_c[0], grad_d])
         *pair_parts, gain_parts = line.send(*pair.to_owner(), (gain_grads, to_owners))
         output.along_rest(line)
         pair_parts = line.land(*pair_parts)

time: 1140 us -> 1130 us (level)
  local copies, waits for them, and re-layouts: 36.8 us -> 22.9 us
    unnamed x124 -> x102, local copies, waits for them, and re-layouts: 26.3 us -> 17.4 us
  transfers between devices with their start and end apart: 61 -> 61, of which waited for: 27 -> 27; matrix products, arithmetic and copies ran while one was open for 4% -> 4% of each run, Pallas kernels for 52% -> 53%
where the time goes in v6:
time: 1130 us; the launch traced here: 1120 us
  Pallas kernels  622 us (55%)
  waiting for transfers between devices  348 us (31%)
  starting transfers between devices  64.5 us (6%)
  other arithmetic  44.2 us (4%)
  local copies, waits for them, and re-layouts  22.9 us (2%)
  between operations  14.7 us (1%)
    pallas_call x57, Pallas kernels, call(): pl.pallas_call(kernel, grid_spec=pltpu.PrefetchScalarGridSpec(num_scalar_...  619 us
    ppermute x14, waiting for transfers between devices, swap(): return lax.ppermute(rows, 'tensor', [(0, 1), (1, 0)])  112 us
    all_gather x1, waiting for transfers between devices, body(): lax.all_gather(joined([query_weight, key_weight, value_weight, w_output.T...  100 us
    ppermute x29, waiting for transfers between devices, flip(): return lax.ppermute(array, 'dp', [(i, i ^ 1 << bit) for i in range(dp)])  51.7 us
    all_gather x1, waiting for transfers between devices, body(): full_down_t = lax.all_gather(w_down.T, 'dp', axis=0, tiled=True)  37.5 us
    ppermute x6, waiting for transfers between devices, to_owner(): lax.ppermute(array, 'dp', pairs)  32.7 us
    ppermute x29, starting transfers between devices, flip(): return lax.ppermute(array, 'dp', [(i, i ^ 1 << bit) for i in range(dp)])  25.1 us
  transfers between devices with their start and end apart: 61, of which 27 were waited for; matrix products, arithmetic and copies ran while one was open for 4% of the time, Pallas kernels for 53%

profile of v6, /device:TPU:0, one launch (start us, length us, event | category | flops | bytes accessed | tf_op | source)
XLA Modules:
  0.0 1117.0 jit_solution(5473490632508492919)
XLA Ops:
  41.8 43.0 %collective-permute-done.5.refs_0_.refs_1_ = bf16[512,2304]{1,0:T(8,128)(2,1)} collective-permute-done((bf16[512,2304]{1,0:T(8,128)(2,1)}, bf16[512,2304]{1,0:T(8,128)(2,1)}, u32[]{:S(2)}, u32[]{:S(2)}) %collective-permute-start.5) | collective-permute-done | bytes 2359328 | tf_op jit(solution)/shard_map/ppermute | solution.py:26
  90.6 100.0 %all-gather.4.cloned.1.call-done.refs_2_.refs_1_.gate_ref.refs_4_.refs_5_.refs_6_.refs_3_ = bf16[2304,7680]{1,0:T(8,128)(2,1)} async-done(((bf16[144,7680]{1,0:T(8,128)(2,1)}), bf16[2304,7680]{1,0:T(8,128)(2,1)}) %all-gather.4.cloned.1.call-update) | async-done | bytes 35389456 | tf_op jit(solution)/shard_map/all_gather | solution.py:757
  190.6 15.3 %shard_map.231.query_ref.key_ref.value_ref.pair_ref = bf16[1024,2048]{1,0:T(8,128)(2,1)} custom-call(s32[3]{0:T(128)} %pad_add_fusion._.scalar_ref, bf16[512,2304]{1,0:T(8,128)(2,1)} %fusion.2.refs_0_, bf16[512,2304]{1,0:T(8,128)(2,1)} %collective-permute-done.5.refs_0_.refs_1_, ...), custom_call_target="tpu_custom_call" | custom-call | flops 1 | bytes 1 | tf_op jit(solution)/shard_map/pallas_call | solution.py:68
  205.9 11.4 %shard_map.232.refs_0_.refs_2_.refs_3_ = bf16[1024,1024]{1,0:T(8,128)(2,1)} custom-call(s32[3]{0:T(128)} %pad_add_fusion._.scalar_ref, bf16[1024,2048]{1,0:T(8,128)(2,1)} %shard_map.231.query_ref.key_ref.value_ref.pair_ref, bf16[1024,2048]{1,0:T(8,128)(2,1)} %shard_map.231.query_ref.key_ref.value_ref.pair_ref, ...), custom_call_target="tpu_custom_call" | custom-call | flops 1 | bytes 1 | tf_op jit(solution)/shard_map/pallas_call | solution.py:68
  217.3 9.9 shard_map.233
  228.6 10.3 shard_map.234
  238.9 41.8 %collective-permute-done.6 = bf16[512,2304]{1,0:T(8,128)(2,1)S(1)} collective-permute-done((bf16[512,2304]{1,0:T(8,128)(2,1)}, bf16[512,2304]{1,0:T(8,128)(2,1)S(1)}, u32[]{:S(2)}, u32[]{:S(2)}) %collective-permute-start.6) | collective-permute-done | bytes 2359328 | tf_op jit(solution)/shard_map/ppermute | solution.py:26
  289.6 12.6 %all-gather.6.cloned.1.call-done.up_ref.refs_7_ = bf16[2304,4608]{1,0:T(8,128)(2,1)} async-done(((bf16[144,4608]{1,0:T(8,128)(2,1)}), bf16[2304,4608]{1,0:T(8,128)(2,1)}) %all-gather.6.cloned.1.call-update) | async-done | bytes 21233680 | tf_op jit(solution)/shard_map/all_gather | solution.py:763
  302.3 30.8 %shard_map.235 = (bf16[512,4608]{1,0:T(8,128)(2,1)}, bf16[512,4608]{1,0:T(8,128)(2,1)}, bf16[512,4608]{1,0:T(8,128)(2,1)}) custom-call(s32[3]{0:T(128)} %pad_add_fusion._.scalar_ref, bf16[512,2304]{1,0:T(8,128)(2,1)} %copy-done.6, bf16[2304,7680]{1,0:T(8,128)(2,1)} %all-gather.4.cloned.1.call-done.refs_2_.refs_1_.gate_ref.refs_4_.refs_5_.refs_6_.refs_3_, ...), custom_call_target="tpu_custom_call" | custom-call | flops 1 | bytes 1 | tf_op jit(solution)/shard_map/pallas_call | solution.py:68
  341.0 29.8 %shard_map.237 = (bf16[512,4608]{1,0:T(8,128)(2,1)}, bf16[512,4608]{1,0:T(8,128)(2,1)}, bf16[512,4608]{1,0:T(8,128)(2,1)}) custom-call(s32[3]{0:T(128)} %pad_add_fusion._.scalar_ref, bf16[512,2304]{1,0:T(8,128)(2,1)} %collective-permute-done.7.mid_ref.refs_0_, ...), custom_call_target="tpu_custom_call" | custom-call | flops 1 | bytes 1 | tf_op jit(solution)/shard_map/pallas_call | solution.py:68
  376.5 37.5 %all-gather.8.cloned.1.call-done.down_ref.refs_3_.refs_6_ = bf16[2304,4608]{1,0:T(8,128)(2,1)} async-done(((bf16[144,4608]{1,0:T(8,128)(2,1)}), bf16[2304,4608]{1,0:T(8,128)(2,1)}) %all-gather.8.cloned.1.call-update) | async-done | bytes 21233680 | tf_op jit(solution)/shard_map/all_gather | solution.py:764
  414.0 15.4 %shard_map.239 = bf16[256,2304]{1,0:T(8,128)(2,1)} custom-call(s32[3]{0:T(128)} %pad_add_fusion._.scalar_ref, bf16[512,4608]{1,0:T(8,128)(2,1)} %get-tuple-element.242.hidden_ref.refs_3_, bf16[2304,4608]{1,0:T(8,128)(2,1)} %all-gather.8.cloned.1.call-done.down_ref.refs_3_.refs_6_), custom_call_target="tpu_custom_call" | custom-call | flops 1 | bytes 1 | tf_op jit(solution)/shard_map/pallas_call | solution.py:68
  433.4 15.4 %shard_map.240 = bf16[256,2304]{1,0:T(8,128)(2,1)} custom-call(s32[3]{0:T(128)} %pad_add_fusion._.scalar_ref, bf16[512,4608]{1,0:T(8,128)(2,1)} %get-tuple-element.242.hidden_ref.refs_3_, bf16[2304,4608]{1,0:T(8,128)(2,1)} %all-gather.8.cloned.1.call-done.down_ref.refs_3_.refs_6_), custom_call_target="tpu_custom_call" | custom-call | flops 1 | bytes 1 | tf_op jit(solution)/shard_map/pallas_call | solution.py:68
  459.2 19.2 %shard_map.241 = f32[512,2304]{1,0:T(8,128)} custom-call(s32[3]{0:T(128)} %pad_add_fusion._.scalar_ref, bf16[512,4608]{1,0:T(8,128)(2,1)} %get-tuple-element.244.hidden_ref.refs_2_, bf16[2304,4608]{1,0:T(8,128)(2,1)} %all-gather.8.cloned.1.call-done.down_ref.refs_3_.refs_6_), custom_call_target="tpu_custom_call" | custom-call | flops 1 | bytes 1 | tf_op jit(solution)/shard_map/pallas_call | solution.py:68
  498.9 16.7 %shard_map.243 = (bf16[256,4608]{1,0:T(8,128)(2,1)}, bf16[256,4608]{1,0:T(8,128)(2,1)}) custom-call(s32[3]{0:T(128)} %pad_add_fusion._.scalar_ref, bf16[256,2304]{1,0:T(8,128)(2,1)} %copy-done.8, bf16[512,4608]{1,0:T(8,128)(2,1)} %get-tuple-element.253.refs_1_.refs_2_, bf16[512,4608]{1,0:T(8,128)(2,1)} %get-tuple-element.254.refs_2_.refs_4_, ...), custom_call_target="tpu_custom_call" | custom-call | flops 1 | bytes 1 | tf_op jit(solution)/shard_map/pallas_call | solution.py:68
  517.9 21.2 %shard_map.244 = (bf16[256,4608]{1,0:T(8,128)(2,1)}, bf16[256,4608]{1,0:T(8,128)(2,1)}, bf16[256,4608]{1,0:T(8,128)(2,1)}, bf16[256,4608]{1,0:T(8,128)(2,1)}) custom-call(s32[3]{0:T(128)} %pad_add_fusion._.scalar_ref, bf16[256,2304]{1,0:T(8,128)(2,1)} %copy-done.9, bf16[256,2304]{1,0:T(8,128)(2,1)} %collective-permute-done.10.refs_1_.refs_0_, ...), custom_call_target="tpu_custom_call" | custom-call | flops 1 | bytes 1 | tf_op jit(solution)/shard_map/pallas_call | solution.py:68
  554.4 11.2 %shard_map.247 = bf16[4,2,144,2560]{3,2,1,0:T(8,128)(2,1)} custom-call(s32[3]{0:T(128)} %pad_add_fusion._.scalar_ref, bf16[4,2,2,144,512]{4,3,2,1,0:T(8,128)(2,1)} %bitcast.97, bf16[4,2,2,144,512]{4,3,2,1,0:T(8,128)(2,1)} %bitcast.105, bf16[512,4608]{1,0:T(8,128)(2,1)} %get-tuple-element.244.hidden_ref.refs_2_, ...), custom_call_target="tpu_custom_call" | custom-call | flops 1 | bytes 1 | tf_op jit(solution)/shard_map/pallas_call | solution.py:68
  580.3 17.0 %shard_map.250 = (bf16[256,4608]{1,0:T(8,128)(2,1)}, bf16[256,4608]{1,0:T(8,128)(2,1)}) custom-call(s32[3]{0:T(128)} %pad_add_fusion._.scalar_ref, bf16[256,2304]{1,0:T(8,128)(2,1)} %copy-done.18, bf16[512,4608]{1,0:T(8,128)(2,1)} %get-tuple-element.259.refs_3_.refs_1_, bf16[512,4608]{1,0:T(8,128)(2,1)} %get-tuple-element.260.refs_5_.refs_2_, ...), custom_call_target="tpu_custom_call" | custom-call | flops 1 | bytes 1 | tf_op jit(solution)/shard_map/pallas_call | solution.py:68
  614.8 11.2 %shard_map.253 = bf16[4,2,144,2560]{3,2,1,0:T(8,128)(2,1)} custom-call(s32[3]{0:T(128)} %pad_add_fusion._.scalar_ref, bf16[4,2,2,144,512]{4,3,2,1,0:T(8,128)(2,1)} %bitcast.72, bf16[4,2,2,144,512]{4,3,2,1,0:T(8,128)(2,1)} %bitcast.84, bf16[256,4608]{1,0:T(8,128)(2,1)} %get-tuple-element.312.refs_2_.refs_0_, ...), custom_call_target="tpu_custom_call" | custom-call | flops 1 | bytes 1 | tf_op jit(solution)/shard_map/pallas_call | solution.py:68
  646.0 31.0 %shard_map.256 = (bf16[256,2304]{1,0:T(8,128)(2,1)}, bf16[256,2304]{1,0:T(8,128)(2,1)}) custom-call(s32[3]{0:T(128)} %pad_add_fusion._.scalar_ref, bf16[256,4608]{1,0:T(8,128)(2,1)} %get-tuple-element.291.refs_4_.refs_0_, bf16[256,4608]{1,0:T(8,128)(2,1)} %get-tuple-element.286.refs_5_.refs_1_, bf16[256,4608]{1,0:T(8,128)(2,1)} %get-tuple-element.344.refs_2_.refs_4_, ...), custom_call_target="tpu_custom_call" | custom-call | flops 1 | bytes 1 | tf_op jit(solution)/shard_map/pallas_call | solution.py:68
  690.0 9.8 shard_map.258
  707.3 11.2 %shard_map.260 = bf16[4,2,144,2560]{3,2,1,0:T(8,128)(2,1)} custom-call(s32[3]{0:T(128)} %pad_add_fusion._.scalar_ref, bf16[4,2,2,144,512]{4,3,2,1,0:T(8,128)(2,1)} %bitcast.76, bf16[4,2,2,144,512]{4,3,2,1,0:T(8,128)(2,1)} %bitcast.88, bf16[256,4608]{1,0:T(8,128)(2,1)} %get-tuple-element.342.refs_2_, bf16[256,4608]{1,0:T(8,128)(2,1)} %get-tuple-element.343.refs_3_, ...), custom_call_target="tpu_custom_call" | custom-call | flops 1 | bytes 1 | tf_op jit(solution)/shard_map/pallas_call | solution.py:68
  718.5 30.9 %shard_map.261 = (f32[256,2304]{1,0:T(8,128)}, f32[256,2304]{1,0:T(8,128)}) custom-call(s32[3]{0:T(128)} %pad_add_fusion._.scalar_ref, bf16[256,4608]{1,0:T(8,128)(2,1)} %get-tuple-element.312.refs_2_.refs_0_, bf16[256,4608]{1,0:T(8,128)(2,1)} %get-tuple-element.284.refs_3_.refs_1_, bf16[256,4608]{1,0:T(8,128)(2,1)} %get-tuple-element.342.refs_2_, ...), custom_call_target="tpu_custom_call" | custom-call | flops 1 | bytes 1 | tf_op jit(solution)/shard_map/pallas_call | solution.py:68
  752.8 14.2 %shard_map.262 = (f32[512,2304]{1,0:T(8,128)}, bf16[256,2304]{1,0:T(8,128)(2,1)}, bf16[256,2304]{1,0:T(8,128)(2,1)}, f32[1,2304]{1,0:T(1,128)}, f32[1,2304]{1,0:T(1,128)}) custom-call(s32[3]{0:T(128)} %pad_add_fusion._.scalar_ref, f32[256,2304]{1,0:T(8,128)} %get-tuple-element.322.refs_0_, bf16[256,2304]{1,0:T(8,128)(2,1)} %copy-done.29, ...), custom_call_target="tpu_custom_call" | custom-call | flops 1 | bytes 1 | tf_op jit(solution)/shard_map/pallas_call | solution.py:68
  852.1 10.4 shard_map.269.d_ref
  868.3 18.2 %shard_map.271 = (bf16[1024,1024]{1,0:T(8,128)(2,1)}, bf16[1024,1024]{1,0:T(8,128)(2,1)}) custom-call(s32[3]{0:T(128)} %pad_add_fusion._.scalar_ref, bf16[1024,2048]{1,0:T(8,128)(2,1)} %shard_map.231.query_ref.key_ref.value_ref.pair_ref, bf16[1024,2048]{1,0:T(8,128)(2,1)} %shard_map.231.query_ref.key_ref.value_ref.pair_ref, bf16[1024,1024]{1,0:T(8,128)(2,1)} %shard_map.269.d_ref), custom_call_target="tpu_custom_call" | custom-call | flops 1 | bytes 1 | tf_op jit(solution)/shard_map/pallas_call | solution.py:68
  919.0 12.2 %shard_map.276 = (bf16[256,2304]{1,0:T(8,128)(2,1)}, bf16[256,2304]{1,0:T(8,128)(2,1)}) custom-call(s32[3]{0:T(128)} %pad_add_fusion._.scalar_ref, bf16[1024,1024]{1,0:T(8,128)(2,1)} %get-tuple-element.394.refs_2_.refs_3_.refs_0_, bf16[1024,1024]{1,0:T(8,128)(2,1)} %get-tuple-element.375.refs_2_.refs_3_.refs_1_, ...), custom_call_target="tpu_custom_call" | custom-call | flops 1 | bytes 1 | tf_op jit(solution)/shard_map/pallas_call | solution.py:68
  958.3 12.5 %shard_map.281 = (f32[256,2304]{1,0:T(8,128)}, f32[256,2304]{1,0:T(8,128)}) custom-call(s32[3]{0:T(128)} %pad_add_fusion._.scalar_ref, bf16[1024,1024]{1,0:T(8,128)(2,1)} %get-tuple-element.394.refs_2_.refs_3_.refs_0_, bf16[1024,1024]{1,0:T(8,128)(2,1)} %get-tuple-element.375.refs_2_.refs_3_.refs_1_, ...), custom_call_target="tpu_custom_call" | custom-call | flops 1 | bytes 1 | tf_op jit(solution)/shard_map/pallas_call | solution.py:68
  984.6 19.8 %collective-permute-done.40.refs_5_ = bf16[4,144,1024]{2,1,0:T(8,128)(2,1)S(1)} collective-permute-done((bf16[4,144,1024]{2,1,0:T(8,128)(2,1)S(1)}, bf16[4,144,1024]{2,1,0:T(8,128)(2,1)S(1)}, u32[]{:S(2)}, u32[]{:S(2)}) %collective-permute-start.40) | collective-permute-done | bytes 1179680 | tf_op jit(solution)/shard_map/ppermute | solution.py:30
  1023.6 11.0 shard_map.284
  1053.1 10.0 all-to-all-start
  1083.1 20.1 %collective-permute-done.47 = bf16[144,1024]{1,0:T(8,128)(2,1)} collective-permute-done((bf16[144,1024]{1,0:T(8,128)(2,1)S(1)}, bf16[144,1024]{1,0:T(8,128)(2,1)}, u32[]{:S(2)}, u32[]{:S(2)}) %collective-permute-start.47) | collective-permute-done | bytes 294944 | tf_op jit(solution)/shard_map/ppermute | solution.py:485
  (314 shorter events, 421.4 us)
Async XLA Ops:
  7.2 183.4 %all-gather.4.cloned.1.call-start = ((), (), s32[]{:S(2)}) async-start(), calls=%async_computation.9 | async-start | bytes 37601280 | tf_op jit(solution)/shard_map/all_gather | solution.py:757
  10.4 291.9 %all-gather.6.cloned.1.call-start = ((), (), s32[]{:S(2)}) async-start(), calls=%async_computation.10 | async-start | bytes 22560768 | tf_op jit(solution)/shard_map/all_gather | solution.py:763
  11.2 402.8 %all-gather.8.cloned.1.call-start = ((), (), s32[]{:S(2)}) async-start(), calls=%async_computation.11 | async-start | bytes 22560768 | tf_op jit(solution)/shard_map/all_gather | solution.py:764
  11.9 673.9 %reduce-scatter.9.cloned.1.call-start = ((), (), s32[]{:S(2)}) async-start(), calls=%async_computation.12 | async-start | bytes 1474560 | tf_op jit(solution)/shard_map/reduce_scatter | solution.py:471
  33.5 51.3 %collective-permute-start.5 = (bf16[512,2304]{1,0:T(8,128)(2,1)}, bf16[512,2304]{1,0:T(8,128)(2,1)}, u32[]{:S(2)}, u32[]{:S(2)}) collective-permute-start(bf16[512,2304]{1,0:T(8,128)(2,1)} %fusion.2.refs_0_), channel_id=1, source_target_pairs={{0,1},{1,0},{2,3},{3,2},{4,5},{5,4},{6,7},{7,6},{8,9},{9,8},{10,11... | collective-permute-start | bytes 7077896 | tf_op jit(solution)/shard_map/ppermute | solution.py:26
  227.2 53.6 %collective-permute-start.6 = (bf16[512,2304]{1,0:T(8,128)(2,1)}, bf16[512,2304]{1,0:T(8,128)(2,1)S(1)}, u32[]{:S(2)}, u32[]{:S(2)}) collective-permute-start(bf16[512,2304]{1,0:T(8,128)(2,1)} %shard_map.233), channel_id=1, source_target_pairs={{0,1},{1,0},{2,3},{3,2},{4,5},{5,4},{6,7},{7,6},{8,9},{9,8},{10,11... | collective-permute-start | bytes 7077896 | tf_op jit(solution)/shard_map/ppermute | solution.py:26
  288.2 52.8 %collective-permute-start.7 = (bf16[512,2304]{1,0:T(8,128)(2,1)S(1)}, bf16[512,2304]{1,0:T(8,128)(2,1)}, u32[]{:S(2)}, u32[]{:S(2)}) collective-permute-start(bf16[512,2304]{1,0:T(8,128)(2,1)S(1)} %multiply_convert_fusion.mid_ref.refs_0_), channel_id=1, source_target_pairs={{0,1},{1,0},{2,3},{3,2},{4,5},{5,4},{6,7},{7,6},{8,9},{9,8},{10,11... | collective-permute-start | bytes 7077896 | tf_op jit(solution)/shard_map/ppermute | solution.py:26
  491.7 49.5 %collective-permute-start.11 = (bf16[256,2304]{1,0:T(8,128)(2,1)S(1)}, bf16[256,2304]{1,0:T(8,128)(2,1)S(1)}, u32[]{:S(2)}, u32[]{:S(2)}) collective-permute-start(bf16[256,2304]{1,0:T(8,128)(2,1)S(1)} %get-tuple-element.453.refs_1_.refs_0_), channel_id=1, source_target_pairs={{0,1},{1,0},{2,3},{3,2},{4,5},{5,4},{6,7},{7,6},{8,9},{9,8},{10,11... | collective-permute-start | bytes 3538952 | tf_op jit(solution)/shard_map/ppermute | solution.py:26
  572.5 36.1 %collective-permute-start.13 = (bf16[4,144,1024]{2,1,0:T(8,128)(2,1)}, bf16[4,144,1024]{2,1,0:T(8,128)(2,1)}, u32[]{:S(2)}, u32[]{:S(2)}) collective-permute-start(bf16[4,144,1024]{2,1,0:T(8,128)(2,1)} %shard_map.248), channel_id=1, source_target_pairs={{0,4},{2,6},{4,0},{6,2},{8,12},{10,14},{12,8},{14,10},{16,20},{18,... | collective-permute-start | bytes 3538952 | tf_op jit(solution)/shard_map/ppermute | solution.py:30
  608.7 35.3 %collective-permute-start.16 = (bf16[2,144,2560]{2,1,0:T(8,128)(2,1)}, bf16[2,144,2560]{2,1,0:T(8,128)(2,1)}, u32[]{:S(2)}, u32[]{:S(2)}) collective-permute-start(bf16[2,144,2560]{2,1,0:T(8,128)(2,1)} %get-tuple-element.287), channel_id=1, source_target_pairs={{0,4},{2,6},{4,0},{6,2},{8,12},{10,14},{12,8},{14,10},{16,20},{18,... | collective-permute-start | bytes 4423688 | tf_op jit(solution)/shard_map/ppermute | solution.py:30
  644.0 33.0 %collective-permute-start.17 = (bf16[4,2,144,2560]{3,2,1,0:T(8,128)(2,1)}, bf16[4,2,144,2560]{3,2,1,0:T(8,128)(2,1)}, u32[]{:S(2)}, u32[]{:S(2)}) collective-permute-start(bf16[4,2,144,2560]{3,2,1,0:T(8,128)(2,1)} %shard_map.253), channel_id=1, source_target_pairs={{0,2},{2,0},{4,6},{6,4},{8,10},{10,8},{12,14},{14,12},{16,18},{18,... | collective-permute-start | bytes 17694728 | tf_op jit(solution)/shard_map/ppermute | solution.py:30
  644.2 32.8 %collective-permute-start.18 = (bf16[4,2,144,2048]{3,2,1,0:T(8,128)(2,1)}, bf16[4,2,144,2048]{3,2,1,0:T(8,128)(2,1)}, u32[]{:S(2)}, u32[]{:S(2)}) collective-permute-start(bf16[4,2,144,2048]{3,2,1,0:T(8,128)(2,1)} %shard_map.255), channel_id=1, source_target_pairs={{0,2},{2,0},{4,6},{6,4},{8,10},{10,8},{12,14},{14,12},{16,18},{18,... | collective-permute-start | bytes 14155784 | tf_op jit(solution)/shard_map/ppermute | solution.py:30
  644.6 107.3 %reduce-scatter.11.cloned.1.call-start = ((), (), s32[]{:S(2)}) async-start(), calls=%async_computation.13 | async-start | bytes 2949120 | tf_op jit(solution)/shard_map/reduce_scatter | solution.py:471
  644.6 41.1 %collective-permute-start.19 = (bf16[2,144,2560]{2,1,0:T(8,128)(2,1)S(1)}, bf16[2,144,2560]{2,1,0:T(8,128)(2,1)S(1)}, u32[]{:S(2)}, u32[]{:S(2)}) collective-permute-start(bf16[2,144,2560]{2,1,0:T(8,128)(2,1)S(1)} %copy-done.46), channel_id=1, source_target_pairs={{0,4},{2,6},{4,0},{6,2},{8,12},{10,14},{12,8},{14,10},{16,20},{18,... | collective-permute-start | bytes 4423688 | tf_op jit(solution)/shard_map/ppermute | solution.py:30
  685.8 124.1 %reduce-scatter.13.cloned.1.call-start = ((), (), s32[]{:S(2)}) async-start(), calls=%async_computation.14 | async-start | bytes 3686400 | tf_op jit(solution)/shard_map/reduce_scatter | solution.py:471
  685.9 63.5 %collective-permute-start.20 = (bf16[2,144,2560]{2,1,0:T(8,128)(2,1)}, bf16[2,144,2560]{2,1,0:T(8,128)(2,1)}, u32[]{:S(2)}, u32[]{:S(2)}) collective-permute-start(bf16[2,144,2560]{2,1,0:T(8,128)(2,1)} %get-tuple-element.314), channel_id=1, source_target_pairs={{0,4},{2,6},{4,0},{6,2},{8,12},{10,14},{12,8},{14,10},{16,20},{18,... | collective-permute-start | bytes 4423688 | tf_op jit(solution)/shard_map/ppermute | solution.py:30
  686.7 65.3 %collective-permute-start.21 = (bf16[2,144,2560]{2,1,0:T(8,128)(2,1)}, bf16[2,144,2560]{2,1,0:T(8,128)(2,1)}, u32[]{:S(2)}, u32[]{:S(2)}) collective-permute-start(bf16[2,144,2560]{2,1,0:T(8,128)(2,1)} %get-tuple-element.316), channel_id=1, source_target_pairs={{0,4},{2,6},{4,0},{6,2},{8,12},{10,14},{12,8},{14,10},{16,20},{18,... | collective-permute-start | bytes 4423688 | tf_op jit(solution)/shard_map/ppermute | solution.py:30
  688.0 61.4 %collective-permute-start.22 = (bf16[256,2304]{1,0:T(8,128)(2,1)}, bf16[256,2304]{1,0:T(8,128)(2,1)S(1)}, u32[]{:S(2)}, u32[]{:S(2)}) collective-permute-start(bf16[256,2304]{1,0:T(8,128)(2,1)} %get-tuple-element.317), channel_id=1, source_target_pairs={{0,1},{1,0},{2,3},{3,2},{4,5},{5,4},{6,7},{7,6},{8,9},{9,8},{10,11... | collective-permute-start | bytes 3538952 | tf_op jit(solution)/shard_map/ppermute | solution.py:26
  688.4 61.0 %collective-permute-start.23 = (bf16[256,2304]{1,0:T(8,128)(2,1)}, bf16[256,2304]{1,0:T(8,128)(2,1)}, u32[]{:S(2)}, u32[]{:S(2)}) collective-permute-start(bf16[256,2304]{1,0:T(8,128)(2,1)} %get-tuple-element.319), channel_id=1, source_target_pairs={{0,1},{1,0},{2,3},{3,2},{4,5},{5,4},{6,7},{7,6},{8,9},{9,8},{10,11... | collective-permute-start | bytes 3538952 | tf_op jit(solution)/shard_map/ppermute | solution.py:26
  752.0 134.5 %reduce-scatter.15.cloned.1.call-start = ((), (), s32[]{:S(2)}) async-start(), calls=%async_computation.15 | async-start | bytes 3686400 | tf_op jit(solution)/shard_map/reduce_scatter | solution.py:471
  781.7 34.3 %collective-permute-start.26 = (bf16[2,144,2048]{2,1,0:T(8,128)(2,1)}, bf16[2,144,2048]{2,1,0:T(8,128)(2,1)}, u32[]{:S(2)}, u32[]{:S(2)}) collective-permute-start(bf16[2,144,2048]{2,1,0:T(8,128)(2,1)} %get-tuple-element.334), channel_id=1, source_target_pairs={{0,4},{2,6},{4,0},{6,2},{8,12},{10,14},{12,8},{14,10},{16,20},{18,... | collective-permute-start | bytes 3538952 | tf_op jit(solution)/shard_map/ppermute | solution.py:30
  782.4 33.6 %collective-permute-start.27 = (bf16[256,2304]{1,0:T(8,128)(2,1)S(1)}, bf16[256,2304]{1,0:T(8,128)(2,1)S(1)}, u32[]{:S(2)}, u32[]{:S(2)}) collective-permute-start(bf16[256,2304]{1,0:T(8,128)(2,1)S(1)} %copy-done.15), channel_id=1, source_target_pairs={{0,1},{1,0},{2,3},{3,2},{4,5},{5,4},{6,7},{7,6},{8,9},{9,8},{10,11... | collective-permute-start | bytes 3538952 | tf_op jit(solution)/shard_map/ppermute | solution.py:26
  783.6 32.5 %collective-permute-start.28 = (bf16[144,1024]{1,0:T(8,128)(2,1)}, bf16[144,1024]{1,0:T(8,128)(2,1)}, u32[]{:S(2)}, u32[]{:S(2)}) collective-permute-start(bf16[144,1024]{1,0:T(8,128)(2,1)} %dynamic-slice_bitcast_fusion.6), channel_id=1, source_target_pairs={{0,4},{2,6},{4,0},{6,2},{8,12},{10,14},{12,8},{14,10},{16,20},{18,... | collective-permute-start | bytes 884744 | tf_op jit(solution)/shard_map/ppermute | solution.py:30
  816.1 131.6 %reduce-scatter.17.cloned.1.call-start = ((), (), s32[]{:S(2)}) async-start(), calls=%async_computation.16 | async-start | bytes 2949120 | tf_op jit(solution)/shard_map/reduce_scatter | solution.py:471
  816.2 35.0 %collective-permute-start.29 = (bf16[2,144,2560]{2,1,0:T(8,128)(2,1)}, bf16[2,144,2560]{2,1,0:T(8,128)(2,1)}, u32[]{:S(2)}, u32[]{:S(2)}) collective-permute-start(bf16[2,144,2560]{2,1,0:T(8,128)(2,1)} %get-tuple-element.349), channel_id=1, source_target_pairs={{0,4},{2,6},{4,0},{6,2},{8,12},{10,14},{12,8},{14,10},{16,20},{18,... | collective-permute-start | bytes 4423688 | tf_op jit(solution)/shard_map/ppermute | solution.py:30
  851.3 154.4 %reduce-scatter.19.cloned.1.call-start = ((), (), s32[]{:S(2)}) async-start(), calls=%async_computation.17 | async-start | bytes 3686400 | tf_op jit(solution)/shard_map/reduce_scatter | solution.py:471
  851.3 35.1 %collective-permute-start.32 = (bf16[2,144,2560]{2,1,0:T(8,128)(2,1)}, bf16[2,144,2560]{2,1,0:T(8,128)(2,1)S(1)}, u32[]{:S(2)}, u32[]{:S(2)}) collective-permute-start(bf16[2,144,2560]{2,1,0:T(8,128)(2,1)} %get-tuple-element.365), channel_id=1, source_target_pairs={{0,4},{2,6},{4,0},{6,2},{8,12},{10,14},{12,8},{14,10},{16,20},{18,... | collective-permute-start | bytes 4423688 | tf_op jit(solution)/shard_map/ppermute | solution.py:30
  917.0 133.1 %reduce-scatter.21.cloned.1.call-start = ((), (), s32[]{:S(2)}) async-start(), calls=%async_computation.18 | async-start | bytes 2949120 | tf_op jit(solution)/shard_map/reduce_scatter | solution.py:471
  977.2 131.2 %reduce-scatter.23.cloned.1.call-start = ((), (), s32[]{:S(2)}) async-start(), calls=%async_computation.19 | async-start | bytes 1474560 | tf_op jit(solution)/shard_map/reduce_scatter | solution.py:471
  1017.9 32.3 %collective-permute-start.43 = (bf16[144,1024]{1,0:T(8,128)(2,1)}, bf16[144,1024]{1,0:T(8,128)(2,1)}, u32[]{:S(2)}, u32[]{:S(2)}) collective-permute-start(bf16[144,1024]{1,0:T(8,128)(2,1)} %get-tuple-element.412), channel_id=1, source_target_pairs={{0,16},{2,18},{4,20},{6,22},{8,24},{10,26},{12,28},{14,30},{16,0},... | collective-permute-start | bytes 884744 | tf_op jit(solution)/shard_map/ppermute | solution.py:485
  1064.9 38.3 %collective-permute-start.47 = (bf16[144,1024]{1,0:T(8,128)(2,1)S(1)}, bf16[144,1024]{1,0:T(8,128)(2,1)}, u32[]{:S(2)}, u32[]{:S(2)}) collective-permute-start(bf16[144,1024]{1,0:T(8,128)(2,1)S(1)} %get-tuple-element.425), channel_id=1, source_target_pairs={{0,16},{2,18},{4,20},{6,22},{8,24},{10,26},{12,28},{14,30},{16,0},... | collective-permute-start | bytes 884744 | tf_op jit(solution)/shard_map/ppermute | solution.py:485
  1067.3 35.8 %collective-permute-start.48 = (bf16[144,1024]{1,0:T(8,128)(2,1)S(1)}, bf16[144,1024]{1,0:T(8,128)(2,1)}, u32[]{:S(2)}, u32[]{:S(2)}) collective-permute-start(bf16[144,1024]{1,0:T(8,128)(2,1)S(1)} %get-tuple-element.426), channel_id=1, source_target_pairs={{0,24},{2,26},{4,28},{6,30},{8,0},{10,2},{12,4},{14,6},{16,8},{18,... | collective-permute-start | bytes 884744 | tf_op jit(solution)/shard_map/ppermute | solution.py:485
  (79 other events, 1011.8 us)
Sparse Core Ops, SparseCore 0:
  10.5 180.0 all-gather.3
  192.2 110.0 all-gather.5
  303.9 110.0 all-gather.7
  644.7 28.2 reduce-scatter.8
  685.9 47.3 reduce-scatter.10
  752.1 56.6 reduce-scatter.12
  816.2 56.4 reduce-scatter.14
  875.0 47.9 reduce-scatter.16
  925.3 56.6 reduce-scatter.18
  984.3 60.1 reduce-scatter.20
  1050.3 52.8 reduce-scatter.22

commit v7 on v6

--- a/solution.py
+++ b/solution.py
@@ -1044,10 +1044,11 @@
         gain_grads = line.mark(owner_parts(gain_grads))
         (pair_side,) = line.land(pair_side)
         line.mark(pair.own(line.next(pair_side)))
+        output.along_rest(line)
         query_parts = line.land(*query_parts, sums=[up_1])
-        *pair_parts, gain_parts = line.send(*pair.to_owner(), (gain_grads, to_owners))
-        output.along_rest(line)
+        pair_parts = line.send(*pair.to_owner())
         pair_parts = line.land(*pair_parts)
+        (gain_parts,) = line.send((gain_grads, to_owners))
         (gain_parts,) = line.land(gain_parts)
         small = jnp.sum(gain_parts, axis=0)
         query.gather(query_parts)

time: 1130 us -> 1140 us (level)
  starting transfers between devices: 64.5 us -> 87.4 us
  waiting for transfers between devices: 348 us -> 336 us
    ppermute x6, starting transfers between devices: 11.1 us -> 33.7 us  [to_owner(): lax.ppermute(array, 'dp', pairs)]
    ppermute x6, waiting for transfers between devices: 32.7 us -> 17.7 us  [to_owner(): lax.ppermute(array, 'dp', pairs)]
  transfers between devices with their start and end apart: 61 -> 61, of which waited for: 27 -> 28; matrix products, arithmetic and copies ran while one was open for 4% -> 4% of each run, Pallas kernels for 53% -> 52%
where the time goes in v7:
time: 1140 us; the launch traced here: 1130 us
  Pallas kernels  622 us (55%)
  waiting for transfers between devices  336 us (29%)
  starting transfers between devices  87.4 us (8%)
  other arithmetic  42.9 us (4%)
  local copies, waits for them, and re-layouts  24.8 us (2%)
  between operations  14.7 us (1%)
    pallas_call x57, Pallas kernels, call(): pl.pallas_call(kernel, grid_spec=pltpu.PrefetchScalarGridSpec(num_scalar_...  619 us
    ppermute x14, waiting for transfers between devices, swap(): return lax.ppermute(rows, 'tensor', [(0, 1), (1, 0)])  112 us
    all_gather x1, waiting for transfers between devices, body(): lax.all_gather(joined([query_weight, key_weight, value_weight, w_output.T...  100 us
    ppermute x29, waiting for transfers between devices, flip(): return lax.ppermute(array, 'dp', [(i, i ^ 1 << bit) for i in range(dp)])  50.3 us
    all_gather x1, waiting for transfers between devices, body(): full_down_t = lax.all_gather(w_down.T, 'dp', axis=0, tiled=True)  37.5 us
    ppermute x6, starting transfers between devices, to_owner(): lax.ppermute(array, 'dp', pairs)  33.7 us
    ppermute x29, starting transfers between devices, flip(): return lax.ppermute(array, 'dp', [(i, i ^ 1 << bit) for i in range(dp)])  25.4 us
  transfers between devices with their start and end apart: 61, of which 28 were waited for; matrix products, arithmetic and copies ran while one was open for 4% of the time, Pallas kernels for 52%

profile of v7, /device:TPU:0, one launch (start us, length us, event | category | flops | bytes accessed | tf_op | source)
XLA Modules:
  0.0 1128.4 jit_solution(13497527618429479893)
XLA Ops:
  41.8 43.0 %collective-permute-done.5.refs_0_.refs_1_ = bf16[512,2304]{1,0:T(8,128)(2,1)} collective-permute-done((bf16[512,2304]{1,0:T(8,128)(2,1)}, bf16[512,2304]{1,0:T(8,128)(2,1)}, u32[]{:S(2)}, u32[]{:S(2)}) %collective-permute-start.5) | collective-permute-done | bytes 2359328 | tf_op jit(solution)/shard_map/ppermute | solution.py:26
  90.6 100.0 %all-gather.4.cloned.1.call-done.refs_2_.refs_1_.gate_ref.refs_4_.refs_5_.refs_6_.refs_3_ = bf16[2304,7680]{1,0:T(8,128)(2,1)} async-done(((bf16[144,7680]{1,0:T(8,128)(2,1)}), bf16[2304,7680]{1,0:T(8,128)(2,1)}) %all-gather.4.cloned.1.call-update) | async-done | bytes 35389456 | tf_op jit(solution)/shard_map/all_gather | solution.py:757
  190.6 15.3 %shard_map.231.query_ref.key_ref.value_ref.pair_ref = bf16[1024,2048]{1,0:T(8,128)(2,1)} custom-call(s32[3]{0:T(128)} %pad_add_fusion._.scalar_ref, bf16[512,2304]{1,0:T(8,128)(2,1)} %fusion.2.refs_0_, bf16[512,2304]{1,0:T(8,128)(2,1)} %collective-permute-done.5.refs_0_.refs_1_, ...), custom_call_target="tpu_custom_call" | custom-call | flops 1 | bytes 1 | tf_op jit(solution)/shard_map/pallas_call | solution.py:68
  205.9 11.4 %shard_map.232.refs_0_.refs_2_.refs_3_ = bf16[1024,1024]{1,0:T(8,128)(2,1)} custom-call(s32[3]{0:T(128)} %pad_add_fusion._.scalar_ref, bf16[1024,2048]{1,0:T(8,128)(2,1)} %shard_map.231.query_ref.key_ref.value_ref.pair_ref, bf16[1024,2048]{1,0:T(8,128)(2,1)} %shard_map.231.query_ref.key_ref.value_ref.pair_ref, ...), custom_call_target="tpu_custom_call" | custom-call | flops 1 | bytes 1 | tf_op jit(solution)/shard_map/pallas_call | solution.py:68
  217.3 9.9 shard_map.233
  228.6 10.3 shard_map.234
  238.9 41.8 %collective-permute-done.6 = bf16[512,2304]{1,0:T(8,128)(2,1)S(1)} collective-permute-done((bf16[512,2304]{1,0:T(8,128)(2,1)}, bf16[512,2304]{1,0:T(8,128)(2,1)S(1)}, u32[]{:S(2)}, u32[]{:S(2)}) %collective-permute-start.6) | collective-permute-done | bytes 2359328 | tf_op jit(solution)/shard_map/ppermute | solution.py:26
  289.6 12.6 %all-gather.6.cloned.1.call-done.up_ref.refs_7_ = bf16[2304,4608]{1,0:T(8,128)(2,1)} async-done(((bf16[144,4608]{1,0:T(8,128)(2,1)}), bf16[2304,4608]{1,0:T(8,128)(2,1)}) %all-gather.6.cloned.1.call-update) | async-done | bytes 21233680 | tf_op jit(solution)/shard_map/all_gather | solution.py:763
  302.3 30.8 %shard_map.235 = (bf16[512,4608]{1,0:T(8,128)(2,1)}, bf16[512,4608]{1,0:T(8,128)(2,1)}, bf16[512,4608]{1,0:T(8,128)(2,1)}) custom-call(s32[3]{0:T(128)} %pad_add_fusion._.scalar_ref, bf16[512,2304]{1,0:T(8,128)(2,1)} %copy-done.6, bf16[2304,7680]{1,0:T(8,128)(2,1)} %all-gather.4.cloned.1.call-done.refs_2_.refs_1_.gate_ref.refs_4_.refs_5_.refs_6_.refs_3_, ...), custom_call_target="tpu_custom_call" | custom-call | flops 1 | bytes 1 | tf_op jit(solution)/shard_map/pallas_call | solution.py:68
  341.0 29.8 %shard_map.237 = (bf16[512,4608]{1,0:T(8,128)(2,1)}, bf16[512,4608]{1,0:T(8,128)(2,1)}, bf16[512,4608]{1,0:T(8,128)(2,1)}) custom-call(s32[3]{0:T(128)} %pad_add_fusion._.scalar_ref, bf16[512,2304]{1,0:T(8,128)(2,1)} %collective-permute-done.7.mid_ref.refs_0_, ...), custom_call_target="tpu_custom_call" | custom-call | flops 1 | bytes 1 | tf_op jit(solution)/shard_map/pallas_call | solution.py:68
  376.5 37.5 %all-gather.8.cloned.1.call-done.down_ref.refs_3_.refs_6_ = bf16[2304,4608]{1,0:T(8,128)(2,1)} async-done(((bf16[144,4608]{1,0:T(8,128)(2,1)}), bf16[2304,4608]{1,0:T(8,128)(2,1)}) %all-gather.8.cloned.1.call-update) | async-done | bytes 21233680 | tf_op jit(solution)/shard_map/all_gather | solution.py:764
  414.0 15.4 %shard_map.239 = bf16[256,2304]{1,0:T(8,128)(2,1)} custom-call(s32[3]{0:T(128)} %pad_add_fusion._.scalar_ref, bf16[512,4608]{1,0:T(8,128)(2,1)} %get-tuple-element.244.hidden_ref.refs_3_, bf16[2304,4608]{1,0:T(8,128)(2,1)} %all-gather.8.cloned.1.call-done.down_ref.refs_3_.refs_6_), custom_call_target="tpu_custom_call" | custom-call | flops 1 | bytes 1 | tf_op jit(solution)/shard_map/pallas_call | solution.py:68
  433.4 15.4 %shard_map.240 = bf16[256,2304]{1,0:T(8,128)(2,1)} custom-call(s32[3]{0:T(128)} %pad_add_fusion._.scalar_ref, bf16[512,4608]{1,0:T(8,128)(2,1)} %get-tuple-element.244.hidden_ref.refs_3_, bf16[2304,4608]{1,0:T(8,128)(2,1)} %all-gather.8.cloned.1.call-done.down_ref.refs_3_.refs_6_), custom_call_target="tpu_custom_call" | custom-call | flops 1 | bytes 1 | tf_op jit(solution)/shard_map/pallas_call | solution.py:68
  459.2 19.2 %shard_map.241 = f32[512,2304]{1,0:T(8,128)} custom-call(s32[3]{0:T(128)} %pad_add_fusion._.scalar_ref, bf16[512,4608]{1,0:T(8,128)(2,1)} %get-tuple-element.246.hidden_ref.refs_2_, bf16[2304,4608]{1,0:T(8,128)(2,1)} %all-gather.8.cloned.1.call-done.down_ref.refs_3_.refs_6_), custom_call_target="tpu_custom_call" | custom-call | flops 1 | bytes 1 | tf_op jit(solution)/shard_map/pallas_call | solution.py:68
  498.9 16.7 %shard_map.243 = (bf16[256,4608]{1,0:T(8,128)(2,1)}, bf16[256,4608]{1,0:T(8,128)(2,1)}) custom-call(s32[3]{0:T(128)} %pad_add_fusion._.scalar_ref, bf16[256,2304]{1,0:T(8,128)(2,1)} %copy-done.8, bf16[512,4608]{1,0:T(8,128)(2,1)} %get-tuple-element.255.refs_1_.refs_2_, bf16[512,4608]{1,0:T(8,128)(2,1)} %get-tuple-element.256.refs_2_.refs_4_, ...), custom_call_target="tpu_custom_call" | custom-call | flops 1 | bytes 1 | tf_op jit(solution)/shard_map/pallas_call | solution.py:68
  517.9 21.2 %shard_map.244 = (bf16[256,4608]{1,0:T(8,128)(2,1)}, bf16[256,4608]{1,0:T(8,128)(2,1)}, bf16[256,4608]{1,0:T(8,128)(2,1)}, bf16[256,4608]{1,0:T(8,128)(2,1)}) custom-call(s32[3]{0:T(128)} %pad_add_fusion._.scalar_ref, bf16[256,2304]{1,0:T(8,128)(2,1)} %copy-done.9, bf16[256,2304]{1,0:T(8,128)(2,1)} %collective-permute-done.10.refs_1_.refs_0_, ...), custom_call_target="tpu_custom_call" | custom-call | flops 1 | bytes 1 | tf_op jit(solution)/shard_map/pallas_call | solution.py:68
  554.5 11.2 shard_map.247
  580.3 17.0 %shard_map.250 = (bf16[256,4608]{1,0:T(8,128)(2,1)}, bf16[256,4608]{1,0:T(8,128)(2,1)}) custom-call(s32[3]{0:T(128)} %pad_add_fusion._.scalar_ref, bf16[256,2304]{1,0:T(8,128)(2,1)} %copy-done.18, bf16[512,4608]{1,0:T(8,128)(2,1)} %get-tuple-element.261.refs_3_.refs_1_, bf16[512,4608]{1,0:T(8,128)(2,1)} %get-tuple-element.262.refs_5_.refs_2_, ...), custom_call_target="tpu_custom_call" | custom-call | flops 1 | bytes 1 | tf_op jit(solution)/shard_map/pallas_call | solution.py:68
  614.8 11.2 shard_map.253
  646.0 30.9 %shard_map.256 = (bf16[256,2304]{1,0:T(8,128)(2,1)}, bf16[256,2304]{1,0:T(8,128)(2,1)}) custom-call(s32[3]{0:T(128)} %pad_add_fusion._.scalar_ref, bf16[256,4608]{1,0:T(8,128)(2,1)} %get-tuple-element.293.refs_4_.refs_0_, bf16[256,4608]{1,0:T(8,128)(2,1)} %get-tuple-element.288.refs_5_.refs_1_, bf16[256,4608]{1,0:T(8,128)(2,1)} %get-tuple-element.346.refs_2_.refs_4_, ...), custom_call_target="tpu_custom_call" | custom-call | flops 1 | bytes 1 | tf_op jit(solution)/shard_map/pallas_call | solution.py:68
  707.2 11.2 shard_map.260
  718.5 30.9 %shard_map.261 = (f32[256,2304]{1,0:T(8,128)}, f32[256,2304]{1,0:T(8,128)}) custom-call(s32[3]{0:T(128)} %pad_add_fusion._.scalar_ref, bf16[256,4608]{1,0:T(8,128)(2,1)} %get-tuple-element.314.refs_2_.refs_0_, bf16[256,4608]{1,0:T(8,128)(2,1)} %get-tuple-element.286.refs_3_.refs_1_, bf16[256,4608]{1,0:T(8,128)(2,1)} %get-tuple-element.344.refs_2_, ...), custom_call_target="tpu_custom_call" | custom-call | flops 1 | bytes 1 | tf_op jit(solution)/shard_map/pallas_call | solution.py:68
  752.9 14.1 %shard_map.262 = (f32[512,2304]{1,0:T(8,128)}, bf16[256,2304]{1,0:T(8,128)(2,1)}, bf16[256,2304]{1,0:T(8,128)(2,1)}, f32[1,2304]{1,0:T(1,128)}, f32[1,2304]{1,0:T(1,128)}) custom-call(s32[3]{0:T(128)} %pad_add_fusion._.scalar_ref, f32[256,2304]{1,0:T(8,128)} %get-tuple-element.324.refs_0_, bf16[256,2304]{1,0:T(8,128)(2,1)} %copy-done.29, ...), custom_call_target="tpu_custom_call" | custom-call | flops 1 | bytes 1 | tf_op jit(solution)/shard_map/pallas_call | solution.py:68
  835.2 9.9 collective-permute-done.30.refs_3_.refs_1_
  852.2 10.4 shard_map.269.d_ref
  868.3 18.2 %shard_map.271 = (bf16[1024,1024]{1,0:T(8,128)(2,1)}, bf16[1024,1024]{1,0:T(8,128)(2,1)}) custom-call(s32[3]{0:T(128)} %pad_add_fusion._.scalar_ref, bf16[1024,2048]{1,0:T(8,128)(2,1)} %shard_map.231.query_ref.key_ref.value_ref.pair_ref, bf16[1024,2048]{1,0:T(8,128)(2,1)} %shard_map.231.query_ref.key_ref.value_ref.pair_ref, bf16[1024,1024]{1,0:T(8,128)(2,1)} %shard_map.269.d_ref), custom_call_target="tpu_custom_call" | custom-call | flops 1 | bytes 1 | tf_op jit(solution)/shard_map/pallas_call | solution.py:68
  918.9 12.2 %shard_map.276 = (bf16[256,2304]{1,0:T(8,128)(2,1)}, bf16[256,2304]{1,0:T(8,128)(2,1)}) custom-call(s32[3]{0:T(128)} %pad_add_fusion._.scalar_ref, bf16[1024,1024]{1,0:T(8,128)(2,1)} %get-tuple-element.396.refs_2_.refs_3_.refs_0_, bf16[1024,1024]{1,0:T(8,128)(2,1)} %get-tuple-element.377.refs_2_.refs_3_.refs_1_, ...), custom_call_target="tpu_custom_call" | custom-call | flops 1 | bytes 1 | tf_op jit(solution)/shard_map/pallas_call | solution.py:68
  958.4 12.5 %shard_map.281 = (f32[256,2304]{1,0:T(8,128)}, f32[256,2304]{1,0:T(8,128)}) custom-call(s32[3]{0:T(128)} %pad_add_fusion._.scalar_ref, bf16[1024,1024]{1,0:T(8,128)(2,1)} %get-tuple-element.396.refs_2_.refs_3_.refs_0_, bf16[1024,1024]{1,0:T(8,128)(2,1)} %get-tuple-element.377.refs_2_.refs_3_.refs_1_, ...), custom_call_target="tpu_custom_call" | custom-call | flops 1 | bytes 1 | tf_op jit(solution)/shard_map/pallas_call | solution.py:68
  984.6 19.7 %collective-permute-done.40.refs_5_ = bf16[4,144,1024]{2,1,0:T(8,128)(2,1)S(1)} collective-permute-done((bf16[4,144,1024]{2,1,0:T(8,128)(2,1)S(1)}, bf16[4,144,1024]{2,1,0:T(8,128)(2,1)S(1)}, u32[]{:S(2)}, u32[]{:S(2)}) %collective-permute-start.40) | collective-permute-done | bytes 1179680 | tf_op jit(solution)/shard_map/ppermute | solution.py:30
  1018.4 11.2 shard_map.284
  1056.8 24.2 %collective-permute-start.46 = (bf16[144,1024]{1,0:T(8,128)(2,1)S(1)}, bf16[144,1024]{1,0:T(8,128)(2,1)S(1)}, u32[]{:S(2)}, u32[]{:S(2)}) collective-permute-start(bf16[144,1024]{1,0:T(8,128)(2,1)S(1)} %get-tuple-element.426), channel_id=1, source_target_pairs={{0,8},{2,10},{4,12},{6,14},{8,16},{10,18},{12,20},{14,22},{16,24},... | collective-permute-start | bytes 884744 | tf_op jit(solution)/shard_map/ppermute | solution.py:485
  1101.5 10.2 all-to-all-start
  (314 shorter events, 428.5 us)
Async XLA Ops:
  7.2 183.4 %all-gather.4.cloned.1.call-start = ((), (), s32[]{:S(2)}) async-start(), calls=%async_computation.9 | async-start | bytes 37601280 | tf_op jit(solution)/shard_map/all_gather | solution.py:757
  10.4 291.9 %all-gather.6.cloned.1.call-start = ((), (), s32[]{:S(2)}) async-start(), calls=%async_computation.10 | async-start | bytes 22560768 | tf_op jit(solution)/shard_map/all_gather | solution.py:763
  11.2 402.8 %all-gather.8.cloned.1.call-start = ((), (), s32[]{:S(2)}) async-start(), calls=%async_computation.11 | async-start | bytes 22560768 | tf_op jit(solution)/shard_map/all_gather | solution.py:764
  11.9 673.8 %reduce-scatter.9.cloned.1.call-start = ((), (), s32[]{:S(2)}) async-start(), calls=%async_computation.12 | async-start | bytes 1474560 | tf_op jit(solution)/shard_map/reduce_scatter | solution.py:471
  33.5 51.3 %collective-permute-start.5 = (bf16[512,2304]{1,0:T(8,128)(2,1)}, bf16[512,2304]{1,0:T(8,128)(2,1)}, u32[]{:S(2)}, u32[]{:S(2)}) collective-permute-start(bf16[512,2304]{1,0:T(8,128)(2,1)} %fusion.2.refs_0_), channel_id=1, source_target_pairs={{0,1},{1,0},{2,3},{3,2},{4,5},{5,4},{6,7},{7,6},{8,9},{9,8},{10,11... | collective-permute-start | bytes 7077896 | tf_op jit(solution)/shard_map/ppermute | solution.py:26
  227.1 53.6 %collective-permute-start.6 = (bf16[512,2304]{1,0:T(8,128)(2,1)}, bf16[512,2304]{1,0:T(8,128)(2,1)S(1)}, u32[]{:S(2)}, u32[]{:S(2)}) collective-permute-start(bf16[512,2304]{1,0:T(8,128)(2,1)} %shard_map.233), channel_id=1, source_target_pairs={{0,1},{1,0},{2,3},{3,2},{4,5},{5,4},{6,7},{7,6},{8,9},{9,8},{10,11... | collective-permute-start | bytes 7077896 | tf_op jit(solution)/shard_map/ppermute | solution.py:26
  288.2 52.8 %collective-permute-start.7 = (bf16[512,2304]{1,0:T(8,128)(2,1)S(1)}, bf16[512,2304]{1,0:T(8,128)(2,1)}, u32[]{:S(2)}, u32[]{:S(2)}) collective-permute-start(bf16[512,2304]{1,0:T(8,128)(2,1)S(1)} %multiply_convert_fusion.mid_ref.refs_0_), channel_id=1, source_target_pairs={{0,1},{1,0},{2,3},{3,2},{4,5},{5,4},{6,7},{7,6},{8,9},{9,8},{10,11... | collective-permute-start | bytes 7077896 | tf_op jit(solution)/shard_map/ppermute | solution.py:26
  491.7 49.6 %collective-permute-start.11 = (bf16[256,2304]{1,0:T(8,128)(2,1)S(1)}, bf16[256,2304]{1,0:T(8,128)(2,1)S(1)}, u32[]{:S(2)}, u32[]{:S(2)}) collective-permute-start(bf16[256,2304]{1,0:T(8,128)(2,1)S(1)} %get-tuple-element.457.refs_1_.refs_0_), channel_id=1, source_target_pairs={{0,1},{1,0},{2,3},{3,2},{4,5},{5,4},{6,7},{7,6},{8,9},{9,8},{10,11... | collective-permute-start | bytes 3538952 | tf_op jit(solution)/shard_map/ppermute | solution.py:26
  572.6 36.0 %collective-permute-start.13 = (bf16[4,144,1024]{2,1,0:T(8,128)(2,1)}, bf16[4,144,1024]{2,1,0:T(8,128)(2,1)}, u32[]{:S(2)}, u32[]{:S(2)}) collective-permute-start(bf16[4,144,1024]{2,1,0:T(8,128)(2,1)} %shard_map.248), channel_id=1, source_target_pairs={{0,4},{2,6},{4,0},{6,2},{8,12},{10,14},{12,8},{14,10},{16,20},{18,... | collective-permute-start | bytes 3538952 | tf_op jit(solution)/shard_map/ppermute | solution.py:30
  608.7 35.4 %collective-permute-start.16 = (bf16[2,144,2560]{2,1,0:T(8,128)(2,1)}, bf16[2,144,2560]{2,1,0:T(8,128)(2,1)}, u32[]{:S(2)}, u32[]{:S(2)}) collective-permute-start(bf16[2,144,2560]{2,1,0:T(8,128)(2,1)} %get-tuple-element.289), channel_id=1, source_target_pairs={{0,4},{2,6},{4,0},{6,2},{8,12},{10,14},{12,8},{14,10},{16,20},{18,... | collective-permute-start | bytes 4423688 | tf_op jit(solution)/shard_map/ppermute | solution.py:30
  644.1 32.9 %collective-permute-start.17 = (bf16[4,2,144,2560]{3,2,1,0:T(8,128)(2,1)}, bf16[4,2,144,2560]{3,2,1,0:T(8,128)(2,1)}, u32[]{:S(2)}, u32[]{:S(2)}) collective-permute-start(bf16[4,2,144,2560]{3,2,1,0:T(8,128)(2,1)} %shard_map.253), channel_id=1, source_target_pairs={{0,2},{2,0},{4,6},{6,4},{8,10},{10,8},{12,14},{14,12},{16,18},{18,... | collective-permute-start | bytes 17694728 | tf_op jit(solution)/shard_map/ppermute | solution.py:30
  644.3 32.6 %collective-permute-start.18 = (bf16[4,2,144,2048]{3,2,1,0:T(8,128)(2,1)}, bf16[4,2,144,2048]{3,2,1,0:T(8,128)(2,1)}, u32[]{:S(2)}, u32[]{:S(2)}) collective-permute-start(bf16[4,2,144,2048]{3,2,1,0:T(8,128)(2,1)} %shard_map.255), channel_id=1, source_target_pairs={{0,2},{2,0},{4,6},{6,4},{8,10},{10,8},{12,14},{14,12},{16,18},{18,... | collective-permute-start | bytes 14155784 | tf_op jit(solution)/shard_map/ppermute | solution.py:30
  644.6 107.3 %reduce-scatter.11.cloned.1.call-start = ((), (), s32[]{:S(2)}) async-start(), calls=%async_computation.13 | async-start | bytes 2949120 | tf_op jit(solution)/shard_map/reduce_scatter | solution.py:471
  644.7 41.0 %collective-permute-start.19 = (bf16[2,144,2560]{2,1,0:T(8,128)(2,1)S(1)}, bf16[2,144,2560]{2,1,0:T(8,128)(2,1)S(1)}, u32[]{:S(2)}, u32[]{:S(2)}) collective-permute-start(bf16[2,144,2560]{2,1,0:T(8,128)(2,1)S(1)} %copy-done.46), channel_id=1, source_target_pairs={{0,4},{2,6},{4,0},{6,2},{8,12},{10,14},{12,8},{14,10},{16,20},{18,... | collective-permute-start | bytes 4423688 | tf_op jit(solution)/shard_map/ppermute | solution.py:30
  685.8 124.3 %reduce-scatter.13.cloned.1.call-start = ((), (), s32[]{:S(2)}) async-start(), calls=%async_computation.14 | async-start | bytes 3686400 | tf_op jit(solution)/shard_map/reduce_scatter | solution.py:471
  685.8 63.6 %collective-permute-start.20 = (bf16[2,144,2560]{2,1,0:T(8,128)(2,1)}, bf16[2,144,2560]{2,1,0:T(8,128)(2,1)}, u32[]{:S(2)}, u32[]{:S(2)}) collective-permute-start(bf16[2,144,2560]{2,1,0:T(8,128)(2,1)} %get-tuple-element.316), channel_id=1, source_target_pairs={{0,4},{2,6},{4,0},{6,2},{8,12},{10,14},{12,8},{14,10},{16,20},{18,... | collective-permute-start | bytes 4423688 | tf_op jit(solution)/shard_map/ppermute | solution.py:30
  686.7 65.2 %collective-permute-start.21 = (bf16[2,144,2560]{2,1,0:T(8,128)(2,1)}, bf16[2,144,2560]{2,1,0:T(8,128)(2,1)}, u32[]{:S(2)}, u32[]{:S(2)}) collective-permute-start(bf16[2,144,2560]{2,1,0:T(8,128)(2,1)} %get-tuple-element.318), channel_id=1, source_target_pairs={{0,4},{2,6},{4,0},{6,2},{8,12},{10,14},{12,8},{14,10},{16,20},{18,... | collective-permute-start | bytes 4423688 | tf_op jit(solution)/shard_map/ppermute | solution.py:30
  687.9 61.5 %collective-permute-start.22 = (bf16[256,2304]{1,0:T(8,128)(2,1)}, bf16[256,2304]{1,0:T(8,128)(2,1)S(1)}, u32[]{:S(2)}, u32[]{:S(2)}) collective-permute-start(bf16[256,2304]{1,0:T(8,128)(2,1)} %get-tuple-element.319), channel_id=1, source_target_pairs={{0,1},{1,0},{2,3},{3,2},{4,5},{5,4},{6,7},{7,6},{8,9},{9,8},{10,11... | collective-permute-start | bytes 3538952 | tf_op jit(solution)/shard_map/ppermute | solution.py:26
  688.5 60.9 %collective-permute-start.23 = (bf16[256,2304]{1,0:T(8,128)(2,1)}, bf16[256,2304]{1,0:T(8,128)(2,1)}, u32[]{:S(2)}, u32[]{:S(2)}) collective-permute-start(bf16[256,2304]{1,0:T(8,128)(2,1)} %get-tuple-element.321), channel_id=1, source_target_pairs={{0,1},{1,0},{2,3},{3,2},{4,5},{5,4},{6,7},{7,6},{8,9},{9,8},{10,11... | collective-permute-start | bytes 3538952 | tf_op jit(solution)/shard_map/ppermute | solution.py:26
  751.9 134.5 %reduce-scatter.15.cloned.1.call-start = ((), (), s32[]{:S(2)}) async-start(), calls=%async_computation.15 | async-start | bytes 3686400 | tf_op jit(solution)/shard_map/reduce_scatter | solution.py:471
  781.7 34.3 %collective-permute-start.26 = (bf16[2,144,2048]{2,1,0:T(8,128)(2,1)}, bf16[2,144,2048]{2,1,0:T(8,128)(2,1)}, u32[]{:S(2)}, u32[]{:S(2)}) collective-permute-start(bf16[2,144,2048]{2,1,0:T(8,128)(2,1)} %get-tuple-element.336), channel_id=1, source_target_pairs={{0,4},{2,6},{4,0},{6,2},{8,12},{10,14},{12,8},{14,10},{16,20},{18,... | collective-permute-start | bytes 3538952 | tf_op jit(solution)/shard_map/ppermute | solution.py:30
  782.5 33.5 %collective-permute-start.27 = (bf16[256,2304]{1,0:T(8,128)(2,1)S(1)}, bf16[256,2304]{1,0:T(8,128)(2,1)S(1)}, u32[]{:S(2)}, u32[]{:S(2)}) collective-permute-start(bf16[256,2304]{1,0:T(8,128)(2,1)S(1)} %copy-done.15), channel_id=1, source_target_pairs={{0,1},{1,0},{2,3},{3,2},{4,5},{5,4},{6,7},{7,6},{8,9},{9,8},{10,11... | collective-permute-start | bytes 3538952 | tf_op jit(solution)/shard_map/ppermute | solution.py:26
  783.5 32.5 %collective-permute-start.28 = (bf16[144,1024]{1,0:T(8,128)(2,1)}, bf16[144,1024]{1,0:T(8,128)(2,1)}, u32[]{:S(2)}, u32[]{:S(2)}) collective-permute-start(bf16[144,1024]{1,0:T(8,128)(2,1)} %dynamic-slice_bitcast_fusion.6), channel_id=1, source_target_pairs={{0,4},{2,6},{4,0},{6,2},{8,12},{10,14},{12,8},{14,10},{16,20},{18,... | collective-permute-start | bytes 884744 | tf_op jit(solution)/shard_map/ppermute | solution.py:30
  816.1 131.7 %reduce-scatter.17.cloned.1.call-start = ((), (), s32[]{:S(2)}) async-start(), calls=%async_computation.16 | async-start | bytes 2949120 | tf_op jit(solution)/shard_map/reduce_scatter | solution.py:471
  816.2 35.0 %collective-permute-start.29 = (bf16[2,144,2560]{2,1,0:T(8,128)(2,1)}, bf16[2,144,2560]{2,1,0:T(8,128)(2,1)}, u32[]{:S(2)}, u32[]{:S(2)}) collective-permute-start(bf16[2,144,2560]{2,1,0:T(8,128)(2,1)} %get-tuple-element.351), channel_id=1, source_target_pairs={{0,4},{2,6},{4,0},{6,2},{8,12},{10,14},{12,8},{14,10},{16,20},{18,... | collective-permute-start | bytes 4423688 | tf_op jit(solution)/shard_map/ppermute | solution.py:30
  851.2 154.4 %reduce-scatter.19.cloned.1.call-start = ((), (), s32[]{:S(2)}) async-start(), calls=%async_computation.17 | async-start | bytes 3686400 | tf_op jit(solution)/shard_map/reduce_scatter | solution.py:471
  851.3 35.2 %collective-permute-start.32 = (bf16[2,144,2560]{2,1,0:T(8,128)(2,1)}, bf16[2,144,2560]{2,1,0:T(8,128)(2,1)S(1)}, u32[]{:S(2)}, u32[]{:S(2)}) collective-permute-start(bf16[2,144,2560]{2,1,0:T(8,128)(2,1)} %get-tuple-element.367), channel_id=1, source_target_pairs={{0,4},{2,6},{4,0},{6,2},{8,12},{10,14},{12,8},{14,10},{16,20},{18,... | collective-permute-start | bytes 4423688 | tf_op jit(solution)/shard_map/ppermute | solution.py:30
  886.5 30.4 %collective-permute-start.33 = (bf16[2,144,2048]{2,1,0:T(8,128)(2,1)S(1)}, bf16[2,144,2048]{2,1,0:T(8,128)(2,1)}, u32[]{:S(2)}, u32[]{:S(2)}) collective-permute-start(bf16[2,144,2048]{2,1,0:T(8,128)(2,1)S(1)} %copy-done.47), channel_id=1, source_target_pairs={{0,4},{2,6},{4,0},{6,2},{8,12},{10,14},{12,8},{14,10},{16,20},{18,... | collective-permute-start | bytes 3538952 | tf_op jit(solution)/shard_map/ppermute | solution.py:30
  917.0 139.8 %reduce-scatter.21.cloned.1.call-start = ((), (), s32[]{:S(2)}) async-start(), calls=%async_computation.18 | async-start | bytes 2949120 | tf_op jit(solution)/shard_map/reduce_scatter | solution.py:471
  917.9 29.8 %collective-permute-start.34 = (bf16[2,144,2048]{2,1,0:T(8,128)(2,1)}, bf16[2,144,2048]{2,1,0:T(8,128)(2,1)S(1)}, u32[]{:S(2)}, u32[]{:S(2)}) collective-permute-start(bf16[2,144,2048]{2,1,0:T(8,128)(2,1)} %get-tuple-element.381), channel_id=1, source_target_pairs={{0,4},{2,6},{4,0},{6,2},{8,12},{10,14},{12,8},{14,10},{16,20},{18,... | collective-permute-start | bytes 3538952 | tf_op jit(solution)/shard_map/ppermute | solution.py:30
  977.2 142.7 %reduce-scatter.23.cloned.1.call-start = ((), (), s32[]{:S(2)}) async-start(), calls=%async_computation.19 | async-start | bytes 1474560 | tf_op jit(solution)/shard_map/reduce_scatter | solution.py:471
  1056.8 33.4 %collective-permute-start.46 = (bf16[144,1024]{1,0:T(8,128)(2,1)S(1)}, bf16[144,1024]{1,0:T(8,128)(2,1)S(1)}, u32[]{:S(2)}, u32[]{:S(2)}) collective-permute-start(bf16[144,1024]{1,0:T(8,128)(2,1)S(1)} %get-tuple-element.426), channel_id=1, source_target_pairs={{0,8},{2,10},{4,12},{6,14},{8,16},{10,18},{12,20},{14,22},{16,24},... | collective-permute-start | bytes 884744 | tf_op jit(solution)/shard_map/ppermute | solution.py:485
  (79 other events, 941.9 us)
Sparse Core Ops, SparseCore 0:
  10.5 180.0 all-gather.3
  192.2 110.0 all-gather.5
  303.9 110.0 all-gather.7
  644.8 28.2 reduce-scatter.8
  685.9 47.3 reduce-scatter.10
  752.1 56.5 reduce-scatter.12
  816.2 56.4 reduce-scatter.14
  875.0 47.9 reduce-scatter.16
  925.3 56.6 reduce-scatter.18
  984.2 47.9 reduce-scatter.20
  1046.0 35.4 reduce-scatter.22

commit v8 on v6

--- a/solution.py
+++ b/solution.py
@@ -1044,9 +1044,9 @@
         gain_grads = line.mark(owner_parts(gain_grads))
         (pair_side,) = line.land(pair_side)
         line.mark(pair.own(line.next(pair_side)))
+        output.along_rest(line)
         query_parts = line.land(*query_parts, sums=[up_1])
         *pair_parts, gain_parts = line.send(*pair.to_owner(), (gain_grads, to_owners))
-        output.along_rest(line)
         pair_parts = line.land(*pair_parts)
         (gain_parts,) = line.land(gain_parts)
         small = jnp.sum(gain_parts, axis=0)

time: 1130 us -> 1130 us (level)
  starting transfers between devices: 64.5 us -> 82.5 us
  waiting for transfers between devices: 348 us -> 332 us
    ppermute x6, waiting for transfers between devices: 32.7 us -> 14.9 us  [to_owner(): lax.ppermute(array, 'dp', pairs)]
    all_to_all x1, starting transfers between devices: 10 us -> 26 us  [to_owners(): return lax.all_to_all(parts, ('dp', 'tensor'), 0, 0, tiled=True)]
where the time goes in v8:
time: 1130 us; the launch traced here: 1120 us
  Pallas kernels  622 us (55%)
  waiting for transfers between devices  332 us (29%)
  starting transfers between devices  82.5 us (7%)
  other arithmetic  42.8 us (4%)
  local copies, waits for them, and re-layouts  23.1 us (2%)
  between operations  14.8 us (1%)
    pallas_call x57, Pallas kernels, call(): pl.pallas_call(kernel, grid_spec=pltpu.PrefetchScalarGridSpec(num_scalar_...  619 us
    ppermute x14, waiting for transfers between devices, swap(): return lax.ppermute(rows, 'tensor', [(0, 1), (1, 0)])  112 us
    all_gather x1, waiting for transfers between devices, body(): lax.all_gather(joined([query_weight, key_weight, value_weight, w_output.T...  100 us
    ppermute x29, waiting for transfers between devices, flip(): return lax.ppermute(array, 'dp', [(i, i ^ 1 << bit) for i in range(dp)])  53.1 us
    all_gather x1, waiting for transfers between devices, body(): full_down_t = lax.all_gather(w_down.T, 'dp', axis=0, tiled=True)  37.4 us
    all_to_all x1, starting transfers between devices, to_owners(): return lax.all_to_all(parts, ('dp', 'tensor'), 0, 0, tiled=True)  26 us
    ppermute x29, starting transfers between devices, flip(): return lax.ppermute(array, 'dp', [(i, i ^ 1 << bit) for i in range(dp)])  25.2 us
  transfers between devices with their start and end apart: 61, of which 27 were waited for; matrix products, arithmetic and copies ran while one was open for 4% of the time, Pallas kernels for 53%

profile of v8, /device:TPU:0, one launch (start us, length us, event | category | flops | bytes accessed | tf_op | source)
XLA Modules:
  0.0 1117.2 jit_solution(339858974640362423)
XLA Ops:
  41.8 43.0 %collective-permute-done.5.refs_0_.refs_1_ = bf16[512,2304]{1,0:T(8,128)(2,1)} collective-permute-done((bf16[512,2304]{1,0:T(8,128)(2,1)}, bf16[512,2304]{1,0:T(8,128)(2,1)}, u32[]{:S(2)}, u32[]{:S(2)}) %collective-permute-start.5) | collective-permute-done | bytes 2359328 | tf_op jit(solution)/shard_map/ppermute | solution.py:26
  90.5 100.0 %all-gather.4.cloned.1.call-done.refs_2_.refs_1_.gate_ref.refs_4_.refs_5_.refs_6_.refs_3_ = bf16[2304,7680]{1,0:T(8,128)(2,1)} async-done(((bf16[144,7680]{1,0:T(8,128)(2,1)}), bf16[2304,7680]{1,0:T(8,128)(2,1)}) %all-gather.4.cloned.1.call-update) | async-done | bytes 35389456 | tf_op jit(solution)/shard_map/all_gather | solution.py:757
  190.6 15.3 %shard_map.231.query_ref.key_ref.value_ref.pair_ref = bf16[1024,2048]{1,0:T(8,128)(2,1)} custom-call(s32[3]{0:T(128)} %pad_add_fusion._.scalar_ref, bf16[512,2304]{1,0:T(8,128)(2,1)} %fusion.2.refs_0_, bf16[512,2304]{1,0:T(8,128)(2,1)} %collective-permute-done.5.refs_0_.refs_1_, ...), custom_call_target="tpu_custom_call" | custom-call | flops 1 | bytes 1 | tf_op jit(solution)/shard_map/pallas_call | solution.py:68
  205.9 11.4 %shard_map.232.refs_0_.refs_2_.refs_3_ = bf16[1024,1024]{1,0:T(8,128)(2,1)} custom-call(s32[3]{0:T(128)} %pad_add_fusion._.scalar_ref, bf16[1024,2048]{1,0:T(8,128)(2,1)} %shard_map.231.query_ref.key_ref.value_ref.pair_ref, bf16[1024,2048]{1,0:T(8,128)(2,1)} %shard_map.231.query_ref.key_ref.value_ref.pair_ref, ...), custom_call_target="tpu_custom_call" | custom-call | flops 1 | bytes 1 | tf_op jit(solution)/shard_map/pallas_call | solution.py:68
  217.3 9.9 shard_map.233
  228.6 10.3 shard_map.234
  238.9 41.8 %collective-permute-done.6 = bf16[512,2304]{1,0:T(8,128)(2,1)S(1)} collective-permute-done((bf16[512,2304]{1,0:T(8,128)(2,1)}, bf16[512,2304]{1,0:T(8,128)(2,1)S(1)}, u32[]{:S(2)}, u32[]{:S(2)}) %collective-permute-start.6) | collective-permute-done | bytes 2359328 | tf_op jit(solution)/shard_map/ppermute | solution.py:26
  289.6 12.7 %all-gather.6.cloned.1.call-done.up_ref.refs_7_ = bf16[2304,4608]{1,0:T(8,128)(2,1)} async-done(((bf16[144,4608]{1,0:T(8,128)(2,1)}), bf16[2304,4608]{1,0:T(8,128)(2,1)}) %all-gather.6.cloned.1.call-update) | async-done | bytes 21233680 | tf_op jit(solution)/shard_map/all_gather | solution.py:763
  302.3 30.8 %shard_map.235 = (bf16[512,4608]{1,0:T(8,128)(2,1)}, bf16[512,4608]{1,0:T(8,128)(2,1)}, bf16[512,4608]{1,0:T(8,128)(2,1)}) custom-call(s32[3]{0:T(128)} %pad_add_fusion._.scalar_ref, bf16[512,2304]{1,0:T(8,128)(2,1)} %copy-done.6, bf16[2304,7680]{1,0:T(8,128)(2,1)} %all-gather.4.cloned.1.call-done.refs_2_.refs_1_.gate_ref.refs_4_.refs_5_.refs_6_.refs_3_, ...), custom_call_target="tpu_custom_call" | custom-call | flops 1 | bytes 1 | tf_op jit(solution)/shard_map/pallas_call | solution.py:68
  341.0 29.9 %shard_map.237 = (bf16[512,4608]{1,0:T(8,128)(2,1)}, bf16[512,4608]{1,0:T(8,128)(2,1)}, bf16[512,4608]{1,0:T(8,128)(2,1)}) custom-call(s32[3]{0:T(128)} %pad_add_fusion._.scalar_ref, bf16[512,2304]{1,0:T(8,128)(2,1)} %collective-permute-done.7.mid_ref.refs_0_, ...), custom_call_target="tpu_custom_call" | custom-call | flops 1 | bytes 1 | tf_op jit(solution)/shard_map/pallas_call | solution.py:68
  376.6 37.4 %all-gather.8.cloned.1.call-done.down_ref.refs_3_.refs_6_ = bf16[2304,4608]{1,0:T(8,128)(2,1)} async-done(((bf16[144,4608]{1,0:T(8,128)(2,1)}), bf16[2304,4608]{1,0:T(8,128)(2,1)}) %all-gather.8.cloned.1.call-update) | async-done | bytes 21233680 | tf_op jit(solution)/shard_map/all_gather | solution.py:764
  414.0 15.3 %shard_map.239 = bf16[256,2304]{1,0:T(8,128)(2,1)} custom-call(s32[3]{0:T(128)} %pad_add_fusion._.scalar_ref, bf16[512,4608]{1,0:T(8,128)(2,1)} %get-tuple-element.242.hidden_ref.refs_3_, bf16[2304,4608]{1,0:T(8,128)(2,1)} %all-gather.8.cloned.1.call-done.down_ref.refs_3_.refs_6_), custom_call_target="tpu_custom_call" | custom-call | flops 1 | bytes 1 | tf_op jit(solution)/shard_map/pallas_call | solution.py:68
  433.4 15.4 %shard_map.240 = bf16[256,2304]{1,0:T(8,128)(2,1)} custom-call(s32[3]{0:T(128)} %pad_add_fusion._.scalar_ref, bf16[512,4608]{1,0:T(8,128)(2,1)} %get-tuple-element.242.hidden_ref.refs_3_, bf16[2304,4608]{1,0:T(8,128)(2,1)} %all-gather.8.cloned.1.call-done.down_ref.refs_3_.refs_6_), custom_call_target="tpu_custom_call" | custom-call | flops 1 | bytes 1 | tf_op jit(solution)/shard_map/pallas_call | solution.py:68
  459.2 19.2 %shard_map.241 = f32[512,2304]{1,0:T(8,128)} custom-call(s32[3]{0:T(128)} %pad_add_fusion._.scalar_ref, bf16[512,4608]{1,0:T(8,128)(2,1)} %get-tuple-element.244.hidden_ref.refs_2_, bf16[2304,4608]{1,0:T(8,128)(2,1)} %all-gather.8.cloned.1.call-done.down_ref.refs_3_.refs_6_), custom_call_target="tpu_custom_call" | custom-call | flops 1 | bytes 1 | tf_op jit(solution)/shard_map/pallas_call | solution.py:68
  498.8 16.7 %shard_map.243 = (bf16[256,4608]{1,0:T(8,128)(2,1)}, bf16[256,4608]{1,0:T(8,128)(2,1)}) custom-call(s32[3]{0:T(128)} %pad_add_fusion._.scalar_ref, bf16[256,2304]{1,0:T(8,128)(2,1)} %copy-done.8, bf16[512,4608]{1,0:T(8,128)(2,1)} %get-tuple-element.253.refs_1_.refs_2_, bf16[512,4608]{1,0:T(8,128)(2,1)} %get-tuple-element.254.refs_2_.refs_4_, ...), custom_call_target="tpu_custom_call" | custom-call | flops 1 | bytes 1 | tf_op jit(solution)/shard_map/pallas_call | solution.py:68
  517.9 21.2 %shard_map.244 = (bf16[256,4608]{1,0:T(8,128)(2,1)}, bf16[256,4608]{1,0:T(8,128)(2,1)}, bf16[256,4608]{1,0:T(8,128)(2,1)}, bf16[256,4608]{1,0:T(8,128)(2,1)}) custom-call(s32[3]{0:T(128)} %pad_add_fusion._.scalar_ref, bf16[256,2304]{1,0:T(8,128)(2,1)} %copy-done.9, bf16[256,2304]{1,0:T(8,128)(2,1)} %collective-permute-done.10.refs_1_.refs_0_, ...), custom_call_target="tpu_custom_call" | custom-call | flops 1 | bytes 1 | tf_op jit(solution)/shard_map/pallas_call | solution.py:68
  554.4 11.2 %shard_map.247 = bf16[4,2,144,2560]{3,2,1,0:T(8,128)(2,1)} custom-call(s32[3]{0:T(128)} %pad_add_fusion._.scalar_ref, bf16[4,2,2,144,512]{4,3,2,1,0:T(8,128)(2,1)} %bitcast.97, bf16[4,2,2,144,512]{4,3,2,1,0:T(8,128)(2,1)} %bitcast.105, bf16[512,4608]{1,0:T(8,128)(2,1)} %get-tuple-element.244.hidden_ref.refs_2_, ...), custom_call_target="tpu_custom_call" | custom-call | flops 1 | bytes 1 | tf_op jit(solution)/shard_map/pallas_call | solution.py:68
  580.4 16.9 %shard_map.250 = (bf16[256,4608]{1,0:T(8,128)(2,1)}, bf16[256,4608]{1,0:T(8,128)(2,1)}) custom-call(s32[3]{0:T(128)} %pad_add_fusion._.scalar_ref, bf16[256,2304]{1,0:T(8,128)(2,1)} %copy-done.18, bf16[512,4608]{1,0:T(8,128)(2,1)} %get-tuple-element.259.refs_3_.refs_1_, bf16[512,4608]{1,0:T(8,128)(2,1)} %get-tuple-element.260.refs_5_.refs_2_, ...), custom_call_target="tpu_custom_call" | custom-call | flops 1 | bytes 1 | tf_op jit(solution)/shard_map/pallas_call | solution.py:68
  614.8 11.3 %shard_map.253 = bf16[4,2,144,2560]{3,2,1,0:T(8,128)(2,1)} custom-call(s32[3]{0:T(128)} %pad_add_fusion._.scalar_ref, bf16[4,2,2,144,512]{4,3,2,1,0:T(8,128)(2,1)} %bitcast.72, bf16[4,2,2,144,512]{4,3,2,1,0:T(8,128)(2,1)} %bitcast.84, bf16[256,4608]{1,0:T(8,128)(2,1)} %get-tuple-element.312.refs_2_.refs_0_, ...), custom_call_target="tpu_custom_call" | custom-call | flops 1 | bytes 1 | tf_op jit(solution)/shard_map/pallas_call | solution.py:68
  646.1 31.0 %shard_map.256 = (bf16[256,2304]{1,0:T(8,128)(2,1)}, bf16[256,2304]{1,0:T(8,128)(2,1)}) custom-call(s32[3]{0:T(128)} %pad_add_fusion._.scalar_ref, bf16[256,4608]{1,0:T(8,128)(2,1)} %get-tuple-element.291.refs_4_.refs_0_, bf16[256,4608]{1,0:T(8,128)(2,1)} %get-tuple-element.286.refs_5_.refs_1_, bf16[256,4608]{1,0:T(8,128)(2,1)} %get-tuple-element.344.refs_2_.refs_4_, ...), custom_call_target="tpu_custom_call" | custom-call | flops 1 | bytes 1 | tf_op jit(solution)/shard_map/pallas_call | solution.py:68
  690.1 9.8 shard_map.258
  707.4 11.2 %shard_map.260 = bf16[4,2,144,2560]{3,2,1,0:T(8,128)(2,1)} custom-call(s32[3]{0:T(128)} %pad_add_fusion._.scalar_ref, bf16[4,2,2,144,512]{4,3,2,1,0:T(8,128)(2,1)} %bitcast.76, bf16[4,2,2,144,512]{4,3,2,1,0:T(8,128)(2,1)} %bitcast.88, bf16[256,4608]{1,0:T(8,128)(2,1)} %get-tuple-element.342.refs_2_, bf16[256,4608]{1,0:T(8,128)(2,1)} %get-tuple-element.343.refs_3_, ...), custom_call_target="tpu_custom_call" | custom-call | flops 1 | bytes 1 | tf_op jit(solution)/shard_map/pallas_call | solution.py:68
  718.6 30.8 %shard_map.261 = (f32[256,2304]{1,0:T(8,128)}, f32[256,2304]{1,0:T(8,128)}) custom-call(s32[3]{0:T(128)} %pad_add_fusion._.scalar_ref, bf16[256,4608]{1,0:T(8,128)(2,1)} %get-tuple-element.312.refs_2_.refs_0_, bf16[256,4608]{1,0:T(8,128)(2,1)} %get-tuple-element.284.refs_3_.refs_1_, bf16[256,4608]{1,0:T(8,128)(2,1)} %get-tuple-element.342.refs_2_, ...), custom_call_target="tpu_custom_call" | custom-call | flops 1 | bytes 1 | tf_op jit(solution)/shard_map/pallas_call | solution.py:68
  752.9 14.2 %shard_map.262 = (f32[512,2304]{1,0:T(8,128)}, bf16[256,2304]{1,0:T(8,128)(2,1)}, bf16[256,2304]{1,0:T(8,128)(2,1)}, f32[1,2304]{1,0:T(1,128)}, f32[1,2304]{1,0:T(1,128)}) custom-call(s32[3]{0:T(128)} %pad_add_fusion._.scalar_ref, f32[256,2304]{1,0:T(8,128)} %get-tuple-element.322.refs_0_, bf16[256,2304]{1,0:T(8,128)(2,1)} %copy-done.29, ...), custom_call_target="tpu_custom_call" | custom-call | flops 1 | bytes 1 | tf_op jit(solution)/shard_map/pallas_call | solution.py:68
  852.2 10.4 shard_map.269.d_ref
  868.4 18.2 %shard_map.271 = (bf16[1024,1024]{1,0:T(8,128)(2,1)}, bf16[1024,1024]{1,0:T(8,128)(2,1)}) custom-call(s32[3]{0:T(128)} %pad_add_fusion._.scalar_ref, bf16[1024,2048]{1,0:T(8,128)(2,1)} %shard_map.231.query_ref.key_ref.value_ref.pair_ref, bf16[1024,2048]{1,0:T(8,128)(2,1)} %shard_map.231.query_ref.key_ref.value_ref.pair_ref, bf16[1024,1024]{1,0:T(8,128)(2,1)} %shard_map.269.d_ref), custom_call_target="tpu_custom_call" | custom-call | flops 1 | bytes 1 | tf_op jit(solution)/shard_map/pallas_call | solution.py:68
  919.1 12.1 %shard_map.276 = (bf16[256,2304]{1,0:T(8,128)(2,1)}, bf16[256,2304]{1,0:T(8,128)(2,1)}) custom-call(s32[3]{0:T(128)} %pad_add_fusion._.scalar_ref, bf16[1024,1024]{1,0:T(8,128)(2,1)} %get-tuple-element.394.refs_2_.refs_3_.refs_0_, bf16[1024,1024]{1,0:T(8,128)(2,1)} %get-tuple-element.375.refs_2_.refs_3_.refs_1_, ...), custom_call_target="tpu_custom_call" | custom-call | flops 1 | bytes 1 | tf_op jit(solution)/shard_map/pallas_call | solution.py:68
  958.4 12.5 %shard_map.281 = (f32[256,2304]{1,0:T(8,128)}, f32[256,2304]{1,0:T(8,128)}) custom-call(s32[3]{0:T(128)} %pad_add_fusion._.scalar_ref, bf16[1024,1024]{1,0:T(8,128)(2,1)} %get-tuple-element.394.refs_2_.refs_3_.refs_0_, bf16[1024,1024]{1,0:T(8,128)(2,1)} %get-tuple-element.375.refs_2_.refs_3_.refs_1_, ...), custom_call_target="tpu_custom_call" | custom-call | flops 1 | bytes 1 | tf_op jit(solution)/shard_map/pallas_call | solution.py:68
  984.7 19.8 %collective-permute-done.40.refs_5_ = bf16[4,144,1024]{2,1,0:T(8,128)(2,1)S(1)} collective-permute-done((bf16[4,144,1024]{2,1,0:T(8,128)(2,1)S(1)}, bf16[4,144,1024]{2,1,0:T(8,128)(2,1)S(1)}, u32[]{:S(2)}, u32[]{:S(2)}) %collective-permute-start.40) | collective-permute-done | bytes 1179680 | tf_op jit(solution)/shard_map/ppermute | solution.py:30
  1017.3 11.2 %shard_map.284 = (f32[512,2304]{1,0:T(8,128)}, f32[1,2304]{1,0:T(1,128)}) custom-call(s32[3]{0:T(128)} %pad_add_fusion._.scalar_ref, f32[256,2304]{1,0:T(8,128)} %get-tuple-element.406.refs_0_, bf16[256,2304]{1,0:T(8,128)(2,1)} %collective-permute-done.39.refs_1_, f32[256,2304]{1,0:T(8,128)} %get-tuple-element.408.refs_2_, ...), custom_call_target="tpu_custom_call" | custom-call | flops 1 | bytes 1 | tf_op jit(solution)/shard_map/pallas_call | solution.py:68
  1052.6 26.0 %all-to-all-start = ((f32[32,4,72]{2,1,0:T(4,128)}), f32[32,4,72]{2,1,0:T(4,128)}, u32[]{:S(2)}, u32[]{:S(2)}) async-start(f32[32,4,72]{2,1,0:T(4,128)} %maximum_bitcast_fusion.1), calls=%async_computation.8 | async-start | bytes 131072 | tf_op jit(solution)/shard_map/all_to_all | solution.py:725
  1092.3 11.1 collective-permute-done.47
  (318 shorter events, 414.3 us)
Async XLA Ops:
  7.2 183.4 %all-gather.4.cloned.1.call-start = ((), (), s32[]{:S(2)}) async-start(), calls=%async_computation.9 | async-start | bytes 37601280 | tf_op jit(solution)/shard_map/all_gather | solution.py:757
  10.4 291.9 %all-gather.6.cloned.1.call-start = ((), (), s32[]{:S(2)}) async-start(), calls=%async_computation.10 | async-start | bytes 22560768 | tf_op jit(solution)/shard_map/all_gather | solution.py:763
  11.2 402.8 %all-gather.8.cloned.1.call-start = ((), (), s32[]{:S(2)}) async-start(), calls=%async_computation.11 | async-start | bytes 22560768 | tf_op jit(solution)/shard_map/all_gather | solution.py:764
  11.9 674.0 %reduce-scatter.9.cloned.1.call-start = ((), (), s32[]{:S(2)}) async-start(), calls=%async_computation.12 | async-start | bytes 1474560 | tf_op jit(solution)/shard_map/reduce_scatter | solution.py:471
  33.5 51.3 %collective-permute-start.5 = (bf16[512,2304]{1,0:T(8,128)(2,1)}, bf16[512,2304]{1,0:T(8,128)(2,1)}, u32[]{:S(2)}, u32[]{:S(2)}) collective-permute-start(bf16[512,2304]{1,0:T(8,128)(2,1)} %fusion.2.refs_0_), channel_id=1, source_target_pairs={{0,1},{1,0},{2,3},{3,2},{4,5},{5,4},{6,7},{7,6},{8,9},{9,8},{10,11... | collective-permute-start | bytes 7077896 | tf_op jit(solution)/shard_map/ppermute | solution.py:26
  227.1 53.6 %collective-permute-start.6 = (bf16[512,2304]{1,0:T(8,128)(2,1)}, bf16[512,2304]{1,0:T(8,128)(2,1)S(1)}, u32[]{:S(2)}, u32[]{:S(2)}) collective-permute-start(bf16[512,2304]{1,0:T(8,128)(2,1)} %shard_map.233), channel_id=1, source_target_pairs={{0,1},{1,0},{2,3},{3,2},{4,5},{5,4},{6,7},{7,6},{8,9},{9,8},{10,11... | collective-permute-start | bytes 7077896 | tf_op jit(solution)/shard_map/ppermute | solution.py:26
  288.2 52.8 %collective-permute-start.7 = (bf16[512,2304]{1,0:T(8,128)(2,1)S(1)}, bf16[512,2304]{1,0:T(8,128)(2,1)}, u32[]{:S(2)}, u32[]{:S(2)}) collective-permute-start(bf16[512,2304]{1,0:T(8,128)(2,1)S(1)} %multiply_convert_fusion.mid_ref.refs_0_), channel_id=1, source_target_pairs={{0,1},{1,0},{2,3},{3,2},{4,5},{5,4},{6,7},{7,6},{8,9},{9,8},{10,11... | collective-permute-start | bytes 7077896 | tf_op jit(solution)/shard_map/ppermute | solution.py:26
  491.7 49.5 %collective-permute-start.11 = (bf16[256,2304]{1,0:T(8,128)(2,1)S(1)}, bf16[256,2304]{1,0:T(8,128)(2,1)S(1)}, u32[]{:S(2)}, u32[]{:S(2)}) collective-permute-start(bf16[256,2304]{1,0:T(8,128)(2,1)S(1)} %get-tuple-element.453.refs_1_.refs_0_), channel_id=1, source_target_pairs={{0,1},{1,0},{2,3},{3,2},{4,5},{5,4},{6,7},{7,6},{8,9},{9,8},{10,11... | collective-permute-start | bytes 3538952 | tf_op jit(solution)/shard_map/ppermute | solution.py:26
  572.6 36.1 %collective-permute-start.13 = (bf16[4,144,1024]{2,1,0:T(8,128)(2,1)}, bf16[4,144,1024]{2,1,0:T(8,128)(2,1)}, u32[]{:S(2)}, u32[]{:S(2)}) collective-permute-start(bf16[4,144,1024]{2,1,0:T(8,128)(2,1)} %shard_map.248), channel_id=1, source_target_pairs={{0,4},{2,6},{4,0},{6,2},{8,12},{10,14},{12,8},{14,10},{16,20},{18,... | collective-permute-start | bytes 3538952 | tf_op jit(solution)/shard_map/ppermute | solution.py:30
  608.8 35.3 %collective-permute-start.16 = (bf16[2,144,2560]{2,1,0:T(8,128)(2,1)}, bf16[2,144,2560]{2,1,0:T(8,128)(2,1)}, u32[]{:S(2)}, u32[]{:S(2)}) collective-permute-start(bf16[2,144,2560]{2,1,0:T(8,128)(2,1)} %get-tuple-element.287), channel_id=1, source_target_pairs={{0,4},{2,6},{4,0},{6,2},{8,12},{10,14},{12,8},{14,10},{16,20},{18,... | collective-permute-start | bytes 4423688 | tf_op jit(solution)/shard_map/ppermute | solution.py:30
  644.1 33.1 %collective-permute-start.17 = (bf16[4,2,144,2560]{3,2,1,0:T(8,128)(2,1)}, bf16[4,2,144,2560]{3,2,1,0:T(8,128)(2,1)}, u32[]{:S(2)}, u32[]{:S(2)}) collective-permute-start(bf16[4,2,144,2560]{3,2,1,0:T(8,128)(2,1)} %shard_map.253), channel_id=1, source_target_pairs={{0,2},{2,0},{4,6},{6,4},{8,10},{10,8},{12,14},{14,12},{16,18},{18,... | collective-permute-start | bytes 17694728 | tf_op jit(solution)/shard_map/ppermute | solution.py:30
  644.3 32.8 %collective-permute-start.18 = (bf16[4,2,144,2048]{3,2,1,0:T(8,128)(2,1)}, bf16[4,2,144,2048]{3,2,1,0:T(8,128)(2,1)}, u32[]{:S(2)}, u32[]{:S(2)}) collective-permute-start(bf16[4,2,144,2048]{3,2,1,0:T(8,128)(2,1)} %shard_map.255), channel_id=1, source_target_pairs={{0,2},{2,0},{4,6},{6,4},{8,10},{10,8},{12,14},{14,12},{16,18},{18,... | collective-permute-start | bytes 14155784 | tf_op jit(solution)/shard_map/ppermute | solution.py:30
  644.7 107.4 %reduce-scatter.11.cloned.1.call-start = ((), (), s32[]{:S(2)}) async-start(), calls=%async_computation.13 | async-start | bytes 2949120 | tf_op jit(solution)/shard_map/reduce_scatter | solution.py:471
  644.7 41.1 %collective-permute-start.19 = (bf16[2,144,2560]{2,1,0:T(8,128)(2,1)S(1)}, bf16[2,144,2560]{2,1,0:T(8,128)(2,1)S(1)}, u32[]{:S(2)}, u32[]{:S(2)}) collective-permute-start(bf16[2,144,2560]{2,1,0:T(8,128)(2,1)S(1)} %copy-done.48), channel_id=1, source_target_pairs={{0,4},{2,6},{4,0},{6,2},{8,12},{10,14},{12,8},{14,10},{16,20},{18,... | collective-permute-start | bytes 4423688 | tf_op jit(solution)/shard_map/ppermute | solution.py:30
  685.9 124.2 %reduce-scatter.13.cloned.1.call-start = ((), (), s32[]{:S(2)}) async-start(), calls=%async_computation.14 | async-start | bytes 3686400 | tf_op jit(solution)/shard_map/reduce_scatter | solution.py:471
  686.0 63.5 %collective-permute-start.20 = (bf16[2,144,2560]{2,1,0:T(8,128)(2,1)}, bf16[2,144,2560]{2,1,0:T(8,128)(2,1)}, u32[]{:S(2)}, u32[]{:S(2)}) collective-permute-start(bf16[2,144,2560]{2,1,0:T(8,128)(2,1)} %get-tuple-element.314), channel_id=1, source_target_pairs={{0,4},{2,6},{4,0},{6,2},{8,12},{10,14},{12,8},{14,10},{16,20},{18,... | collective-permute-start | bytes 4423688 | tf_op jit(solution)/shard_map/ppermute | solution.py:30
  686.8 65.3 %collective-permute-start.21 = (bf16[2,144,2560]{2,1,0:T(8,128)(2,1)}, bf16[2,144,2560]{2,1,0:T(8,128)(2,1)}, u32[]{:S(2)}, u32[]{:S(2)}) collective-permute-start(bf16[2,144,2560]{2,1,0:T(8,128)(2,1)} %get-tuple-element.316), channel_id=1, source_target_pairs={{0,4},{2,6},{4,0},{6,2},{8,12},{10,14},{12,8},{14,10},{16,20},{18,... | collective-permute-start | bytes 4423688 | tf_op jit(solution)/shard_map/ppermute | solution.py:30
  688.1 61.4 %collective-permute-start.22 = (bf16[256,2304]{1,0:T(8,128)(2,1)}, bf16[256,2304]{1,0:T(8,128)(2,1)S(1)}, u32[]{:S(2)}, u32[]{:S(2)}) collective-permute-start(bf16[256,2304]{1,0:T(8,128)(2,1)} %get-tuple-element.317), channel_id=1, source_target_pairs={{0,1},{1,0},{2,3},{3,2},{4,5},{5,4},{6,7},{7,6},{8,9},{9,8},{10,11... | collective-permute-start | bytes 3538952 | tf_op jit(solution)/shard_map/ppermute | solution.py:26
  688.6 60.9 %collective-permute-start.23 = (bf16[256,2304]{1,0:T(8,128)(2,1)}, bf16[256,2304]{1,0:T(8,128)(2,1)}, u32[]{:S(2)}, u32[]{:S(2)}) collective-permute-start(bf16[256,2304]{1,0:T(8,128)(2,1)} %get-tuple-element.319), channel_id=1, source_target_pairs={{0,1},{1,0},{2,3},{3,2},{4,5},{5,4},{6,7},{7,6},{8,9},{9,8},{10,11... | collective-permute-start | bytes 3538952 | tf_op jit(solution)/shard_map/ppermute | solution.py:26
  752.1 134.5 %reduce-scatter.15.cloned.1.call-start = ((), (), s32[]{:S(2)}) async-start(), calls=%async_computation.15 | async-start | bytes 3686400 | tf_op jit(solution)/shard_map/reduce_scatter | solution.py:471
  781.8 34.3 %collective-permute-start.26 = (bf16[2,144,2048]{2,1,0:T(8,128)(2,1)}, bf16[2,144,2048]{2,1,0:T(8,128)(2,1)}, u32[]{:S(2)}, u32[]{:S(2)}) collective-permute-start(bf16[2,144,2048]{2,1,0:T(8,128)(2,1)} %get-tuple-element.334), channel_id=1, source_target_pairs={{0,4},{2,6},{4,0},{6,2},{8,12},{10,14},{12,8},{14,10},{16,20},{18,... | collective-permute-start | bytes 3538952 | tf_op jit(solution)/shard_map/ppermute | solution.py:30
  782.6 33.6 %collective-permute-start.27 = (bf16[256,2304]{1,0:T(8,128)(2,1)S(1)}, bf16[256,2304]{1,0:T(8,128)(2,1)S(1)}, u32[]{:S(2)}, u32[]{:S(2)}) collective-permute-start(bf16[256,2304]{1,0:T(8,128)(2,1)S(1)} %copy-done.15), channel_id=1, source_target_pairs={{0,1},{1,0},{2,3},{3,2},{4,5},{5,4},{6,7},{7,6},{8,9},{9,8},{10,11... | collective-permute-start | bytes 3538952 | tf_op jit(solution)/shard_map/ppermute | solution.py:26
  783.7 32.5 %collective-permute-start.28 = (bf16[144,1024]{1,0:T(8,128)(2,1)}, bf16[144,1024]{1,0:T(8,128)(2,1)}, u32[]{:S(2)}, u32[]{:S(2)}) collective-permute-start(bf16[144,1024]{1,0:T(8,128)(2,1)} %dynamic-slice_bitcast_fusion.6), channel_id=1, source_target_pairs={{0,4},{2,6},{4,0},{6,2},{8,12},{10,14},{12,8},{14,10},{16,20},{18,... | collective-permute-start | bytes 884744 | tf_op jit(solution)/shard_map/ppermute | solution.py:30
  816.2 131.6 %reduce-scatter.17.cloned.1.call-start = ((), (), s32[]{:S(2)}) async-start(), calls=%async_computation.16 | async-start | bytes 2949120 | tf_op jit(solution)/shard_map/reduce_scatter | solution.py:471
  816.3 35.0 %collective-permute-start.29 = (bf16[2,144,2560]{2,1,0:T(8,128)(2,1)}, bf16[2,144,2560]{2,1,0:T(8,128)(2,1)}, u32[]{:S(2)}, u32[]{:S(2)}) collective-permute-start(bf16[2,144,2560]{2,1,0:T(8,128)(2,1)} %get-tuple-element.349), channel_id=1, source_target_pairs={{0,4},{2,6},{4,0},{6,2},{8,12},{10,14},{12,8},{14,10},{16,20},{18,... | collective-permute-start | bytes 4423688 | tf_op jit(solution)/shard_map/ppermute | solution.py:30
  851.4 154.4 %reduce-scatter.19.cloned.1.call-start = ((), (), s32[]{:S(2)}) async-start(), calls=%async_computation.17 | async-start | bytes 3686400 | tf_op jit(solution)/shard_map/reduce_scatter | solution.py:471
  851.4 35.1 %collective-permute-start.32 = (bf16[2,144,2560]{2,1,0:T(8,128)(2,1)}, bf16[2,144,2560]{2,1,0:T(8,128)(2,1)S(1)}, u32[]{:S(2)}, u32[]{:S(2)}) collective-permute-start(bf16[2,144,2560]{2,1,0:T(8,128)(2,1)} %get-tuple-element.365), channel_id=1, source_target_pairs={{0,4},{2,6},{4,0},{6,2},{8,12},{10,14},{12,8},{14,10},{16,20},{18,... | collective-permute-start | bytes 4423688 | tf_op jit(solution)/shard_map/ppermute | solution.py:30
  886.6 30.5 %collective-permute-start.33 = (bf16[2,144,2048]{2,1,0:T(8,128)(2,1)S(1)}, bf16[2,144,2048]{2,1,0:T(8,128)(2,1)}, u32[]{:S(2)}, u32[]{:S(2)}) collective-permute-start(bf16[2,144,2048]{2,1,0:T(8,128)(2,1)S(1)} %copy-done.49), channel_id=1, source_target_pairs={{0,4},{2,6},{4,0},{6,2},{8,12},{10,14},{12,8},{14,10},{16,20},{18,... | collective-permute-start | bytes 3538952 | tf_op jit(solution)/shard_map/ppermute | solution.py:30
  917.1 135.5 %reduce-scatter.21.cloned.1.call-start = ((), (), s32[]{:S(2)}) async-start(), calls=%async_computation.18 | async-start | bytes 2949120 | tf_op jit(solution)/shard_map/reduce_scatter | solution.py:471
  918.0 29.8 %collective-permute-start.34 = (bf16[2,144,2048]{2,1,0:T(8,128)(2,1)}, bf16[2,144,2048]{2,1,0:T(8,128)(2,1)S(1)}, u32[]{:S(2)}, u32[]{:S(2)}) collective-permute-start(bf16[2,144,2048]{2,1,0:T(8,128)(2,1)} %get-tuple-element.379), channel_id=1, source_target_pairs={{0,4},{2,6},{4,0},{6,2},{8,12},{10,14},{12,8},{14,10},{16,20},{18,... | collective-permute-start | bytes 3538952 | tf_op jit(solution)/shard_map/ppermute | solution.py:30
  977.3 131.3 %reduce-scatter.23.cloned.1.call-start = ((), (), s32[]{:S(2)}) async-start(), calls=%async_computation.19 | async-start | bytes 1474560 | tf_op jit(solution)/shard_map/reduce_scatter | solution.py:471
  1052.6 38.2 %all-to-all-start = ((f32[32,4,72]{2,1,0:T(4,128)}), f32[32,4,72]{2,1,0:T(4,128)}, u32[]{:S(2)}, u32[]{:S(2)}) async-start(f32[32,4,72]{2,1,0:T(4,128)} %maximum_bitcast_fusion.1), calls=%async_computation.8 | async-start | bytes 131072 | tf_op jit(solution)/shard_map/all_to_all | solution.py:725
  (81 other events, 1009.0 us)
Sparse Core Ops, SparseCore 0:
  10.5 180.0 all-gather.3
  192.2 110.0 all-gather.5
  303.9 110.0 all-gather.7
  644.8 28.3 reduce-scatter.8
  686.1 47.2 reduce-scatter.10
  752.2 56.6 reduce-scatter.12
  816.3 56.4 reduce-scatter.14
  875.2 47.9 reduce-scatter.16
  925.5 56.6 reduce-scatter.18
  984.5 47.9 reduce-scatter.20
  1046.1 31.8 reduce-scatter.22
